TPU v7x, 32 devices: a whole 2x2x4 slice. The times are simulated.
32 devices in a mesh: dp: 8 (over y, x, core), seq: 4 (over z).
Axes of the slice: x: 2, y: 2, z: 4, core: 2. Of those that a mesh axis runs over, the one named last changes fastest.
Arguments:
- inputs: bfloat16 [8, 1024, 1024], P('dp', 'seq'), may hold values from -6 to 6
- noise_buckets: int32 [8], P('dp'), may hold values from 0 to 255
- first_gain: bfloat16 [2, 1024], P(None, 'dp'), may hold values from 0.5 to 1.5
- first_shift: bfloat16 [2, 1024], P(None, 'dp'), may hold values from -1 to 1
- attention_in: bfloat16 [2, 1024, 3072], P(None, 'dp'), may hold values from -0.1875 to 0.1875
- attention_out: bfloat16 [2, 1024, 1024], P(None, 'dp'), may hold values from -1.5 to 1.5
- attention_bias: bfloat16 [2, 1024], P(None, 'dp'), may hold values from -1 to 1
- second_gain: bfloat16 [2, 1024], P(None, 'dp'), may hold values from 0.5 to 1.5
- second_shift: bfloat16 [2, 1024], P(None, 'dp'), may hold values from -1 to 1
- expand_weight: bfloat16 [2, 1024, 4096], P(None, 'dp'), may hold values from -0.1875 to 0.1875
- expand_bias: bfloat16 [2, 4096], P(None, 'dp'), may hold values from -1 to 1
- reduce_weight: bfloat16 [2, 4096, 1024], P(None, 'dp'), may hold values from -0.09375 to 0.09375
- reduce_bias: bfloat16 [2, 1024], P(None, 'dp'), may hold values from -1 to 1
- time_table: bfloat16 [2, 256, 1024], P(None, 'dp'), may hold values from -1.5 to 1.5
- cotangent: bfloat16 [8, 1024, 1024], P('dp', 'seq'), may hold values from -6 to 6
Outputs:
- outputs: bfloat16 [8, 1024, 1024], P('dp', 'seq')
- input_grad: float32 [8, 1024, 1024], P('dp', 'seq')
- first_gain_grad: float32 [2, 1024], P(None, ('dp', 'seq'))
- first_shift_grad: float32 [2, 1024], P(None, ('dp', 'seq'))
- attention_in_grad: float32 [2, 1024, 3072], P(None, ('dp', 'seq'))
- attention_out_grad: float32 [2, 1024, 1024], P(None, ('dp', 'seq'))
- attention_bias_grad: float32 [2, 1024], P(None, ('dp', 'seq'))
- second_gain_grad: float32 [2, 1024], P(None, ('dp', 'seq'))
- second_shift_grad: float32 [2, 1024], P(None, ('dp', 'seq'))
- expand_weight_grad: float32 [2, 1024, 4096], P(None, ('dp', 'seq'))
- expand_bias_grad: float32 [2, 4096], P(None, ('dp', 'seq'))
- reduce_weight_grad: float32 [2, 4096, 1024], P(None, ('dp', 'seq'))
- reduce_bias_grad: float32 [2, 1024], P(None, ('dp', 'seq'))
- time_table_grad: float32 [2, 256, 1024], P(None, ('dp', 'seq'))
All inputs are finite; a program needn't handle non-finite values.
Results may differ from a plain program's by a relative error of at most 0.024.
Values may be sent and summed in bfloat16 or wider, within the bound.
No kernel may reach another device: no remote copies, remote signals or barrier semaphores. Data moves between devices by JAX's collectives and lax.ppermute only.
A program may use at most 384 MiB of HBM per device.

v0:
```python
import math

import jax
import jax.numpy as jnp
from jax import lax
from jax.sharding import PartitionSpec as P

HEAD = 64
BUCKETS = 256


highest = lax.Precision.HIGHEST
epsilon = 1e-05


def modulated_norm(activations, norm_gain, norm_shift, scaling):
    center = activations - jnp.mean(activations, axis=-1, keepdims=True)
    spread = jnp.mean(center * center, axis=-1, keepdims=True)
    return (center * lax.rsqrt(spread + epsilon) * norm_gain + norm_shift) * (1.0 + scaling)


def head_scale(per_head):
    return jnp.repeat(jnp.swapaxes(per_head, 1, 2), HEAD, axis=-1)


def attend_forward(queries, key_values):
    seq_count, local_len, model_width = queries.shape
    head_count = model_width // HEAD
    query_heads = queries.reshape(seq_count, local_len, head_count, HEAD)
    factor = 1.0 / math.sqrt(HEAD)
    key_block = lax.all_gather(key_values, "seq", axis=1, tiled=True)
    running_max = jnp.full((seq_count, head_count, local_len), -1e30, jnp.float32)
    running_out = jnp.zeros((seq_count, local_len, model_width), jnp.float32)
    block_len = key_block.shape[1]
    key_heads = key_block[..., :model_width].reshape(seq_count, block_len, head_count, HEAD)
    value_heads = key_block[..., model_width:].reshape(seq_count, block_len, head_count, HEAD)
    scores = (
        jnp.einsum("sqhd,skhd->shqk", query_heads, key_heads, preferred_element_type=jnp.float32)
        * factor
    )
    new_max = jnp.maximum(running_max, jnp.max(scores, axis=-1))
    exponent = jnp.exp(scores - new_max[..., None])
    fading = jnp.exp(running_max - new_max)
    running_sum = jnp.sum(exponent, axis=-1)
    update = jnp.einsum(
        "shqk,skhd->sqhd",
        exponent.astype(jnp.bfloat16),
        value_heads,
        preferred_element_type=jnp.float32,
    ).reshape(seq_count, local_len, model_width)
    running_out = running_out * head_scale(fading) + update
    running_max, running_sum, running_out = (new_max, running_sum, running_out)
    return (running_out / head_scale(running_sum)).astype(jnp.bfloat16)


def layer_forward(stream, weights, selector):
    (
        first_gain,
        first_shift,
        attention_in,
        attention_out,
        attention_bias,
        second_gain,
        second_shift,
        expand_weight,
        expand_bias,
        reduce_weight,
        reduce_bias,
        table_rows,
    ) = weights
    seq_count, local_len, model_width = stream.shape
    row_total = seq_count * local_len
    scaling = jnp.dot(selector, table_rows.astype(jnp.float32), precision=highest)[:, None, :]
    normed = modulated_norm(
        stream, first_gain.astype(jnp.float32), first_shift.astype(jnp.float32), scaling
    )
    normed = normed.astype(jnp.bfloat16).reshape(row_total, model_width)
    project = jnp.dot(normed, attention_in, preferred_element_type=jnp.float32).astype(jnp.bfloat16)
    project = project.reshape(seq_count, local_len, 3 * model_width)
    mixture = attend_forward(project[..., :model_width], project[..., model_width:])
    branch = jnp.dot(
        mixture.reshape(row_total, model_width), attention_out, preferred_element_type=jnp.float32
    )
    middle = stream + (branch + attention_bias.astype(jnp.float32)).reshape(stream.shape)
    second = modulated_norm(
        middle, second_gain.astype(jnp.float32), second_shift.astype(jnp.float32), scaling
    )
    second = second.astype(jnp.bfloat16).reshape(row_total, model_width)
    hidden = jnp.dot(
        second, expand_weight, preferred_element_type=jnp.float32
    ) + expand_bias.astype(jnp.float32)
    active = jax.nn.gelu(hidden).astype(jnp.bfloat16)
    result = jnp.dot(
        active, reduce_weight, preferred_element_type=jnp.float32
    ) + reduce_bias.astype(jnp.float32)
    return middle + result.reshape(stream.shape)


def layer_backward(stream, weights, selector, grad_out):
    (
        first_gain,
        first_shift,
        attention_in,
        attention_out,
        attention_bias,
        second_gain,
        second_shift,
        expand_weight,
        expand_bias,
        reduce_weight,
        reduce_bias,
        table_rows,
    ) = weights
    seq_count, local_len, model_width = stream.shape
    row_total = seq_count * local_len
    head_count = model_width // HEAD
    factor = 1.0 / math.sqrt(HEAD)
    scaling = jnp.dot(selector, table_rows.astype(jnp.float32), precision=highest)[:, None, :]
    normed_full, first_back = jax.vjp(
        modulated_norm,
        stream,
        first_gain.astype(jnp.float32),
        first_shift.astype(jnp.float32),
        scaling,
    )
    normed = normed_full.astype(jnp.bfloat16).reshape(row_total, model_width)
    project = jnp.dot(normed, attention_in, preferred_element_type=jnp.float32).astype(jnp.bfloat16)
    project = project.reshape(seq_count, local_len, 3 * model_width)
    query_heads = project[..., :model_width].reshape(seq_count, local_len, head_count, HEAD)
    whole = lax.all_gather(project[..., model_width:], "seq", axis=1, tiled=True)
    seq_len = whole.shape[1]
    key_heads = whole[..., :model_width].reshape(seq_count, seq_len, head_count, HEAD)
    value_heads = whole[..., model_width:].reshape(seq_count, seq_len, head_count, HEAD)
    scores = (
        jnp.einsum("sqhd,skhd->shqk", query_heads, key_heads, preferred_element_type=jnp.float32)
        * factor
    )
    exponent = jnp.exp(scores - jnp.max(scores, axis=-1, keepdims=True))
    softmax_probs = exponent / jnp.sum(exponent, axis=-1, keepdims=True)
    probs_low = softmax_probs.astype(jnp.bfloat16)
    mixture = jnp.einsum(
        "shqk,skhd->sqhd", probs_low, value_heads, preferred_element_type=jnp.float32
    )
    mixture = mixture.reshape(row_total, model_width).astype(jnp.bfloat16)
    branch = jnp.dot(
        mixture, attention_out, preferred_element_type=jnp.float32
    ) + attention_bias.astype(jnp.float32)
    middle = stream + branch.reshape(stream.shape)
    second_full, second_back = jax.vjp(
        modulated_norm,
        middle,
        second_gain.astype(jnp.float32),
        second_shift.astype(jnp.float32),
        scaling,
    )
    second = second_full.astype(jnp.bfloat16).reshape(row_total, model_width)
    hidden = jnp.dot(
        second, expand_weight, preferred_element_type=jnp.float32
    ) + expand_bias.astype(jnp.float32)
    active_full, gelu_back = jax.vjp(jax.nn.gelu, hidden)
    active = active_full.astype(jnp.bfloat16)
    grad_rows = grad_out.reshape(row_total, model_width)
    grad_low = grad_rows.astype(jnp.bfloat16)
    reduce_bias_grad = jnp.sum(grad_rows, axis=0)
    reduce_weight_grad = jnp.einsum(
        "rf,rd->fd", active, grad_low, preferred_element_type=jnp.float32
    )
    active_grad = jnp.einsum(
        "rd,fd->rf", grad_low, reduce_weight, preferred_element_type=jnp.float32
    )
    hidden_grad = gelu_back(active_grad)[0]
    expand_bias_grad = jnp.sum(hidden_grad, axis=0)
    hidden_low = hidden_grad.astype(jnp.bfloat16)
    expand_weight_grad = jnp.einsum(
        "rd,rf->df", second, hidden_low, preferred_element_type=jnp.float32
    )
    second_grad = jnp.einsum(
        "rf,df->rd", hidden_low, expand_weight, preferred_element_type=jnp.float32
    )
    middle_part, second_gain_grad, second_shift_grad, second_scaling_grad = second_back(
        second_grad.reshape(stream.shape)
    )
    middle_grad = grad_out + middle_part
    middle_rows = middle_grad.reshape(row_total, model_width)
    attention_bias_grad = jnp.sum(middle_rows, axis=0)
    middle_low = middle_rows.astype(jnp.bfloat16)
    attention_out_grad = jnp.einsum(
        "rd,re->de", mixture, middle_low, preferred_element_type=jnp.float32
    )
    mixture_grad = jnp.einsum(
        "re,de->rd", middle_low, attention_out, preferred_element_type=jnp.float32
    )
    mixture_grad = mixture_grad.astype(jnp.bfloat16).reshape(seq_count, local_len, head_count, HEAD)
    prob_grad = jnp.einsum(
        "sqhd,skhd->shqk", mixture_grad, value_heads, preferred_element_type=jnp.float32
    )
    along = jnp.sum(softmax_probs * prob_grad, axis=-1, keepdims=True)
    score_grad = (softmax_probs * (prob_grad - along)).astype(jnp.bfloat16)
    query_grad = (
        jnp.einsum("shqk,skhd->sqhd", score_grad, key_heads, preferred_element_type=jnp.float32)
        * factor
    )
    query_grad = query_grad.astype(jnp.bfloat16).reshape(seq_count, local_len, model_width)
    block_len = local_len * lax.axis_size("seq")
    key_part = (
        jnp.einsum("shqk,sqhd->kshd", score_grad, query_heads, preferred_element_type=jnp.float32)
        * factor
    )
    value_part = jnp.einsum(
        "shqk,sqhd->kshd", probs_low, mixture_grad, preferred_element_type=jnp.float32
    )
    key_value_grad = lax.psum_scatter(
        jnp.concatenate(
            [
                key_part.reshape(block_len, seq_count, model_width),
                value_part.reshape(block_len, seq_count, model_width),
            ],
            axis=-1,
        ).astype(jnp.bfloat16),
        "seq",
        scatter_dimension=0,
        tiled=True,
    )
    key_value_low = jnp.swapaxes(key_value_grad, 0, 1)
    project_grad = jnp.concatenate([query_grad, key_value_low], axis=-1).reshape(
        row_total, 3 * model_width
    )
    attention_in_grad = jnp.einsum(
        "rd,re->de", normed, project_grad, preferred_element_type=jnp.float32
    )
    normed_grad = jnp.einsum(
        "re,de->rd", project_grad, attention_in, preferred_element_type=jnp.float32
    )
    stream_part, first_gain_grad, first_shift_grad, first_scaling_grad = first_back(
        normed_grad.reshape(stream.shape)
    )
    stream_grad = middle_grad + stream_part
    table_grad = jnp.dot(
        selector.T, (first_scaling_grad + second_scaling_grad)[:, 0, :], precision=highest
    )
    return (
        stream_grad,
        (
            first_gain_grad,
            first_shift_grad,
            attention_in_grad,
            attention_out_grad,
            attention_bias_grad,
            second_gain_grad,
            second_shift_grad,
            expand_weight_grad,
            expand_bias_grad,
            reduce_weight_grad,
            reduce_bias_grad,
            table_grad,
        ),
    )


def on_device(
    inputs,
    noise_buckets,
    first_gain,
    first_shift,
    attention_in,
    attention_out,
    attention_bias,
    second_gain,
    second_shift,
    expand_weight,
    expand_bias,
    reduce_weight,
    reduce_bias,
    time_table,
    cotangent,
):
    layers = first_gain.shape[0]
    selector = (noise_buckets[:, None] == jnp.arange(BUCKETS, dtype=jnp.int32)[None, :]).astype(
        jnp.float32
    )
    stream = inputs.astype(jnp.float32)
    kept_inputs = []
    for layer_index in range(layers):
        gathered = (
            lax.all_gather(first_gain[layer_index], "dp", axis=0, tiled=True),
            lax.all_gather(first_shift[layer_index], "dp", axis=0, tiled=True),
            lax.all_gather(attention_in[layer_index], "dp", axis=0, tiled=True),
            lax.all_gather(attention_out[layer_index], "dp", axis=0, tiled=True),
            lax.all_gather(attention_bias[layer_index], "dp", axis=0, tiled=True),
            lax.all_gather(second_gain[layer_index], "dp", axis=0, tiled=True),
            lax.all_gather(second_shift[layer_index], "dp", axis=0, tiled=True),
            lax.all_gather(expand_weight[layer_index], "dp", axis=0, tiled=True),
            lax.all_gather(expand_bias[layer_index], "dp", axis=0, tiled=True),
            lax.all_gather(reduce_weight[layer_index], "dp", axis=0, tiled=True),
            lax.all_gather(reduce_bias[layer_index], "dp", axis=0, tiled=True),
            lax.all_gather(time_table[layer_index], "dp", axis=0, tiled=True),
        )
        kept_inputs.append(stream)
        stream = layer_forward(stream, gathered, selector)
    outputs = stream.astype(jnp.bfloat16)
    grad_flow = cotangent.astype(jnp.float32)
    shares = [None] * layers
    for layer_index in reversed(range(layers)):
        gathered = (
            lax.all_gather(first_gain[layer_index], "dp", axis=0, tiled=True),
            lax.all_gather(first_shift[layer_index], "dp", axis=0, tiled=True),
            lax.all_gather(attention_in[layer_index], "dp", axis=0, tiled=True),
            lax.all_gather(attention_out[layer_index], "dp", axis=0, tiled=True),
            lax.all_gather(attention_bias[layer_index], "dp", axis=0, tiled=True),
            lax.all_gather(second_gain[layer_index], "dp", axis=0, tiled=True),
            lax.all_gather(second_shift[layer_index], "dp", axis=0, tiled=True),
            lax.all_gather(expand_weight[layer_index], "dp", axis=0, tiled=True),
            lax.all_gather(expand_bias[layer_index], "dp", axis=0, tiled=True),
            lax.all_gather(reduce_weight[layer_index], "dp", axis=0, tiled=True),
            lax.all_gather(reduce_bias[layer_index], "dp", axis=0, tiled=True),
            lax.all_gather(time_table[layer_index], "dp", axis=0, tiled=True),
        )
        grad_flow, gradients = layer_backward(
            kept_inputs[layer_index], gathered, selector, grad_flow
        )
        shares[layer_index] = (
            lax.psum_scatter(gradients[0], ("dp", "seq"), scatter_dimension=0, tiled=True),
            lax.psum_scatter(gradients[1], ("dp", "seq"), scatter_dimension=0, tiled=True),
            lax.psum_scatter(gradients[2], ("dp", "seq"), scatter_dimension=0, tiled=True),
            lax.psum_scatter(gradients[3], ("dp", "seq"), scatter_dimension=0, tiled=True),
            lax.psum_scatter(gradients[4], ("dp", "seq"), scatter_dimension=0, tiled=True),
            lax.psum_scatter(gradients[5], ("dp", "seq"), scatter_dimension=0, tiled=True),
            lax.psum_scatter(gradients[6], ("dp", "seq"), scatter_dimension=0, tiled=True),
            lax.psum_scatter(gradients[7], ("dp", "seq"), scatter_dimension=0, tiled=True),
            lax.psum_scatter(gradients[8], ("dp", "seq"), scatter_dimension=0, tiled=True),
            lax.psum_scatter(gradients[9], ("dp", "seq"), scatter_dimension=0, tiled=True),
            lax.psum_scatter(gradients[10], ("dp", "seq"), scatter_dimension=0, tiled=True),
            lax.psum_scatter(gradients[11], ("dp", "seq"), scatter_dimension=0, tiled=True),
        )
    stacked = [
        jnp.stack([shares[layer_index][member] for layer_index in range(layers)])
        for member in range(12)
    ]
    return (
        outputs,
        grad_flow,
        stacked[0],
        stacked[1],
        stacked[2],
        stacked[3],
        stacked[4],
        stacked[5],
        stacked[6],
        stacked[7],
        stacked[8],
        stacked[9],
        stacked[10],
        stacked[11],
    )


def solution(mesh):
    return jax.shard_map(
        on_device,
        mesh=mesh,
        in_specs=(
            P("dp", "seq", None),
            P("dp"),
            P(None, "dp"),
            P(None, "dp"),
            P(None, "dp", None),
            P(None, "dp", None),
            P(None, "dp"),
            P(None, "dp"),
            P(None, "dp"),
            P(None, "dp", None),
            P(None, "dp"),
            P(None, "dp", None),
            P(None, "dp"),
            P(None, "dp", None),
            P("dp", "seq", None),
        ),
        out_specs=(
            P("dp", "seq", None),
            P("dp", "seq", None),
            P(None, ("dp", "seq")),
            P(None, ("dp", "seq")),
            P(None, ("dp", "seq"), None),
            P(None, ("dp", "seq"), None),
            P(None, ("dp", "seq")),
            P(None, ("dp", "seq")),
            P(None, ("dp", "seq")),
            P(None, ("dp", "seq"), None),
            P(None, ("dp", "seq")),
            P(None, ("dp", "seq"), None),
            P(None, ("dp", "seq")),
            P(None, ("dp", "seq"), None),
        ),
        check_vma=False,
    )
```

profile of v0, /device:TPU:0, one launch (start us, length us, event | category | flops | bytes accessed | tf_op | source)
XLA Modules:
  0.0 3340.0 jit_solution(11688103889484426817)
XLA Ops:
  11.4 10.2 all-gather.1
  22.3 8.7 all-gather
  31.9 8.9 all-gather.2
  42.0 16.7 all-gather.39.cloned.1.call-done
  58.8 4.8 fusion.113
  72.2 8.7 all-gather.5
  81.4 7.8 all-gather.11
  89.2 8.9 all-gather.9
  98.1 7.8 all-gather.7
  105.9 8.7 all-gather.6
  114.7 7.8 all-gather.13
  122.4 8.7 all-gather.12
  131.1 9.1 all-gather.14
  140.7 6.3 all-gather.35.cloned.1.call-done
  164.7 7.8 fusion.7
  178.6 54.0 %all-gather.45.cloned.1.call-done = bf16[1,4096,1024]{2,1,0:T(8,128)(2,1)} async-done(((bf16[1,512,1024]{2,1,0:T(8,128)(2,1)}), bf16[1,4096,1024]{2,1,0:T(8,128)(2,1)}) %all-gather.45.cloned.1.call-update) | async-done | bytes 8388624 | tf_op jit(solution)/shard_map/all_gather | solution.py:294
  232.6 56.2 %all-gather.43.cloned.1.call-done = bf16[1,1024,4096]{2,1,0:T(8,128)(2,1)} async-done(((bf16[1,128,4096]{2,1,0:T(8,128)(2,1)}), bf16[1,1024,4096]{2,1,0:T(8,128)(2,1)}) %all-gather.43.cloned.1.call-update) | async-done | bytes 8388624 | tf_op jit(solution)/shard_map/all_gather | solution.py:292
  288.8 11.0 fusion.363
  300.1 36.5 %all-gather.47.cloned.1.call-done = bf16[1,1024,3072]{2,1,0:T(8,128)(2,1)} async-done(((bf16[1,128,3072]{2,1,0:T(8,128)(2,1)}), bf16[1,1024,3072]{2,1,0:T(8,128)(2,1)}) %all-gather.47.cloned.1.call-update) | async-done | bytes 6291472 | tf_op jit(solution)/shard_map/all_gather | solution.py:287
  336.7 4.7 fusion.110
  344.6 8.7 all-gather.17
  353.3 7.8 all-gather.19
  361.1 8.7 all-gather.18
  369.8 7.9 all-gather.21
  378.8 44.6 %all-gather.37.cloned.1.call-done = bf16[1,1024,2048]{2,1,0:T(8,128)(2,1)} async-done(((bf16[1,256,2048]{2,1,0:T(8,128)(2,1)}), bf16[1,1024,2048]{2,1,0:T(8,128)(2,1)}) %all-gather.37.cloned.1.call-update) | async-done | bytes 4194320 | tf_op jit(solution)/shard_map/all_gather | solution.py:31
  443.9 4.6 fusion.211
  455.7 52.9 %all-gather.51.cloned.1.call-done = bf16[1,1024,4096]{2,1,0:T(8,128)(2,1)} async-done(((bf16[1,128,4096]{2,1,0:T(8,128)(2,1)}), bf16[1,1024,4096]{2,1,0:T(8,128)(2,1)}) %all-gather.51.cloned.1.call-update) | async-done | bytes 8388624 | tf_op jit(solution)/shard_map/all_gather | solution.py:292
  508.6 7.8 fusion.53
  516.5 48.9 %all-gather.53.cloned.1.call-done = bf16[1,4096,1024]{2,1,0:T(8,128)(2,1)} async-done(((bf16[1,512,1024]{2,1,0:T(8,128)(2,1)}), bf16[1,4096,1024]{2,1,0:T(8,128)(2,1)}) %all-gather.53.cloned.1.call-update) | async-done | bytes 8388624 | tf_op jit(solution)/shard_map/all_gather | solution.py:294
  565.4 12.3 fusion.371
  583.9 7.9 fusion.138
  591.8 15.5 multiply_reduce_fusion.1
  607.3 12.1 multiply_convert_fusion.1
  625.2 9.5 fusion.214
  635.9 8.1 fusion.47
  647.5 54.5 %reduce-scatter.13.cloned.1.call-done = bf16[256,1,2048]{0,2,1:T(8,128)(2,1)} async-done(((bf16[1024,1,2048]{0,2,1:T(8,128)(2,1)}), bf16[256,1,2048]{0,2,1:T(8,128)(2,1)}) %reduce-scatter.13.cloned.1.call-update) | async-done | bytes 1048592 | tf_op jit(solution)/shard_map/reduce_scatter | solution.py:212
  702.1 6.3 fusion.232
  710.9 5.9 fusion.372
  725.9 8.5 fusion.141
  734.5 13.3 multiply_reduce_fusion
  747.8 12.2 multiply_convert_fusion
  776.7 7.5 fusion.210
  784.2 59.1 %reduce-scatter.15.cloned.1.call-done = bf16[256,1,2048]{0,2,1:T(8,128)(2,1)} async-done(((bf16[1024,1,2048]{0,2,1:T(8,128)(2,1)}), bf16[256,1,2048]{0,2,1:T(8,128)(2,1)}) %reduce-scatter.15.cloned.1.call-update) | async-done | bytes 1048592 | tf_op jit(solution)/shard_map/reduce_scatter | solution.py:212
  843.3 5.3 fusion.226
  853.1 8.0 fusion.247
  861.4 8.0 fusion.246
  870.1 10.2 fusion.243
  880.4 9.9 fusion.240
  890.3 10.7 fusion.117
  902.3 10.9 fusion.116
  913.8 8.7 all-gather.23
  922.5 8.3 fusion.8
  932.8 12.5 fusion.200
  945.3 48.1 %reduce-scatter.23.cloned.1.call-done = f32[32,1024]{1,0:T(8,128)} async-done(((f32[1024,1024]{1,0:T(8,128)}), f32[32,1024]{1,0:T(8,128)}) %reduce-scatter.23.cloned.1.call-update) | async-done | bytes 131088 | tf_op jit(solution)/shard_map/reduce_scatter | solution.py:325
  993.4 148.6 %reduce-scatter.21.cloned.1.call-done = f32[32,1024]{1,0:T(8,128)} async-done(((f32[1024,1024]{1,0:T(8,128)}), f32[32,1024]{1,0:T(8,128)}) %reduce-scatter.21.cloned.1.call-update) | async-done | bytes 131088 | tf_op jit(solution)/shard_map/reduce_scatter | solution.py:325
  1145.0 134.2 %all-reduce.17.cloned.1.call-done = (f32[1024]{0:T(1024)}, f32[1024]{0:T(1024)}, f32[1024]{0:T(1024)}, f32[1024]{0:T(1024)}, f32[1024]{0:T(1024)}, /*index=5*/f3...) async-done(((f32[1024]{0:T(1024)}, f32[1024]{0:T(1024)}, ...) | async-done | bytes 81936
  1288.6 129.8 %reduce-scatter.35.cloned.1.call-done = f32[8,1024]{1,0:T(8,128)} async-done(((f32[256,1024]{1,0:T(8,128)}), f32[8,1024]{1,0:T(8,128)}) %reduce-scatter.35.cloned.1.call-update) | async-done | bytes 32784 | tf_op jit(solution)/shard_map/reduce_scatter | solution.py:333
  1418.3 134.2 %reduce-scatter.33.cloned.1.call-done = f32[8,1024]{1,0:T(8,128)} async-done(((f32[256,1024]{1,0:T(8,128)}), f32[8,1024]{1,0:T(8,128)}) %reduce-scatter.33.cloned.1.call-update) | async-done | bytes 32784 | tf_op jit(solution)/shard_map/reduce_scatter | solution.py:333
  1553.9 156.4 %reduce-scatter.19.cloned.1.call-done = f32[32,3072]{1,0:T(8,128)} async-done(((f32[1024,3072]{1,0:T(8,128)}), f32[32,3072]{1,0:T(8,128)}) %reduce-scatter.19.cloned.1.call-update) | async-done | bytes 393232 | tf_op jit(solution)/shard_map/reduce_scatter | solution.py:324
  1710.3 161.5 %reduce-scatter.17.cloned.1.call-done = f32[32,3072]{1,0:T(8,128)} async-done(((f32[1024,3072]{1,0:T(8,128)}), f32[32,3072]{1,0:T(8,128)}) %reduce-scatter.17.cloned.1.call-update) | async-done | bytes 393232 | tf_op jit(solution)/shard_map/reduce_scatter | solution.py:324
  1873.9 363.4 %reduce-scatter.27.cloned.1.call-done = f32[32,4096]{1,0:T(8,128)} async-done(((f32[1024,4096]{1,0:T(8,128)}), f32[32,4096]{1,0:T(8,128)}) %reduce-scatter.27.cloned.1.call-update) | async-done | bytes 524304 | tf_op jit(solution)/shard_map/reduce_scatter | solution.py:329
  2237.3 364.5 %reduce-scatter.25.cloned.1.call-done = f32[32,4096]{1,0:T(8,128)} async-done(((f32[1024,4096]{1,0:T(8,128)}), f32[32,4096]{1,0:T(8,128)}) %reduce-scatter.25.cloned.1.call-update) | async-done | bytes 524304 | tf_op jit(solution)/shard_map/reduce_scatter | solution.py:329
  2604.1 362.2 %reduce-scatter.31.cloned.1.call-done = f32[128,1024]{1,0:T(8,128)} async-done(((f32[4096,1024]{1,0:T(8,128)}), f32[128,1024]{1,0:T(8,128)}) %reduce-scatter.31.cloned.1.call-update) | async-done | bytes 524304 | tf_op jit(solution)/shard_map/reduce_scatter | solution.py:331
  2966.3 364.5 %reduce-scatter.29.cloned.1.call-done = f32[128,1024]{1,0:T(8,128)} async-done(((f32[4096,1024]{1,0:T(8,128)}), f32[128,1024]{1,0:T(8,128)}) %reduce-scatter.29.cloned.1.call-update) | async-done | bytes 524304 | tf_op jit(solution)/shard_map/reduce_scatter | solution.py:331
  (388 shorter events, 146.0 us)
Async XLA Ops:
  7.2 33.6 %copy-start.4 = (bf16[1,256,1024]{2,1,0:T(8,128)(2,1)S(1)}, bf16[1,256,1024]{2,1,0:T(8,128)(2,1)}, u32[]{:S(2)}) copy-start(bf16[1,256,1024]{2,1,0:T(8,128)(2,1)} %param.15) | copy-start | bytes 1572868
  7.2 51.6 %all-gather.39.cloned.1.call-start = ((), (), s32[]{:S(2)}) async-start(), calls=%async_computation.26 | async-start | bytes 7077888 | tf_op jit(solution)/shard_map/all_gather | solution.py:287
  9.9 137.0 %all-gather.35.cloned.1.call-start = ((), (), s32[]{:S(2)}) async-start(), calls=%async_computation.12 | async-start | bytes 5242880 | tf_op jit(solution)/shard_map/all_gather | solution.py:31
  21.6 42.0 %copy-start.56 = (f32[1,1024]{1,0:T(1,128)}, f32[1,1024]{1,0:T(1,128)S(1)}, u32[]{:S(2)}) copy-start(f32[1,1024]{1,0:T(1,128)S(1)} %convert_element_type.309) | copy-start | bytes 12292
  31.0 32.5 copy-start.50
  41.0 17.8 copy-start.71
  41.8 16.9 copy-start.69
  42.0 246.8 %copy-start.42 = (f32[1024]{0:T(1024)}, f32[1024]{0:T(1024)S(1)}, u32[]{:S(2)}) copy-start(f32[1024]{0:T(1024)S(1)} %broadcast_add_fusion.1) | copy-start | bytes 12292
  65.8 110.1 %all-gather.41.cloned.1.call-start = ((), (), s32[]{:S(2)}) async-start(), calls=%async_computation.27 | async-start | bytes 2359296 | tf_op jit(solution)/shard_map/all_gather | solution.py:288
  66.7 165.9 %all-gather.45.cloned.1.call-start = ((), (), s32[]{:S(2)}) async-start(), calls=%async_computation.29 | async-start | bytes 9437184 | tf_op jit(solution)/shard_map/all_gather | solution.py:294
  68.3 12.6 copy-start.93
  68.3 20.9 copy-start.90
  68.3 29.8 copy-start.94
  68.3 37.6 %copy-start.95 = (bf16[2,128]{1,0:T(2,128)(2,1)S(1)}, bf16[2,128]{1,0:T(2,128)(2,1)}, u32[]{:S(2)}) copy-start(bf16[2,128]{1,0:T(2,128)(2,1)} %param.22) | copy-start | bytes 1540
  68.3 72.1 %slice-start.2 = ((bf16[1,256,3072]{2,1,0:T(8,128)(2,1)}), bf16[1,256,1024]{2,1,0:T(8,128)(2,1)S(1)}, s32[]{:S(2)}) async-start(bf16[1,256,3072]{2,1,0:T(8,128)(2,1)} %copy-done.39), calls=%async_computation.37 | async-start | bytes 1048576 | tf_op jit(solution)/shard_map/slice | solution.py:80
  68.3 220.5 %all-gather.43.cloned.1.call-start = ((), (), s32[]{:S(2)}) async-start(), calls=%async_computation.28 | async-start | bytes 9437184 | tf_op jit(solution)/shard_map/all_gather | solution.py:292
  71.6 265.1 %all-gather.47.cloned.1.call-start = ((), (), s32[]{:S(2)}) async-start(), calls=%async_computation.30 | async-start | bytes 7077888 | tf_op jit(solution)/shard_map/all_gather | solution.py:287
  72.1 351.3 %all-gather.37.cloned.1.call-start = ((), (), s32[]{:S(2)}) async-start(), calls=%async_computation.13 | async-start | bytes 5242880 | tf_op jit(solution)/shard_map/all_gather | solution.py:31
  80.9 95.0 %copy-start.60 = (f32[1,1024]{1,0:T(1,128)}, f32[1,1024]{1,0:T(1,128)S(1)}, u32[]{:S(2)}) copy-start(f32[1,1024]{1,0:T(1,128)S(1)} %convert_element_type.310) | copy-start | bytes 12292
  98.1 190.7 %copy-start.84 = (f32[1,4096]{1,0:T(1,128)}, f32[1,4096]{1,0:T(1,128)S(1)}, u32[]{:S(2)}) copy-start(f32[1,4096]{1,0:T(1,128)S(1)} %convert_element_type.313) | copy-start | bytes 49156
  105.9 182.9 %copy-start.52 = (f32[1,1024]{1,0:T(1,128)}, f32[1,1024]{1,0:T(1,128)S(1)}, u32[]{:S(2)}) copy-start(f32[1,1024]{1,0:T(1,128)S(1)} %convert_element_type.312) | copy-start | bytes 12292
  114.7 174.1 %copy-start.46 = (f32[1,1024]{1,0:T(1,128)}, f32[1,1024]{1,0:T(1,128)S(1)}, u32[]{:S(2)}) copy-start(f32[1,1024]{1,0:T(1,128)S(1)} %convert_element_type.311) | copy-start | bytes 12292
  122.4 214.2 %copy-start.64 = (f32[1,1024]{1,0:T(1,128)}, f32[1,1024]{1,0:T(1,128)S(1)}, u32[]{:S(2)}) copy-start(f32[1,1024]{1,0:T(1,128)S(1)} %convert_element_type.316) | copy-start | bytes 12292
  131.1 205.5 %copy-start.58 = (f32[1,1024]{1,0:T(1,128)}, f32[1,1024]{1,0:T(1,128)S(1)}, u32[]{:S(2)}) copy-start(f32[1,1024]{1,0:T(1,128)S(1)} %convert_element_type.315) | copy-start | bytes 12292
  140.6 15.8 copy-start.26
  299.8 41.5 %copy-start.77 = (f32[256]{0:T(256)}, f32[256]{0:T(256)S(1)}, u32[]{:S(2)}) copy-start(f32[256]{0:T(256)S(1)} %broadcast_multiply_fusion.5) | copy-start | bytes 3076
  300.1 41.3 %copy-start.88 = (f32[256]{0:T(256)}, f32[256]{0:T(256)S(1)}, u32[]{:S(2)}) copy-start(f32[256]{0:T(256)S(1)} %multiply_reduce_fusion.7) | copy-start | bytes 3076
  300.1 41.3 %copy-start.80 = (f32[256]{0:T(256)}, f32[256]{0:T(256)S(1)}, u32[]{:S(2)}) copy-start(f32[256]{0:T(256)S(1)} %fusion.303) | copy-start | bytes 3076
  342.5 109.8 %all-gather.49.cloned.1.call-start = ((), (), s32[]{:S(2)}) async-start(), calls=%async_computation.31 | async-start | bytes 2359296 | tf_op jit(solution)/shard_map/all_gather | solution.py:288
  343.2 165.4 %all-gather.51.cloned.1.call-start = ((), (), s32[]{:S(2)}) async-start(), calls=%async_computation.32 | async-start | bytes 9437184 | tf_op jit(solution)/shard_map/all_gather | solution.py:292
  344.0 221.4 %all-gather.53.cloned.1.call-start = ((), (), s32[]{:S(2)}) async-start(), calls=%async_computation.33 | async-start | bytes 9437184 | tf_op jit(solution)/shard_map/all_gather | solution.py:294
  344.5 357.5 %reduce-scatter.13.cloned.1.call-start = ((), (), s32[]{:S(2)}) async-start(), calls=%async_computation.14 | async-start | bytes 5242880 | tf_op jit(solution)/shard_map/reduce_scatter | solution.py:212
  353.3 99.0 %copy-start.62 = (f32[1,1024]{1,0:T(1,128)}, f32[1,1024]{1,0:T(1,128)S(1)}, u32[]{:S(2)}) copy-start(f32[1,1024]{1,0:T(1,128)S(1)} %convert_element_type.317) | copy-start | bytes 12292
  361.1 216.5 %copy-start.54 = (f32[1,1024]{1,0:T(1,128)}, f32[1,1024]{1,0:T(1,128)S(1)}, u32[]{:S(2)}) copy-start(f32[1,1024]{1,0:T(1,128)S(1)} %convert_element_type.319) | copy-start | bytes 12292
  369.8 211.1 %copy-start.48 = (f32[1,1024]{1,0:T(1,128)}, f32[1,1024]{1,0:T(1,128)S(1)}, u32[]{:S(2)}) copy-start(f32[1,1024]{1,0:T(1,128)S(1)} %convert_element_type.318) | copy-start | bytes 12292
  377.7 130.9 %copy-start.82 = (f32[1,4096]{1,0:T(1,128)}, f32[1,4096]{1,0:T(1,128)S(1)}, u32[]{:S(2)}) copy-start(f32[1,4096]{1,0:T(1,128)S(1)} %convert_element_type.320) | copy-start | bytes 49156
  448.5 68.0 %copy-start.41 = (bf16[16,64,256]{2,1,0:T(8,128)(2,1)}, bf16[16,64,256]{2,1,0:T(8,128)(2,1)S(1)}, u32[]{:S(2)}) copy-start(bf16[16,64,256]{2,1,0:T(8,128)(2,1)S(1)} %fusion.211) | copy-start | bytes 1572868
  454.7 126.2 %copy-start.11 = (f32[1,256,1024]{2,1,0:T(8,128)}, f32[1,256,1024]{2,1,0:T(8,128)S(1)}, u32[]{:S(2)}) copy-start(f32[1,256,1024]{2,1,0:T(8,128)S(1)} %get-tuple-element.105) | copy-start | bytes 3145732
  454.7 126.2 %copy-start.73 = (f32[256]{0:T(256)}, f32[256]{0:T(256)S(1)}, u32[]{:S(2)}) copy-start(f32[256]{0:T(256)S(1)} %broadcast_multiply_fusion.3) | copy-start | bytes 3076
  455.0 125.9 %copy-start.75 = (f32[256]{0:T(256)}, f32[256]{0:T(256)S(1)}, u32[]{:S(2)}) copy-start(f32[256]{0:T(256)S(1)} %fusion.304) | copy-start | bytes 3076
  455.7 136.1 %copy-start.67 = (f32[16,256]{1,0:T(8,128)}, f32[16,256]{1,0:T(8,128)S(1)}, u32[]{:S(2)}) copy-start(f32[16,256]{1,0:T(8,128)S(1)} %get-tuple-element.77) | copy-start | bytes 49156
  508.6 56.7 %copy-start.30 = (bf16[1,256,1024]{2,1,0:T(8,128)(2,1)S(1)}, bf16[1,256,1024]{2,1,0:T(8,128)(2,1)}, u32[]{:S(2)}) copy-start(bf16[1,256,1024]{2,1,0:T(8,128)(2,1)} %param.29) | copy-start | bytes 1572868
  565.4 12.3 copy-start.97
  625.1 218.2 %reduce-scatter.15.cloned.1.call-start = ((), (), s32[]{:S(2)}) async-start(), calls=%async_computation.15 | async-start | bytes 5242880 | tf_op jit(solution)/shard_map/reduce_scatter | solution.py:212
  644.0 58.0 %copy-start.59 = (f32[1,1024]{1,0:T(1,128)S(1)}, f32[1,1024]{1,0:T(1,128)}, u32[]{:S(2)}) copy-start(f32[1,1024]{1,0:T(1,128)} %copy-done.58) | copy-start | bytes 12292
  644.0 58.0 %copy-start.65 = (f32[1,1024]{1,0:T(1,128)S(1)}, f32[1,1024]{1,0:T(1,128)}, u32[]{:S(2)}) copy-start(f32[1,1024]{1,0:T(1,128)} %copy-done.64) | copy-start | bytes 12292
  644.0 58.0 %copy-start.78 = (f32[256]{0:T(256)S(1)}, f32[256]{0:T(256)}, u32[]{:S(2)}) copy-start(f32[256]{0:T(256)} %copy-done.77) | copy-start | bytes 3076
  644.1 58.0 %copy-start.81 = (f32[256]{0:T(256)S(1)}, f32[256]{0:T(256)}, u32[]{:S(2)}) copy-start(f32[256]{0:T(256)} %copy-done.80) | copy-start | bytes 3076
  747.8 12.3 copy-start.27
  765.8 227.6 %reduce-scatter.23.cloned.1.call-start = ((), (), s32[]{:S(2)}) async-start(), calls=%async_computation.19 | async-start | bytes 4325376 | tf_op jit(solution)/shard_map/reduce_scatter | solution.py:325
  770.1 371.9 %reduce-scatter.21.cloned.1.call-start = ((), (), s32[]{:S(2)}) async-start(), calls=%async_computation.18 | async-start | bytes 4325376 | tf_op jit(solution)/shard_map/reduce_scatter | solution.py:325
  774.2 505.0 %all-reduce.17.cloned.1.call-start = ((), (), s32[]{:S(2)}) async-start(), calls=%async_computation.34 | async-start | bytes 163840
  776.7 66.6 %copy-start.51 = (f32[1,1024]{1,0:T(1,128)S(1)}, f32[1,1024]{1,0:T(1,128)}, u32[]{:S(2)}) copy-start(f32[1,1024]{1,0:T(1,128)} %copy-done.50) | copy-start | bytes 12292
  776.7 66.6 %copy-start.72 = (f32[256]{0:T(256)S(1)}, f32[256]{0:T(256)}, u32[]{:S(2)}) copy-start(f32[256]{0:T(256)} %copy-done.71) | copy-start | bytes 3076
  850.9 567.5 %reduce-scatter.35.cloned.1.call-start = ((), (), s32[]{:S(2)}) async-start(), calls=%async_computation.25 | async-start | bytes 1081344 | tf_op jit(solution)/shard_map/reduce_scatter | solution.py:333
  852.5 700.0 %reduce-scatter.33.cloned.1.call-start = ((), (), s32[]{:S(2)}) async-start(), calls=%async_computation.24 | async-start | bytes 1081344 | tf_op jit(solution)/shard_map/reduce_scatter | solution.py:333
  853.1 857.2 %reduce-scatter.19.cloned.1.call-start = ((), (), s32[]{:S(2)}) async-start(), calls=%async_computation.17 | async-start | bytes 12976128 | tf_op jit(solution)/shard_map/reduce_scatter | solution.py:324
  861.1 1010.7 %reduce-scatter.17.cloned.1.call-start = ((), (), s32[]{:S(2)}) async-start(), calls=%async_computation.16 | async-start | bytes 12976128 | tf_op jit(solution)/shard_map/reduce_scatter | solution.py:324
  869.4 1367.9 %reduce-scatter.27.cloned.1.call-start = ((), (), s32[]{:S(2)}) async-start(), calls=%async_computation.21 | async-start | bytes 17301504 | tf_op jit(solution)/shard_map/reduce_scatter | solution.py:329
  880.3 1721.5 %reduce-scatter.25.cloned.1.call-start = ((), (), s32[]{:S(2)}) async-start(), calls=%async_computation.20 | async-start | bytes 17301504 | tf_op jit(solution)/shard_map/reduce_scatter | solution.py:329
  890.3 2076.0 %reduce-scatter.31.cloned.1.call-start = ((), (), s32[]{:S(2)}) async-start(), calls=%async_computation.23 | async-start | bytes 17301504 | tf_op jit(solution)/shard_map/reduce_scatter | solution.py:331
  901.1 2429.7 %reduce-scatter.29.cloned.1.call-start = ((), (), s32[]{:S(2)}) async-start(), calls=%async_computation.22 | async-start | bytes 17301504 | tf_op jit(solution)/shard_map/reduce_scatter | solution.py:331
  932.8 210.8 %copy-start.13 = (f32[1,256,1024]{2,1,0:T(8,128)S(1)}, f32[1,256,1024]{2,1,0:T(8,128)}, u32[]{:S(2)}) copy-start(f32[1,256,1024]{2,1,0:T(8,128)} %copy-done.12) | copy-start | bytes 3145732
  932.8 210.8 %copy-start.17 = (f32[256,1024]{1,0:T(8,128)S(1)}, f32[256,1024]{1,0:T(8,128)}, u32[]{:S(2)}) copy-start(f32[256,1024]{1,0:T(8,128)} %copy-done.16) | copy-start | bytes 3145732
  (64 other events, 302.2 us)
Sparse Core Ops, SparseCore 0:
  10.5 48.2 all-gather.38
  65.9 80.9 all-gather.34
  149.4 26.4 all-gather.40
  178.2 54.3 all-gather.44
  234.4 54.3 all-gather.42
  291.1 45.5 all-gather.46
  342.6 80.7 all-gather.36
  425.8 26.4 all-gather.48
  454.2 54.3 all-gather.50
  510.9 54.3 all-gather.52
  625.2 76.7 reduce-scatter.12
  765.9 77.2 reduce-scatter.14
  845.5 147.7 reduce-scatter.22
  995.5 146.3 reduce-scatter.20
  1148.2 130.9 all-reduce.16
  1281.3 136.9 reduce-scatter.34
  1420.5 131.9 reduce-scatter.32
  1558.4 151.8 reduce-scatter.18
  1717.4 154.4 reduce-scatter.16
  1874.0 363.2 reduce-scatter.26
  2239.6 362.1 reduce-scatter.24
  2604.1 362.1 reduce-scatter.30
  2968.6 362.1 reduce-scatter.28
where the time goes:
time: 3350 us; the launch traced here: 3340 us
  waiting for transfers between devices  2810 us (84%)
  matrix products  252 us (8%)
  blocking collectives  137 us (4%)
  other arithmetic  67.6 us (2%)
  local copies, waits for them, and re-layouts  58.1 us (2%)
    reduce_scatter x2, waiting for transfers between devices, on_device(): lax.psum_scatter(gradients[7], ('dp', 'seq'), scatter_dimension=0, tiled=...  728 us
    reduce_scatter x2, waiting for transfers between devices, on_device(): lax.psum_scatter(gradients[9], ('dp', 'seq'), scatter_dimension=0, tiled=...  727 us
    reduce_scatter x2, waiting for transfers between devices, on_device(): lax.psum_scatter(gradients[2], ('dp', 'seq'), scatter_dimension=0, tiled=...  318 us
    reduce_scatter x2, waiting for transfers between devices, on_device(): lax.psum_scatter(gradients[11], ('dp', 'seq'), scatter_dimension=0, tiled...  264 us
    reduce_scatter x2, waiting for transfers between devices, on_device(): lax.psum_scatter(gradients[3], ('dp', 'seq'), scatter_dimension=0, tiled=...  197 us
    unnamed x24, waiting for transfers between devices  137 us
    reduce_scatter x2, waiting for transfers between devices, layer_backward(): lax.psum_scatter(jnp.concatenate([key_part.reshape(block_len, seq_count,...  114 us
    all_gather x2, waiting for transfers between devices, on_device(): lax.all_gather(expand_weight[layer_index], 'dp', axis=0, tiled=True)  109 us
  transfers between devices with their start and end apart: 23, of which 23 were waited for; matrix products, arithmetic and copies ran while one was open for 7% of the time, Pallas kernels for 0%

commit v1 on v0

v1 whole, which is shorter than its diff:
```python
import functools
import math

import jax
import jax.numpy as jnp
from jax import lax
from jax.experimental import pallas as pl
from jax.experimental.pallas import tpu as pltpu
from jax.sharding import PartitionSpec as P

HEAD = 64
BUCKETS = 256
SMALL = 8
WIDE = 1024

epsilon = 1e-05
bf16 = jnp.bfloat16
f32 = jnp.float32


def modulated_norm(activations, norm_gain, norm_shift, scaling):
    center = activations - jnp.mean(activations, axis=-1, keepdims=True)
    spread = jnp.mean(center * center, axis=-1, keepdims=True)
    return (center * lax.rsqrt(spread + epsilon) * norm_gain + norm_shift) * (1.0 + scaling)


def swap(array, bit):
    count = lax.axis_size("dp")
    return lax.ppermute(array, "dp", [(i, i ^ bit) for i in range(count)])


def swap_seq(array, bit):
    count = lax.axis_size("seq")
    return lax.ppermute(array, "seq", [(i, i ^ bit) for i in range(count)])


def after(array, *earlier):
    return lax.optimization_barrier((array,) + earlier)[0]


def layout_moves(back):
    moves = []
    for index in range(lax.axis_size("dp")):
        core, pair = index % 2, index - index % 2
        for plane in range(4):
            source = index * 4 + plane
            target = (pair + plane % 2) * 4 + 2 * core + plane // 2
            moves.append((target, source) if back else (source, target))
    return moves


def gather_rows(shard, route):
    if lax.axis_size("dp") != SMALL:
        return lax.all_gather(shard, "dp", axis=0, tiled=True)
    along_x = swap(shard, 2)
    along_y = swap(shard, 4)
    across = swap(along_x, 4) if route == 0 else swap(along_y, 2)
    mine = [shard, along_x, along_y, across]
    parts = []
    for part in mine:
        parts += [part, swap(part, 1)]
    return parts


def order_of(parts):
    me = lax.axis_index("dp")
    return [me ^ bit for bit in range(parts)]


def scatter_dense(left, right, orders):
    count, planes = lax.axis_size("dp"), lax.axis_size("seq")
    rows, columns = left.shape[1], right.shape[1]
    if count != SMALL:
        whole = jnp.einsum("tr,tc->rc", left, right, preferred_element_type=f32)
        return lax.psum_scatter(whole, ("dp", "seq"), scatter_dimension=0, tiled=True)
    me, plane = lax.axis_index("dp"), lax.axis_index("seq")
    block = rows // count
    width = columns // len(orders)

    def pick(masks):
        return jnp.concatenate(
            [lax.dynamic_slice_in_dim(left, (me ^ mask) * block, block, 1) for mask in masks], axis=1
        )

    def product(a, b):
        return jnp.einsum("tr,tc->rc", a, b, preferred_element_type=f32)

    pieces = []
    for position, (first, second) in enumerate(orders):
        part = right[:, position * width : (position + 1) * width]
        masks = [first | second, first, second, 0]
        arrived = swap(product(pick([mask | 1 for mask in masks]), part).astype(bf16), 1)
        half = 2 * block
        leaving = (product(pick(masks[:2]), part) + arrived[:half].astype(f32)).astype(bf16)
        staying = (product(pick(masks[2:]), part) + arrived[half:].astype(f32)).astype(bf16)
        arrived = swap(leaving, first)
        leaving = (staying[:block].astype(f32) + arrived[:block].astype(f32)).astype(bf16)
        staying = (staying[block:].astype(f32) + arrived[block:].astype(f32)).astype(bf16)
        arrived = swap(leaving, second)
        pieces.append((staying, arrived))
    total = jnp.concatenate([(a.astype(f32) + b.astype(f32)).astype(bf16) for a, b in pieces], axis=1)
    return scatter_planes(total, plane, planes)


def scatter_planes(total, plane, planes):
    rows, columns = total.shape
    low, high = plane & 1, plane >> 1
    cut = total.reshape(2, 2, rows // planes, columns)
    arrived = swap_seq(lax.dynamic_index_in_dim(cut, 1 - low, 1, keepdims=False), 1)
    kept = lax.dynamic_index_in_dim(cut, low, 1, keepdims=False)
    joined = kept.astype(f32) + arrived.astype(f32)
    arrived = swap_seq(lax.dynamic_index_in_dim(joined, 1 - high, 0, keepdims=False).astype(bf16), 2)
    return lax.dynamic_index_in_dim(joined, high, 0, keepdims=False) + arrived.astype(f32)


def scatter_small(array):
    count, planes = lax.axis_size("dp"), lax.axis_size("seq")
    if count != SMALL:
        return lax.psum_scatter(array, ("dp", "seq"), scatter_dimension=0, tiled=True)[0]
    me, plane = lax.axis_index("dp"), lax.axis_index("seq")
    columns = array.shape[1]
    shape = [count, planes]
    current = array.reshape(shape[0], shape[1], columns)
    for axis, index, send in ((0, me, swap), (1, plane, swap_seq)):
        bit = 1
        while current.shape[axis] > 1:
            pairs = current.shape[axis] // 2
            view = jnp.moveaxis(current, axis, 0).reshape(pairs, 2, -1, columns)
            mine = (index // bit) % 2
            leaving = lax.dynamic_index_in_dim(view, 1 - mine, 1, keepdims=False)
            staying = lax.dynamic_index_in_dim(view, mine, 1, keepdims=False)
            current = jnp.moveaxis((staying + send(leaving, bit)).reshape(pairs, -1, columns), 0, axis)
            bit *= 2
    return current.reshape(columns)


def gather_small(array, axes):
    if lax.axis_size("dp") != SMALL:
        stacked = lax.all_gather(array, axes, axis=0, tiled=False)
        stacked = stacked.reshape((-1,) + array.shape)
        places = jnp.arange(stacked.shape[0])
        if "seq" in axes:
            planes = lax.axis_size("seq")
            return stacked, places // planes, places % planes
        return stacked, places, None
    current = array[None]
    me = lax.axis_index("dp")
    for bit in (1, 2, 4):
        current = jnp.concatenate([current, swap(current, bit)], axis=0)
    sources = me ^ jnp.arange(SMALL)
    if "seq" not in axes:
        return current, sources, None
    plane = lax.axis_index("seq")
    for bit in (1, 2):
        current = jnp.concatenate([current, swap_seq(current, bit)], axis=0)
    places = jnp.arange(SMALL * 4)
    return current, me ^ (places % SMALL), plane ^ (places // SMALL)


VMEM_LIMIT = 56 * 1024 * 1024


def forward_kernel(count, depth, place, a_ref, *refs):
    weights, out, ordered = refs[:count], refs[count], refs[count + 1]

    @pl.when(pl.program_id(0) == 0)
    def _():
        for part in range(count):
            start = pl.multiple_of((place[0] ^ part) * depth, 128)
            ordered[:, part * depth : (part + 1) * depth] = a_ref[:, pl.ds(start, depth)]

    whole = jnp.concatenate([weight[...] for weight in weights], axis=0)
    out[...] = jnp.dot(ordered[...], whole, preferred_element_type=f32).astype(out.dtype)


def times(a, parts, out_type):
    if not isinstance(parts, list):
        return jnp.dot(a, parts, preferred_element_type=f32).astype(out_type)
    tokens, inner = a.shape
    depth, columns = parts[0].shape
    tile = min(512, columns)
    count = len(parts)
    place = lax.axis_index("dp").astype(jnp.int32).reshape(1)
    return pl.pallas_call(
        functools.partial(forward_kernel, count, depth),
        out_shape=jax.ShapeDtypeStruct((tokens, columns), out_type),
        grid_spec=pltpu.PrefetchScalarGridSpec(
            num_scalar_prefetch=1,
            grid=(columns // tile,),
            in_specs=[pl.BlockSpec((tokens, inner), lambda i, s: (0, 0))]
            + [pl.BlockSpec((depth, tile), lambda i, s: (0, i))] * count,
            out_specs=pl.BlockSpec((tokens, tile), lambda i, s: (0, i)),
            scratch_shapes=[pltpu.VMEM((tokens, inner), bf16)],
        ),
        compiler_params=pltpu.CompilerParams(vmem_limit_bytes=VMEM_LIMIT),
        cost_estimate=pl.CostEstimate(
            flops=2 * tokens * inner * columns,
            bytes_accessed=2 * inner * columns + 6 * tokens * (inner + columns),
            transcendentals=0,
        ),
    )(place, a, *parts)


def backward_kernel(count, depth, rows, place, a_ref, *refs):
    weights, out, total = refs[:count], refs[count], refs[count + 1]
    step, steps = pl.program_id(0), pl.num_programs(0)
    whole = jnp.concatenate([weight[...] for weight in weights], axis=0)
    product = lax.dot_general(
        a_ref[...], whole, (((1,), (1,)), ((), ())), preferred_element_type=f32
    )
    if rows == depth:

        @pl.when(step == 0)
        def _():
            total[...] = product

        @pl.when(step > 0)
        def _():
            total[...] += product

        @pl.when(step == steps - 1)
        def _():
            for part in range(count):
                start = pl.multiple_of((place[0] ^ part) * depth, 128)
                out[:, pl.ds(start, depth)] = total[:, part * depth : (part + 1) * depth].astype(
                    out.dtype
                )

    else:
        for part in range(count):
            start = pl.multiple_of((place[0] ^ part) * depth + step * rows, 128)
            out[:, pl.ds(start, rows)] = product[:, part * rows : (part + 1) * rows].astype(out.dtype)


def times_transposed(a, parts, out_type):
    if not isinstance(parts, list):
        return lax.dot_general(
            a, parts, (((1,), (1,)), ((), ())), preferred_element_type=f32
        ).astype(out_type)
    tokens, inner = a.shape
    depth = parts[0].shape[0]
    count = len(parts)
    place = lax.axis_index("dp").astype(jnp.int32).reshape(1)
    if depth > 128:
        rows, tile = 128, inner
        grid = depth // rows
        a_spec = pl.BlockSpec((tokens, inner), lambda i, s: (0, 0))
        w_spec = pl.BlockSpec((rows, inner), lambda i, s: (i, 0))
    else:
        rows, tile = depth, min(512, inner)
        grid = inner // tile
        a_spec = pl.BlockSpec((tokens, tile), lambda i, s: (0, i))
        w_spec = pl.BlockSpec((rows, tile), lambda i, s: (0, i))
    return pl.pallas_call(
        functools.partial(backward_kernel, count, depth, rows),
        out_shape=jax.ShapeDtypeStruct((tokens, count * depth), out_type),
        grid_spec=pltpu.PrefetchScalarGridSpec(
            num_scalar_prefetch=1,
            grid=(grid,),
            in_specs=[a_spec] + [w_spec] * count,
            out_specs=pl.BlockSpec((tokens, count * depth), lambda i, s: (0, 0)),
            scratch_shapes=[pltpu.VMEM((tokens, count * rows), f32)],
        ),
        compiler_params=pltpu.CompilerParams(vmem_limit_bytes=VMEM_LIMIT),
        cost_estimate=pl.CostEstimate(
            flops=2 * tokens * inner * count * depth,
            bytes_accessed=2 * inner * count * depth + 6 * tokens * (inner + count * depth),
            transcendentals=0,
        ),
    )(place, a, *parts)


def spread_keys(own):
    far = swap_seq(own, 1)
    return [own, swap(own, 1), far, swap(far, 1)]


def heads_of(rows):
    return rows.reshape(rows.shape[0], rows.shape[1] // HEAD, HEAD)


def attend(queries, chunks):
    model_width = queries.shape[1]
    whole = jnp.concatenate(chunks, axis=0)
    key_heads, value_heads = heads_of(whole[:, :model_width]), heads_of(whole[:, model_width:])
    scores = jnp.einsum("qhd,khd->hqk", heads_of(queries), key_heads, preferred_element_type=f32)
    scores = scores * (1.0 / math.sqrt(HEAD))
    exponent = jnp.exp(scores - jnp.max(scores, axis=-1, keepdims=True))
    probs = exponent / jnp.sum(exponent, axis=-1, keepdims=True)
    probs_low = probs.astype(bf16)
    mixture = jnp.einsum("hqk,khd->qhd", probs_low, value_heads, preferred_element_type=f32)
    return mixture.reshape(queries.shape).astype(bf16), (probs, probs_low)


def attend_back(queries, chunks, kept, mixture, mixture_grad):
    probs, probs_low = kept
    model_width = queries.shape[1]
    factor = 1.0 / math.sqrt(HEAD)
    whole = jnp.concatenate(chunks, axis=0)
    key_heads, value_heads = heads_of(whole[:, :model_width]), heads_of(whole[:, model_width:])
    grad_heads = heads_of(mixture_grad)
    prob_grad = jnp.einsum("qhd,khd->hqk", grad_heads, value_heads, preferred_element_type=f32)
    along = jnp.sum(probs * prob_grad, axis=-1, keepdims=True)
    score_grad = (probs * (prob_grad - along)).astype(bf16)
    query_grad = jnp.einsum("hqk,khd->qhd", score_grad, key_heads, preferred_element_type=f32)
    query_grad = (query_grad * factor).astype(bf16).reshape(queries.shape)
    key_part = jnp.einsum("hqk,qhd->khd", score_grad, heads_of(queries), preferred_element_type=f32)
    value_part = jnp.einsum("hqk,qhd->khd", probs_low, grad_heads, preferred_element_type=f32)
    parts = jnp.concatenate(
        [
            (key_part * factor).reshape(whole.shape[0], model_width),
            value_part.reshape(whole.shape[0], model_width),
        ],
        axis=1,
    ).astype(bf16)
    return query_grad, parts


def join_key_grads(parts):
    local = parts.shape[0] // 4
    cut = [parts[i * local : (i + 1) * local] for i in range(4)]
    far = cut[2].astype(f32) + swap(cut[3], 1).astype(f32)
    far = swap_seq(far.astype(bf16), 1)
    near = cut[0].astype(f32) + swap(cut[1], 1).astype(f32)
    return (near + far.astype(f32)).astype(bf16)


def layer_forward(stream, weights, vectors):
    w_query, w_keys, w_out, w_expand, w_reduce = weights
    first_gain, first_shift, attention_bias, second_gain, second_shift, reduce_bias, expand_bias, scaling = vectors
    normed = modulated_norm(stream, first_gain, first_shift, scaling).astype(bf16)
    chunks = spread_keys(times(normed, w_keys, bf16))
    queries = times(normed, w_query, bf16)
    mixture, kept = attend(queries, chunks)
    middle = stream + (times(mixture, w_out, f32) + attention_bias)
    second = modulated_norm(middle, second_gain, second_shift, scaling).astype(bf16)
    hidden = times(second, w_expand, f32) + expand_bias
    active = jax.nn.gelu(hidden).astype(bf16)
    result = middle + (times(active, w_reduce, f32) + reduce_bias)
    return result, (stream, normed, queries, chunks, kept, mixture, middle, second, hidden, active)


def layer_backward(saved, weights, vectors, grad_out):
    w_query, w_keys, w_out, w_expand, w_reduce = weights
    first_gain, first_shift, attention_bias, second_gain, second_shift, reduce_bias, expand_bias, scaling = vectors
    stream, normed, queries, chunks, kept, mixture, middle, second, hidden, active = saved
    both = ((2, 4), (4, 2))
    grad_low = grad_out.astype(bf16)
    reduce_bias_grad = jnp.sum(grad_out, axis=0)
    reduce_weight_grad = scatter_dense(active, grad_low, both)
    active_grad = times_transposed(grad_low, w_reduce, f32)
    hidden_grad = jax.vjp(jax.nn.gelu, hidden)[1](active_grad)[0]
    expand_bias_grad = jnp.sum(hidden_grad, axis=0)
    hidden_low = hidden_grad.astype(bf16)
    second_grad = times_transposed(hidden_low, w_expand, f32)
    expand_weight_grad = scatter_dense(second, hidden_low, both)
    _, second_back = jax.vjp(modulated_norm, middle, second_gain, second_shift, scaling)
    middle_part, second_gain_grad, second_shift_grad, second_scaling_grad = second_back(second_grad)
    middle_grad = grad_out + middle_part
    attention_bias_grad = jnp.sum(middle_grad, axis=0)
    middle_low = middle_grad.astype(bf16)
    mixture_grad = times_transposed(middle_low, w_out, bf16)
    attention_out_grad = scatter_dense(mixture, middle_low, both)
    query_grad, parts = attend_back(queries, chunks, kept, mixture, mixture_grad)
    key_grad = join_key_grads(parts)
    normed_grad = times_transposed(query_grad, w_query, f32) + times_transposed(key_grad, w_keys, f32)
    project_grad = jnp.concatenate([query_grad, key_grad], axis=1)
    attention_in_grad = scatter_dense(normed, project_grad, both)
    _, first_back = jax.vjp(modulated_norm, stream, first_gain, first_shift, scaling)
    stream_part, first_gain_grad, first_shift_grad, first_scaling_grad = first_back(normed_grad)
    stream_grad = middle_grad + stream_part
    small = (
        first_gain_grad,
        first_shift_grad,
        attention_bias_grad,
        second_gain_grad,
        second_shift_grad,
        reduce_bias_grad,
        expand_bias_grad,
    )
    dense = (attention_in_grad, attention_out_grad, expand_weight_grad, reduce_weight_grad)
    return stream_grad, dense, small, (first_scaling_grad + second_scaling_grad)[0]


def pack_small(vectors, rows):
    flat = jnp.concatenate([vector.reshape(-1) for vector in vectors])
    length = -(-flat.shape[0] // WIDE) * WIDE
    return jnp.pad(flat, (0, length - flat.shape[0])).reshape(-1, WIDE)


def on_device(
    inputs,
    noise_buckets,
    first_gain,
    first_shift,
    attention_in,
    attention_out,
    attention_bias,
    second_gain,
    second_shift,
    expand_weight,
    expand_bias,
    reduce_weight,
    reduce_bias,
    time_table,
    cotangent,
):
    layers = first_gain.shape[0]
    count, planes = lax.axis_size("dp"), lax.axis_size("seq")
    me, plane = lax.axis_index("dp"), lax.axis_index("seq")
    model_width = inputs.shape[-1]
    table_rows = time_table.shape[1]

    stream = lax.ppermute(inputs[0], ("dp", "seq"), layout_moves(False)).astype(f32)

    sequence = (me // 2) * 2 + plane // 2
    packs = []
    for layer in range(layers):
        rows = [
            time_table[layer],
            pack_small(
                [
                    member[layer]
                    for member in (
                        first_gain,
                        first_shift,
                        attention_bias,
                        second_gain,
                        second_shift,
                        reduce_bias,
                        expand_bias,
                    )
                ],
                WIDE,
            ),
            jnp.broadcast_to(noise_buckets.astype(bf16)[:, None], (1, model_width)),
        ]
        packs.append(jnp.concatenate(rows, axis=0))

    def unpack(pack):
        stacked, sources, _ = gather_small(pack, ("dp",))
        slot = me ^ jnp.arange(count) if count == SMALL else jnp.arange(count)
        per_pack = stacked.shape[1]
        flat = stacked.reshape(count * per_pack, model_width)

        def place(index):
            return (me ^ index) if count == SMALL else index

        buckets = jnp.stack(
            [lax.dynamic_index_in_dim(flat, place(index) * per_pack + per_pack - 1, 0, False)[0] for index in range(count)]
        ).astype(jnp.int32)
        bucket = lax.dynamic_index_in_dim(buckets, sequence, 0, False)
        row = place(bucket // table_rows) * per_pack + bucket % table_rows
        scaling = lax.dynamic_slice_in_dim(flat, row, 1, 0).astype(f32)
        vectors = jnp.stack(
            [
                lax.dynamic_slice_in_dim(
                    flat, place(index) * per_pack + table_rows, per_pack - 1 - table_rows, 0
                ).reshape(-1)
                for index in range(count)
            ]
        ).astype(f32)
        share = model_width // count
        members = [vectors[:, i * share : (i + 1) * share].reshape(1, -1) for i in range(6)]
        members.append(vectors[:, 6 * share : 6 * share + expand_bias.shape[1]].reshape(1, -1))
        return tuple(members) + (scaling,), buckets

    keys_at = model_width
    shards = []
    for layer in range(layers):
        shards += [
            attention_in[layer][:, keys_at:],
            attention_in[layer][:, :keys_at],
            attention_out[layer],
            expand_weight[layer],
            reduce_weight[layer],
        ]
    gathered = []
    for position, shard in enumerate(shards):
        if count == SMALL and position >= 2:
            shard = after(shard, gathered[position - 2][2], gathered[position - 2][4])
        gathered.append(gather_rows(shard, position % 2))

    all_vectors, buckets = [], None
    for layer in range(layers):
        vectors, buckets = unpack(packs[layer])
        all_vectors.append(vectors)

    saved, all_weights = [], []
    for layer in range(layers):
        w_keys, w_query, w_out, w_expand, w_reduce = gathered[5 * layer : 5 * layer + 5]
        weights = (w_query, w_keys, w_out, w_expand, w_reduce)
        all_weights.append(weights)
        stream, kept = layer_forward(stream, weights, all_vectors[layer])
        saved.append(kept)
    back_moves = layout_moves(True)
    outputs = lax.ppermute(stream.astype(bf16), ("dp", "seq"), back_moves)[None]

    grad_flow = lax.ppermute(cotangent[0], ("dp", "seq"), layout_moves(False)).astype(f32)
    dense, small, modulation = [None] * layers, [None] * layers, [None] * layers
    for layer in reversed(range(layers)):
        grad_flow, dense[layer], small[layer], modulation[layer] = layer_backward(
            saved[layer], all_weights[layer], all_vectors[layer], grad_flow
        )
    input_grad = lax.ppermute(grad_flow, ("dp", "seq"), back_moves)[None]

    devices = count * planes
    packed = jnp.concatenate(
        [member.reshape(devices, -1) for layer in range(layers) for member in small[layer]], axis=1
    )
    row = scatter_small(packed)
    small_out, start = [[] for _ in range(7)], 0
    for layer in range(layers):
        for member in range(7):
            width = small[layer][member].size // devices
            small_out[member].append(row[start : start + width])
            start += width
    small_out = [jnp.stack(member) for member in small_out]

    changes, from_dp, from_seq = gather_small(jnp.concatenate(modulation), ("dp", "seq"))
    owners = (from_dp // 2) * 2 + from_seq // 2
    source_buckets = jnp.sum(
        jnp.where(owners[:, None] == jnp.arange(count)[None, :], buckets[None, :], 0), axis=1
    )
    table_share = BUCKETS // devices
    first_row = (me * planes + plane) * table_share
    chosen = (source_buckets[None, :] == (first_row + jnp.arange(table_share))[:, None]).astype(f32)
    table_grad = jnp.dot(chosen, changes, precision=lax.Precision.HIGHEST)
    table_grad = jnp.stack(
        [table_grad[:, layer * model_width : (layer + 1) * model_width] for layer in range(layers)]
    )

    dense_out = [jnp.stack([dense[layer][member] for layer in range(layers)]) for member in range(4)]
    return (
        outputs,
        input_grad,
        small_out[0],
        small_out[1],
        dense_out[0],
        dense_out[1],
        small_out[2],
        small_out[3],
        small_out[4],
        dense_out[2],
        small_out[6],
        dense_out[3],
        small_out[5],
        table_grad,
    )


def solution(mesh):
    return jax.shard_map(
        on_device,
        mesh=mesh,
        in_specs=(
            P("dp", "seq", None),
            P("dp"),
            P(None, "dp"),
            P(None, "dp"),
            P(None, "dp", None),
            P(None, "dp", None),
            P(None, "dp"),
            P(None, "dp"),
            P(None, "dp"),
            P(None, "dp", None),
            P(None, "dp"),
            P(None, "dp", None),
            P(None, "dp"),
            P(None, "dp", None),
            P("dp", "seq", None),
        ),
        out_specs=(
            P("dp", "seq", None),
            P("dp", "seq", None),
            P(None, ("dp", "seq")),
            P(None, ("dp", "seq")),
            P(None, ("dp", "seq"), None),
            P(None, ("dp", "seq"), None),
            P(None, ("dp", "seq")),
            P(None, ("dp", "seq")),
            P(None, ("dp", "seq")),
            P(None, ("dp", "seq"), None),
            P(None, ("dp", "seq")),
            P(None, ("dp", "seq"), None),
            P(None, ("dp", "seq")),
            P(None, ("dp", "seq"), None),
        ),
        check_vma=False,
    )
```

time: 3350 us -> 1170 us (0.35)
  waiting for transfers between devices: 2810 us -> 385 us
  starting transfers between devices: 1.4 us -> 157 us
  blocking collectives: 137 us -> 0 us
  Pallas kernels: 0 us -> 132 us
  local copies, waits for them, and re-layouts: 58.1 us -> 150 us
  matrix products: 252 us -> 176 us
  other arithmetic: 67.6 us -> 143 us
    reduce_scatter x12 -> x0, waiting for transfers between devices: 2350 us -> none  [the longest x2 728 us: on_device(): lax.psum_scatter(gradients[7], ('dp', 'seq'), scatter_dimension=0, tiled=...]
    ppermute x0 -> x166, waiting for transfers between devices: none -> 385 us  [the longest x138 302 us: swap(): return lax.ppermute(array, 'dp', [(i, i ^ bit) for i in range(count)])]
    all_gather x10 -> x0, waiting for transfers between devices: 323 us -> none  [the longest x2 109 us: on_device(): lax.all_gather(expand_weight[layer_index], 'dp', axis=0, tiled=True)]
    ppermute x0 -> x166, starting transfers between devices: none -> 157 us  [the longest x138 104 us: swap(): return lax.ppermute(array, 'dp', [(i, i ^ bit) for i in range(count)])]
    unnamed x24 -> x0, waiting for transfers between devices: 137 us -> none
    all_gather x16 -> x0, blocking collectives: 137 us -> none  [the longest x2 18 us: on_device(): lax.all_gather(time_table[layer_index], 'dp', axis=0, tiled=True)]
    pallas_call x0 -> x20, Pallas kernels: none -> 132 us  [the longest x10 70.7 us: times(): pl.pallas_call(functools.partial(forward_kernel, count, depth), out_shape...]
    dot_general x42 -> x59, matrix products: 252 us -> 156 us  [the longest x48 83.9 us: product(): return jnp.einsum('tr,tc->rc', a, b, preferred_element_type=f32)]
  transfers between devices with their start and end apart: 23 -> 166, of which waited for: 23 -> 59; matrix products, arithmetic and copies ran while one was open for 7% -> 33% of each run, Pallas kernels for 0% -> 9%
where the time goes in v1:
time: 1170 us; the launch traced here: 1150 us
  waiting for transfers between devices  385 us (33%)
  matrix products  176 us (15%)
  starting transfers between devices  157 us (13%)
  local copies, waits for them, and re-layouts  150 us (13%)
  other arithmetic  143 us (12%)
  Pallas kernels  132 us (11%)
    ppermute x138, waiting for transfers between devices, swap(): return lax.ppermute(array, 'dp', [(i, i ^ bit) for i in range(count)])  302 us
    ppermute x138, starting transfers between devices, swap(): return lax.ppermute(array, 'dp', [(i, i ^ bit) for i in range(count)])  104 us
    dot_general x48, matrix products, product(): return jnp.einsum('tr,tc->rc', a, b, preferred_element_type=f32)  83.9 us
    ppermute x24, waiting for transfers between devices, swap_seq(): return lax.ppermute(array, 'seq', [(i, i ^ bit) for i in range(count)])  83.3 us
    pallas_call x10, Pallas kernels, times(): pl.pallas_call(functools.partial(forward_kernel, count, depth), out_shape...  70.7 us
    pallas_call x10, Pallas kernels, times_transposed(): pl.pallas_call(functools.partial(backward_kernel, count, depth, rows), ou...  61.8 us
    ppermute x24, starting transfers between devices, swap_seq(): return lax.ppermute(array, 'seq', [(i, i ^ bit) for i in range(count)])  35.6 us
  transfers between devices with their start and end apart: 166, of which 59 were waited for; matrix products, arithmetic and copies ran while one was open for 33% of the time, Pallas kernels for 9%

profile of v1, /device:TPU:0, one launch (start us, length us, event | category | flops | bytes accessed | tf_op | source)
XLA Modules:
  0.0 1153.2 jit_solution(12387995783755175394)
XLA Ops:
  49.1 5.2 stack.121
  60.8 23.3 %collective-permute-done.9.refs_6_ = bf16[128,2048]{1,0:T(8,128)(2,1)} collective-permute-done((bf16[128,2048]{1,0:T(8,128)(2,1)}, bf16[128,2048]{1,0:T(8,128)(2,1)}, u32[]{:S(2)}, u32[]{:S(2)}) %collective-permute-start.9) | collective-permute-done | bytes 524320 | tf_op jit(solution)/shard_map/ppermute | solution.py:29
  88.3 16.8 %shard_map.254 = bf16[256,2048]{1,0:T(8,128)(2,1)} custom-call(s32[1]{0:T(128)} %bitcast.1.place, bf16[256,1024]{1,0:T(8,128)(2,1)} %fusion.65.a_ref, bf16[128,2048]{1,0:T(8,128)(2,1)} %copy-done.31, bf16[128,2048]{1,0:T(8,128)(2,1)} %collective-permute-done.4.refs_1_, bf16[128,2048]{1,0:T(8,128)(2,1)} %collective-permute-done.5.refs_2_, ...), custom_call_target="tpu_custom_call" | custom-call | flops 1073741824 | bytes 8912896 | tf_op jit(solution)/shard_map/pallas_call | solution.py:184
  112.0 4.9 collective-permute-done.22.refs_2_
  125.0 6.9 collective-permute-done.48.refs_4_
  133.1 5.3 stack.123
  141.6 15.6 %collective-permute-done.46.refs_2_ = bf16[128,2048]{1,0:T(8,128)(2,1)} collective-permute-done((bf16[128,2048]{1,0:T(8,128)(2,1)}, bf16[128,2048]{1,0:T(8,128)(2,1)}, u32[]{:S(2)}, u32[]{:S(2)}) %collective-permute-start.46) | collective-permute-done | bytes 524320 | tf_op jit(solution)/shard_map/ppermute | solution.py:29
  168.1 5.2 collective-permute-done.65.refs_4_
  188.8 9.7 fusion.364
  198.5 9.1 fusion.50
  218.5 16.7 %collective-permute-done.40.refs_6_ = bf16[512,1024]{1,0:T(8,128)(2,1)} collective-permute-done((bf16[512,1024]{1,0:T(8,128)(2,1)}, bf16[512,1024]{1,0:T(8,128)(2,1)}, u32[]{:S(2)}, u32[]{:S(2)}) %collective-permute-start.40) | collective-permute-done | bytes 1048608 | tf_op jit(solution)/shard_map/ppermute | solution.py:29
  235.7 9.8 shard_map.257
  245.6 5.1 multiply_convert_fusion.5.a_ref
  254.4 7.1 shard_map.258
  263.2 7.1 collective-permute-done.50.refs_6_
  278.4 5.8 shard_map.259
  286.4 4.5 collective-permute-start.53
  296.6 13.8 %collective-permute-done.77.refs_2_ = bf16[512,1024]{1,0:T(8,128)(2,1)} collective-permute-done((bf16[512,1024]{1,0:T(8,128)(2,1)S(1)}, bf16[512,1024]{1,0:T(8,128)(2,1)}, u32[]{:S(2)}, u32[]{:S(2)}) %collective-permute-start.77) | collective-permute-done | bytes 1048608 | tf_op jit(solution)/shard_map/ppermute | solution.py:29
  310.9 21.0 %collective-permute-done.81.refs_6_ = bf16[512,1024]{1,0:T(8,128)(2,1)} collective-permute-done((bf16[512,1024]{1,0:T(8,128)(2,1)}, bf16[512,1024]{1,0:T(8,128)(2,1)}, u32[]{:S(2)}, u32[]{:S(2)}) %collective-permute-start.81) | collective-permute-done | bytes 1048608 | tf_op jit(solution)/shard_map/ppermute | solution.py:29
  349.0 8.2 shard_map.264
  367.5 9.9 fusion.365
  382.9 9.9 fusion.53
  395.6 12.2 %collective-permute-done.74.refs_6_ = bf16[128,4096]{1,0:T(8,128)(2,1)} collective-permute-done((bf16[128,4096]{1,0:T(8,128)(2,1)}, bf16[128,4096]{1,0:T(8,128)(2,1)}, u32[]{:S(2)}, u32[]{:S(2)}) %collective-permute-start.74) | collective-permute-done | bytes 1048608 | tf_op jit(solution)/shard_map/ppermute | solution.py:29
  415.8 10.0 shard_map.262
  425.8 7.6 fusion.350
  433.4 9.5 shard_map.265
  445.3 7.2 shard_map.263
  461.4 9.4 fusion.41
  470.8 10.7 multiply_reduce_fusion.1
  481.5 11.8 %multiply_convert_fusion.1 = bf16[16,256,1024]{2,1,0:T(8,128)(2,1)S(1)} fusion(f32[16,256,1024]{2,1,0:T(8,128)} %get-tuple-element.242, f32[16,256]{1,0:T(8,128)S(1)} %get-tuple-element.241, f32[16,256,1024]{2,1,0:T(8,128)} %get-tuple-element.240, f32[16,256]{1,0:T(8,128)S(1)} %get-tuple-element.239), kind=kLoop, calls=%fused_computation.4 | loop fusion | flops 16777216 | bytes 41975808 | tf_op jit(solution)/shard_map/convert_element_type | solution.py:304
  522.5 6.6 collective-permute-done.122
  542.2 5.3 collective-permute-start.83
  558.8 10.6 collective-permute-start.156
  574.7 5.7 shard_map.268
  585.9 8.4 shard_map.269
  594.3 6.3 fusion.352
  600.6 9.5 shard_map.270
  620.5 8.5 fusion.38
  629.0 11.0 multiply_reduce_fusion
  647.1 11.6 %multiply_convert_fusion = bf16[16,256,1024]{2,1,0:T(8,128)(2,1)S(1)} fusion(f32[16,256,1024]{2,1,0:T(8,128)} %get-tuple-element.244, f32[16,256]{1,0:T(8,128)S(1)} %get-tuple-element.243, f32[16,256,1024]{2,1,0:T(8,128)} %get-tuple-element.238, f32[16,256]{1,0:T(8,128)S(1)} %copy-done.208), kind=kLoop, calls=%fused_computation.2 | loop fusion | flops 16777216 | bytes 41975808 | tf_op jit(solution)/shard_map/convert_element_type | solution.py:304
  724.3 6.0 collective-permute-done.114
  732.4 4.5 collective-permute-done.115
  737.5 20.4 %collective-permute-done.118 = bf16[128,512]{1,0:T(8,128)(2,1)S(1)} collective-permute-done((bf16[128,512]{1,0:T(8,128)(2,1)S(1)}, bf16[128,512]{1,0:T(8,128)(2,1)S(1)}, u32[]{:S(2)}, u32[]{:S(2)}) %collective-permute-start.118) | collective-permute-done | bytes 131104 | tf_op jit(solution)/shard_map/ppermute | solution.py:29
  767.8 13.9 %collective-permute-done.138 = bf16[256,2048]{1,0:T(8,128)(2,1)S(1)} collective-permute-done((bf16[256,2048]{1,0:T(8,128)(2,1)S(1)}, bf16[256,2048]{1,0:T(8,128)(2,1)S(1)}, u32[]{:S(2)}, u32[]{:S(2)}) %collective-permute-start.138) | collective-permute-done | bytes 1048608 | tf_op jit(solution)/shard_map/ppermute | solution.py:29
  782.8 8.7 collective-permute-done.141
  792.6 17.9 %collective-permute-done.157 = bf16[1024,512]{0,1:T(8,128)(2,1)S(1)} collective-permute-done((bf16[1024,512]{0,1:T(8,128)(2,1)S(1)}, bf16[1024,512]{0,1:T(8,128)(2,1)S(1)}, u32[]{:S(2)}, u32[]{:S(2)}) %collective-permute-start.157) | collective-permute-done | bytes 1048608 | tf_op jit(solution)/shard_map/ppermute | solution.py:29
  823.8 7.0 collective-permute-done.155
  838.3 6.3 collective-permute-done.139
  863.7 9.3 collective-permute-done.90
  876.7 5.7 shard_map.273
  918.2 5.7 collective-permute-done.143
  929.0 9.6 collective-permute-start.91
  953.8 4.6 collective-permute-done.96
  964.4 5.6 collective-permute-done.165
  979.2 15.9 %collective-permute-done.144 = bf16[32,4096]{1,0:T(8,128)(2,1)S(1)} collective-permute-done((bf16[32,4096]{1,0:T(8,128)(2,1)S(1)}, bf16[32,4096]{1,0:T(8,128)(2,1)S(1)}, u32[]{:S(2)}, u32[]{:S(2)}) %collective-permute-start.144) | collective-permute-done | bytes 262176 | tf_op jit(solution)/shard_map/ppermute | solution.py:34
  998.1 9.1 collective-permute-done.107
  1010.0 7.0 collective-permute-done.110
  1019.9 17.6 %collective-permute-done.130 = bf16[256,2048]{1,0:T(8,128)(2,1)S(1)} collective-permute-done((bf16[256,2048]{1,0:T(8,128)(2,1)S(1)}, bf16[256,2048]{1,0:T(8,128)(2,1)S(1)}, u32[]{:S(2)}, u32[]{:S(2)}) %collective-permute-start.130) | collective-permute-done | bytes 1048608 | tf_op jit(solution)/shard_map/ppermute | solution.py:29
  1043.0 5.0 collective-permute-done.111
  1048.3 15.2 %collective-permute-done.133 = bf16[256,2048]{1,0:T(8,128)(2,1)S(1)} collective-permute-done((bf16[256,2048]{1,0:T(8,128)(2,1)S(1)}, bf16[256,2048]{1,0:T(8,128)(2,1)S(1)}, u32[]{:S(2)}, u32[]{:S(2)}) %collective-permute-start.133) | collective-permute-done | bytes 1048608 | tf_op jit(solution)/shard_map/ppermute | solution.py:29
  1064.6 7.6 collective-permute-done.112
  1121.2 5.2 collective-permute-done.136
  1134.2 4.7 collective-permute-done.103
  1141.6 6.2 collective-permute-done.104
  (1128 shorter events, 542.0 us)
Async XLA Ops:
  20.2 27.3 %collective-permute-start.5 = (bf16[128,2048]{1,0:T(8,128)(2,1)S(1)}, bf16[128,2048]{1,0:T(8,128)(2,1)}, u32[]{:S(2)}, u32[]{:S(2)}) collective-permute-start(bf16[128,2048]{1,0:T(8,128)(2,1)S(1)} %slice.878.refs_0_), channel_id=1, source_target_pairs={{0,8},{4,12},{8,0},{12,4},{16,24},{20,28},{24,16},{28,20},{1,9},{5... | collective-permute-start | bytes 1572872 | tf_op jit(solution)/shard_map/ppermute | solution.py:29
  27.7 33.0 %collective-permute-start.7 = (bf16[128,2048]{1,0:T(8,128)(2,1)S(1)}, bf16[128,2048]{1,0:T(8,128)(2,1)}, u32[]{:S(2)}, u32[]{:S(2)}) collective-permute-start(bf16[128,2048]{1,0:T(8,128)(2,1)S(1)} %slice.878.refs_0_), channel_id=1, source_target_pairs={{0,16},{4,20},{8,24},{12,28},{16,0},{20,4},{24,8},{28,12},{1,17},{... | collective-permute-start | bytes 1572872 | tf_op jit(solution)/shard_map/ppermute | solution.py:29
  29.2 55.2 %collective-permute-start.4 = (bf16[128,2048]{1,0:T(8,128)(2,1)S(1)}, bf16[128,2048]{1,0:T(8,128)(2,1)}, u32[]{:S(2)}, u32[]{:S(2)}) collective-permute-start(bf16[128,2048]{1,0:T(8,128)(2,1)S(1)} %slice.878.refs_0_), channel_id=1, source_target_pairs={{0,4},{4,0},{8,12},{12,8},{16,20},{20,16},{24,28},{28,24},{1,5},{5... | collective-permute-start | bytes 1572872 | tf_op jit(solution)/shard_map/ppermute | solution.py:29
  40.0 68.1 %collective-permute-start.31 = (bf16[128,4096]{1,0:T(8,128)(2,1)S(1)}, bf16[128,4096]{1,0:T(8,128)(2,1)}, u32[]{:S(2)}, u32[]{:S(2)}) collective-permute-start(bf16[128,4096]{1,0:T(8,128)(2,1)S(1)} %get-tuple-element.23.refs_0_), channel_id=1, source_target_pairs={{0,16},{4,20},{8,24},{12,28},{16,0},{20,4},{24,8},{28,12},{1,17},{... | collective-permute-start | bytes 3145736 | tf_op jit(solution)/shard_map/ppermute | solution.py:29
  47.5 36.6 %collective-permute-start.9 = (bf16[128,2048]{1,0:T(8,128)(2,1)}, bf16[128,2048]{1,0:T(8,128)(2,1)}, u32[]{:S(2)}, u32[]{:S(2)}) collective-permute-start(bf16[128,2048]{1,0:T(8,128)(2,1)} %collective-permute-done.5.refs_2_), channel_id=1, source_target_pairs={{0,16},{4,20},{8,24},{12,28},{16,0},{20,4},{24,8},{28,12},{1,17},{... | collective-permute-start | bytes 1572872 | tf_op jit(solution)/shard_map/ppermute | solution.py:29
  58.5 28.6 %collective-permute-start.6 = (bf16[128,2048]{1,0:T(8,128)(2,1)}, bf16[128,2048]{1,0:T(8,128)(2,1)S(1)}, u32[]{:S(2)}, u32[]{:S(2)}) collective-permute-start(bf16[128,2048]{1,0:T(8,128)(2,1)} %collective-permute-done.5.refs_2_), channel_id=1, source_target_pairs={{0,4},{4,0},{8,12},{12,8},{16,20},{20,16},{24,28},{28,24},{1,5},{5... | collective-permute-start | bytes 1572872 | tf_op jit(solution)/shard_map/ppermute | solution.py:29
  60.7 26.7 %collective-permute-start.8 = (bf16[128,2048]{1,0:T(8,128)(2,1)}, bf16[128,2048]{1,0:T(8,128)(2,1)S(1)}, u32[]{:S(2)}, u32[]{:S(2)}) collective-permute-start(bf16[128,2048]{1,0:T(8,128)(2,1)} %collective-permute-done.7.refs_4_), channel_id=1, source_target_pairs={{0,4},{4,0},{8,12},{12,8},{16,20},{20,16},{24,28},{28,24},{1,5},{5... | collective-permute-start | bytes 1572872 | tf_op jit(solution)/shard_map/ppermute | solution.py:29
  84.4 26.1 %collective-permute-start.29 = (bf16[128,4096]{1,0:T(8,128)(2,1)S(1)}, bf16[128,4096]{1,0:T(8,128)(2,1)}, u32[]{:S(2)}, u32[]{:S(2)}) collective-permute-start(bf16[128,4096]{1,0:T(8,128)(2,1)S(1)} %get-tuple-element.23.refs_0_), channel_id=1, source_target_pairs={{0,8},{4,12},{8,0},{12,4},{16,24},{20,28},{24,16},{28,20},{1,9},{5... | collective-permute-start | bytes 3145736 | tf_op jit(solution)/shard_map/ppermute | solution.py:29
  105.2 26.7 %collective-permute-start.12 = (bf16[256,2048]{1,0:T(8,128)(2,1)}, bf16[256,2048]{1,0:T(8,128)(2,1)}, u32[]{:S(2)}, u32[]{:S(2)}) collective-permute-start(bf16[256,2048]{1,0:T(8,128)(2,1)} %shard_map.254), channel_id=1, source_target_pairs={{0,1},{1,0},{2,3},{3,2},{4,5},{5,4},{6,7},{7,6},{8,9},{9,8},{10,11... | collective-permute-start | bytes 3145736 | tf_op jit(solution)/shard_map/ppermute | solution.py:34
  121.4 39.1 %collective-permute-start.36 = (bf16[512,1024]{1,0:T(8,128)(2,1)S(1)}, bf16[512,1024]{1,0:T(8,128)(2,1)}, u32[]{:S(2)}, u32[]{:S(2)}) collective-permute-start(bf16[512,1024]{1,0:T(8,128)(2,1)S(1)} %get-tuple-element.24.refs_0_), channel_id=1, source_target_pairs={{0,8},{4,12},{8,0},{12,4},{16,24},{20,28},{24,16},{28,20},{1,9},{5... | collective-permute-start | bytes 3145736 | tf_op jit(solution)/shard_map/ppermute | solution.py:29
  122.8 38.3 %collective-permute-start.38 = (bf16[512,1024]{1,0:T(8,128)(2,1)S(1)}, bf16[512,1024]{1,0:T(8,128)(2,1)}, u32[]{:S(2)}, u32[]{:S(2)}) collective-permute-start(bf16[512,1024]{1,0:T(8,128)(2,1)S(1)} %get-tuple-element.24.refs_0_), channel_id=1, source_target_pairs={{0,16},{4,20},{8,24},{12,28},{16,0},{20,4},{24,8},{28,12},{1,17},{... | collective-permute-start | bytes 3145736 | tf_op jit(solution)/shard_map/ppermute | solution.py:29
  124.3 33.0 %collective-permute-start.46 = (bf16[128,2048]{1,0:T(8,128)(2,1)}, bf16[128,2048]{1,0:T(8,128)(2,1)}, u32[]{:S(2)}, u32[]{:S(2)}) collective-permute-start(bf16[128,2048]{1,0:T(8,128)(2,1)} %slice.889.refs_0_), channel_id=1, source_target_pairs={{0,8},{4,12},{8,0},{12,4},{16,24},{20,28},{24,16},{28,20},{1,9},{5... | collective-permute-start | bytes 1572872 | tf_op jit(solution)/shard_map/ppermute | solution.py:29
  131.9 42.0 %collective-permute-start.11 = (bf16[256,2048]{1,0:T(8,128)(2,1)}, bf16[256,2048]{1,0:T(8,128)(2,1)}, u32[]{:S(2)}, u32[]{:S(2)}) collective-permute-start(bf16[256,2048]{1,0:T(8,128)(2,1)} %shard_map.254), channel_id=1, source_target_pairs={{0,4},{4,0},{8,12},{12,8},{16,20},{20,16},{24,28},{28,24},{1,5},{5... | collective-permute-start | bytes 3145736 | tf_op jit(solution)/shard_map/ppermute | solution.py:29
  131.9 42.4 %collective-permute-start.13 = (bf16[256,2048]{1,0:T(8,128)(2,1)}, bf16[256,2048]{1,0:T(8,128)(2,1)}, u32[]{:S(2)}, u32[]{:S(2)}) collective-permute-start(bf16[256,2048]{1,0:T(8,128)(2,1)} %collective-permute-done.12), channel_id=1, source_target_pairs={{0,4},{4,0},{8,12},{12,8},{16,20},{20,16},{24,28},{28,24},{1,5},{5... | collective-permute-start | bytes 3145736 | tf_op jit(solution)/shard_map/ppermute | solution.py:29
  173.3 35.4 %collective-permute-start.21 = (bf16[128,1024]{1,0:T(8,128)(2,1)S(1)}, bf16[128,1024]{1,0:T(8,128)(2,1)S(1)}, u32[]{:S(2)}, u32[]{:S(2)}) collective-permute-start(bf16[128,1024]{1,0:T(8,128)(2,1)S(1)} %copy-done.65), channel_id=1, source_target_pairs={{0,4},{4,0},{8,12},{12,8},{16,20},{20,16},{24,28},{28,24},{1,5},{5... | collective-permute-start | bytes 786440 | tf_op jit(solution)/shard_map/ppermute | solution.py:29
  173.3 35.5 %collective-permute-start.23 = (bf16[128,1024]{1,0:T(8,128)(2,1)}, bf16[128,1024]{1,0:T(8,128)(2,1)S(1)}, u32[]{:S(2)}, u32[]{:S(2)}) collective-permute-start(bf16[128,1024]{1,0:T(8,128)(2,1)} %collective-permute-done.22.refs_2_), channel_id=1, source_target_pairs={{0,4},{4,0},{8,12},{12,8},{16,20},{20,16},{24,28},{28,24},{1,5},{5... | collective-permute-start | bytes 786440 | tf_op jit(solution)/shard_map/ppermute | solution.py:29
  173.8 35.5 %collective-permute-start.25 = (bf16[128,1024]{1,0:T(8,128)(2,1)}, bf16[128,1024]{1,0:T(8,128)(2,1)S(1)}, u32[]{:S(2)}, u32[]{:S(2)}) collective-permute-start(bf16[128,1024]{1,0:T(8,128)(2,1)} %copy-done.111), channel_id=1, source_target_pairs={{0,4},{4,0},{8,12},{12,8},{16,20},{20,16},{24,28},{28,24},{1,5},{5... | collective-permute-start | bytes 786440 | tf_op jit(solution)/shard_map/ppermute | solution.py:29
  173.9 35.5 %collective-permute-start.27 = (bf16[128,1024]{1,0:T(8,128)(2,1)}, bf16[128,1024]{1,0:T(8,128)(2,1)S(1)}, u32[]{:S(2)}, u32[]{:S(2)}) collective-permute-start(bf16[128,1024]{1,0:T(8,128)(2,1)} %collective-permute-done.26.refs_6_), channel_id=1, source_target_pairs={{0,4},{4,0},{8,12},{12,8},{16,20},{20,16},{24,28},{28,24},{1,5},{5... | collective-permute-start | bytes 786440 | tf_op jit(solution)/shard_map/ppermute | solution.py:29
  174.3 36.6 %collective-permute-start.33 = (bf16[128,4096]{1,0:T(8,128)(2,1)}, bf16[128,4096]{1,0:T(8,128)(2,1)}, u32[]{:S(2)}, u32[]{:S(2)}) collective-permute-start(bf16[128,4096]{1,0:T(8,128)(2,1)} %collective-permute-done.31.refs_4_), channel_id=1, source_target_pairs={{0,8},{4,12},{8,0},{12,4},{16,24},{20,28},{24,16},{28,20},{1,9},{5... | collective-permute-start | bytes 3145736 | tf_op jit(solution)/shard_map/ppermute | solution.py:29
  217.6 33.1 %collective-permute-start.35 = (bf16[512,1024]{1,0:T(8,128)(2,1)S(1)}, bf16[512,1024]{1,0:T(8,128)(2,1)S(1)}, u32[]{:S(2)}, u32[]{:S(2)}) collective-permute-start(bf16[512,1024]{1,0:T(8,128)(2,1)S(1)} %copy-done.20), channel_id=1, source_target_pairs={{0,4},{4,0},{8,12},{12,8},{16,20},{20,16},{24,28},{28,24},{1,5},{5... | collective-permute-start | bytes 3145736 | tf_op jit(solution)/shard_map/ppermute | solution.py:29
  218.0 45.0 %collective-permute-start.45 = (bf16[128,2048]{1,0:T(8,128)(2,1)}, bf16[128,2048]{1,0:T(8,128)(2,1)S(1)}, u32[]{:S(2)}, u32[]{:S(2)}) collective-permute-start(bf16[128,2048]{1,0:T(8,128)(2,1)} %slice.889.refs_0_), channel_id=1, source_target_pairs={{0,4},{4,0},{8,12},{12,8},{16,20},{20,16},{24,28},{28,24},{1,5},{5... | collective-permute-start | bytes 1572872 | tf_op jit(solution)/shard_map/ppermute | solution.py:29
  218.2 32.9 %collective-permute-start.37 = (bf16[512,1024]{1,0:T(8,128)(2,1)}, bf16[512,1024]{1,0:T(8,128)(2,1)}, u32[]{:S(2)}, u32[]{:S(2)}) collective-permute-start(bf16[512,1024]{1,0:T(8,128)(2,1)} %collective-permute-done.36.refs_2_), channel_id=1, source_target_pairs={{0,4},{4,0},{8,12},{12,8},{16,20},{20,16},{24,28},{28,24},{1,5},{5... | collective-permute-start | bytes 3145736 | tf_op jit(solution)/shard_map/ppermute | solution.py:29
  252.8 31.7 %collective-permute-start.79 = (bf16[512,1024]{1,0:T(8,128)(2,1)S(1)}, bf16[512,1024]{1,0:T(8,128)(2,1)}, u32[]{:S(2)}, u32[]{:S(2)}) collective-permute-start(bf16[512,1024]{1,0:T(8,128)(2,1)S(1)} %copy-done.21), channel_id=1, source_target_pairs={{0,16},{4,20},{8,24},{12,28},{16,0},{20,4},{24,8},{28,12},{1,17},{... | collective-permute-start | bytes 3145736 | tf_op jit(solution)/shard_map/ppermute | solution.py:29
  284.2 26.2 %collective-permute-start.77 = (bf16[512,1024]{1,0:T(8,128)(2,1)S(1)}, bf16[512,1024]{1,0:T(8,128)(2,1)}, u32[]{:S(2)}, u32[]{:S(2)}) collective-permute-start(bf16[512,1024]{1,0:T(8,128)(2,1)S(1)} %copy-done.21), channel_id=1, source_target_pairs={{0,8},{4,12},{8,0},{12,4},{16,24},{20,28},{24,16},{28,20},{1,9},{5... | collective-permute-start | bytes 3145736 | tf_op jit(solution)/shard_map/ppermute | solution.py:29
  285.0 46.9 %collective-permute-start.81 = (bf16[512,1024]{1,0:T(8,128)(2,1)}, bf16[512,1024]{1,0:T(8,128)(2,1)}, u32[]{:S(2)}, u32[]{:S(2)}) collective-permute-start(bf16[512,1024]{1,0:T(8,128)(2,1)} %collective-permute-done.79.refs_4_), channel_id=1, source_target_pairs={{0,8},{4,12},{8,0},{12,4},{16,24},{20,28},{24,16},{28,20},{1,9},{5... | collective-permute-start | bytes 3145736 | tf_op jit(solution)/shard_map/ppermute | solution.py:29
  286.4 45.5 %collective-permute-start.53 = (bf16[256,2048]{1,0:T(8,128)(2,1)}, bf16[256,2048]{1,0:T(8,128)(2,1)}, u32[]{:S(2)}, u32[]{:S(2)}) collective-permute-start(bf16[256,2048]{1,0:T(8,128)(2,1)} %shard_map.259), channel_id=1, source_target_pairs={{0,1},{1,0},{2,3},{3,2},{4,5},{5,4},{6,7},{7,6},{8,9},{9,8},{10,11... | collective-permute-start | bytes 3145736 | tf_op jit(solution)/shard_map/ppermute | solution.py:34
  296.5 51.1 %collective-permute-start.80 = (bf16[512,1024]{1,0:T(8,128)(2,1)}, bf16[512,1024]{1,0:T(8,128)(2,1)}, u32[]{:S(2)}, u32[]{:S(2)}) collective-permute-start(bf16[512,1024]{1,0:T(8,128)(2,1)} %collective-permute-done.79.refs_4_), channel_id=1, source_target_pairs={{0,4},{4,0},{8,12},{12,8},{16,20},{20,16},{24,28},{28,24},{1,5},{5... | collective-permute-start | bytes 3145736 | tf_op jit(solution)/shard_map/ppermute | solution.py:29
  310.4 37.2 %collective-permute-start.78 = (bf16[512,1024]{1,0:T(8,128)(2,1)}, bf16[512,1024]{1,0:T(8,128)(2,1)}, u32[]{:S(2)}, u32[]{:S(2)}) collective-permute-start(bf16[512,1024]{1,0:T(8,128)(2,1)} %collective-permute-done.77.refs_2_), channel_id=1, source_target_pairs={{0,4},{4,0},{8,12},{12,8},{16,20},{20,16},{24,28},{28,24},{1,5},{5... | collective-permute-start | bytes 3145736 | tf_op jit(solution)/shard_map/ppermute | solution.py:29
  310.4 46.8 %collective-permute-start.52 = (bf16[256,2048]{1,0:T(8,128)(2,1)}, bf16[256,2048]{1,0:T(8,128)(2,1)}, u32[]{:S(2)}, u32[]{:S(2)}) collective-permute-start(bf16[256,2048]{1,0:T(8,128)(2,1)} %shard_map.259), channel_id=1, source_target_pairs={{0,4},{4,0},{8,12},{12,8},{16,20},{20,16},{24,28},{28,24},{1,5},{5... | collective-permute-start | bytes 3145736 | tf_op jit(solution)/shard_map/ppermute | solution.py:29
  331.9 27.1 %collective-permute-start.54 = (bf16[256,2048]{1,0:T(8,128)(2,1)}, bf16[256,2048]{1,0:T(8,128)(2,1)}, u32[]{:S(2)}, u32[]{:S(2)}) collective-permute-start(bf16[256,2048]{1,0:T(8,128)(2,1)} %collective-permute-done.53), channel_id=1, source_target_pairs={{0,4},{4,0},{8,12},{12,8},{16,20},{20,16},{24,28},{28,24},{1,5},{5... | collective-permute-start | bytes 3145736 | tf_op jit(solution)/shard_map/ppermute | solution.py:29
  347.6 33.8 %collective-permute-start.62 = (bf16[128,1024]{1,0:T(8,128)(2,1)S(1)}, bf16[128,1024]{1,0:T(8,128)(2,1)}, u32[]{:S(2)}, u32[]{:S(2)}) collective-permute-start(bf16[128,1024]{1,0:T(8,128)(2,1)S(1)} %copy-done.66), channel_id=1, source_target_pairs={{0,4},{4,0},{8,12},{12,8},{16,20},{20,16},{24,28},{28,24},{1,5},{5... | collective-permute-start | bytes 786440 | tf_op jit(solution)/shard_map/ppermute | solution.py:29
  347.7 34.3 %collective-permute-start.70 = (bf16[128,4096]{1,0:T(8,128)(2,1)S(1)}, bf16[128,4096]{1,0:T(8,128)(2,1)}, u32[]{:S(2)}, u32[]{:S(2)}) collective-permute-start(bf16[128,4096]{1,0:T(8,128)(2,1)S(1)} %copy-done.18), channel_id=1, source_target_pairs={{0,8},{4,12},{8,0},{12,4},{16,24},{20,28},{24,16},{28,20},{1,9},{5... | collective-permute-start | bytes 3145736 | tf_op jit(solution)/shard_map/ppermute | solution.py:29
  348.0 47.4 %collective-permute-start.72 = (bf16[128,4096]{1,0:T(8,128)(2,1)S(1)}, bf16[128,4096]{1,0:T(8,128)(2,1)}, u32[]{:S(2)}, u32[]{:S(2)}) collective-permute-start(bf16[128,4096]{1,0:T(8,128)(2,1)S(1)} %copy-done.18), channel_id=1, source_target_pairs={{0,16},{4,20},{8,24},{12,28},{16,0},{20,4},{24,8},{28,12},{1,17},{... | collective-permute-start | bytes 3145736 | tf_op jit(solution)/shard_map/ppermute | solution.py:29
  359.1 35.9 %collective-permute-start.66 = (bf16[128,1024]{1,0:T(8,128)(2,1)}, bf16[128,1024]{1,0:T(8,128)(2,1)}, u32[]{:S(2)}, u32[]{:S(2)}) collective-permute-start(bf16[128,1024]{1,0:T(8,128)(2,1)} %collective-permute-done.65.refs_4_), channel_id=1, source_target_pairs={{0,4},{4,0},{8,12},{12,8},{16,20},{20,16},{24,28},{28,24},{1,5},{5... | collective-permute-start | bytes 786440 | tf_op jit(solution)/shard_map/ppermute | solution.py:29
  514.3 57.1 %collective-permute-start.85 = (bf16[256,2048]{1,0:T(8,128)(2,1)}, bf16[256,2048]{1,0:T(8,128)(2,1)}, u32[]{:S(2)}, u32[]{:S(2)}) collective-permute-start(bf16[256,2048]{1,0:T(8,128)(2,1)} %get-tuple-element.76), channel_id=1, source_target_pairs={{0,4},{4,0},{8,12},{12,8},{16,20},{20,16},{24,28},{28,24},{1,5},{5... | collective-permute-start | bytes 3145736 | tf_op jit(solution)/shard_map/ppermute | solution.py:29
  540.1 31.5 %collective-permute-start.87 = (bf16[256,2048]{1,0:T(8,128)(2,1)}, bf16[256,2048]{1,0:T(8,128)(2,1)}, u32[]{:S(2)}, u32[]{:S(2)}) collective-permute-start(bf16[256,2048]{1,0:T(8,128)(2,1)} %add_convert_fusion.19), channel_id=1, source_target_pairs={{0,1},{1,0},{2,3},{3,2},{4,5},{5,4},{6,7},{7,6},{8,9},{9,8},{10,11... | collective-permute-start | bytes 3145736 | tf_op jit(solution)/shard_map/ppermute | solution.py:34
  542.2 162.8 %collective-permute-start.153 = (bf16[2048,512]{0,1:T(8,128)(2,1)}, bf16[2048,512]{0,1:T(8,128)(2,1)}, u32[]{:S(2)}, u32[]{:S(2)}) collective-permute-start(bf16[2048,512]{0,1:T(8,128)(2,1)} %convolution_convert_fusion.1), channel_id=1, source_target_pairs={{0,4},{4,0},{8,12},{12,8},{16,20},{20,16},{24,28},{28,24},{1,5},{5... | collective-permute-start | bytes 6291464 | tf_op jit(solution)/shard_map/ppermute | solution.py:29
  558.8 158.9 %collective-permute-start.156 = (bf16[2048,512]{0,1:T(8,128)(2,1)}, bf16[2048,512]{0,1:T(8,128)(2,1)}, u32[]{:S(2)}, u32[]{:S(2)}) collective-permute-start(bf16[2048,512]{0,1:T(8,128)(2,1)} %convolution_convert_fusion), channel_id=1, source_target_pairs={{0,4},{4,0},{8,12},{12,8},{16,20},{20,16},{24,28},{28,24},{1,5},{5... | collective-permute-start | bytes 6291464 | tf_op jit(solution)/shard_map/ppermute | solution.py:29
  570.0 139.4 %collective-permute-start.137 = (bf16[512,2048]{1,0:T(8,128)(2,1)}, bf16[512,2048]{1,0:T(8,128)(2,1)}, u32[]{:S(2)}, u32[]{:S(2)}) collective-permute-start(bf16[512,2048]{1,0:T(8,128)(2,1)} %convolution_convert_fusion.5), channel_id=1, source_target_pairs={{0,4},{4,0},{8,12},{12,8},{16,20},{20,16},{24,28},{28,24},{1,5},{5... | collective-permute-start | bytes 6291464 | tf_op jit(solution)/shard_map/ppermute | solution.py:29
  571.4 141.9 %collective-permute-start.140 = (bf16[512,2048]{1,0:T(8,128)(2,1)}, bf16[512,2048]{1,0:T(8,128)(2,1)}, u32[]{:S(2)}, u32[]{:S(2)}) collective-permute-start(bf16[512,2048]{1,0:T(8,128)(2,1)} %convolution_convert_fusion.4), channel_id=1, source_target_pairs={{0,4},{4,0},{8,12},{12,8},{16,20},{20,16},{24,28},{28,24},{1,5},{5... | collective-permute-start | bytes 6291464 | tf_op jit(solution)/shard_map/ppermute | solution.py:29
  669.5 89.9 %collective-permute-start.89 = (bf16[256,2048]{1,0:T(8,128)(2,1)}, bf16[256,2048]{1,0:T(8,128)(2,1)}, u32[]{:S(2)}, u32[]{:S(2)}) collective-permute-start(bf16[256,2048]{1,0:T(8,128)(2,1)} %get-tuple-element.75), channel_id=1, source_target_pairs={{0,4},{4,0},{8,12},{12,8},{16,20},{20,16},{24,28},{28,24},{1,5},{5... | collective-permute-start | bytes 3145736 | tf_op jit(solution)/shard_map/ppermute | solution.py:29
  705.0 158.5 %collective-permute-start.88 = (bf16[256,2048]{1,0:T(8,128)(2,1)}, bf16[256,2048]{1,0:T(8,128)(2,1)}, u32[]{:S(2)}, u32[]{:S(2)}) collective-permute-start(bf16[256,2048]{1,0:T(8,128)(2,1)} %get-tuple-element.74), channel_id=1, source_target_pairs={{0,4},{4,0},{8,12},{12,8},{16,20},{20,16},{24,28},{28,24},{1,5},{5... | collective-permute-start | bytes 3145736 | tf_op jit(solution)/shard_map/ppermute | solution.py:29
  709.4 183.4 %collective-permute-start.145 = (bf16[2048,512]{0,1:T(8,128)(2,1)}, bf16[2048,512]{0,1:T(8,128)(2,1)}, u32[]{:S(2)}, u32[]{:S(2)}) collective-permute-start(bf16[2048,512]{0,1:T(8,128)(2,1)} %convolution_convert_fusion.3), channel_id=1, source_target_pairs={{0,4},{4,0},{8,12},{12,8},{16,20},{20,16},{24,28},{28,24},{1,5},{5... | collective-permute-start | bytes 6291464 | tf_op jit(solution)/shard_map/ppermute | solution.py:29
  730.4 35.7 %collective-permute-start.154 = (bf16[1024,512]{0,1:T(8,128)(2,1)S(1)}, bf16[1024,512]{0,1:T(8,128)(2,1)S(1)}, u32[]{:S(2)}, u32[]{:S(2)}) collective-permute-start(bf16[1024,512]{0,1:T(8,128)(2,1)S(1)} %add_convert_fusion.2), channel_id=1, source_target_pairs={{0,8},{4,12},{8,0},{12,4},{16,24},{20,28},{24,16},{28,20},{1,9},{5... | collective-permute-start | bytes 3145736 | tf_op jit(solution)/shard_map/ppermute | solution.py:29
  765.5 26.1 %collective-permute-start.141 = (bf16[256,2048]{1,0:T(8,128)(2,1)S(1)}, bf16[256,2048]{1,0:T(8,128)(2,1)S(1)}, u32[]{:S(2)}, u32[]{:S(2)}) collective-permute-start(bf16[256,2048]{1,0:T(8,128)(2,1)S(1)} %add_convert_fusion.8), channel_id=1, source_target_pairs={{0,16},{4,20},{8,24},{12,28},{16,0},{20,4},{24,8},{28,12},{1,17},{... | collective-permute-start | bytes 3145736 | tf_op jit(solution)/shard_map/ppermute | solution.py:29
  766.1 44.4 %collective-permute-start.157 = (bf16[1024,512]{0,1:T(8,128)(2,1)S(1)}, bf16[1024,512]{0,1:T(8,128)(2,1)S(1)}, u32[]{:S(2)}, u32[]{:S(2)}) collective-permute-start(bf16[1024,512]{0,1:T(8,128)(2,1)S(1)} %add_convert_fusion), channel_id=1, source_target_pairs={{0,16},{4,20},{8,24},{12,28},{16,0},{20,4},{24,8},{28,12},{1,17},{... | collective-permute-start | bytes 3145736 | tf_op jit(solution)/shard_map/ppermute | solution.py:29
  781.8 34.7 %collective-permute-start.108 = (bf16[512,1536]{1,0:T(8,128)(2,1)S(1)}, bf16[512,1536]{1,0:T(8,128)(2,1)S(1)}, u32[]{:S(2)}, u32[]{:S(2)}) collective-permute-start(bf16[512,1536]{1,0:T(8,128)(2,1)S(1)} %copy-done.232), channel_id=1, source_target_pairs={{0,4},{4,0},{8,12},{12,8},{16,20},{20,16},{24,28},{28,24},{1,5},{5... | collective-permute-start | bytes 4718600 | tf_op jit(solution)/shard_map/ppermute | solution.py:29
  791.6 28.1 %collective-permute-start.105 = (bf16[512,1536]{1,0:T(8,128)(2,1)S(1)}, bf16[512,1536]{1,0:T(8,128)(2,1)S(1)}, u32[]{:S(2)}, u32[]{:S(2)}) collective-permute-start(bf16[512,1536]{1,0:T(8,128)(2,1)S(1)} %copy-done.90), channel_id=1, source_target_pairs={{0,4},{4,0},{8,12},{12,8},{16,20},{20,16},{24,28},{28,24},{1,5},{5... | collective-permute-start | bytes 4718600 | tf_op jit(solution)/shard_map/ppermute | solution.py:29
  815.7 84.0 %collective-permute-start.148 = (bf16[2048,512]{0,1:T(8,128)(2,1)}, bf16[2048,512]{0,1:T(8,128)(2,1)}, u32[]{:S(2)}, u32[]{:S(2)}) collective-permute-start(bf16[2048,512]{0,1:T(8,128)(2,1)} %convolution_convert_fusion.2), channel_id=1, source_target_pairs={{0,4},{4,0},{8,12},{12,8},{16,20},{20,16},{24,28},{28,24},{1,5},{5... | collective-permute-start | bytes 6291464 | tf_op jit(solution)/shard_map/ppermute | solution.py:29
  844.7 59.5 %collective-permute-start.129 = (bf16[512,2048]{1,0:T(8,128)(2,1)}, bf16[512,2048]{1,0:T(8,128)(2,1)}, u32[]{:S(2)}, u32[]{:S(2)}) collective-permute-start(bf16[512,2048]{1,0:T(8,128)(2,1)} %convolution_convert_fusion.7), channel_id=1, source_target_pairs={{0,4},{4,0},{8,12},{12,8},{16,20},{20,16},{24,28},{28,24},{1,5},{5... | collective-permute-start | bytes 6291464 | tf_op jit(solution)/shard_map/ppermute | solution.py:29
  863.5 46.7 %collective-permute-start.132 = (bf16[512,2048]{1,0:T(8,128)(2,1)}, bf16[512,2048]{1,0:T(8,128)(2,1)}, u32[]{:S(2)}, u32[]{:S(2)}) collective-permute-start(bf16[512,2048]{1,0:T(8,128)(2,1)} %convolution_convert_fusion.6), channel_id=1, source_target_pairs={{0,4},{4,0},{8,12},{12,8},{16,20},{20,16},{24,28},{28,24},{1,5},{5... | collective-permute-start | bytes 6291464 | tf_op jit(solution)/shard_map/ppermute | solution.py:29
  873.0 100.8 %collective-permute-start.106 = (bf16[256,1536]{1,0:T(8,128)(2,1)}, bf16[256,1536]{1,0:T(8,128)(2,1)}, u32[]{:S(2)}, u32[]{:S(2)}) collective-permute-start(bf16[256,1536]{1,0:T(8,128)(2,1)} %add_convert_fusion.20), channel_id=1, source_target_pairs={{0,8},{4,12},{8,0},{12,4},{16,24},{20,28},{24,16},{28,20},{1,9},{5... | collective-permute-start | bytes 2359304 | tf_op jit(solution)/shard_map/ppermute | solution.py:29
  892.7 82.3 %collective-permute-start.109 = (bf16[256,1536]{1,0:T(8,128)(2,1)}, bf16[256,1536]{1,0:T(8,128)(2,1)}, u32[]{:S(2)}, u32[]{:S(2)}) collective-permute-start(bf16[256,1536]{1,0:T(8,128)(2,1)} %fusion.33), channel_id=1, source_target_pairs={{0,16},{4,20},{8,24},{12,28},{16,0},{20,4},{24,8},{28,12},{1,17},{... | collective-permute-start | bytes 2359304 | tf_op jit(solution)/shard_map/ppermute | solution.py:29
  910.1 28.6 %collective-permute-start.161 = (f32[1,2048]{1,0:T(1,128)S(1)}, f32[1,2048]{1,0:T(1,128)S(1)}, u32[]{:S(2)}, u32[]{:S(2)}) collective-permute-start(f32[1,2048]{1,0:T(1,128)S(1)} %bitcast.441), channel_id=1, source_target_pairs={{0,4},{4,0},{8,12},{12,8},{16,20},{20,16},{24,28},{28,24},{1,5},{5... | collective-permute-start | bytes 24584 | tf_op jit(solution)/shard_map/ppermute | solution.py:29
  924.1 149.9 %collective-permute-start.97 = (bf16[512,1536]{1,0:T(8,128)(2,1)}, bf16[512,1536]{1,0:T(8,128)(2,1)}, u32[]{:S(2)}, u32[]{:S(2)}) collective-permute-start(bf16[512,1536]{1,0:T(8,128)(2,1)} %convolution_convert_fusion.11), channel_id=1, source_target_pairs={{0,4},{4,0},{8,12},{12,8},{16,20},{20,16},{24,28},{28,24},{1,5},{5... | collective-permute-start | bytes 4718600 | tf_op jit(solution)/shard_map/ppermute | solution.py:29
  929.0 90.8 %collective-permute-start.91 = (f32[256,1024]{1,0:T(8,128)}, f32[256,1024]{1,0:T(8,128)}, u32[]{:S(2)}, u32[]{:S(2)}) collective-permute-start(f32[256,1024]{1,0:T(8,128)} %add_add_fusion.4), channel_id=1, source_target_pairs={{0,0},{4,1},{1,2},{5,3},{2,4},{6,5},{3,6},{7,7},{8,8},{12,9},{9,10... | collective-permute-start | bytes 3145736 | tf_op jit(solution)/shard_map/ppermute | solution.py:505
  970.7 69.5 %collective-permute-start.146 = (bf16[1024,512]{0,1:T(8,128)(2,1)}, bf16[1024,512]{0,1:T(8,128)(2,1)}, u32[]{:S(2)}, u32[]{:S(2)}) collective-permute-start(bf16[1024,512]{0,1:T(8,128)(2,1)} %add_convert_fusion.6), channel_id=1, source_target_pairs={{0,8},{4,12},{8,0},{12,4},{16,24},{20,28},{24,16},{28,20},{1,9},{5... | collective-permute-start | bytes 3145736 | tf_op jit(solution)/shard_map/ppermute | solution.py:29
  997.8 44.6 %collective-permute-start.149 = (bf16[1024,512]{0,1:T(8,128)(2,1)S(1)}, bf16[1024,512]{0,1:T(8,128)(2,1)S(1)}, u32[]{:S(2)}, u32[]{:S(2)}) collective-permute-start(bf16[1024,512]{0,1:T(8,128)(2,1)S(1)} %copy-done.234), channel_id=1, source_target_pairs={{0,16},{4,20},{8,24},{12,28},{16,0},{20,4},{24,8},{28,12},{1,17},{... | collective-permute-start | bytes 3145736 | tf_op jit(solution)/shard_map/ppermute | solution.py:29
  1019.8 57.0 %collective-permute-start.100 = (bf16[512,1536]{1,0:T(8,128)(2,1)S(1)}, bf16[512,1536]{1,0:T(8,128)(2,1)S(1)}, u32[]{:S(2)}, u32[]{:S(2)}) collective-permute-start(bf16[512,1536]{1,0:T(8,128)(2,1)S(1)} %copy-done.231), channel_id=1, source_target_pairs={{0,4},{4,0},{8,12},{12,8},{16,20},{20,16},{24,28},{28,24},{1,5},{5... | collective-permute-start | bytes 4718600 | tf_op jit(solution)/shard_map/ppermute | solution.py:29
  1042.4 38.9 %collective-permute-start.147 = (bf16[512,512]{0,1:T(8,128)(2,1)S(1)}, bf16[512,512]{0,1:T(8,128)(2,1)S(1)}, u32[]{:S(2)}, u32[]{:S(2)}) collective-permute-start(bf16[512,512]{0,1:T(8,128)(2,1)S(1)} %add_convert_fusion.34), channel_id=1, source_target_pairs={{0,16},{4,20},{8,24},{12,28},{16,0},{20,4},{24,8},{28,12},{1,17},{... | collective-permute-start | bytes 1572872 | tf_op jit(solution)/shard_map/ppermute | solution.py:29
  1047.9 34.8 %collective-permute-start.150 = (bf16[512,512]{0,1:T(8,128)(2,1)S(1)}, bf16[512,512]{0,1:T(8,128)(2,1)S(1)}, u32[]{:S(2)}, u32[]{:S(2)}) collective-permute-start(bf16[512,512]{0,1:T(8,128)(2,1)S(1)} %add_convert_fusion.31), channel_id=1, source_target_pairs={{0,8},{4,12},{8,0},{12,4},{16,24},{20,28},{24,16},{28,20},{1,9},{5... | collective-permute-start | bytes 1572872 | tf_op jit(solution)/shard_map/ppermute | solution.py:29
  1076.8 39.7 %collective-permute-start.98 = (bf16[256,1536]{1,0:T(8,128)(2,1)}, bf16[256,1536]{1,0:T(8,128)(2,1)}, u32[]{:S(2)}, u32[]{:S(2)}) collective-permute-start(bf16[256,1536]{1,0:T(8,128)(2,1)} %add_convert_fusion.22), channel_id=1, source_target_pairs={{0,8},{4,12},{8,0},{12,4},{16,24},{20,28},{24,16},{28,20},{1,9},{5... | collective-permute-start | bytes 2359304 | tf_op jit(solution)/shard_map/ppermute | solution.py:29
  1081.2 38.7 %collective-permute-start.101 = (bf16[256,1536]{1,0:T(8,128)(2,1)}, bf16[256,1536]{1,0:T(8,128)(2,1)}, u32[]{:S(2)}, u32[]{:S(2)}) collective-permute-start(bf16[256,1536]{1,0:T(8,128)(2,1)} %fusion.31), channel_id=1, source_target_pairs={{0,16},{4,20},{8,24},{12,28},{16,0},{20,4},{24,8},{28,12},{1,17},{... | collective-permute-start | bytes 2359304 | tf_op jit(solution)/shard_map/ppermute | solution.py:29
  1107.1 33.4 %collective-permute-start.152 = (bf16[128,1024]{1,0:T(8,128)(2,1)S(1)}, bf16[128,1024]{1,0:T(8,128)(2,1)S(1)}, u32[]{:S(2)}, u32[]{:S(2)}) collective-permute-start(bf16[128,1024]{1,0:T(8,128)(2,1)S(1)} %fusion.162), channel_id=1, source_target_pairs={{0,2},{1,3},{2,0},{3,1},{4,6},{5,7},{6,4},{7,5},{8,10},{9,11},{10,... | collective-permute-start | bytes 786440 | tf_op jit(solution)/shard_map/ppermute | solution.py:34
  (345 other events, 4823.8 us)

commit v2 on v1

--- a/solution.py
+++ b/solution.py
@@ -157,117 +157,12 @@
     return current, me ^ (places % SMALL), plane ^ (places // SMALL)
 
 
-VMEM_LIMIT = 56 * 1024 * 1024
-
-
-def forward_kernel(count, depth, place, a_ref, *refs):
-    weights, out, ordered = refs[:count], refs[count], refs[count + 1]
-
-    @pl.when(pl.program_id(0) == 0)
-    def _():
-        for part in range(count):
-            start = pl.multiple_of((place[0] ^ part) * depth, 128)
-            ordered[:, part * depth : (part + 1) * depth] = a_ref[:, pl.ds(start, depth)]
-
-    whole = jnp.concatenate([weight[...] for weight in weights], axis=0)
-    out[...] = jnp.dot(ordered[...], whole, preferred_element_type=f32).astype(out.dtype)
-
-
-def times(a, parts, out_type):
-    if not isinstance(parts, list):
-        return jnp.dot(a, parts, preferred_element_type=f32).astype(out_type)
-    tokens, inner = a.shape
-    depth, columns = parts[0].shape
-    tile = min(512, columns)
-    count = len(parts)
-    place = lax.axis_index("dp").astype(jnp.int32).reshape(1)
-    return pl.pallas_call(
-        functools.partial(forward_kernel, count, depth),
-        out_shape=jax.ShapeDtypeStruct((tokens, columns), out_type),
-        grid_spec=pltpu.PrefetchScalarGridSpec(
-            num_scalar_prefetch=1,
-            grid=(columns // tile,),
-            in_specs=[pl.BlockSpec((tokens, inner), lambda i, s: (0, 0))]
-            + [pl.BlockSpec((depth, tile), lambda i, s: (0, i))] * count,
-            out_specs=pl.BlockSpec((tokens, tile), lambda i, s: (0, i)),
-            scratch_shapes=[pltpu.VMEM((tokens, inner), bf16)],
-        ),
-        compiler_params=pltpu.CompilerParams(vmem_limit_bytes=VMEM_LIMIT),
-        cost_estimate=pl.CostEstimate(
-            flops=2 * tokens * inner * columns,
-            bytes_accessed=2 * inner * columns + 6 * tokens * (inner + columns),
-            transcendentals=0,
-        ),
-    )(place, a, *parts)
-
-
-def backward_kernel(count, depth, rows, place, a_ref, *refs):
-    weights, out, total = refs[:count], refs[count], refs[count + 1]
-    step, steps = pl.program_id(0), pl.num_programs(0)
-    whole = jnp.concatenate([weight[...] for weight in weights], axis=0)
-    product = lax.dot_general(
-        a_ref[...], whole, (((1,), (1,)), ((), ())), preferred_element_type=f32
-    )
-    if rows == depth:
-
-        @pl.when(step == 0)
-        def _():
-            total[...] = product
-
-        @pl.when(step > 0)
-        def _():
-            total[...] += product
-
-        @pl.when(step == steps - 1)
-        def _():
-            for part in range(count):
-                start = pl.multiple_of((place[0] ^ part) * depth, 128)
-                out[:, pl.ds(start, depth)] = total[:, part * depth : (part + 1) * depth].astype(
-                    out.dtype
-                )
-
-    else:
-        for part in range(count):
-            start = pl.multiple_of((place[0] ^ part) * depth + step * rows, 128)
-            out[:, pl.ds(start, rows)] = product[:, part * rows : (part + 1) * rows].astype(out.dtype)
-
-
-def times_transposed(a, parts, out_type):
-    if not isinstance(parts, list):
-        return lax.dot_general(
-            a, parts, (((1,), (1,)), ((), ())), preferred_element_type=f32
-        ).astype(out_type)
-    tokens, inner = a.shape
-    depth = parts[0].shape[0]
-    count = len(parts)
-    place = lax.axis_index("dp").astype(jnp.int32).reshape(1)
-    if depth > 128:
-        rows, tile = 128, inner
-        grid = depth // rows
-        a_spec = pl.BlockSpec((tokens, inner), lambda i, s: (0, 0))
-        w_spec = pl.BlockSpec((rows, inner), lambda i, s: (i, 0))
-    else:
-        rows, tile = depth, min(512, inner)
-        grid = inner // tile
-        a_spec = pl.BlockSpec((tokens, tile), lambda i, s: (0, i))
-        w_spec = pl.BlockSpec((rows, tile), lambda i, s: (0, i))
-    return pl.pallas_call(
-        functools.partial(backward_kernel, count, depth, rows),
-        out_shape=jax.ShapeDtypeStruct((tokens, count * depth), out_type),
-        grid_spec=pltpu.PrefetchScalarGridSpec(
-            num_scalar_prefetch=1,
-            grid=(grid,),
-            in_specs=[a_spec] + [w_spec] * count,
-            out_specs=pl.BlockSpec((tokens, count * depth), lambda i, s: (0, 0)),
-            scratch_shapes=[pltpu.VMEM((tokens, count * rows), f32)],
-        ),
-        compiler_params=pltpu.CompilerParams(vmem_limit_bytes=VMEM_LIMIT),
-        cost_estimate=pl.CostEstimate(
-            flops=2 * tokens * inner * count * depth,
-            bytes_accessed=2 * inner * count * depth + 6 * tokens * (inner + count * depth),
-            transcendentals=0,
-        ),
-    )(place, a, *parts)
+def times(a, weight, out_type):
+    return jnp.dot(a, weight, preferred_element_type=f32).astype(out_type)
+
+
+def times_transposed(a, weight, out_type):
+    return lax.dot_general(a, weight, (((1,), (1,)), ((), ())), preferred_element_type=f32).astype(out_type)
 
 
 def spread_keys(own):
@@ -388,6 +283,1150 @@
     return jnp.pad(flat, (0, length - flat.shape[0])).reshape(-1, WIDE)
 
 
+def table_rows_of(changes, from_dp, from_seq, buckets, layers, model_width):
+    count, planes = lax.axis_size("dp"), lax.axis_size("seq")
+    owners = (from_dp // 2) * 2 + from_seq // 2
+    source_buckets = jnp.sum(
+        jnp.where(owners[:, None] == jnp.arange(count)[None, :], buckets[None, :], 0), axis=1
+    )
+    return chosen_rows(changes, source_buckets, layers, model_width)
+
+
+def chosen_rows(changes, source_buckets, layers, model_width):
+    count, planes = lax.axis_size("dp"), lax.axis_size("seq")
+    table_share = BUCKETS // (count * planes)
+    first_row = (lax.axis_index("dp") * planes + lax.axis_index("seq")) * table_share
+    chosen = (source_buckets[None, :] == (first_row + jnp.arange(table_share))[:, None]).astype(f32)
+    table_grad = jnp.dot(chosen, changes, precision=lax.Precision.HIGHEST)
+    return jnp.stack(
+        [table_grad[:, layer * model_width : (layer + 1) * model_width] for layer in range(layers)]
+    )
+
+
+VMEM_LIMIT = 64_000 * 1024
+TILE = 1024
+BLOCK = 128
+NT = (((1,), (1,)), ((), ()))
+TN = (((0,), (0,)), ((), ()))
+
+
+def whole_spec(array):
+    zeros = (0,) * len(array.shape)
+    return pl.BlockSpec(array.shape, lambda *_: zeros)
+
+
+def run(body, grid, inputs, outputs, scratch=(), deps=(), aliases=(), cost=4):
+    deps = tuple(aliases) + tuple(deps)
+    arrays = [array for array, _ in inputs]
+    specs = [spec if spec is not None else whole_spec(array) for array, spec in inputs]
+    shapes = [jax.ShapeDtypeStruct(shape, kind) for shape, kind, _ in outputs]
+    out_specs = [
+        spec if spec is not None else whole_spec(shape) for shape, (_, _, spec) in zip(shapes, outputs)
+    ]
+    count, extra = len(arrays), len(deps)
+
+    def kernel(place, *refs):
+        body(place, refs[:count], refs[count + extra : count + extra + len(shapes)], refs[count + extra + len(shapes) :])
+
+    place = jnp.stack([lax.axis_index("dp"), lax.axis_index("seq")]).astype(jnp.int32)
+    return pl.pallas_call(
+        kernel,
+        out_shape=shapes,
+        grid_spec=pltpu.PrefetchScalarGridSpec(
+            num_scalar_prefetch=1,
+            grid=(grid,),
+            in_specs=specs + [pl.BlockSpec(memory_space=pl.ANY)] * extra,
+            out_specs=out_specs,
+            scratch_shapes=list(scratch),
+        ),
+        input_output_aliases={1 + count + i: i for i in range(len(aliases))},
+        compiler_params=pltpu.CompilerParams(vmem_limit_bytes=VMEM_LIMIT),
+        cost_estimate=pl.CostEstimate(flops=0, bytes_accessed=cost * 3_000_000, transcendentals=0),
+    )(place, *arrays, *deps)
+
+
+def pack_inputs(pack, tile_of):
+    return [
+        (array, pl.BlockSpec((rows, TILE), lambda i, s, r=row_block: (r, tile_of(i))))
+        for array, row_block, rows in pack
+    ]
+
+
+def join(refs):
+    return jnp.concatenate([ref[...] for ref in refs], axis=0)
+
+
+def block_at(place, part, stride=BLOCK, offset=0):
+    return pl.ds(pl.multiple_of((place[0] ^ part) * stride + offset, BLOCK), BLOCK)
+
+
+def columns_in_order(place, ref, stride=BLOCK, offset=0):
+    return jnp.concatenate(
+        [ref[:, block_at(place, part, stride, offset)] for part in range(SMALL)], axis=1
+    )
+
+
+def normalise(v):
+    center = v - jnp.mean(v, axis=-1, keepdims=True)
+    inverse = lax.rsqrt(jnp.mean(center * center, axis=-1, keepdims=True) + epsilon)
+    return center * inverse, inverse
+
+
+def modulated(v, vec, gain_row):
+    unit, _ = normalise(v)
+    return (unit * vec[gain_row : gain_row + 1, :] + vec[gain_row + 1 : gain_row + 2, :]) * vec[6:7, :]
+
+
+def modulated_back(v, vec, gain_row, grad):
+    unit, inverse = normalise(v)
+    gain, shift, scale = vec[gain_row : gain_row + 1, :], vec[gain_row + 1 : gain_row + 2, :], vec[6:7, :]
+    scale_grad = jnp.sum(grad * (unit * gain + shift), axis=0, keepdims=True)
+    inner = grad * scale
+    gain_grad = jnp.sum(inner * unit, axis=0, keepdims=True)
+    shift_grad = jnp.sum(inner, axis=0, keepdims=True)
+    inner = inner * gain
+    back = inverse * (
+        inner
+        - jnp.mean(inner, axis=-1, keepdims=True)
+        - unit * jnp.mean(inner * unit, axis=-1, keepdims=True)
+    )
+    return back, gain_grad, shift_grad, scale_grad
+
+
+ROOT = math.sqrt(2.0 / math.pi)
+CUBIC = 0.044715
+
+
+def first_norm(x, vec, deps=()):
+    def body(place, ins, outs, _):
+        outs[0][...] = modulated(ins[0][...].astype(f32), ins[1], 0).astype(bf16)
+
+    return run(body, 1, [(x, None), (vec, None)], [(x.shape, bf16, None)], deps=deps)[0]
+
+
+def project(a, pack, first_tile, tiles, deps=()):
+    tokens, width = a.shape
+
+    def body(place, ins, outs, scratch):
+        @pl.when(pl.program_id(0) == 0)
+        def _():
+            scratch[0][...] = columns_in_order(place, ins[0])
+
+        outs[0][...] = jnp.dot(scratch[0][...], join(ins[1:]), preferred_element_type=f32).astype(bf16)
+
+    return run(
+        body,
+        tiles,
+        [(a, None)] + pack_inputs(pack, lambda i: first_tile + i),
+        [((tokens, tiles * TILE), bf16, pl.BlockSpec((tokens, TILE), lambda i, s: (0, i)))],
+        [pltpu.VMEM((tokens, width), bf16)],
+        deps=deps,
+    )[0]
+
+
+def key_specs(chunks):
+    return [
+        (chunk, pl.BlockSpec((chunk.shape[0], 4 * HEAD), lambda i, s: (0, i))) for chunk in chunks
+    ]
+
+
+def head_masks(rows):
+    lane = lax.broadcasted_iota(jnp.int32, (rows, 2 * HEAD), 1)
+    return lane < HEAD, lane >= HEAD
+
+
+def attend_fast(queries, chunks, deps=()):
+    tokens, width = queries.shape
+    pairs = width // (2 * HEAD)
+
+    def body(place, ins, outs, _):
+        both = join(ins[1:5])
+        keys, values = both[:, : 2 * HEAD], both[:, 2 * HEAD :]
+        scaled = ins[0][...] * jnp.asarray(1.0 / math.sqrt(HEAD), bf16)
+        halves, tops = [], []
+        for head, mask in enumerate(head_masks(tokens)):
+            query = jnp.where(mask, scaled, jnp.zeros_like(scaled))
+            scores = lax.dot_general(keys, query, NT, preferred_element_type=f32)
+            most = jnp.max(scores, axis=0, keepdims=True)
+            exponent = jnp.exp(scores - most)
+            total = jnp.sum(exponent, axis=0, keepdims=True)
+            mixed = lax.dot_general(values, exponent.astype(bf16), TN, preferred_element_type=f32)
+            halves.append(mixed[head * HEAD : (head + 1) * HEAD] / total)
+            tops.append(most + jnp.log(total))
+        outs[0][...] = jnp.concatenate(halves, axis=0).T.astype(bf16)
+        outs[1][0, 0:1, :] = tops[0]
+        outs[1][0, 1:2, :] = tops[1]
+
+    return run(
+        body,
+        pairs,
+        [(queries, pl.BlockSpec((tokens, 2 * HEAD), lambda i, s: (0, i)))] + key_specs(chunks),
+        [
+            (queries.shape, bf16, pl.BlockSpec((tokens, 2 * HEAD), lambda i, s: (0, i))),
+            ((pairs, 8, tokens), f32, pl.BlockSpec((1, 8, tokens), lambda i, s: (i, 0, 0))),
+        ],
+        deps=deps,
+        cost=15,
+    )
+
+
+def attend_fast_back(queries, chunks, kept, mixture_grad, tops, deps=()):
+    tokens, width = queries.shape
+    pairs = width // (2 * HEAD)
+
+    def body(place, ins, outs, _):
+        both = join(ins[1:5])
+        keys, values = both[:, : 2 * HEAD], both[:, 2 * HEAD :]
+        scaled = ins[0][...] * jnp.asarray(1.0 / math.sqrt(HEAD), bf16)
+        grads = ins[6][...]
+        masks = head_masks(tokens)
+        select = jnp.concatenate([mask[0:1].astype(f32) for mask in masks] + [jnp.zeros((6, 2 * HEAD), f32)], axis=0)
+        along = lax.dot_general(
+            select,
+            ins[5][...].astype(f32) * grads.astype(f32),
+            NT,
+            precision=lax.Precision.HIGHEST,
+            preferred_element_type=f32,
+        )
+        key_grad = value_grad = None
+        halves = []
+        for head, mask in enumerate(masks):
+            query = jnp.where(mask, scaled, jnp.zeros_like(scaled))
+            grad = jnp.where(mask, grads, jnp.zeros_like(grads))
+            scores = lax.dot_general(keys, query, NT, preferred_element_type=f32)
+            probs = jnp.exp(scores - ins[7][0, head : head + 1, :])
+            prob_grad = lax.dot_general(values, grad, NT, preferred_element_type=f32)
+            score_grad = (probs * (prob_grad - along[head : head + 1, :])).astype(bf16)
+            key_part = jnp.dot(score_grad, query, preferred_element_type=f32)
+            value_part = jnp.dot(probs.astype(bf16), grad, preferred_element_type=f32)
+            key_grad = key_part if head == 0 else key_grad + key_part
+            value_grad = value_part if head == 0 else value_grad + value_part
+            query_part = lax.dot_general(keys, score_grad, TN, preferred_element_type=f32)
+            halves.append(query_part[head * HEAD : (head + 1) * HEAD])
+        query_grad = jnp.concatenate(halves, axis=0) * (1.0 / math.sqrt(HEAD))
+        outs[0][...] = query_grad.T.astype(bf16)
+        for chunk in range(4):
+            rows = slice(chunk * tokens, (chunk + 1) * tokens)
+            outs[1 + chunk][:, : 2 * HEAD] = key_grad[rows].astype(bf16)
+            outs[1 + chunk][:, 2 * HEAD :] = value_grad[rows].astype(bf16)
+
+    pair_spec = pl.BlockSpec((tokens, 2 * HEAD), lambda i, s: (0, i))
+    part = ((tokens, 2 * width), bf16, pl.BlockSpec((tokens, 4 * HEAD), lambda i, s: (0, i)))
+    return run(
+        body,
+        pairs,
+        [(queries, pair_spec)]
+        + key_specs(chunks)
+        + [
+            (kept, pl.BlockSpec((tokens, 2 * HEAD), lambda i, s: (0, MIXTURE // (2 * HEAD) + i))),
+            (mixture_grad, pair_spec),
+            (tops, pl.BlockSpec((1, 8, tokens), lambda i, s: (i, 0, 0))),
+        ],
+        [(queries.shape, bf16, pair_spec)] + [part] * 4,
+        deps=deps,
+        cost=18,
+    )
+
+
+def window(step, tile):
+    return pl.ds(pl.multiple_of((step - tile) * TILE, BLOCK), TILE)
+
+
+ACTIVE, SECOND, MIXTURE, NORMED, KEPT = 0, 4 * TILE, 5 * TILE, 6 * TILE, 7 * TILE
+
+
+def feed_forward(normed, mixture, packs, stream, vec, bias, next_vec, deps=()):
+    tokens, width = mixture.shape
+    columns = bias.shape[1]
+    attention_pack, expand_pack, reduce_pack = packs
+    one = len(attention_pack)
+
+    def body(place, ins, outs, scratch):
+        step = pl.program_id(0)
+        mixture_ref, stream_ref, vec_ref, next_ref, bias_ref, normed_ref = ins[:6]
+        middle_ref, kept_ref, slope_ref, result_ref, following_ref = outs
+        ordered, total = scratch
+
+        @pl.when(step == 0)
+        def _():
+            branch = jnp.dot(
+                columns_in_order(place, mixture_ref), join(ins[6 : 6 + one]), preferred_element_type=f32
+            )
+            middle = stream_ref[...].astype(f32) + (branch + vec_ref[2:3, :])
+            middle_ref[...] = middle
+            kept_ref[:, SECOND:MIXTURE] = modulated(middle, vec_ref, 3).astype(bf16)
+            kept_ref[:, MIXTURE:NORMED] = mixture_ref[...]
+            kept_ref[:, NORMED:KEPT] = normed_ref[...]
+            ordered[...] = columns_in_order(place, kept_ref, BLOCK, SECOND)
+
+        @pl.when((step > 0) & (step < 5))
+        def _():
+            at = window(step, 1)
+            hidden = jnp.dot(
+                ordered[...], join(ins[6 + one : 6 + 2 * one]), preferred_element_type=f32
+            ) + bias_ref[:, at]
+            square = hidden * hidden
+            bent = jnp.tanh(ROOT * hidden * (1.0 + CUBIC * square))
+            half = 0.5 * (1.0 + bent)
+            kept_ref[:, at] = (hidden * half).astype(bf16)
+            slope = half + (0.5 * ROOT) * hidden * (1.0 - bent * bent) * (1.0 + (3.0 * CUBIC) * square)
+            slope_ref[:, at] = slope.astype(bf16)
+
+        @pl.when(step >= 5)
+        def _():
+            a = columns_in_order(place, kept_ref, 4 * BLOCK, (step - 5) * BLOCK)
+            product = jnp.dot(a, join(ins[6 + 2 * one :]), preferred_element_type=f32)
+
+            @pl.when(step == 5)
+            def _():
+                total[...] = product
+
+            @pl.when(step > 5)
+            def _():
+                total[...] += product
+
+            @pl.when(step == 8)
+            def _():
+                result = middle_ref[...] + (total[...] + vec_ref[5:6, :])
+                result_ref[...] = result
+                if next_vec is None:
+                    following_ref[...] = result.astype(bf16)
+                else:
+                    following_ref[...] = modulated(result, next_ref, 0).astype(bf16)
+
+    wide_shape = (tokens, columns)
+    return run(
+        body,
+        9,
+        [
+            (mixture, None),
+            (stream, None),
+            (vec, None),
+            (vec if next_vec is None else next_vec, None),
+            (bias, None),
+            (normed, None),
+        ]
+        + pack_inputs(attention_pack, lambda i: 3)
+        + pack_inputs(expand_pack, lambda i: jnp.clip(i - 1, 0, 3))
+        + pack_inputs(reduce_pack, lambda i: jnp.clip(i - 5, 0, 3)),
+        [
+            (mixture.shape, f32, None),
+            ((tokens, KEPT), bf16, None),
+            (wide_shape, bf16, None),
+            (mixture.shape, f32, None),
+            (mixture.shape, bf16, None),
+        ],
+        [pltpu.VMEM((tokens, width), bf16), pltpu.VMEM((tokens, width), f32)],
+        deps=deps,
+        cost=19,
+    )
+
+
+def feed_forward_back(grad, grad_low, slope, middle, packs, vec, deps=()):
+    tokens, width = grad.shape
+    columns = slope.shape[1]
+    attention_pack, expand_pack, reduce_pack = packs
+    one = len(attention_pack)
+
+    def body(place, ins, outs, scratch):
+        step = pl.program_id(0)
+        grad_ref, grad_low_ref, slope_ref, middle_ref, vec_ref = ins[:5]
+        hidden_refs, low_ref = outs[:2], outs[2]
+        bias_ref, middle_grad_ref, sums_ref, mixture_ref = outs[3:]
+        total, ordered = scratch
+
+        @pl.when(step < 4)
+        def _():
+            product = lax.dot_general(
+                grad_low_ref[...], join(ins[5 : 5 + one]), NT, preferred_element_type=f32
+            )
+            for part in range(SMALL):
+                at = block_at(place, part, 4 * BLOCK, step * BLOCK)
+                piece = product[:, part * BLOCK : (part + 1) * BLOCK] * slope_ref[:, at].astype(f32)
+                bias_ref[:, at] = jnp.sum(piece, axis=0, keepdims=True)
+                half = (place[0] ^ part) // 4
+                within = pl.ds(pl.multiple_of(((place[0] ^ part) % 4) * 4 * BLOCK + step * BLOCK, BLOCK), BLOCK)
+                for number in range(2):
+
+                    @pl.when(half == number)
+                    def _(number=number, piece=piece, within=within):
+                        hidden_refs[number][:, within] = piece.astype(bf16)
+
+        @pl.when((step >= 4) & (step < 8))
+        def _():
+            for number in range(4):
+
+                @pl.when(step == 4 + number)
+                def _(number=number):
+                    start = (number % 2) * TILE
+                    product = lax.dot_general(
+                        hidden_refs[number // 2][:, start : start + TILE],
+                        join(ins[5 + one : 5 + 2 * one]),
+                        NT,
+                        preferred_element_type=f32,
+                    )
+                    total[...] = product if number == 0 else total[...] + product
+
+            @pl.when(step == 7)
+            def _():
+                for part in range(SMALL):
+                    ordered[:, block_at(place, part)] = total[:, part * BLOCK : (part + 1) * BLOCK]
+                back, gain_grad, shift_grad, scale_grad = modulated_back(
+                    middle_ref[...], vec_ref, 3, ordered[...]
+                )
+                upstream = grad_ref[...].astype(f32)
+                middle_grad = upstream + back
+                middle_grad_ref[...] = middle_grad
+                low_ref[...] = middle_grad.astype(bf16)
+                sums_ref[0:1, :] = gain_grad
+                sums_ref[1:2, :] = shift_grad
+                sums_ref[2:3, :] = scale_grad
+                sums_ref[3:4, :] = jnp.sum(middle_grad, axis=0, keepdims=True)
+                sums_ref[4:5, :] = jnp.sum(upstream, axis=0, keepdims=True)
+
+        @pl.when(step == 8)
+        def _():
+            product = lax.dot_general(
+                low_ref[...], join(ins[5 + 2 * one :]), NT, preferred_element_type=f32
+            ).astype(bf16)
+            for part in range(SMALL):
+                mixture_ref[:, block_at(place, part)] = product[:, part * BLOCK : (part + 1) * BLOCK]
+
+    return run(
+        body,
+        9,
+        [
+            (grad, None),
+            (grad_low[0], pl.BlockSpec((tokens, TILE), lambda i, s: (0, grad_low[1]))),
+            (slope, None),
+            (middle, None),
+            (vec, None),
+        ]
+        + pack_inputs(reduce_pack, lambda i: jnp.minimum(i, 3))
+        + pack_inputs(expand_pack, lambda i: jnp.clip(i - 4, 0, 3))
+        + pack_inputs(attention_pack, lambda i: 3),
+        [
+            ((tokens, 2 * TILE), bf16, None),
+            ((tokens, 2 * TILE), bf16, None),
+            (grad.shape, bf16, None),
+            ((1, columns), f32, None),
+            (grad.shape, f32, None),
+            ((8, width), f32, None),
+            (grad.shape, bf16, None),
+        ],
+        [pltpu.VMEM((tokens, width), f32), pltpu.VMEM((tokens, width), f32)],
+        deps=deps,
+        cost=18,
+    )
+
+
+def first_back(query_grad, key_parts, pack, stream, middle_grad, vec, deps=()):
+    tokens, width = stream.shape
+    kept, arrived, far = key_parts
+
+    def body(place, ins, outs, scratch):
+        step = pl.program_id(0)
+        weights = join(ins[7:])
+
+        @pl.when(step == 0)
+        def _():
+            outs[1][:, :TILE] = ins[0][...]
+            scratch[0][...] = lax.dot_general(ins[0][...], weights, NT, preferred_element_type=f32)
+
+        @pl.when(step > 0)
+        def _():
+            total = ins[1][...].astype(f32) + ins[2][...].astype(f32) + ins[3][...].astype(f32)
+            rounded = total.astype(bf16)
+            outs[3][...] = rounded
+            scratch[0][...] += lax.dot_general(rounded, weights, NT, preferred_element_type=f32)
+
+        @pl.when(step == 2)
+        def _():
+            for part in range(SMALL):
+                scratch[1][:, block_at(place, part)] = scratch[0][:, part * BLOCK : (part + 1) * BLOCK]
+            back, gain_grad, shift_grad, scale_grad = modulated_back(
+                ins[4][...].astype(f32), ins[6], 0, scratch[1][...]
+            )
+            result = ins[5][...] + back
+            outs[0][...] = result
+            outs[1][:, TILE:] = result.astype(bf16)
+            outs[2][0:1, :] = gain_grad
+            outs[2][1:2, :] = shift_grad
+            outs[2][2:3, :] = scale_grad
+
+    tile = pl.BlockSpec((tokens, TILE), lambda i, s: (0, jnp.maximum(i - 1, 0)))
+    return run(
+        body,
+        3,
+        [
+            (query_grad, None),
+            (kept, tile),
+            (arrived, tile),
+            (far, tile),
+            (stream, None),
+            (middle_grad, None),
+            (vec, None),
+        ]
+        + pack_inputs(pack, lambda i: i),
+        [
+            (stream.shape, f32, None),
+            ((tokens, 2 * TILE), bf16, None),
+            ((8, width), f32, None),
+            (far.shape, bf16, tile),
+        ],
+        [pltpu.VMEM((tokens, width), f32), pltpu.VMEM((tokens, width), f32)],
+        deps=deps,
+        cost=10,
+    )
+
+
+ORDERS = ((6, 2, 4, 0), (6, 4, 2, 0))
+
+
+class Group:
+    def __init__(self, arrays, left_of, right_of):
+        self.left_of, self.right_of = left_of, right_of
+        self.inputs = [(side, spec) for pair, spec in arrays for side in pair]
+
+    def product(self, place, refs, tile):
+        array, stride, offset = self.left_of[tile]
+        left = [
+            jnp.concatenate(
+                [refs[2 * array + side][:, block_at(place, mask, stride, offset)] for mask in ORDERS[tile // 2]],
+                axis=1,
+            )
+            for side in range(2)
+        ]
+        array = self.right_of[tile]
+        return lax.dot_general(
+            jnp.concatenate(left, axis=0), join(refs[2 * array : 2 * array + 2]), TN, preferred_element_type=f32
+        )
+
+
+def part_of(rows, first):
+    at = first if callable(first) else (lambda i: first)
+    return pl.BlockSpec((rows, TILE), lambda i, s: (0, at(i)))
+
+
+def reduce_group(kept, lower, block):
+    rows = kept[0].shape[0]
+    return Group(
+        [(kept, pl.BlockSpec((rows, 4 * TILE), lambda i, s: (0, 0))), (lower, part_of(rows, block))],
+        [(0, 4 * BLOCK, u * BLOCK) for u in range(4)],
+        [1] * 4,
+    )
+
+
+def expand_group(kept, back):
+    rows = kept[0].shape[0]
+    return Group(
+        [
+            (kept, part_of(rows, SECOND // TILE)),
+            (back[0], part_of(rows, lambda i: jnp.minimum(i, 1))),
+            (back[1], part_of(rows, lambda i: jnp.maximum(i - 2, 0))),
+        ],
+        [(0, BLOCK, 0)] * 4,
+        [1, 1, 2, 2],
+    )
+
+
+def attention_group(kept, back, lower, key_grad):
+    rows = kept[0].shape[0]
+    return Group(
+        [
+            (kept, part_of(rows, NORMED // TILE)),
+            (kept, part_of(rows, MIXTURE // TILE)),
+            (lower, part_of(rows, 0)),
+            (key_grad, part_of(rows, lambda i: jnp.clip(i - 1, 0, 1))),
+            (back[2], part_of(rows, 0)),
+        ],
+        [(0, BLOCK, 0)] * 3 + [(1, BLOCK, 0)],
+        [2, 3, 3, 4],
+    )
+
+
+def wide(value):
+    return value.astype(f32)
+
+
+def half_spec(rows, half):
+    return pl.BlockSpec((rows, TILE), lambda i, s: (0, jnp.maximum(i - 2, 0) if half else jnp.minimum(i, 1)))
+
+
+def both_spec(rows):
+    return pl.BlockSpec((1, rows, TILE), lambda i, s: (i // 2, 0, i % 2))
+
+
+class Reduction:
+    def __init__(self, group, stacked=False):
+        self.group, self.stacked = group, stacked
+
+
+def advance(seconds=(), thirds=(), fourths=(), joint=(), deps=()):
+    inputs, outputs, works = [], [], []
+    quarter, eighth = (2 * BLOCK, 2 * TILE), (BLOCK, 2 * TILE)
+    for one in seconds:
+        group, base, out = one.group, len(inputs), len(outputs)
+        inputs += group.inputs
+        outputs += [
+            (quarter, bf16, half_spec(2 * BLOCK, 0)),
+            (quarter, bf16, half_spec(2 * BLOCK, 1)),
+            ((2,) + quarter, bf16, both_spec(2 * BLOCK)),
+        ]
+
+        def product(place, ins, outs, tile, group=group, base=base, out=out):
+            total = group.product(place, ins[base : base + len(group.inputs)], tile)
+            outs[out + tile // 2][...] = total[: 2 * BLOCK].astype(bf16)
+            outs[out + 2][0] = total[2 * BLOCK :].astype(bf16)
+
+        works.append(product)
+    for one in thirds:
+        base, out = len(inputs), len(outputs)
+        inputs += [
+            (one.staying, both_spec(2 * BLOCK)),
+            (one.from_x, half_spec(2 * BLOCK, 0)),
+            (one.from_y, half_spec(2 * BLOCK, 1)),
+        ]
+        outputs += [
+            (eighth, bf16, half_spec(BLOCK, 0)),
+            (eighth, bf16, half_spec(BLOCK, 1)),
+            ((2,) + eighth, bf16, both_spec(BLOCK)),
+        ]
+
+        def add(place, ins, outs, tile, base=base, out=out):
+            total = (wide(ins[base][0]) + wide(ins[base + 1 + tile // 2][...])).astype(bf16)
+            outs[out + tile // 2][...] = total[:BLOCK]
+            outs[out + 2][0] = total[BLOCK:]
+
+        works.append(add)
+    for one in fourths:
+        base, out = len(inputs), len(outputs)
+        inputs += [
+            (one.kept, both_spec(BLOCK)),
+            (one.second_y, half_spec(BLOCK, 0)),
+            (one.second_x, half_spec(BLOCK, 1)),
+        ]
+        shape = (4 * BLOCK, TILE) if one.stacked else (BLOCK, 4 * TILE)
+        spec = pl.BlockSpec((BLOCK, TILE), lambda i, s, stacked=one.stacked: (i, 0) if stacked else (0, i))
+        outputs.append((shape, bf16, spec))
+
+        def finish(place, ins, outs, tile, base=base, out=out):
+            outs[out][...] = (wide(ins[base][0]) + wide(ins[base + 1 + tile // 2][...])).astype(bf16)
+
+        works.append(finish)
+
+    if joint:
+        base, out, share = len(inputs), len(outputs), BLOCK // 4
+        for one in joint:
+            inputs += [
+                (one.kept, both_spec(BLOCK)),
+                (one.second_y, half_spec(BLOCK, 0)),
+                (one.second_x, half_spec(BLOCK, 1)),
+            ]
+        rows = len(joint) * BLOCK
+        outputs.append(((rows, 4 * TILE), bf16, pl.BlockSpec((rows, TILE), lambda i, s: (0, i))))
+
+        def interleave(place, ins, outs, tile):
+            for number in range(len(joint)):
+                at = base + 3 * number
+                total = (wide(ins[at][0]) + wide(ins[at + 1 + tile // 2][...])).astype(bf16)
+                for plane in range(4):
+                    start = (plane * len(joint) + number) * share
+                    outs[out][start : start + share, :] = total[plane * share : (plane + 1) * share]
+
+        works.append(interleave)
+
+    def body(place, ins, outs, _):
+        for tile in range(4):
+
+            @pl.when(pl.program_id(0) == tile)
+            def _(tile=tile):
+                for work in works:
+                    work(place, ins, outs, tile)
+
+    results = list(run(body, 4, inputs, outputs, deps=deps, cost=7 if seconds else 5))
+    token = results[0]
+    for one in seconds:
+        along_x, along_y, one.staying = results[:3]
+        results = results[3:]
+        one.from_x, one.from_y = swap(along_x, 2), swap(along_y, 4)
+    for one in thirds:
+        along_y, along_x, one.kept = results[:3]
+        results = results[3:]
+        one.second_y, one.second_x = swap(along_y, 4), swap(along_x, 2)
+    for one in fourths:
+        one.share = lax.psum_scatter(results[0], "seq", scatter_dimension=0, tiled=True)
+        results = results[1:]
+    if joint:
+        both = lax.psum_scatter(results[0], "seq", scatter_dimension=0, tiled=True)
+        for number, one in enumerate(joint):
+            one.share = both[number * share : (number + 1) * share]
+    return token
+
+
+HALF = BLOCK // 2
+EXTRA = 32
+
+
+def raw_inputs(kind, layer, arrays):
+    if kind == "attention":
+        return [
+            (arrays[0], pl.BlockSpec((1,) + arrays[0].shape[1:], lambda i, s: (layer, 0, 0))),
+            (arrays[1], pl.BlockSpec((1,) + arrays[1].shape[1:], lambda i, s: (layer, 0, 0))),
+        ]
+    if kind == "expand":
+        return [(arrays[0], pl.BlockSpec((1, BLOCK, TILE), lambda i, s: (layer, 0, i)))]
+    return [(arrays[0], pl.BlockSpec((1, BLOCK, TILE), lambda i, s: (layer, i, 0)))]
+
+
+def raw_tile(kind, ins, targets):
+    if kind != "attention":
+        for target in targets:
+            target[:BLOCK, :] = ins[0][0]
+        return
+    pairs = TILE // (2 * BLOCK)
+    for tile in range(4):
+
+        @pl.when(pl.program_id(0) == tile)
+        def _(tile=tile):
+            for target in targets:
+                if tile == 0:
+                    target[:BLOCK, :] = ins[0][0, :, :TILE]
+                elif tile == 3:
+                    target[:BLOCK, :] = ins[1][0]
+                else:
+                    for pair in range(pairs):
+                        start = (pairs * (tile - 1) + pair) * BLOCK
+                        at = pair * 2 * BLOCK
+                        target[:BLOCK, at : at + BLOCK] = ins[0][0, :, TILE + start : TILE + start + BLOCK]
+                        target[:BLOCK, at + BLOCK : at + 2 * BLOCK] = ins[0][
+                            0, :, 2 * TILE + start : 2 * TILE + start + BLOCK
+                        ]
+
+
+def column_spec(rows, row_block=0):
+    return pl.BlockSpec((rows, TILE), lambda i, s: (row_block, i))
+
+
+def first_pack(raw, time_table, members, noise_buckets):
+    layers = time_table.shape[0]
+    buckets = jnp.broadcast_to(noise_buckets.astype(bf16), (layers, BLOCK))
+    chunks = [(2 + 1 + index, layer, 0) for index in range(6) for layer in range(layers)]
+    bias_chunks = members[6].shape[1] // BLOCK
+    chunks += [(2 + 1 + 6, layer, part) for layer in range(layers) for part in range(bias_chunks)]
+    chunks.append((2 + 1 + 7, 0, 0))
+    per_tile = TILE // BLOCK
+
+    def body(place, ins, outs, _):
+        raw_tile("attention", ins[:2], outs)
+        for tile in range(4):
+
+            @pl.when(pl.program_id(0) == tile)
+            def _(tile=tile):
+                start = (tile % 2) * 16
+                outs[0][BLOCK : BLOCK + 16, :] = ins[2][tile // 2, start : start + 16, :]
+                for slot in range(per_tile):
+                    index = tile * per_tile + slot
+                    at = slot * BLOCK
+                    row = jnp.zeros((1, BLOCK), bf16)
+                    if index < len(chunks):
+                        array, layer, part = chunks[index]
+                        row = ins[array][layer : layer + 1, part * BLOCK : (part + 1) * BLOCK]
+                    outs[0][BLOCK + 16 :, at : at + BLOCK] = jnp.broadcast_to(row.astype(f32), (16, BLOCK)).astype(bf16)
+
+    return run(
+        body,
+        4,
+        raw_inputs("attention", 0, raw)
+        + [(time_table, None)]
+        + [(member, None) for member in members]
+        + [(buckets, None)],
+        [((BLOCK + EXTRA, 4 * TILE), bf16, column_spec(BLOCK + EXTRA))],
+    )[0]
+
+
+def other_packs(kinds, raws, deps=()):
+    inputs, counts = [], []
+    for (kind, layer), raw in zip(kinds, raws):
+        inputs += raw_inputs(kind, layer, raw)
+        counts.append(len(raw))
+
+    def body(place, ins, outs, _):
+        at = 0
+        for position, ((kind, _), taken) in enumerate(zip(kinds, counts)):
+            raw_tile(kind, ins[at : at + taken], [outs[0].at[position * BLOCK : (position + 1) * BLOCK]])
+            at += taken
+
+    rows = len(kinds) * BLOCK
+    return run(body, 4, inputs, [((rows, 4 * TILE), bf16, column_spec(rows))], deps=deps)[0]
+
+
+def own_rows(rest, position, rows, deps=()):
+    def body(place, ins, outs, _):
+        outs[0][...] = ins[0][...]
+        outs[1][...] = ins[0][...]
+
+    out = ((rows, 4 * TILE), bf16, column_spec(BLOCK))
+    return run(body, 4, [(rest, column_spec(BLOCK, position))], [out, out], deps=deps)
+
+
+def diagonal_rows(x, y, buffers, deps=()):
+    def body(place, ins, outs, _):
+        outs[0][...] = ins[1][...]
+        outs[1][...] = ins[0][...]
+
+    rows, block = (buffers[0].shape[0], BLOCK // HALF) if buffers else (HALF, 0)
+
+    def spec(at):
+        return pl.BlockSpec((HALF, 4 * TILE), lambda i, s: (at, 0))
+
+    out = ((rows, 4 * TILE), bf16, spec(block))
+    return run(body, 1, [(x, spec(1)), (y, spec(0))], [out, out], deps=deps, aliases=buffers)
+
+
+def first_step(rest, x, y, deps=()):
+    half = EXTRA // 2
+
+    def body(place, ins, outs, _):
+        from_x, from_y, own = ins
+        for out, source, at in ((outs[0], from_y, 0), (outs[1], from_x, 1)):
+            out[:BLOCK, :] = own[...]
+            out[BLOCK : BLOCK + HALF, :] = source[at * HALF : (at + 1) * HALF, :]
+            out[BLOCK + HALF :, :] = source[BLOCK + at * half : BLOCK + (at + 1) * half, :]
+
+    rows = BLOCK + HALF + half
+    out = ((rows, 4 * TILE), bf16, column_spec(rows))
+    whole = column_spec(x.shape[0])
+    return run(body, 4, [(x, whole), (y, whole), (rest, column_spec(BLOCK))], [out, out], deps=deps)
+
+
+class Gather:
+    def __init__(self, kinds, raws, time_table, members, noise_buckets):
+        self.count = len(kinds)
+        self.first = first_pack(raws[0], time_table, members, noise_buckets)
+        self.xs, self.ys = [swap(self.first, 2)], [swap(self.first, 4)]
+        self.core_first = swap(self.first, 1)
+        self.kinds, self.raws = kinds, raws
+        self.core_xs, self.core_ys = [], []
+
+    def others(self, deps):
+        self.rest = other_packs(self.kinds[1:], self.raws[1:], deps)
+        self.ready = tuple(own_rows(self.rest, 1, BLOCK + HALF))
+        return self.ready[0]
+
+    def prepare(self, deps=()):
+        step = len(self.xs)
+        self.ready = ()
+        if step < self.count:
+            self.ready = tuple(own_rows(self.rest, step - 1, BLOCK + HALF, deps))
+            return self.ready[0]
+        return deps[0]
+
+    def step(self, deps=(), token=None):
+        step = len(self.xs)
+        if step == 2:
+            deps = (self.core_rest,) + tuple(deps)
+        if step > 1:
+            deps = (self.core_xs[-1], self.core_ys[-1]) + tuple(deps)
+            on_x, on_y = diagonal_rows(self.xs[-1], self.ys[-1], self.ready, deps)
+        else:
+            on_x, on_y = first_step(self.rest, self.xs[-1], self.ys[-1], deps)
+            self.core_rest = swap(after(self.rest, on_x), 1)
+        self.cross(on_x if token is None else token)
+        self.xs.append(swap(on_x, 2))
+        self.ys.append(swap(on_y, 4))
+        return on_x
+
+    def cross(self, token):
+        self.core_xs.append(swap(after(self.xs[-1], token), 1))
+        self.core_ys.append(swap(after(self.ys[-1], token), 1))
+
+    def pack(self, k):
+        row = 2 if k + 1 < self.count else 0
+        own = [(self.first, 0, BLOCK), (self.core_first, 0, BLOCK)] if k == 0 else [(self.rest, k - 1, BLOCK), (self.core_rest, k - 1, BLOCK)]
+        sides = (self.xs, self.core_xs, self.ys, self.core_ys)
+        return (
+            own
+            + [(side[k], 0, BLOCK) for side in sides]
+            + [(sides[i][k + 1], row, HALF) for i in (0, 2, 1, 3)]
+        )
+
+    def extras(self):
+        whole = [(self.first, BLOCK, EXTRA), (self.core_first, BLOCK, EXTRA)]
+        whole += [(side[0], BLOCK, EXTRA) for side in (self.xs, self.core_xs, self.ys, self.core_ys)]
+        at, rows = BLOCK + HALF, EXTRA // 2
+        parts = [
+            [(self.xs[1], at, rows), (self.ys[1], at, rows)],
+            [(self.core_xs[1], at, rows), (self.core_ys[1], at, rows)],
+        ]
+        return [[piece] for piece in whole] + parts
+
+
+def vectors_of(extras, members, layers, table_rows, width):
+    share = members[6].shape[1]
+    bias_at, bucket_at = 6 * layers * BLOCK, 6 * layers * BLOCK + layers * share
+    pieces = [piece for parts in extras for piece in parts]
+    tables, rows_at, at = [], [], 0
+    for parts in extras:
+        tables.append(at)
+        rows_at.append((at + len(parts) - 1, 0 if len(parts) == 2 else EXTRA // 2))
+        at += len(parts)
+
+    def body(place, ins, outs, _):
+        me = place[0]
+        row = [ins[at][start : start + 16, :].astype(f32)[0:1, :] for at, start in rows_at]
+        mine = (me // 2) * 2 + place[1] // 2 == me
+        bucket = jnp.where(mine, row[0][:, bucket_at : bucket_at + 1], row[1][:, bucket_at : bucket_at + 1])
+        for layer in range(layers):
+            scaling = jnp.ones((1, width), f32)
+            for part in range(SMALL):
+                owner = me ^ part
+                for member in range(6):
+                    start = (member * layers + layer) * BLOCK
+                    outs[2 * layer][member : member + 1, block_at(place, part)] = row[part][:, start : start + BLOCK]
+                start = bias_at + layer * share
+                outs[2 * layer + 1][:, pl.ds(pl.multiple_of(owner * share, BLOCK), share)] = row[part][
+                    :, start : start + share
+                ]
+                for half in range(2):
+                    block = ins[tables[part]][0:16, (2 * layer + half) * TILE : (2 * layer + half + 1) * TILE].astype(f32)
+                    place_of = lax.broadcasted_iota(jnp.int32, block.shape, 0) + (owner * table_rows + half * 16)
+                    hit = place_of.astype(f32) == bucket
+                    scaling += jnp.sum(jnp.where(hit, block, 0.0), axis=0, keepdims=True)
+            outs[2 * layer][6:7, :] = scaling
+            outs[2 * layer][7:8, :] = jnp.zeros((1, width), f32)
+        for part in range(SMALL):
+            outs[2 * layers][pl.ds(me ^ part, 1), :] = row[part][:, bucket_at : bucket_at + BLOCK]
+
+    result = run(
+        body,
+        1,
+        [
+            (array, pl.BlockSpec((rows, 4 * TILE), lambda i, s, r=start // rows: (r, 0)))
+            for array, start, rows in pieces
+        ],
+        [
+            item
+            for _ in range(layers)
+            for item in (((8, width), f32, None), ((1, SMALL * share), f32, None))
+        ]
+        + [((SMALL, BLOCK), f32, None)],
+    )
+    pairs = [(result[2 * layer], result[2 * layer + 1]) for layer in range(layers)]
+    return pairs, result[2 * layers][:, 0].astype(jnp.int32)
+
+
+def small_and_changes(sums):
+    columns = []
+    for early, late, hidden_sum in sums:
+        for member in (early[0], early[1], late[3], late[0], late[1], late[4], hidden_sum[0]):
+            columns.append(member.reshape(SMALL * 4, -1))
+    small = jnp.concatenate(columns, axis=1)
+    changes = jnp.concatenate([early[2] + late[2] for early, late, _ in sums])
+    return small.reshape((2, 2, 2, 2, 2, -1)), changes[None]
+
+
+def cross(small, changes, axis, mine, move, add, *tokens):
+    leaving = lax.dynamic_index_in_dim(small, 1 - mine, axis, keepdims=False)
+    staying = lax.dynamic_index_in_dim(small, mine, axis, keepdims=False)
+    moved = move(jnp.concatenate([leaving.reshape(-1), changes.reshape(-1)]))
+    if tokens:
+        moved = after(moved, *tokens)
+    small = staying + moved[: leaving.size].reshape(leaving.shape)
+    arrived = moved[leaving.size :].reshape(changes.shape)
+    return small, changes + arrived if add else jnp.concatenate([changes, arrived], axis=0)
+
+
+def fast_device(
+    inputs,
+    noise_buckets,
+    first_gain,
+    first_shift,
+    attention_in,
+    attention_out,
+    attention_bias,
+    second_gain,
+    second_shift,
+    expand_weight,
+    expand_bias,
+    reduce_weight,
+    reduce_bias,
+    time_table,
+    cotangent,
+):
+    layers, width = first_gain.shape[0], inputs.shape[-1]
+    count, planes = lax.axis_size("dp"), lax.axis_size("seq")
+    me, plane = lax.axis_index("dp"), lax.axis_index("seq")
+    sequence = (me // 2) * 2 + plane // 2
+
+    kinds = [(kind, layer) for layer in range(layers) for kind in ("attention", "expand", "reduce")]
+    raw_of = {"attention": (attention_in, attention_out), "expand": (expand_weight,), "reduce": (reduce_weight,)}
+    members = (first_gain, first_shift, attention_bias, second_gain, second_shift, reduce_bias, expand_bias)
+    gather = Gather(kinds, [raw_of[kind] for kind, _ in kinds], time_table, members, noise_buckets)
+    moved = lax.ppermute(inputs[0], ("dp", "seq"), layout_moves(False))
+    grad_low = lax.ppermute(cotangent[0], ("dp", "seq"), layout_moves(False))
+    lower = (grad_low, swap(grad_low, 1))
+    token = gather.others((moved, gather.first))
+    gather.step((moved, lower[1], token))
+    gather.step()
+    vectors, buckets = vectors_of(gather.extras(), members, layers, time_table.shape[1], width)
+
+    saved = []
+    stream = moved
+    normed = first_norm(stream, vectors[0][0])
+    for layer in range(layers):
+        vec, bias = vectors[layer]
+        attention_pack = gather.pack(3 * layer)
+        own_keys = project(normed, attention_pack, 1, 2, (token,) if layer else ())
+        chunks = spread_keys(own_keys)
+        queries = project(normed, attention_pack, 0, 1, (own_keys,))
+        token = gather.step((gather.prepare((queries,)), queries), queries)
+        if layer == 0:
+            token = gather.prepare((token,))
+        mixture, tops = attend_fast(queries, chunks, (token,))
+        if layer == 0:
+            token = gather.step((mixture,), mixture)
+            token = gather.prepare((token,))
+        else:
+            gather.cross(mixture)
+            token = mixture
+        packs = (attention_pack, gather.pack(3 * layer + 1), gather.pack(3 * layer + 2))
+        next_vec = vectors[layer + 1][0] if layer + 1 < layers else None
+        middle, own_kept, slope, result, following = feed_forward(
+            normed, mixture, packs, stream, vec, bias, next_vec, (token,)
+        )
+        if layer == 0:
+            token = gather.step((following,), following)
+        saved.append([stream, own_kept, queries, chunks, tops, middle, slope, packs])
+        stream, normed = result, following
+    outputs = lax.ppermute(following, ("dp", "seq"), layout_moves(True))
+
+    grad = grad_low
+    block = 0
+    sums = [None] * layers
+    shares = {}
+    for entry in reversed(saved):
+        entry[1] = (entry[1], swap(after(entry[1], following), 1))
+    above = None
+    for layer in reversed(range(layers)):
+        vec, bias = vectors[layer]
+        stream, kept, queries, chunks, tops, middle, slope, packs = saved[layer]
+        of_reduce = Reduction(reduce_group(kept, lower, block), True)
+        deps = (token,) if above is not None else ()
+        *own_back, expand_bias_grad, middle_grad, late_sums, mixture_grad = feed_forward_back(
+            grad, (lower[0], block), slope, middle, packs, vec, deps
+        )
+        back = [(own, swap(own, 1)) for own in own_back]
+        deps = tuple(other for _, other in back)
+        if above is None:
+            token = advance([of_reduce], deps=(own_back[0], saved[0][1][1]))
+        else:
+            upper_reduce, upper_expand, of_attention = above
+            token = advance([of_attention], deps=(own_back[0], outputs, upper_reduce.share))
+            token = advance(fourths=[upper_expand], deps=(token,))
+            token = advance([of_reduce], deps=(token,) + deps)
+            deps = ()
+        query_grad, near, near_leave, far, far_leave = attend_fast_back(
+            queries, chunks, kept[0], mixture_grad, tops, (token,) + deps
+        )
+        far_leave, near_leave = swap(far_leave, 1), swap(near_leave, 1)
+        of_expand = Reduction(expand_group(kept, back))
+        token = query_grad
+        if above is None:
+            token = advance([of_expand], deps=(token,))
+            token = advance(thirds=[of_reduce], deps=(token,))
+        else:
+            token = advance(thirds=[of_attention], deps=(token, upper_expand.share))
+        far, near_leave = after(far, token, near_leave), after(near_leave, token)
+        far = (wide(far) + wide(far_leave)).astype(bf16)
+        far = (far, swap_seq(far, 1))
+        token = far[0]
+        if above is not None:
+            token = advance(thirds=[of_reduce], deps=(token,))
+            token = advance([of_expand], deps=(token, of_attention.second_x, of_attention.second_y))
+        deps = (token,)
+        if above is not None:
+            deps = (token, of_reduce.second_x, of_reduce.second_y)
+        grad, own_lower, early_sums, key_grad = first_back(
+            query_grad, (near, near_leave, far[1]), packs[0], stream, middle_grad, vec, deps
+        )
+        lower, block = (own_lower, swap(own_lower, 1)), 1
+        key_grad = (key_grad, swap(key_grad, 1))
+        deps = (own_lower,)
+        if above is None:
+            deps = (own_lower,)
+        if above is None:
+            token = advance(thirds=[of_expand], fourths=[of_reduce], deps=deps)
+        if above is not None:
+            shares[("attention", layer + 1)] = of_attention
+            shares[("expand", layer + 1)] = upper_expand
+        upper_attention = of_attention if above is not None else None
+        of_attention = Reduction(attention_group(kept, back, lower, key_grad))
+        shares[("reduce", layer)] = of_reduce
+        above = (of_reduce, of_expand, of_attention)
+        sums[layer] = (early_sums, late_sums, expand_bias_grad)
+
+    of_reduce, of_expand, of_last = above
+    small, changes = small_and_changes(sums)
+    small, changes = cross(small, changes, 4, plane % 2, lambda a: swap_seq(a, 1), True)
+    small, changes = cross(small, changes, 3, plane // 2, lambda a: swap_seq(a, 2), False)
+    token = advance(thirds=[of_expand], deps=(own_lower, small, changes))
+    token = advance([of_last], deps=(token,))
+    token = advance(fourths=[upper_attention, of_reduce], deps=(token,))
+    token = advance(thirds=[of_last], deps=(token, upper_attention.share))
+    input_grad = lax.ppermute(after(own_lower[:, TILE:], token), ("dp", "seq"), layout_moves(True)).astype(f32)
+    token = advance(joint=(of_expand, of_last), deps=(token,))
+    shares[("attention", 0)] = of_last
+    shares[("expand", 0)] = of_expand
+    shares = {name: reduction.share.astype(f32) for name, reduction in shares.items()}
+
+    small, changes = after(small, token), after(changes, token)
+    small, changes = cross(small, changes, 2, me % 2, lambda a: swap(a, 1), True)
+    small, changes = cross(small, changes, 1, (me // 2) % 2, lambda a: swap(a, 2), False)
+    small, changes = cross(small, changes, 0, me // 4, lambda a: swap(a, 4), False)
+    row = small.reshape(-1)
+    small_out, start = [[] for _ in range(7)], 0
+    for layer in range(layers):
+        for member in range(7):
+            size = (width if member < 6 else 4 * width) // (count * planes)
+            small_out[member].append(row[start : start + size])
+            start += size
+    small_out = [jnp.stack(member) for member in small_out]
+    entries = jnp.arange(count)
+    owners = 2 * ((me // 2) ^ (entries // 2)) + ((plane // 2) ^ (entries % 2))
+    source_buckets = jnp.sum(jnp.where(owners[:, None] == entries[None, :], buckets[None, :], 0), axis=1)
+    table_grad = chosen_rows(changes, source_buckets, layers, width)
+
+    ins, outs, expands, reduces = [], [], [], []
+    for layer in range(layers):
+        share = shares[("attention", layer)]
+        pairs = share[:, width : 3 * width].reshape(share.shape[0], width // BLOCK, 2, BLOCK)
+        ins.append(
+            jnp.concatenate(
+                [share[:, :width], pairs[:, :, 0].reshape(-1, width), pairs[:, :, 1].reshape(-1, width)], axis=1
+            )
+        )
+        outs.append(share[:, 3 * width :])
+        expands.append(shares[("expand", layer)])
+        reduces.append(shares[("reduce", layer)])
+    return (
+        outputs[None],
+        input_grad[None],
+        small_out[0],
+        small_out[1],
+        jnp.stack(ins),
+        jnp.stack(outs),
+        small_out[2],
+        small_out[3],
+        small_out[4],
+        jnp.stack(expands),
+        small_out[6],
+        jnp.stack(reduces),
+        small_out[5],
+        table_grad,
+    )
+
+
 def on_device(
     inputs,
     noise_buckets,
@@ -518,17 +1557,7 @@
     small_out = [jnp.stack(member) for member in small_out]
 
     changes, from_dp, from_seq = gather_small(jnp.concatenate(modulation), ("dp", "seq"))
-    owners = (from_dp // 2) * 2 + from_seq // 2
-    source_buckets = jnp.sum(
-        jnp.where(owners[:, None] == jnp.arange(count)[None, :], buckets[None, :], 0), axis=1
-    )
-    table_share = BUCKETS // devices
-    first_row = (me * planes + plane) * table_share
-    chosen = (source_buckets[None, :] == (first_row + jnp.arange(table_share))[:, None]).astype(f32)
-    table_grad = jnp.dot(chosen, changes, precision=lax.Precision.HIGHEST)
-    table_grad = jnp.stack(
-        [table_grad[:, layer * model_width : (layer + 1) * model_width] for layer in range(layers)]
-    )
+    table_grad = table_rows_of(changes, from_dp, from_seq, buckets, layers, model_width)
 
     dense_out = [jnp.stack([dense[layer][member] for layer in range(layers)]) for member in range(4)]
     return (
@@ -550,8 +1579,9 @@
 
 
 def solution(mesh):
+    eight_way = mesh.shape["dp"] == SMALL and mesh.shape["seq"] == 4
     return jax.shard_map(
-        on_device,
+        fast_device if eight_way else on_device,
         mesh=mesh,
         in_specs=(
             P("dp", "seq", None),

time: 1170 us -> 733 us (0.63)
  Pallas kernels: 132 us -> 330 us
  matrix products: 176 us -> 0.22 us
  waiting for transfers between devices: 385 us -> 236 us
  local copies, waits for them, and re-layouts: 150 us -> 19.4 us
  other arithmetic: 143 us -> 17.9 us
  starting transfers between devices: 157 us -> 101 us
    pallas_call x20 -> x43, Pallas kernels: 132 us -> 330 us  [run(): pl.pallas_call(kernel, out_shape=shapes, grid_spec=pltpu.PrefetchScalarGr...]
    ppermute x138 -> x78, waiting for transfers between devices: 302 us -> 144 us  [swap(): return lax.ppermute(array, 'dp', [(i, i ^ bit) for i in range(count)])]
    dot_general x59 -> x1, matrix products: 156 us -> 0.22 us  [chosen_rows(): table_grad = jnp.dot(chosen, changes, precision=lax.Precision.HIGHEST)]
    convert_element_type x50 -> x4, other arithmetic: 71.1 us -> 4.01 us  [the longest x2 3.86 us: fast_device(): far = (wide(far) + wide(far_leave)).astype(bf16)]
    ppermute x138 -> x78, starting transfers between devices: 104 us -> 56.6 us  [swap(): return lax.ppermute(array, 'dp', [(i, i ^ bit) for i in range(count)])]
    reduce_scatter x0 -> x5, waiting for transfers between devices: none -> 39.1 us  [the longest x1 36 us: advance(): both = lax.psum_scatter(results[0], 'seq', scatter_dimension=0, tiled=True)]
    reduce_sum x21 -> x1, other arithmetic: 35.2 us -> 0.18 us  [fast_device(): jnp.sum(jnp.where(owners[:, None] == entries[None, :], buckets[None, :],...]
    ppermute x24 -> x6, waiting for transfers between devices: 83.3 us -> 52.1 us  [swap_seq(): return lax.ppermute(array, 'seq', [(i, i ^ bit) for i in range(count)])]
  transfers between devices with their start and end apart: 166 -> 93, of which waited for: 59 -> 36; matrix products, arithmetic and copies ran while one was open for 33% -> 2% of each run, Pallas kernels for 9% -> 37%
where the time goes in v2:
time: 733 us; the launch traced here: 720 us
  Pallas kernels  330 us (45%)
  waiting for transfers between devices  236 us (32%)
  starting transfers between devices  101 us (14%)
  local copies, waits for them, and re-layouts  19.4 us (3%)
  other arithmetic  17.9 us (2%)
  between operations  15.7 us (2%)
    pallas_call x43, Pallas kernels, run(): pl.pallas_call(kernel, out_shape=shapes, grid_spec=pltpu.PrefetchScalarGr...  330 us
    ppermute x78, waiting for transfers between devices, swap(): return lax.ppermute(array, 'dp', [(i, i ^ bit) for i in range(count)])  144 us
    ppermute x78, starting transfers between devices, swap(): return lax.ppermute(array, 'dp', [(i, i ^ bit) for i in range(count)])  56.6 us
    ppermute x6, waiting for transfers between devices, swap_seq(): return lax.ppermute(array, 'seq', [(i, i ^ bit) for i in range(count)])  52.1 us
    reduce_scatter x1, waiting for transfers between devices, advance(): both = lax.psum_scatter(results[0], 'seq', scatter_dimension=0, tiled=True)  36 us
    ppermute x6, starting transfers between devices, swap_seq(): return lax.ppermute(array, 'seq', [(i, i ^ bit) for i in range(count)])  25.9 us
    unnamed x73, local copies, waits for them, and re-layouts  14.7 us
  transfers between devices with their start and end apart: 93, of which 36 were waited for; matrix products, arithmetic and copies ran while one was open for 2% of the time, Pallas kernels for 37%

profile of v2, /device:TPU:0, one launch (start us, length us, event | category | flops | bytes accessed | tf_op | source)
XLA Modules:
  0.0 720.0 jit_solution(15195156272778686579)
XLA Ops:
  9.0 3.8 shard_map.254.refs_7_.refs_0_.refs_1_.refs_6_.refs_25_
  12.7 2.9 collective-permute-start.2
  17.2 5.4 collective-permute-start.4
  22.5 5.4 collective-permute-start
  28.3 6.1 shard_map.255.refs_0_.refs_2_.refs_16_.refs_26_.refs_1_.refs_6_.refs_5_.refs_15_.refs_25_.refs_7_
  34.4 4.3 shard_map.256
  38.7 6.0 collective-permute-done.2.refs_0_.refs_2_.refs_3_.refs_8_.refs_27_.refs_9_
  46.2 5.0 shard_map.257
  54.5 7.5 %collective-permute-done.6.refs_4_.refs_3_.refs_9_.refs_28_.refs_10_ = bf16[160,4096]{1,0:T(8,128)(2,1)S(1)} collective-permute-done((bf16[160,4096]{1,0:T(8,128)(2,1)}, bf16[160,4096]{1,0:T(8,128)(2,1)S(1)}, u32[]{:S(2)}, u32[]{:S(2)}) %collective-permute-start.6) | collective-permute-done | bytes 1310752 | tf_op jit(solution)/shard_map/ppermute | solution.py:29
  63.9 27.3 %collective-permute-done.8.refs_0_.refs_6_.refs_7_.refs_12_.refs_18_.refs_17_.refs_31_.refs_13_ = bf16[208,4096]{1,0:T(8,128)(2,1)} collective-permute-done((bf16[208,4096]{1,0:T(8,128)(2,1)}, bf16[208,4096]{1,0:T(8,128)(2,1)}, u32[]{:S(2)}, u32[]{:S(2)}) %collective-permute-start.8) | collective-permute-done | bytes 1703968 | tf_op jit(solution)/shard_map/ppermute | solution.py:29
  92.2 3.0 shard_map.258
  98.0 4.5 collective-permute-done.1.refs_1_.refs_2_.refs_7_.refs_26_.refs_8_
  103.6 3.3 shard_map.259
  106.9 2.9 shard_map.260.refs_0_.refs_5_
  109.8 5.2 shard_map.261.refs_11_.refs_1_
  115.1 11.6 %collective-permute-start.14 = (bf16[256,2048]{1,0:T(8,128)(2,1)}, bf16[256,2048]{1,0:T(8,128)(2,1)}, u32[]{:S(2)}, u32[]{:S(2)}) collective-permute-start(bf16[256,2048]{1,0:T(8,128)(2,1)} %shard_map.261.refs_11_.refs_1_), channel_id=1, source_target_pairs={{0,1},{1,0},{2,3},{3,2},{4,5},{5,4},{6,7},{7,6},{8,9},{9,8},{10,11... | collective-permute-start | bytes 3145736 | tf_op jit(solution)/shard_map/ppermute | solution.py:34
  126.7 3.8 shard_map.262.refs_1_.refs_7_.refs_0_
  130.5 4.3 shard_map.263
  142.9 7.8 %collective-permute-done.14.refs_3_ = bf16[256,2048]{1,0:T(8,128)(2,1)} collective-permute-done((bf16[256,2048]{1,0:T(8,128)(2,1)}, bf16[256,2048]{1,0:T(8,128)(2,1)}, u32[]{:S(2)}, u32[]{:S(2)}) %collective-permute-start.14) | collective-permute-done | bytes 1048608 | tf_op jit(solution)/shard_map/ppermute | solution.py:34
  150.7 4.3 shard_map.265
  155.0 15.0 %shard_map.266 = (bf16[256,1024]{1,0:T(8,128)(2,1)}, f32[8,8,256]{2,1,0:T(8,128)}) custom-call(s32[2]{0:T(128)} %pad_add_fusion.place, bf16[256,1024]{1,0:T(8,128)(2,1)} %shard_map.262.refs_1_.refs_7_.refs_0_, bf16[256,2048]{1,0:T(8,128)(2,1)} %shard_map.261.refs_11_.refs_1_, bf16[256,2048]{1,0:T(8,128)(2,1)} %copy-done.7, ...), custom_call_target="tpu_custom_call" | custom-call | bytes 45000000 | tf_op jit(solution)/shard_map/pallas_call | solution.py:332
  170.0 7.1 collective-permute-done.20.refs_0_.refs_32_.refs_3_.refs_8_.refs_27_.refs_9_.refs_11_
  182.5 4.3 shard_map.268
  186.8 19.6 %shard_map.269 = (f32[256,1024]{1,0:T(8,128)}, bf16[256,7168]{1,0:T(8,128)(2,1)}, bf16[256,4096]{1,0:T(8,128)(2,1)}, f32[256,1024]{1,0:T(8,128)}, bf16[256,1024]{1,0:T(8,128)(2,1)}) custom-call(s32[2]{0:T(128)} %pad_add_fusion.place, bf16[256,1024]{1,0:T(8,128)(2,1)} %get-tuple-element.162.refs_6_.refs_0_, ...), custom_call_target="tpu_custom_call" | custom-call | bytes 57000000 | tf_op jit(solution)/shard_map/pallas_call | solution.py:332
  206.4 11.9 %collective-permute-done.24.refs_0_.refs_7_.refs_12_.refs_18_.refs_17_.refs_31_.refs_13_ = bf16[192,4096]{1,0:T(8,128)(2,1)} collective-permute-done((bf16[192,4096]{1,0:T(8,128)(2,1)}, bf16[192,4096]{1,0:T(8,128)(2,1)}, u32[]{:S(2)}, u32[]{:S(2)}) %collective-permute-start.24) | collective-permute-done | bytes 1572896 | tf_op jit(solution)/shard_map/ppermute | solution.py:29
  218.8 2.9 shard_map.270
  224.3 5.2 shard_map.271.refs_11_.refs_1_
  229.5 6.5 collective-permute-start.29
  236.0 3.8 shard_map.272.refs_4_.refs_5_.refs_0_
  239.9 19.8 %collective-permute-done.29.refs_3_ = bf16[256,2048]{1,0:T(8,128)(2,1)S(1)} collective-permute-done((bf16[256,2048]{1,0:T(8,128)(2,1)}, bf16[256,2048]{1,0:T(8,128)(2,1)S(1)}, u32[]{:S(2)}, u32[]{:S(2)}) %collective-permute-start.29) | collective-permute-done | bytes 1048608 | tf_op jit(solution)/shard_map/ppermute | solution.py:34
  265.1 15.2 %shard_map.274 = (bf16[256,1024]{1,0:T(8,128)(2,1)}, f32[8,8,256]{2,1,0:T(8,128)}) custom-call(s32[2]{0:T(128)} %pad_add_fusion.place, bf16[256,1024]{1,0:T(8,128)(2,1)} %shard_map.272.refs_4_.refs_5_.refs_0_, bf16[256,2048]{1,0:T(8,128)(2,1)} %shard_map.271.refs_11_.refs_1_, bf16[256,2048]{1,0:T(8,128)(2,1)} %collective-permute-done.28.refs_2_, ...), custom_call_target="tpu_custom_call" | custom-call | bytes 45000000 | tf_op jit(solution)/shard_map/pallas_call | solution.py:332
  284.0 19.4 %shard_map.275 = (f32[256,1024]{1,0:T(8,128)}, bf16[256,7168]{1,0:T(8,128)(2,1)}, bf16[256,4096]{1,0:T(8,128)(2,1)}, f32[256,1024]{1,0:T(8,128)}, bf16[256,1024]{1,0:T(8,128)(2,1)}) custom-call(s32[2]{0:T(128)} %pad_add_fusion.place, bf16[256,1024]{1,0:T(8,128)(2,1)} %get-tuple-element.181.refs_0_.refs_36_, f32[256,1024]{1,0:T(8,128)} %get-tuple-element.182.refs_1_.refs_4_, ...), custom_call_target="tpu_custom_call" | custom-call | bytes 57000000 | tf_op jit(solution)/shard_map/pallas_call | solution.py:332
  304.0 19.4 %shard_map.276 = (bf16[256,2048]{1,0:T(8,128)(2,1)}, bf16[256,2048]{1,0:T(8,128)(2,1)}, bf16[256,1024]{1,0:T(8,128)(2,1)}, f32[1,4096]{1,0:T(1,128)}, f32[256,10...) custom-call(s32[2]{0:T(128)} %pad_add_fusion.place, ...), custom_call_target="tpu_custom_call" | custom-call | bytes 54000000 | tf_op jit(solution)/shard_map/pallas_call | solution.py:332
  324.1 8.3 %shard_map.277 = (bf16[256,2048]{1,0:T(8,128)(2,1)}, bf16[256,2048]{1,0:T(8,128)(2,1)}, bf16[2,256,2048]{2,1,0:T(8,128)(2,1)}) custom-call(s32[2]{0:T(128)} %pad_add_fusion.place, bf16[256,7168]{1,0:T(8,128)(2,1)} %get-tuple-element.196.refs_0_.refs_5_.refs_2_, bf16[256,7168]{1,0:T(8,128)(2,1)} %collective-permute-done.40.refs_1_.refs_3_, ...), custom_call_target="tpu_custom_call" | custom-call | bytes 21000000 | tf_op jit(solution)/shard_map/pallas_call | solution.py:332
  335.5 17.8 %shard_map.278 = (bf16[256,1024]{1,0:T(8,128)(2,1)}, bf16[256,2048]{1,0:T(8,128)(2,1)}, bf16[256,2048]{1,0:T(8,128)(2,1)}, bf16[256,2048]{1,0:T(8,128)(2,1)}, bf16[256,2048]{1,0:T(8,128)(2,1)}) custom-call(s32[2]{0:T(128)} %pad_add_fusion.place, bf16[256,1024]{1,0:T(8,128)(2,1)} %shard_map.272.refs_4_.refs_5_.refs_0_, ...), custom_call_target="tpu_custom_call" | custom-call | bytes 54000000 | tf_op jit(solution)/shard_map/pallas_call | solution.py:332
  353.8 7.7 %shard_map.279 = (bf16[256,2048]{1,0:T(8,128)(2,1)}, bf16[256,2048]{1,0:T(8,128)(2,1)}, bf16[2,256,2048]{2,1,0:T(8,128)(2,1)}) custom-call(s32[2]{0:T(128)} %pad_add_fusion.place, bf16[256,7168]{1,0:T(8,128)(2,1)} %get-tuple-element.196.refs_0_.refs_5_.refs_2_, bf16[256,7168]{1,0:T(8,128)(2,1)} %collective-permute-done.40.refs_1_.refs_3_, ...), custom_call_target="tpu_custom_call" | custom-call | bytes 21000000 | tf_op jit(solution)/shard_map/pallas_call | solution.py:332
  361.6 5.2 shard_map.280
  369.8 6.3 collective-permute-start.49
  380.1 19.3 %collective-permute-done.49.refs_3_ = bf16[256,2048]{1,0:T(8,128)(2,1)S(1)} collective-permute-done((bf16[256,2048]{1,0:T(8,128)(2,1)S(1)}, bf16[256,2048]{1,0:T(8,128)(2,1)S(1)}, u32[]{:S(2)}, u32[]{:S(2)}) %collective-permute-start.49) | collective-permute-done | bytes 1048608 | tf_op jit(solution)/shard_map/ppermute | solution.py:34
  400.4 10.1 %shard_map.281 = (f32[256,1024]{1,0:T(8,128)}, bf16[256,2048]{1,0:T(8,128)(2,1)}, f32[8,1024]{1,0:T(8,128)}, bf16[256,2048]{1,0:T(8,128)(2,1)}) custom-call(s32[2]{0:T(128)} %pad_add_fusion.place, bf16[256,1024]{1,0:T(8,128)(2,1)} %get-tuple-element.202.refs_6_.refs_0_, bf16[256,2048]{1,0:T(8,128)(2,1)} %get-tuple-element.203.refs_1_, ...), custom_call_target="tpu_custom_call" | custom-call | bytes 30000000 | tf_op jit(solution)/shard_map/pallas_call | solution.py:332
  413.4 6.0 shard_map.282
  420.2 5.4 collective-permute-start.39
  427.0 18.9 %shard_map.283 = (bf16[256,2048]{1,0:T(8,128)(2,1)}, bf16[256,2048]{1,0:T(8,128)(2,1)}, bf16[256,1024]{1,0:T(8,128)(2,1)}, f32[1,4096]{1,0:T(1,128)}, f32[256,10...) custom-call(s32[2]{0:T(128)} %pad_add_fusion.place, f32[256,1024]{1,0:T(8,128)} %get-tuple-element.214.refs_0_, ...), custom_call_target="tpu_custom_call" | custom-call | bytes 54000000 | tf_op jit(solution)/shard_map/pallas_call | solution.py:332
  445.9 6.9 collective-permute-start.58
  452.8 8.4 %shard_map.284 = (bf16[256,2048]{1,0:T(8,128)(2,1)}, bf16[256,2048]{1,0:T(8,128)(2,1)}, bf16[2,256,2048]{2,1,0:T(8,128)(2,1)}) custom-call(s32[2]{0:T(128)} %pad_add_fusion.place, bf16[256,7168]{1,0:T(8,128)(2,1)} %get-tuple-element.196.refs_0_.refs_5_.refs_2_, bf16[256,7168]{1,0:T(8,128)(2,1)} %collective-permute-done.40.refs_1_.refs_3_, ...), custom_call_target="tpu_custom_call" | custom-call | bytes 21000000 | tf_op jit(solution)/shard_map/pallas_call | solution.py:332
  461.3 4.4 shard_map.285.refs_4_
  469.8 8.1 %shard_map.286 = (bf16[256,2048]{1,0:T(8,128)(2,1)}, bf16[256,2048]{1,0:T(8,128)(2,1)}, bf16[2,256,2048]{2,1,0:T(8,128)(2,1)}) custom-call(s32[2]{0:T(128)} %pad_add_fusion.place, bf16[256,7168]{1,0:T(8,128)(2,1)} %get-tuple-element.198.refs_0_.refs_5_.refs_2_, bf16[256,7168]{1,0:T(8,128)(2,1)} %collective-permute-done.41.refs_5_.refs_1_.refs_3_, ...), custom_call_target="tpu_custom_call" | custom-call | bytes 21000000 | tf_op jit(solution)/shard_map/pallas_call | solution.py:332
  477.9 17.8 %shard_map.287 = (bf16[256,1024]{1,0:T(8,128)(2,1)}, bf16[256,2048]{1,0:T(8,128)(2,1)}, bf16[256,2048]{1,0:T(8,128)(2,1)}, bf16[256,2048]{1,0:T(8,128)(2,1)}, bf16[256,2048]{1,0:T(8,128)(2,1)}) custom-call(s32[2]{0:T(128)} %pad_add_fusion.place, bf16[256,1024]{1,0:T(8,128)(2,1)} %shard_map.262.refs_1_.refs_7_.refs_0_, ...), custom_call_target="tpu_custom_call" | custom-call | bytes 54000000 | tf_op jit(solution)/shard_map/pallas_call | solution.py:332
  498.7 5.3 shard_map.288
  508.8 13.7 %collective-permute-done.66.refs_1_ = bf16[256,2048]{1,0:T(8,128)(2,1)} collective-permute-done((bf16[256,2048]{1,0:T(8,128)(2,1)}, bf16[256,2048]{1,0:T(8,128)(2,1)}, u32[]{:S(2)}, u32[]{:S(2)}) %collective-permute-start.66) | collective-permute-done | bytes 1048608 | tf_op jit(solution)/shard_map/ppermute | solution.py:29
  523.6 5.3 shard_map.289
  534.8 7.7 %shard_map.290 = (bf16[256,2048]{1,0:T(8,128)(2,1)}, bf16[256,2048]{1,0:T(8,128)(2,1)}, bf16[2,256,2048]{2,1,0:T(8,128)(2,1)}) custom-call(s32[2]{0:T(128)} %pad_add_fusion.place, bf16[256,7168]{1,0:T(8,128)(2,1)} %get-tuple-element.198.refs_0_.refs_5_.refs_2_, bf16[256,7168]{1,0:T(8,128)(2,1)} %collective-permute-done.41.refs_5_.refs_1_.refs_3_, ...), custom_call_target="tpu_custom_call" | custom-call | bytes 21000000 | tf_op jit(solution)/shard_map/pallas_call | solution.py:332
  545.1 10.4 %shard_map.291 = (f32[256,1024]{1,0:T(8,128)}, bf16[256,2048]{1,0:T(8,128)(2,1)}, f32[8,1024]{1,0:T(8,128)}, bf16[256,2048]{1,0:T(8,128)(2,1)}) custom-call(s32[2]{0:T(128)} %pad_add_fusion.place, bf16[256,1024]{1,0:T(8,128)(2,1)} %get-tuple-element.234.refs_3_.refs_0_, bf16[256,2048]{1,0:T(8,128)(2,1)} %get-tuple-element.235.refs_1_, ...), custom_call_target="tpu_custom_call" | custom-call | bytes 30000000 | tf_op jit(solution)/shard_map/pallas_call | solution.py:332
  563.1 3.6 collective-permute-done.77
  568.0 13.8 %collective-permute-done.74.refs_1_ = bf16[256,2048]{1,0:T(8,128)(2,1)S(1)} collective-permute-done((bf16[256,2048]{1,0:T(8,128)(2,1)S(1)}, bf16[256,2048]{1,0:T(8,128)(2,1)S(1)}, u32[]{:S(2)}, u32[]{:S(2)}) %collective-permute-start.74) | collective-permute-done | bytes 1048608 | tf_op jit(solution)/shard_map/ppermute | solution.py:29
  583.1 5.2 shard_map.292
  588.3 8.4 %shard_map.293 = (bf16[256,2048]{1,0:T(8,128)(2,1)}, bf16[256,2048]{1,0:T(8,128)(2,1)}, bf16[2,256,2048]{2,1,0:T(8,128)(2,1)}) custom-call(s32[2]{0:T(128)} %pad_add_fusion.place, bf16[256,7168]{1,0:T(8,128)(2,1)} %get-tuple-element.198.refs_0_.refs_5_.refs_2_, bf16[256,7168]{1,0:T(8,128)(2,1)} %collective-permute-done.41.refs_5_.refs_1_.refs_3_, ...), custom_call_target="tpu_custom_call" | custom-call | bytes 21000000 | tf_op jit(solution)/shard_map/pallas_call | solution.py:332
  596.7 5.1 shard_map.294
  607.1 22.0 %collective-permute-done.78.refs_1_ = bf16[256,2048]{1,0:T(8,128)(2,1)S(1)} collective-permute-done((bf16[256,2048]{1,0:T(8,128)(2,1)S(1)}, bf16[256,2048]{1,0:T(8,128)(2,1)S(1)}, u32[]{:S(2)}, u32[]{:S(2)}) %collective-permute-start.78) | collective-permute-done | bytes 1048608 | tf_op jit(solution)/shard_map/ppermute | solution.py:29
  630.2 5.3 shard_map.295
  641.1 8.6 %collective-permute-done.83.refs_4_ = bf16[128,2048]{1,0:T(8,128)(2,1)} collective-permute-done((bf16[128,2048]{1,0:T(8,128)(2,1)}, bf16[128,2048]{1,0:T(8,128)(2,1)}, u32[]{:S(2)}, u32[]{:S(2)}) %collective-permute-start.83) | collective-permute-done | bytes 524320 | tf_op jit(solution)/shard_map/ppermute | solution.py:29
  649.7 5.2 shard_map.296
  658.1 3.1 reduce-scatter.14.cloned.1.call-done
  670.7 36.0 %reduce-scatter.12.cloned.1.call-done = bf16[64,4096]{1,0:T(8,128)(2,1)} async-done(((bf16[256,4096]{1,0:T(8,128)(2,1)}), bf16[64,4096]{1,0:T(8,128)(2,1)}) %reduce-scatter.12.cloned.1.call-update) | async-done | bytes 524304 | tf_op jit(solution)/shard_map/reduce_scatter | solution.py:961
  (332 shorter events, 120.2 us)
Async XLA Ops:
  7.2 445.7 %reduce-scatter.6.cloned.1.call-start = ((), (), s32[]{:S(2)}) async-start(), calls=%async_computation.5 | async-start | bytes 1310720 | tf_op jit(solution)/shard_map/reduce_scatter | solution.py:958
  12.7 31.9 %collective-permute-start.2 = (bf16[160,4096]{1,0:T(8,128)(2,1)}, bf16[160,4096]{1,0:T(8,128)(2,1)S(1)}, u32[]{:S(2)}, u32[]{:S(2)}) collective-permute-start(bf16[160,4096]{1,0:T(8,128)(2,1)} %shard_map.254.refs_7_.refs_0_.refs_1_.refs_6_.refs_25_), channel_id=1, source_target_pairs={{0,8},{4,12},{8,0},{12,4},{16,24},{20,28},{24,16},{28,20},{1,9},{5... | collective-permute-start | bytes 3932168 | tf_op jit(solution)/shard_map/ppermute | solution.py:29
  15.7 30.6 %collective-permute-start.3 = (bf16[160,4096]{1,0:T(8,128)(2,1)}, bf16[160,4096]{1,0:T(8,128)(2,1)}, u32[]{:S(2)}, u32[]{:S(2)}) collective-permute-start(bf16[160,4096]{1,0:T(8,128)(2,1)} %shard_map.254.refs_7_.refs_0_.refs_1_.refs_6_.refs_25_), channel_id=1, source_target_pairs={{0,16},{4,20},{8,24},{12,28},{16,0},{20,4},{24,8},{28,12},{1,17},{... | collective-permute-start | bytes 3932168 | tf_op jit(solution)/shard_map/ppermute | solution.py:29
  51.3 40.9 %collective-permute-start.10 = (bf16[640,4096]{1,0:T(8,128)(2,1)}, bf16[640,4096]{1,0:T(8,128)(2,1)}, u32[]{:S(2)}, u32[]{:S(2)}) collective-permute-start(bf16[640,4096]{1,0:T(8,128)(2,1)} %shard_map.255.refs_0_.refs_2_.refs_16_.refs_26_.refs_1_.refs_6_.refs_5_.refs_15_.refs_25_.refs_7_), channel_id=1, source_target_pairs={{0,4},{4,0},{8,12},{12,8},{16,20},{20,16},{24,28},{28,24},{1,5},{5... | collective-permute-start | bytes 15728648 | tf_op jit(solution)/shard_map/ppermute | solution.py:29
  51.3 39.9 %collective-permute-start.8 = (bf16[208,4096]{1,0:T(8,128)(2,1)}, bf16[208,4096]{1,0:T(8,128)(2,1)}, u32[]{:S(2)}, u32[]{:S(2)}) collective-permute-start(bf16[208,4096]{1,0:T(8,128)(2,1)} %get-tuple-element.147), channel_id=1, source_target_pairs={{0,8},{4,12},{8,0},{12,4},{16,24},{20,28},{24,16},{28,20},{1,9},{5... | collective-permute-start | bytes 5111816 | tf_op jit(solution)/shard_map/ppermute | solution.py:29
  52.5 39.7 %collective-permute-start.9 = (bf16[208,4096]{1,0:T(8,128)(2,1)}, bf16[208,4096]{1,0:T(8,128)(2,1)}, u32[]{:S(2)}, u32[]{:S(2)}) collective-permute-start(bf16[208,4096]{1,0:T(8,128)(2,1)} %get-tuple-element.150), channel_id=1, source_target_pairs={{0,16},{4,20},{8,24},{12,28},{16,0},{20,4},{24,8},{28,12},{1,17},{... | collective-permute-start | bytes 5111816 | tf_op jit(solution)/shard_map/ppermute | solution.py:29
  95.7 41.8 %collective-permute-start.16 = (bf16[192,4096]{1,0:T(8,128)(2,1)}, bf16[192,4096]{1,0:T(8,128)(2,1)}, u32[]{:S(2)}, u32[]{:S(2)}) collective-permute-start(bf16[192,4096]{1,0:T(8,128)(2,1)} %get-tuple-element.153), channel_id=1, source_target_pairs={{0,8},{4,12},{8,0},{12,4},{16,24},{20,28},{24,16},{28,20},{1,9},{5... | collective-permute-start | bytes 4718600 | tf_op jit(solution)/shard_map/ppermute | solution.py:29
  96.5 41.1 %collective-permute-start.17 = (bf16[192,4096]{1,0:T(8,128)(2,1)}, bf16[192,4096]{1,0:T(8,128)(2,1)}, u32[]{:S(2)}, u32[]{:S(2)}) collective-permute-start(bf16[192,4096]{1,0:T(8,128)(2,1)} %get-tuple-element.157), channel_id=1, source_target_pairs={{0,16},{4,20},{8,24},{12,28},{16,0},{20,4},{24,8},{28,12},{1,17},{... | collective-permute-start | bytes 4718600 | tf_op jit(solution)/shard_map/ppermute | solution.py:29
  115.0 27.4 %collective-permute-start.13 = (bf16[256,2048]{1,0:T(8,128)(2,1)}, bf16[256,2048]{1,0:T(8,128)(2,1)S(1)}, u32[]{:S(2)}, u32[]{:S(2)}) collective-permute-start(bf16[256,2048]{1,0:T(8,128)(2,1)} %shard_map.261.refs_11_.refs_1_), channel_id=1, source_target_pairs={{0,4},{4,0},{8,12},{12,8},{16,20},{20,16},{24,28},{28,24},{1,5},{5... | collective-permute-start | bytes 3145736 | tf_op jit(solution)/shard_map/ppermute | solution.py:29
  115.1 35.6 %collective-permute-start.14 = (bf16[256,2048]{1,0:T(8,128)(2,1)}, bf16[256,2048]{1,0:T(8,128)(2,1)}, u32[]{:S(2)}, u32[]{:S(2)}) collective-permute-start(bf16[256,2048]{1,0:T(8,128)(2,1)} %shard_map.261.refs_11_.refs_1_), channel_id=1, source_target_pairs={{0,1},{1,0},{2,3},{3,2},{4,5},{5,4},{6,7},{7,6},{8,9},{9,8},{10,11... | collective-permute-start | bytes 3145736 | tf_op jit(solution)/shard_map/ppermute | solution.py:34
  140.4 36.7 %collective-permute-start.20 = (bf16[192,4096]{1,0:T(8,128)(2,1)}, bf16[192,4096]{1,0:T(8,128)(2,1)}, u32[]{:S(2)}, u32[]{:S(2)}) collective-permute-start(bf16[192,4096]{1,0:T(8,128)(2,1)} %get-tuple-element.160.refs_1_), channel_id=1, source_target_pairs={{0,8},{4,12},{8,0},{12,4},{16,24},{20,28},{24,16},{28,20},{1,9},{5... | collective-permute-start | bytes 4718600 | tf_op jit(solution)/shard_map/ppermute | solution.py:29
  141.9 36.4 %collective-permute-start.21 = (bf16[192,4096]{1,0:T(8,128)(2,1)}, bf16[192,4096]{1,0:T(8,128)(2,1)}, u32[]{:S(2)}, u32[]{:S(2)}) collective-permute-start(bf16[192,4096]{1,0:T(8,128)(2,1)} %get-tuple-element.167), channel_id=1, source_target_pairs={{0,16},{4,20},{8,24},{12,28},{16,0},{20,4},{24,8},{28,12},{1,17},{... | collective-permute-start | bytes 4718600 | tf_op jit(solution)/shard_map/ppermute | solution.py:29
  142.4 35.9 %collective-permute-start.18 = (bf16[192,4096]{1,0:T(8,128)(2,1)}, bf16[192,4096]{1,0:T(8,128)(2,1)}, u32[]{:S(2)}, u32[]{:S(2)}) collective-permute-start(bf16[192,4096]{1,0:T(8,128)(2,1)} %collective-permute-done.16.refs_0_.refs_22_.refs_28_.refs_7_.refs_21_), channel_id=1, source_target_pairs={{0,4},{4,0},{8,12},{12,8},{16,20},{20,16},{24,28},{28,24},{1,5},{5... | collective-permute-start | bytes 4718600 | tf_op jit(solution)/shard_map/ppermute | solution.py:29
  142.4 35.9 %collective-permute-start.19 = (bf16[192,4096]{1,0:T(8,128)(2,1)}, bf16[192,4096]{1,0:T(8,128)(2,1)}, u32[]{:S(2)}, u32[]{:S(2)}) collective-permute-start(bf16[192,4096]{1,0:T(8,128)(2,1)} %collective-permute-done.17.refs_1_.refs_23_.refs_30_.refs_9_.refs_22_), channel_id=1, source_target_pairs={{0,4},{4,0},{8,12},{12,8},{16,20},{20,16},{24,28},{28,24},{1,5},{5... | collective-permute-start | bytes 4718600 | tf_op jit(solution)/shard_map/ppermute | solution.py:29
  181.2 37.1 %collective-permute-start.24 = (bf16[192,4096]{1,0:T(8,128)(2,1)}, bf16[192,4096]{1,0:T(8,128)(2,1)}, u32[]{:S(2)}, u32[]{:S(2)}) collective-permute-start(bf16[192,4096]{1,0:T(8,128)(2,1)} %get-tuple-element.171.refs_1_), channel_id=1, source_target_pairs={{0,8},{4,12},{8,0},{12,4},{16,24},{20,28},{24,16},{28,20},{1,9},{5... | collective-permute-start | bytes 4718600 | tf_op jit(solution)/shard_map/ppermute | solution.py:29
  182.0 36.6 %collective-permute-start.25 = (bf16[192,4096]{1,0:T(8,128)(2,1)}, bf16[192,4096]{1,0:T(8,128)(2,1)}, u32[]{:S(2)}, u32[]{:S(2)}) collective-permute-start(bf16[192,4096]{1,0:T(8,128)(2,1)} %get-tuple-element.174), channel_id=1, source_target_pairs={{0,16},{4,20},{8,24},{12,28},{16,0},{20,4},{24,8},{28,12},{1,17},{... | collective-permute-start | bytes 4718600 | tf_op jit(solution)/shard_map/ppermute | solution.py:29
  221.7 38.0 %collective-permute-start.31 = (bf16[192,4096]{1,0:T(8,128)(2,1)}, bf16[192,4096]{1,0:T(8,128)(2,1)}, u32[]{:S(2)}, u32[]{:S(2)}) collective-permute-start(bf16[192,4096]{1,0:T(8,128)(2,1)} %get-tuple-element.178.refs_11_), channel_id=1, source_target_pairs={{0,8},{4,12},{8,0},{12,4},{16,24},{20,28},{24,16},{28,20},{1,9},{5... | collective-permute-start | bytes 4718600 | tf_op jit(solution)/shard_map/ppermute | solution.py:29
  223.0 37.2 %collective-permute-start.32 = (bf16[192,4096]{1,0:T(8,128)(2,1)}, bf16[192,4096]{1,0:T(8,128)(2,1)}, u32[]{:S(2)}, u32[]{:S(2)}) collective-permute-start(bf16[192,4096]{1,0:T(8,128)(2,1)} %get-tuple-element.179), channel_id=1, source_target_pairs={{0,16},{4,20},{8,24},{12,28},{16,0},{20,4},{24,8},{28,12},{1,17},{... | collective-permute-start | bytes 4718600 | tf_op jit(solution)/shard_map/ppermute | solution.py:29
  229.5 30.2 %collective-permute-start.29 = (bf16[256,2048]{1,0:T(8,128)(2,1)}, bf16[256,2048]{1,0:T(8,128)(2,1)S(1)}, u32[]{:S(2)}, u32[]{:S(2)}) collective-permute-start(bf16[256,2048]{1,0:T(8,128)(2,1)} %shard_map.271.refs_11_.refs_1_), channel_id=1, source_target_pairs={{0,1},{1,0},{2,3},{3,2},{4,5},{5,4},{6,7},{7,6},{8,9},{9,8},{10,11... | collective-permute-start | bytes 3145736 | tf_op jit(solution)/shard_map/ppermute | solution.py:34
  236.0 28.6 %collective-permute-start.28 = (bf16[256,2048]{1,0:T(8,128)(2,1)}, bf16[256,2048]{1,0:T(8,128)(2,1)}, u32[]{:S(2)}, u32[]{:S(2)}) collective-permute-start(bf16[256,2048]{1,0:T(8,128)(2,1)} %shard_map.271.refs_11_.refs_1_), channel_id=1, source_target_pairs={{0,4},{4,0},{8,12},{12,8},{16,20},{20,16},{24,28},{28,24},{1,5},{5... | collective-permute-start | bytes 3145736 | tf_op jit(solution)/shard_map/ppermute | solution.py:29
  259.7 21.2 %collective-permute-start.33 = (bf16[192,4096]{1,0:T(8,128)(2,1)}, bf16[192,4096]{1,0:T(8,128)(2,1)}, u32[]{:S(2)}, u32[]{:S(2)}) collective-permute-start(bf16[192,4096]{1,0:T(8,128)(2,1)} %collective-permute-done.31.refs_0_.refs_22_.refs_28_.refs_7_.refs_21_), channel_id=1, source_target_pairs={{0,4},{4,0},{8,12},{12,8},{16,20},{20,16},{24,28},{28,24},{1,5},{5... | collective-permute-start | bytes 4718600 | tf_op jit(solution)/shard_map/ppermute | solution.py:29
  260.2 20.7 %collective-permute-start.34 = (bf16[192,4096]{1,0:T(8,128)(2,1)}, bf16[192,4096]{1,0:T(8,128)(2,1)}, u32[]{:S(2)}, u32[]{:S(2)}) collective-permute-start(bf16[192,4096]{1,0:T(8,128)(2,1)} %collective-permute-done.32.refs_1_.refs_23_.refs_30_.refs_9_.refs_22_), channel_id=1, source_target_pairs={{0,4},{4,0},{8,12},{12,8},{16,20},{20,16},{24,28},{28,24},{1,5},{5... | collective-permute-start | bytes 4718600 | tf_op jit(solution)/shard_map/ppermute | solution.py:29
  263.1 17.2 %collective-permute-start.35 = (bf16[64,4096]{1,0:T(8,128)(2,1)}, bf16[64,4096]{1,0:T(8,128)(2,1)}, u32[]{:S(2)}, u32[]{:S(2)}) collective-permute-start(bf16[64,4096]{1,0:T(8,128)(2,1)} %get-tuple-element.180.refs_5_), channel_id=1, source_target_pairs={{0,8},{4,12},{8,0},{12,4},{16,24},{20,28},{24,16},{28,20},{1,9},{5... | collective-permute-start | bytes 1572872 | tf_op jit(solution)/shard_map/ppermute | solution.py:29
  264.6 15.8 %collective-permute-start.36 = (bf16[64,4096]{1,0:T(8,128)(2,1)}, bf16[64,4096]{1,0:T(8,128)(2,1)}, u32[]{:S(2)}, u32[]{:S(2)}) collective-permute-start(bf16[64,4096]{1,0:T(8,128)(2,1)} %get-tuple-element.186), channel_id=1, source_target_pairs={{0,16},{4,20},{8,24},{12,28},{16,0},{20,4},{24,8},{28,12},{1,17},{... | collective-permute-start | bytes 1572872 | tf_op jit(solution)/shard_map/ppermute | solution.py:29
  303.4 20.7 %collective-permute-start.40 = (bf16[256,7168]{1,0:T(8,128)(2,1)}, bf16[256,7168]{1,0:T(8,128)(2,1)}, u32[]{:S(2)}, u32[]{:S(2)}) collective-permute-start(bf16[256,7168]{1,0:T(8,128)(2,1)} %get-tuple-element.196.refs_0_.refs_5_.refs_2_), channel_id=1, source_target_pairs={{0,4},{4,0},{8,12},{12,8},{16,20},{20,16},{24,28},{28,24},{1,5},{5... | collective-permute-start | bytes 11010056 | tf_op jit(solution)/shard_map/ppermute | solution.py:29
  303.7 20.5 %collective-permute-start.41 = (bf16[256,7168]{1,0:T(8,128)(2,1)}, bf16[256,7168]{1,0:T(8,128)(2,1)}, u32[]{:S(2)}, u32[]{:S(2)}) collective-permute-start(bf16[256,7168]{1,0:T(8,128)(2,1)} %get-tuple-element.198.refs_0_.refs_5_.refs_2_), channel_id=1, source_target_pairs={{0,4},{4,0},{8,12},{12,8},{16,20},{20,16},{24,28},{28,24},{1,5},{5... | collective-permute-start | bytes 11010056 | tf_op jit(solution)/shard_map/ppermute | solution.py:29
  332.4 29.2 %collective-permute-start.46 = (bf16[256,2048]{1,0:T(8,128)(2,1)}, bf16[256,2048]{1,0:T(8,128)(2,1)}, u32[]{:S(2)}, u32[]{:S(2)}) collective-permute-start(bf16[256,2048]{1,0:T(8,128)(2,1)} %get-tuple-element.199.refs_8_), channel_id=1, source_target_pairs={{0,8},{4,12},{8,0},{12,4},{16,24},{20,28},{24,16},{28,20},{1,9},{5... | collective-permute-start | bytes 3145736 | tf_op jit(solution)/shard_map/ppermute | solution.py:29
  333.0 28.6 %collective-permute-start.47 = (bf16[256,2048]{1,0:T(8,128)(2,1)}, bf16[256,2048]{1,0:T(8,128)(2,1)}, u32[]{:S(2)}, u32[]{:S(2)}) collective-permute-start(bf16[256,2048]{1,0:T(8,128)(2,1)} %get-tuple-element.206), channel_id=1, source_target_pairs={{0,16},{4,20},{8,24},{12,28},{16,0},{20,4},{24,8},{28,12},{1,17},{... | collective-permute-start | bytes 3145736 | tf_op jit(solution)/shard_map/ppermute | solution.py:29
  353.3 14.5 %collective-permute-start.48 = (bf16[256,2048]{1,0:T(8,128)(2,1)}, bf16[256,2048]{1,0:T(8,128)(2,1)}, u32[]{:S(2)}, u32[]{:S(2)}) collective-permute-start(bf16[256,2048]{1,0:T(8,128)(2,1)} %get-tuple-element.212), channel_id=1, source_target_pairs={{0,4},{4,0},{8,12},{12,8},{16,20},{20,16},{24,28},{28,24},{1,5},{5... | collective-permute-start | bytes 3145736 | tf_op jit(solution)/shard_map/ppermute | solution.py:29
  369.8 29.7 %collective-permute-start.49 = (bf16[256,2048]{1,0:T(8,128)(2,1)S(1)}, bf16[256,2048]{1,0:T(8,128)(2,1)S(1)}, u32[]{:S(2)}, u32[]{:S(2)}) collective-permute-start(bf16[256,2048]{1,0:T(8,128)(2,1)S(1)} %add_convert_fusion.1.refs_17_), channel_id=1, source_target_pairs={{0,1},{1,0},{2,3},{3,2},{4,5},{5,4},{6,7},{7,6},{8,9},{9,8},{10,11... | collective-permute-start | bytes 3145736 | tf_op jit(solution)/shard_map/ppermute | solution.py:34
  376.1 34.5 %collective-permute-start.50 = (bf16[256,2048]{1,0:T(8,128)(2,1)}, bf16[256,2048]{1,0:T(8,128)(2,1)}, u32[]{:S(2)}, u32[]{:S(2)}) collective-permute-start(bf16[256,2048]{1,0:T(8,128)(2,1)} %get-tuple-element.207.refs_3_), channel_id=1, source_target_pairs={{0,8},{4,12},{8,0},{12,4},{16,24},{20,28},{24,16},{28,20},{1,9},{5... | collective-permute-start | bytes 3145736 | tf_op jit(solution)/shard_map/ppermute | solution.py:29
  377.3 33.3 %collective-permute-start.51 = (bf16[256,2048]{1,0:T(8,128)(2,1)}, bf16[256,2048]{1,0:T(8,128)(2,1)}, u32[]{:S(2)}, u32[]{:S(2)}) collective-permute-start(bf16[256,2048]{1,0:T(8,128)(2,1)} %get-tuple-element.219), channel_id=1, source_target_pairs={{0,16},{4,20},{8,24},{12,28},{16,0},{20,4},{24,8},{28,12},{1,17},{... | collective-permute-start | bytes 3145736 | tf_op jit(solution)/shard_map/ppermute | solution.py:29
  377.8 35.6 %collective-permute-start.52 = (bf16[128,2048]{1,0:T(8,128)(2,1)}, bf16[128,2048]{1,0:T(8,128)(2,1)}, u32[]{:S(2)}, u32[]{:S(2)}) collective-permute-start(bf16[128,2048]{1,0:T(8,128)(2,1)} %get-tuple-element.208), channel_id=1, source_target_pairs={{0,16},{4,20},{8,24},{12,28},{16,0},{20,4},{24,8},{28,12},{1,17},{... | collective-permute-start | bytes 1572872 | tf_op jit(solution)/shard_map/ppermute | solution.py:29
  379.3 34.1 %collective-permute-start.53 = (bf16[128,2048]{1,0:T(8,128)(2,1)}, bf16[128,2048]{1,0:T(8,128)(2,1)}, u32[]{:S(2)}, u32[]{:S(2)}) collective-permute-start(bf16[128,2048]{1,0:T(8,128)(2,1)} %get-tuple-element.221), channel_id=1, source_target_pairs={{0,8},{4,12},{8,0},{12,4},{16,24},{20,28},{24,16},{28,20},{1,9},{5... | collective-permute-start | bytes 1572872 | tf_op jit(solution)/shard_map/ppermute | solution.py:29
  419.4 79.3 %reduce-scatter.8.cloned.1.call-start = ((), (), s32[]{:S(2)}) async-start(), calls=%async_computation.6 | async-start | bytes 1310720 | tf_op jit(solution)/shard_map/reduce_scatter | solution.py:958
  419.7 33.2 %collective-permute-start.54 = (bf16[256,2048]{1,0:T(8,128)(2,1)S(1)}, bf16[256,2048]{1,0:T(8,128)(2,1)}, u32[]{:S(2)}, u32[]{:S(2)}) collective-permute-start(bf16[256,2048]{1,0:T(8,128)(2,1)S(1)} %copy-done.5), channel_id=1, source_target_pairs={{0,4},{4,0},{8,12},{12,8},{16,20},{20,16},{24,28},{28,24},{1,5},{5... | collective-permute-start | bytes 3145736 | tf_op jit(solution)/shard_map/ppermute | solution.py:29
  419.7 33.1 %collective-permute-start.57 = (bf16[256,2048]{1,0:T(8,128)(2,1)}, bf16[256,2048]{1,0:T(8,128)(2,1)}, u32[]{:S(2)}, u32[]{:S(2)}) collective-permute-start(bf16[256,2048]{1,0:T(8,128)(2,1)} %get-tuple-element.227.refs_6_), channel_id=1, source_target_pairs={{0,4},{4,0},{8,12},{12,8},{16,20},{20,16},{24,28},{28,24},{1,5},{5... | collective-permute-start | bytes 3145736 | tf_op jit(solution)/shard_map/ppermute | solution.py:29
  420.2 25.7 %collective-permute-start.39 = (bf16[256,1024]{1,0:T(8,128)(2,1)}, bf16[256,1024]{1,0:T(8,128)(2,1)}, u32[]{:S(2)}, u32[]{:S(2)}) collective-permute-start(bf16[256,1024]{1,0:T(8,128)(2,1)} %get-tuple-element.189), channel_id=1, source_target_pairs={{0,0},{4,1},{1,2},{5,3},{2,4},{6,5},{3,6},{7,7},{8,8},{12,9},{9,10... | collective-permute-start | bytes 1572872 | tf_op jit(solution)/shard_map/ppermute | solution.py:1302
  425.6 35.6 %collective-permute-start.55 = (bf16[128,2048]{1,0:T(8,128)(2,1)}, bf16[128,2048]{1,0:T(8,128)(2,1)}, u32[]{:S(2)}, u32[]{:S(2)}) collective-permute-start(bf16[128,2048]{1,0:T(8,128)(2,1)} %get-tuple-element.222.refs_35_), channel_id=1, source_target_pairs={{0,16},{4,20},{8,24},{12,28},{16,0},{20,4},{24,8},{28,12},{1,17},{... | collective-permute-start | bytes 1572872 | tf_op jit(solution)/shard_map/ppermute | solution.py:29
  426.2 35.1 %collective-permute-start.56 = (bf16[128,2048]{1,0:T(8,128)(2,1)}, bf16[128,2048]{1,0:T(8,128)(2,1)}, u32[]{:S(2)}, u32[]{:S(2)}) collective-permute-start(bf16[128,2048]{1,0:T(8,128)(2,1)} %get-tuple-element.226), channel_id=1, source_target_pairs={{0,8},{4,12},{8,0},{12,4},{16,24},{20,28},{24,16},{28,20},{1,9},{5... | collective-permute-start | bytes 1572872 | tf_op jit(solution)/shard_map/ppermute | solution.py:29
  445.9 22.9 %collective-permute-start.58 = (bf16[256,2048]{1,0:T(8,128)(2,1)}, bf16[256,2048]{1,0:T(8,128)(2,1)}, u32[]{:S(2)}, u32[]{:S(2)}) collective-permute-start(bf16[256,2048]{1,0:T(8,128)(2,1)} %get-tuple-element.228.refs_10_.refs_2_), channel_id=1, source_target_pairs={{0,4},{4,0},{8,12},{12,8},{16,20},{20,16},{24,28},{28,24},{1,5},{5... | collective-permute-start | bytes 3145736 | tf_op jit(solution)/shard_map/ppermute | solution.py:29
  452.8 16.0 %collective-permute-start.59 = (bf16[256,2048]{1,0:T(8,128)(2,1)}, bf16[256,2048]{1,0:T(8,128)(2,1)S(1)}, u32[]{:S(2)}, u32[]{:S(2)}) collective-permute-start(bf16[256,2048]{1,0:T(8,128)(2,1)} %get-tuple-element.231.refs_4_), channel_id=1, source_target_pairs={{0,4},{4,0},{8,12},{12,8},{16,20},{20,16},{24,28},{28,24},{1,5},{5... | collective-permute-start | bytes 3145736 | tf_op jit(solution)/shard_map/ppermute | solution.py:29
  465.7 164.5 %reduce-scatter.10.cloned.1.call-start = ((), (), s32[]{:S(2)}) async-start(), calls=%async_computation.7 | async-start | bytes 1310720 | tf_op jit(solution)/shard_map/reduce_scatter | solution.py:958
  466.3 31.0 %collective-permute-start.62 = (bf16[256,2048]{1,0:T(8,128)(2,1)}, bf16[256,2048]{1,0:T(8,128)(2,1)}, u32[]{:S(2)}, u32[]{:S(2)}) collective-permute-start(bf16[256,2048]{1,0:T(8,128)(2,1)} %get-tuple-element.230.refs_3_), channel_id=1, source_target_pairs={{0,8},{4,12},{8,0},{12,4},{16,24},{20,28},{24,16},{28,20},{1,9},{5... | collective-permute-start | bytes 3145736 | tf_op jit(solution)/shard_map/ppermute | solution.py:29
  467.1 31.6 %collective-permute-start.63 = (bf16[256,2048]{1,0:T(8,128)(2,1)}, bf16[256,2048]{1,0:T(8,128)(2,1)}, u32[]{:S(2)}, u32[]{:S(2)}) collective-permute-start(bf16[256,2048]{1,0:T(8,128)(2,1)} %get-tuple-element.238), channel_id=1, source_target_pairs={{0,16},{4,20},{8,24},{12,28},{16,0},{20,4},{24,8},{28,12},{1,17},{... | collective-permute-start | bytes 3145736 | tf_op jit(solution)/shard_map/ppermute | solution.py:29
  496.3 26.3 %collective-permute-start.66 = (bf16[256,2048]{1,0:T(8,128)(2,1)}, bf16[256,2048]{1,0:T(8,128)(2,1)}, u32[]{:S(2)}, u32[]{:S(2)}) collective-permute-start(bf16[256,2048]{1,0:T(8,128)(2,1)} %get-tuple-element.233.refs_8_), channel_id=1, source_target_pairs={{0,8},{4,12},{8,0},{12,4},{16,24},{20,28},{24,16},{28,20},{1,9},{5... | collective-permute-start | bytes 3145736 | tf_op jit(solution)/shard_map/ppermute | solution.py:29
  497.2 26.3 %collective-permute-start.67 = (bf16[256,2048]{1,0:T(8,128)(2,1)}, bf16[256,2048]{1,0:T(8,128)(2,1)}, u32[]{:S(2)}, u32[]{:S(2)}) collective-permute-start(bf16[256,2048]{1,0:T(8,128)(2,1)} %get-tuple-element.246), channel_id=1, source_target_pairs={{0,16},{4,20},{8,24},{12,28},{16,0},{20,4},{24,8},{28,12},{1,17},{... | collective-permute-start | bytes 3145736 | tf_op jit(solution)/shard_map/ppermute | solution.py:29
  506.9 38.1 %collective-permute-start.65 = (bf16[256,2048]{1,0:T(8,128)(2,1)S(1)}, bf16[256,2048]{1,0:T(8,128)(2,1)}, u32[]{:S(2)}, u32[]{:S(2)}) collective-permute-start(bf16[256,2048]{1,0:T(8,128)(2,1)S(1)} %add_convert_fusion.refs_3_), channel_id=1, source_target_pairs={{0,1},{1,0},{2,3},{3,2},{4,5},{5,4},{6,7},{7,6},{8,9},{9,8},{10,11... | collective-permute-start | bytes 3145736 | tf_op jit(solution)/shard_map/ppermute | solution.py:34
  507.1 27.8 %collective-permute-start.69 = (bf16[128,2048]{1,0:T(8,128)(2,1)}, bf16[128,2048]{1,0:T(8,128)(2,1)}, u32[]{:S(2)}, u32[]{:S(2)}) collective-permute-start(bf16[128,2048]{1,0:T(8,128)(2,1)} %get-tuple-element.239), channel_id=1, source_target_pairs={{0,16},{4,20},{8,24},{12,28},{16,0},{20,4},{24,8},{28,12},{1,17},{... | collective-permute-start | bytes 1572872 | tf_op jit(solution)/shard_map/ppermute | solution.py:29
  507.7 26.1 %collective-permute-start.68 = (bf16[128,2048]{1,0:T(8,128)(2,1)}, bf16[128,2048]{1,0:T(8,128)(2,1)}, u32[]{:S(2)}, u32[]{:S(2)}) collective-permute-start(bf16[128,2048]{1,0:T(8,128)(2,1)} %get-tuple-element.248), channel_id=1, source_target_pairs={{0,8},{4,12},{8,0},{12,4},{16,24},{20,28},{24,16},{28,20},{1,9},{5... | collective-permute-start | bytes 1572872 | tf_op jit(solution)/shard_map/ppermute | solution.py:29
  528.9 15.6 %collective-permute-start.70 = (bf16[128,2048]{1,0:T(8,128)(2,1)}, bf16[128,2048]{1,0:T(8,128)(2,1)}, u32[]{:S(2)}, u32[]{:S(2)}) collective-permute-start(bf16[128,2048]{1,0:T(8,128)(2,1)} %get-tuple-element.250), channel_id=1, source_target_pairs={{0,8},{4,12},{8,0},{12,4},{16,24},{20,28},{24,16},{28,20},{1,9},{5... | collective-permute-start | bytes 1572872 | tf_op jit(solution)/shard_map/ppermute | solution.py:29
  530.0 15.1 %collective-permute-start.71 = (bf16[128,2048]{1,0:T(8,128)(2,1)}, bf16[128,2048]{1,0:T(8,128)(2,1)}, u32[]{:S(2)}, u32[]{:S(2)}) collective-permute-start(bf16[128,2048]{1,0:T(8,128)(2,1)} %get-tuple-element.247.refs_6_), channel_id=1, source_target_pairs={{0,16},{4,20},{8,24},{12,28},{16,0},{20,4},{24,8},{28,12},{1,17},{... | collective-permute-start | bytes 1572872 | tf_op jit(solution)/shard_map/ppermute | solution.py:29
  557.5 24.2 %collective-permute-start.74 = (bf16[256,2048]{1,0:T(8,128)(2,1)S(1)}, bf16[256,2048]{1,0:T(8,128)(2,1)S(1)}, u32[]{:S(2)}, u32[]{:S(2)}) collective-permute-start(bf16[256,2048]{1,0:T(8,128)(2,1)S(1)} %copy-done.18), channel_id=1, source_target_pairs={{0,8},{4,12},{8,0},{12,4},{16,24},{20,28},{24,16},{28,20},{1,9},{5... | collective-permute-start | bytes 3145736 | tf_op jit(solution)/shard_map/ppermute | solution.py:29
  558.8 24.3 %collective-permute-start.75 = (bf16[256,2048]{1,0:T(8,128)(2,1)}, bf16[256,2048]{1,0:T(8,128)(2,1)}, u32[]{:S(2)}, u32[]{:S(2)}) collective-permute-start(bf16[256,2048]{1,0:T(8,128)(2,1)} %get-tuple-element.254), channel_id=1, source_target_pairs={{0,16},{4,20},{8,24},{12,28},{16,0},{20,4},{24,8},{28,12},{1,17},{... | collective-permute-start | bytes 3145736 | tf_op jit(solution)/shard_map/ppermute | solution.py:29
  559.6 28.7 %collective-permute-start.72 = (bf16[256,2048]{1,0:T(8,128)(2,1)}, bf16[256,2048]{1,0:T(8,128)(2,1)}, u32[]{:S(2)}, u32[]{:S(2)}) collective-permute-start(bf16[256,2048]{1,0:T(8,128)(2,1)} %get-tuple-element.251.refs_3_.refs_4_), channel_id=1, source_target_pairs={{0,4},{4,0},{8,12},{12,8},{16,20},{20,16},{24,28},{28,24},{1,5},{5... | collective-permute-start | bytes 3145736 | tf_op jit(solution)/shard_map/ppermute | solution.py:29
  559.6 28.7 %collective-permute-start.73 = (bf16[256,2048]{1,0:T(8,128)(2,1)}, bf16[256,2048]{1,0:T(8,128)(2,1)}, u32[]{:S(2)}, u32[]{:S(2)}) collective-permute-start(bf16[256,2048]{1,0:T(8,128)(2,1)} %get-tuple-element.252.refs_6_), channel_id=1, source_target_pairs={{0,4},{4,0},{8,12},{12,8},{16,20},{20,16},{24,28},{28,24},{1,5},{5... | collective-permute-start | bytes 3145736 | tf_op jit(solution)/shard_map/ppermute | solution.py:29
  601.8 59.3 %reduce-scatter.14.cloned.1.call-start = ((), (), s32[]{:S(2)}) async-start(), calls=%async_computation.9 | async-start | bytes 1310720 | tf_op jit(solution)/shard_map/reduce_scatter | solution.py:958
  602.4 104.3 %reduce-scatter.12.cloned.1.call-start = ((), (), s32[]{:S(2)}) async-start(), calls=%async_computation.8 | async-start | bytes 2621440 | tf_op jit(solution)/shard_map/reduce_scatter | solution.py:961
  603.0 26.1 %collective-permute-start.78 = (bf16[256,2048]{1,0:T(8,128)(2,1)S(1)}, bf16[256,2048]{1,0:T(8,128)(2,1)S(1)}, u32[]{:S(2)}, u32[]{:S(2)}) collective-permute-start(bf16[256,2048]{1,0:T(8,128)(2,1)S(1)} %copy-done.24), channel_id=1, source_target_pairs={{0,8},{4,12},{8,0},{12,4},{16,24},{20,28},{24,16},{28,20},{1,9},{5... | collective-permute-start | bytes 3145736 | tf_op jit(solution)/shard_map/ppermute | solution.py:29
  604.0 26.2 %collective-permute-start.79 = (bf16[256,2048]{1,0:T(8,128)(2,1)S(1)}, bf16[256,2048]{1,0:T(8,128)(2,1)}, u32[]{:S(2)}, u32[]{:S(2)}) collective-permute-start(bf16[256,2048]{1,0:T(8,128)(2,1)S(1)} %copy-done.33), channel_id=1, source_target_pairs={{0,16},{4,20},{8,24},{12,28},{16,0},{20,4},{24,8},{28,12},{1,17},{... | collective-permute-start | bytes 3145736 | tf_op jit(solution)/shard_map/ppermute | solution.py:29
  604.8 36.3 %collective-permute-start.81 = (bf16[128,2048]{1,0:T(8,128)(2,1)}, bf16[128,2048]{1,0:T(8,128)(2,1)}, u32[]{:S(2)}, u32[]{:S(2)}) collective-permute-start(bf16[128,2048]{1,0:T(8,128)(2,1)} %get-tuple-element.261.refs_10_), channel_id=1, source_target_pairs={{0,16},{4,20},{8,24},{12,28},{16,0},{20,4},{24,8},{28,12},{1,17},{... | collective-permute-start | bytes 1572872 | tf_op jit(solution)/shard_map/ppermute | solution.py:29
  606.0 35.1 %collective-permute-start.82 = (bf16[128,2048]{1,0:T(8,128)(2,1)}, bf16[128,2048]{1,0:T(8,128)(2,1)}, u32[]{:S(2)}, u32[]{:S(2)}) collective-permute-start(bf16[128,2048]{1,0:T(8,128)(2,1)} %get-tuple-element.271), channel_id=1, source_target_pairs={{0,8},{4,12},{8,0},{12,4},{16,24},{20,28},{24,16},{28,20},{1,9},{5... | collective-permute-start | bytes 1572872 | tf_op jit(solution)/shard_map/ppermute | solution.py:29
  635.5 14.2 %collective-permute-start.83 = (bf16[128,2048]{1,0:T(8,128)(2,1)}, bf16[128,2048]{1,0:T(8,128)(2,1)}, u32[]{:S(2)}, u32[]{:S(2)}) collective-permute-start(bf16[128,2048]{1,0:T(8,128)(2,1)} %get-tuple-element.268.refs_6_), channel_id=1, source_target_pairs={{0,16},{4,20},{8,24},{12,28},{16,0},{20,4},{24,8},{28,12},{1,17},{... | collective-permute-start | bytes 1572872 | tf_op jit(solution)/shard_map/ppermute | solution.py:29
  638.5 26.5 %collective-permute-start.80 = (bf16[256,1024]{1,0:T(8,128)(2,1)}, bf16[256,1024]{1,0:T(8,128)(2,1)S(1)}, u32[]{:S(2)}, u32[]{:S(2)}) collective-permute-start(bf16[256,1024]{1,0:T(8,128)(2,1)} %slice.168), channel_id=1, source_target_pairs={{0,0},{4,1},{1,2},{5,3},{2,4},{6,5},{3,6},{7,7},{8,8},{12,9},{9,10... | collective-permute-start | bytes 1572872 | tf_op jit(solution)/shard_map/ppermute | solution.py:1377
  (63 other events, 446.4 us)
Sparse Core Ops, SparseCore 0:
  419.5 27.6 reduce-scatter.5
  465.8 25.6 reduce-scatter.7
  602.0 25.7 reduce-scatter.9
  630.1 31.0 reduce-scatter.13
  663.3 43.3 reduce-scatter.11

commit v3 on v2

--- a/solution.py
+++ b/solution.py
@@ -345,11 +345,59 @@
     )(place, *arrays, *deps)
 
 
-def pack_inputs(pack, tile_of):
-    return [
-        (array, pl.BlockSpec((rows, TILE), lambda i, s, r=row_block: (r, tile_of(i))))
-        for array, row_block, rows in pack
-    ]
+class Flow:
+    def __init__(self, sems):
+        self.sems, self.count, self.pending = sems, 0, {}
+
+    def start(self, key, source, target):
+        copy = pltpu.make_async_copy(source, target, self.sems.at[self.count])
+        self.count += 1
+        copy.start()
+        self.pending.setdefault(key, []).append(copy)
+
+    def wait(self, key):
+        for copy in self.pending.pop(key):
+            copy.wait()
+
+    def drain(self):
+        for key in list(self.pending):
+            self.wait(key)
+
+    def pack(self, key, pack, refs, target, first, columns):
+        at = 0
+        for (_, block, rows), ref in zip(pack, refs):
+            self.start(
+                key,
+                ref.at[pl.ds(block * rows, rows), pl.ds(first, columns)],
+                target.at[pl.ds(at, rows), :] if target.shape[1] == columns else target.at[pl.ds(at, rows), pl.ds(first, columns)],
+            )
+            at += rows
+
+
+def run_flow(body, arrays, packs, outputs, scratch, copies, deps=(), cost=8):
+    buffers = [buffer for pack in packs for buffer, _, _ in pack]
+    count, extra, made = len(arrays), len(buffers), len(outputs)
+
+    def kernel(place, *refs):
+        outs = refs[count + extra + len(deps) :][:made]
+        held = refs[count + extra + len(deps) + made : -1]
+        weights, at = [], count
+        for pack in packs:
+            weights.append(refs[at : at + len(pack)])
+            at += len(pack)
+        body(place, Flow(refs[-1]), refs[:count], weights, outs, held)
+
+    place = jnp.stack([lax.axis_index("dp"), lax.axis_index("seq")]).astype(jnp.int32)
+    anywhere = pl.BlockSpec(memory_space=pl.ANY)
+    return pl.pallas_call(
+        kernel,
+        out_shape=[jax.ShapeDtypeStruct(shape, kind) for shape, kind in outputs],
+        in_specs=[pl.BlockSpec(memory_space=pltpu.SMEM)] + [anywhere] * (count + extra + len(deps)),
+        out_specs=[anywhere] * made,
+        scratch_shapes=[pltpu.VMEM(shape, kind) for shape, kind in scratch] + [pltpu.SemaphoreType.DMA((copies,))],
+        compiler_params=pltpu.CompilerParams(vmem_limit_bytes=VMEM_LIMIT),
+        cost_estimate=pl.CostEstimate(flops=0, bytes_accessed=cost * 3_000_000, transcendentals=0),
+    )(place, *arrays, *buffers, *deps)
 
 
 def join(refs):
@@ -407,20 +455,29 @@
 def project(a, pack, first_tile, tiles, deps=()):
     tokens, width = a.shape
 
-    def body(place, ins, outs, scratch):
-        @pl.when(pl.program_id(0) == 0)
-        def _():
-            scratch[0][...] = columns_in_order(place, ins[0])
-
-        outs[0][...] = jnp.dot(scratch[0][...], join(ins[1:]), preferred_element_type=f32).astype(bf16)
-
-    return run(
+    def body(place, flow, ins, packs, outs, scratch):
+        a_ref, weights, result, ordered = scratch
+        flow.start("a", ins[0], a_ref)
+        for tile in range(tiles):
+            flow.pack(tile, pack, packs[0], weights.at[tile], (first_tile + tile) * TILE, TILE)
+        flow.wait("a")
+        ordered[...] = columns_in_order(place, a_ref)
+        for tile in range(tiles):
+            flow.wait(tile)
+            at = pl.ds(tile * TILE, TILE)
+            result[:, at] = jnp.dot(ordered[...], weights[tile], preferred_element_type=f32).astype(bf16)
+            flow.start("out", result.at[:, at], outs[0].at[:, at])
+        flow.drain()
+
+    return run_flow(
         body,
-        tiles,
-        [(a, None)] + pack_inputs(pack, lambda i: first_tile + i),
-        [((tokens, tiles * TILE), bf16, pl.BlockSpec((tokens, TILE), lambda i, s: (0, i)))],
-        [pltpu.VMEM((tokens, width), bf16)],
-        deps=deps,
+        [a],
+        [pack],
+        [((tokens, tiles * TILE), bf16)],
+        [(a.shape, bf16), ((tiles, width, TILE), bf16), ((tokens, tiles * TILE), bf16), (a.shape, bf16)],
+        1 + tiles * (len(pack) + 1),
+        deps,
+        4,
     )[0]
 
 
@@ -528,255 +585,271 @@
     )
 
 
-def window(step, tile):
-    return pl.ds(pl.multiple_of((step - tile) * TILE, BLOCK), TILE)
-
-
 ACTIVE, SECOND, MIXTURE, NORMED, KEPT = 0, 4 * TILE, 5 * TILE, 6 * TILE, 7 * TILE
+
+
+def columns(tile, count=1):
+    return pl.ds(tile * TILE, count * TILE)
 
 
 def feed_forward(normed, mixture, packs, stream, vec, bias, next_vec, deps=()):
     tokens, width = mixture.shape
-    columns = bias.shape[1]
-    attention_pack, expand_pack, reduce_pack = packs
-    one = len(attention_pack)
-
-    def body(place, ins, outs, scratch):
-        step = pl.program_id(0)
-        mixture_ref, stream_ref, vec_ref, next_ref, bias_ref, normed_ref = ins[:6]
-        middle_ref, kept_ref, slope_ref, result_ref, following_ref = outs
-        ordered, total = scratch
-
-        @pl.when(step == 0)
-        def _():
-            branch = jnp.dot(
-                columns_in_order(place, mixture_ref), join(ins[6 : 6 + one]), preferred_element_type=f32
-            )
-            middle = stream_ref[...].astype(f32) + (branch + vec_ref[2:3, :])
-            middle_ref[...] = middle
-            kept_ref[:, SECOND:MIXTURE] = modulated(middle, vec_ref, 3).astype(bf16)
-            kept_ref[:, MIXTURE:NORMED] = mixture_ref[...]
-            kept_ref[:, NORMED:KEPT] = normed_ref[...]
-            ordered[...] = columns_in_order(place, kept_ref, BLOCK, SECOND)
-
-        @pl.when((step > 0) & (step < 5))
-        def _():
-            at = window(step, 1)
-            hidden = jnp.dot(
-                ordered[...], join(ins[6 + one : 6 + 2 * one]), preferred_element_type=f32
-            ) + bias_ref[:, at]
+    hidden_width = bias.shape[1]
+    half = 2 * TILE
+
+    def body(place, flow, ins, weights, outs, scratch):
+        (mixture_ref, stream_ref, vec_ref, next_ref, bias_ref, kept, w_out, w_expand, w_reduce) = scratch[:9]
+        (middle, slope, result, following, ordered) = scratch[9:]
+        flow.start("first", ins[0], mixture_ref)
+        flow.start("first", ins[2], vec_ref)
+        flow.pack("out", packs[0], weights[0], w_out, 3 * TILE, TILE)
+        flow.start("out", ins[1], stream_ref)
+        flow.start("out", ins[4], bias_ref)
+        for number in range(2):
+            flow.pack(f"expand{number}", packs[1], weights[1], w_expand, number * half, half)
+        flow.start("normed", ins[5], kept.at[:, pl.ds(NORMED, TILE)])
+        flow.start("next", ins[3], next_ref)
+        for number in range(2):
+            flow.pack(f"reduce{number}", packs[2], weights[2], w_reduce, number * half, half)
+
+        flow.wait("first")
+        kept[:, MIXTURE:NORMED] = mixture_ref[...]
+        ordered[...] = columns_in_order(place, mixture_ref)
+        flow.wait("out")
+        branch = jnp.dot(ordered[...], w_out[...], preferred_element_type=f32)
+        middle[...] = stream_ref[...].astype(f32) + (branch + vec_ref[2:3, :])
+        flow.start("middle", middle, outs[0])
+        kept[:, SECOND:MIXTURE] = modulated(middle[...], vec_ref, 3).astype(bf16)
+        ordered[...] = columns_in_order(place, kept, BLOCK, SECOND)
+        for tile in range(4):
+            if tile % 2 == 0:
+                flow.wait(f"expand{tile // 2}")
+            at = columns(tile)
+            hidden = jnp.dot(ordered[...], w_expand[:, at], preferred_element_type=f32) + bias_ref[:, at]
             square = hidden * hidden
             bent = jnp.tanh(ROOT * hidden * (1.0 + CUBIC * square))
-            half = 0.5 * (1.0 + bent)
-            kept_ref[:, at] = (hidden * half).astype(bf16)
-            slope = half + (0.5 * ROOT) * hidden * (1.0 - bent * bent) * (1.0 + (3.0 * CUBIC) * square)
-            slope_ref[:, at] = slope.astype(bf16)
-
-        @pl.when(step >= 5)
-        def _():
-            a = columns_in_order(place, kept_ref, 4 * BLOCK, (step - 5) * BLOCK)
-            product = jnp.dot(a, join(ins[6 + 2 * one :]), preferred_element_type=f32)
-
-            @pl.when(step == 5)
-            def _():
-                total[...] = product
-
-            @pl.when(step > 5)
-            def _():
-                total[...] += product
-
-            @pl.when(step == 8)
-            def _():
-                result = middle_ref[...] + (total[...] + vec_ref[5:6, :])
-                result_ref[...] = result
-                if next_vec is None:
-                    following_ref[...] = result.astype(bf16)
-                else:
-                    following_ref[...] = modulated(result, next_ref, 0).astype(bf16)
-
-    wide_shape = (tokens, columns)
-    return run(
+            share = 0.5 * (1.0 + bent)
+            kept[:, at] = (hidden * share).astype(bf16)
+            steep = share + (0.5 * ROOT) * hidden * (1.0 - bent * bent) * (1.0 + (3.0 * CUBIC) * square)
+            slope[:, at] = steep.astype(bf16)
+            if tile == 1:
+                flow.start("slope", slope.at[:, columns(0, 2)], outs[2].at[:, columns(0, 2)])
+        flow.start("slope", slope.at[:, columns(2, 2)], outs[2].at[:, columns(2, 2)])
+        flow.wait("normed")
+        flow.start("kept", kept, outs[1])
+        for tile in range(4):
+            if tile % 2 == 0:
+                flow.wait(f"reduce{tile // 2}")
+            a = columns_in_order(place, kept, 4 * BLOCK, tile * BLOCK)
+            product = jnp.dot(a, w_reduce[:, columns(tile)], preferred_element_type=f32)
+            result[...] = product if tile == 0 else result[...] + product
+        result[...] = middle[...] + (result[...] + vec_ref[5:6, :])
+        flow.start("result", result, outs[3])
+        flow.wait("next")
+        if next_vec is None:
+            following[...] = result[...].astype(bf16)
+        else:
+            following[...] = modulated(result[...], next_ref, 0).astype(bf16)
+        flow.start("following", following, outs[4])
+        flow.drain()
+
+    wide_shape = (tokens, hidden_width)
+    rows = SMALL * BLOCK
+    return run_flow(
         body,
-        9,
+        [mixture, stream, vec, vec if next_vec is None else next_vec, bias, normed],
+        packs,
+        [(mixture.shape, f32), ((tokens, KEPT), bf16), (wide_shape, bf16), (mixture.shape, f32), (mixture.shape, bf16)],
         [
-            (mixture, None),
-            (stream, None),
-            (vec, None),
-            (vec if next_vec is None else next_vec, None),
-            (bias, None),
-            (normed, None),
-        ]
-        + pack_inputs(attention_pack, lambda i: 3)
-        + pack_inputs(expand_pack, lambda i: jnp.clip(i - 1, 0, 3))
-        + pack_inputs(reduce_pack, lambda i: jnp.clip(i - 5, 0, 3)),
-        [
-            (mixture.shape, f32, None),
-            ((tokens, KEPT), bf16, None),
-            (wide_shape, bf16, None),
-            (mixture.shape, f32, None),
-            (mixture.shape, bf16, None),
+            (mixture.shape, bf16),
+            (stream.shape, stream.dtype),
+            (vec.shape, f32),
+            (vec.shape, f32),
+            (bias.shape, f32),
+            ((tokens, KEPT), bf16),
+            ((rows, TILE), bf16),
+            ((rows, hidden_width), bf16),
+            ((rows, hidden_width), bf16),
+            (mixture.shape, f32),
+            (wide_shape, bf16),
+            (mixture.shape, f32),
+            (mixture.shape, bf16),
+            (mixture.shape, bf16),
         ],
-        [pltpu.VMEM((tokens, width), bf16), pltpu.VMEM((tokens, width), f32)],
-        deps=deps,
-        cost=19,
+        6 + 5 * len(packs[0]) + 6,
+        deps,
+        12,
     )
 
 
 def feed_forward_back(grad, grad_low, slope, middle, packs, vec, deps=()):
     tokens, width = grad.shape
-    columns = slope.shape[1]
-    attention_pack, expand_pack, reduce_pack = packs
-    one = len(attention_pack)
-
-    def body(place, ins, outs, scratch):
-        step = pl.program_id(0)
-        grad_ref, grad_low_ref, slope_ref, middle_ref, vec_ref = ins[:5]
-        hidden_refs, low_ref = outs[:2], outs[2]
-        bias_ref, middle_grad_ref, sums_ref, mixture_ref = outs[3:]
-        total, ordered = scratch
-
-        @pl.when(step < 4)
-        def _():
+    hidden_width = slope.shape[1]
+    low, low_block = grad_low
+    half = 2 * TILE
+
+    def body(place, flow, ins, weights, outs, scratch):
+        (grad_ref, low_ref, slope_ref, middle_ref, vec_ref, w_out, w_expand, w_reduce) = scratch[:8]
+        (hidden, bias, middle_grad, middle_low, sums, mixture, total, ordered) = scratch[8:]
+        flow.start("low", ins[1].at[:, columns(low_block)], low_ref)
+        flow.pack("reduce0", packs[2], weights[2], w_reduce, 0, half)
+        flow.start("slope", ins[2], slope_ref)
+        flow.pack("reduce1", packs[2], weights[2], w_reduce, half, half)
+        for number in range(2):
+            flow.pack(f"expand{number}", packs[1], weights[1], w_expand, number * half, half)
+        flow.start("norm", ins[3], middle_ref)
+        flow.start("norm", ins[4], vec_ref)
+        flow.start("norm", ins[0], grad_ref)
+        flow.pack("out", packs[0], weights[0], w_out, 3 * TILE, TILE)
+
+        flow.wait("low")
+        for tile in range(4):
+            if tile % 2 == 0:
+                flow.wait(f"reduce{tile // 2}")
+            product = lax.dot_general(low_ref[...], w_reduce[:, columns(tile)], NT, preferred_element_type=f32)
+            if tile == 0:
+                flow.wait("slope")
+            for part in range(SMALL):
+                at = block_at(place, part, 4 * BLOCK, tile * BLOCK)
+                piece = product[:, part * BLOCK : (part + 1) * BLOCK] * slope_ref[:, at].astype(f32)
+                hidden[:, at] = piece.astype(bf16)
+                bias[:, at] = jnp.sum(piece, axis=0, keepdims=True)
+        flow.start("hidden", hidden.at[:, columns(0, 2)], outs[0])
+        flow.start("hidden", hidden.at[:, columns(2, 2)], outs[1])
+        flow.start("bias", bias, outs[3])
+        for tile in range(4):
+            if tile % 2 == 0:
+                flow.wait(f"expand{tile // 2}")
             product = lax.dot_general(
-                grad_low_ref[...], join(ins[5 : 5 + one]), NT, preferred_element_type=f32
+                hidden[:, columns(tile)], w_expand[:, columns(tile)], NT, preferred_element_type=f32
             )
-            for part in range(SMALL):
-                at = block_at(place, part, 4 * BLOCK, step * BLOCK)
-                piece = product[:, part * BLOCK : (part + 1) * BLOCK] * slope_ref[:, at].astype(f32)
-                bias_ref[:, at] = jnp.sum(piece, axis=0, keepdims=True)
-                half = (place[0] ^ part) // 4
-                within = pl.ds(pl.multiple_of(((place[0] ^ part) % 4) * 4 * BLOCK + step * BLOCK, BLOCK), BLOCK)
-                for number in range(2):
-
-                    @pl.when(half == number)
-                    def _(number=number, piece=piece, within=within):
-                        hidden_refs[number][:, within] = piece.astype(bf16)
-
-        @pl.when((step >= 4) & (step < 8))
-        def _():
-            for number in range(4):
-
-                @pl.when(step == 4 + number)
-                def _(number=number):
-                    start = (number % 2) * TILE
-                    product = lax.dot_general(
-                        hidden_refs[number // 2][:, start : start + TILE],
-                        join(ins[5 + one : 5 + 2 * one]),
-                        NT,
-                        preferred_element_type=f32,
-                    )
-                    total[...] = product if number == 0 else total[...] + product
-
-            @pl.when(step == 7)
-            def _():
-                for part in range(SMALL):
-                    ordered[:, block_at(place, part)] = total[:, part * BLOCK : (part + 1) * BLOCK]
-                back, gain_grad, shift_grad, scale_grad = modulated_back(
-                    middle_ref[...], vec_ref, 3, ordered[...]
-                )
-                upstream = grad_ref[...].astype(f32)
-                middle_grad = upstream + back
-                middle_grad_ref[...] = middle_grad
-                low_ref[...] = middle_grad.astype(bf16)
-                sums_ref[0:1, :] = gain_grad
-                sums_ref[1:2, :] = shift_grad
-                sums_ref[2:3, :] = scale_grad
-                sums_ref[3:4, :] = jnp.sum(middle_grad, axis=0, keepdims=True)
-                sums_ref[4:5, :] = jnp.sum(upstream, axis=0, keepdims=True)
-
-        @pl.when(step == 8)
-        def _():
-            product = lax.dot_general(
-                low_ref[...], join(ins[5 + 2 * one :]), NT, preferred_element_type=f32
-            ).astype(bf16)
-            for part in range(SMALL):
-                mixture_ref[:, block_at(place, part)] = product[:, part * BLOCK : (part + 1) * BLOCK]
-
-    return run(
+            total[...] = product if tile == 0 else total[...] + product
+        for part in range(SMALL):
+            ordered[:, block_at(place, part)] = total[:, part * BLOCK : (part + 1) * BLOCK]
+        flow.wait("norm")
+        back, gain_grad, shift_grad, scale_grad = modulated_back(middle_ref[...], vec_ref, 3, ordered[...])
+        upstream = grad_ref[...].astype(f32)
+        middle_grad[...] = upstream + back
+        middle_low[...] = middle_grad[...].astype(bf16)
+        flow.start("middle", middle_low, outs[2])
+        flow.start("middle", middle_grad, outs[4])
+        flow.wait("out")
+        product = lax.dot_general(middle_low[...], w_out[...], NT, preferred_element_type=f32).astype(bf16)
+        for part in range(SMALL):
+            mixture[:, block_at(place, part)] = product[:, part * BLOCK : (part + 1) * BLOCK]
+        flow.start("mixture", mixture, outs[6])
+        sums[0:1, :] = gain_grad
+        sums[1:2, :] = shift_grad
+        sums[2:3, :] = scale_grad
+        sums[3:4, :] = jnp.sum(middle_grad[...], axis=0, keepdims=True)
+        sums[4:5, :] = jnp.sum(upstream, axis=0, keepdims=True)
+        sums[5:8, :] = jnp.zeros((3, width), f32)
+        flow.start("sums", sums, outs[5])
+        flow.drain()
+
+    rows = SMALL * BLOCK
+    return run_flow(
         body,
-        9,
+        [grad, low, slope, middle, vec],
+        packs,
         [
-            (grad, None),
-            (grad_low[0], pl.BlockSpec((tokens, TILE), lambda i, s: (0, grad_low[1]))),
-            (slope, None),
-            (middle, None),
-            (vec, None),
-        ]
-        + pack_inputs(reduce_pack, lambda i: jnp.minimum(i, 3))
-        + pack_inputs(expand_pack, lambda i: jnp.clip(i - 4, 0, 3))
-        + pack_inputs(attention_pack, lambda i: 3),
+            ((tokens, half), bf16),
+            ((tokens, half), bf16),
+            (grad.shape, bf16),
+            ((1, hidden_width), f32),
+            (grad.shape, f32),
+            ((8, width), f32),
+            (grad.shape, bf16),
+        ],
         [
-            ((tokens, 2 * TILE), bf16, None),
-            ((tokens, 2 * TILE), bf16, None),
-            (grad.shape, bf16, None),
-            ((1, columns), f32, None),
-            (grad.shape, f32, None),
-            ((8, width), f32, None),
-            (grad.shape, bf16, None),
+            (grad.shape, grad.dtype),
+            (grad.shape, bf16),
+            (slope.shape, bf16),
+            (middle.shape, f32),
+            (vec.shape, f32),
+            ((rows, TILE), bf16),
+            ((rows, hidden_width), bf16),
+            ((rows, hidden_width), bf16),
+            (slope.shape, bf16),
+            ((1, hidden_width), f32),
+            (grad.shape, f32),
+            (grad.shape, bf16),
+            ((8, width), f32),
+            (grad.shape, bf16),
+            (grad.shape, f32),
+            (grad.shape, f32),
         ],
-        [pltpu.VMEM((tokens, width), f32), pltpu.VMEM((tokens, width), f32)],
-        deps=deps,
-        cost=18,
+        5 + 5 * len(packs[0]) + 7,
+        deps,
+        12,
     )
 
 
 def first_back(query_grad, key_parts, pack, stream, middle_grad, vec, deps=()):
     tokens, width = stream.shape
-    kept, arrived, far = key_parts
-
-    def body(place, ins, outs, scratch):
-        step = pl.program_id(0)
-        weights = join(ins[7:])
-
-        @pl.when(step == 0)
-        def _():
-            outs[1][:, :TILE] = ins[0][...]
-            scratch[0][...] = lax.dot_general(ins[0][...], weights, NT, preferred_element_type=f32)
-
-        @pl.when(step > 0)
-        def _():
-            total = ins[1][...].astype(f32) + ins[2][...].astype(f32) + ins[3][...].astype(f32)
-            rounded = total.astype(bf16)
-            outs[3][...] = rounded
-            scratch[0][...] += lax.dot_general(rounded, weights, NT, preferred_element_type=f32)
-
-        @pl.when(step == 2)
-        def _():
-            for part in range(SMALL):
-                scratch[1][:, block_at(place, part)] = scratch[0][:, part * BLOCK : (part + 1) * BLOCK]
-            back, gain_grad, shift_grad, scale_grad = modulated_back(
-                ins[4][...].astype(f32), ins[6], 0, scratch[1][...]
-            )
-            result = ins[5][...] + back
-            outs[0][...] = result
-            outs[1][:, TILE:] = result.astype(bf16)
-            outs[2][0:1, :] = gain_grad
-            outs[2][1:2, :] = shift_grad
-            outs[2][2:3, :] = scale_grad
-
-    tile = pl.BlockSpec((tokens, TILE), lambda i, s: (0, jnp.maximum(i - 1, 0)))
-    return run(
+    shape = key_parts[0].shape
+
+    def body(place, flow, ins, weights, outs, scratch):
+        (lower, near_ref, leave_ref, far_ref, stream_ref, middle_ref, vec_ref, w_in) = scratch[:8]
+        (key_ref, grad_ref, sums, total, ordered) = scratch[8:]
+        flow.start("query", ins[0], lower.at[:, columns(0)])
+        flow.pack("w0", pack, weights[0], w_in, 0, TILE)
+        for source, target in zip(ins[1:4], (near_ref, leave_ref, far_ref)):
+            flow.start("keys", source, target)
+        flow.pack("w1", pack, weights[0], w_in, TILE, 2 * TILE)
+        for source, target in zip(ins[4:7], (stream_ref, middle_ref, vec_ref)):
+            flow.start("norm", source, target)
+        flow.wait("query")
+        flow.wait("w0")
+        total[...] = lax.dot_general(lower[:, columns(0)], w_in[:, columns(0)], NT, preferred_element_type=f32)
+        flow.wait("keys")
+        key_ref[...] = (
+            near_ref[...].astype(f32) + leave_ref[...].astype(f32) + far_ref[...].astype(f32)
+        ).astype(bf16)
+        flow.start("key", key_ref, outs[3])
+        flow.wait("w1")
+        total[...] += lax.dot_general(key_ref[...], w_in[:, columns(1, 2)], NT, preferred_element_type=f32)
+        for part in range(SMALL):
+            ordered[:, block_at(place, part)] = total[:, part * BLOCK : (part + 1) * BLOCK]
+        flow.wait("norm")
+        back, gain_grad, shift_grad, scale_grad = modulated_back(
+            stream_ref[...].astype(f32), vec_ref, 0, ordered[...]
+        )
+        grad_ref[...] = middle_ref[...] + back
+        lower[:, columns(1)] = grad_ref[...].astype(bf16)
+        flow.start("lower", lower, outs[1])
+        flow.start("grad", grad_ref, outs[0])
+        sums[0:1, :] = gain_grad
+        sums[1:2, :] = shift_grad
+        sums[2:3, :] = scale_grad
+        sums[3:8, :] = jnp.zeros((5, width), f32)
+        flow.start("sums", sums, outs[2])
+        flow.drain()
+
+    rows = SMALL * BLOCK
+    return run_flow(
         body,
-        3,
+        [query_grad, *key_parts, stream, middle_grad, vec],
+        [pack],
+        [(stream.shape, f32), ((tokens, 2 * TILE), bf16), ((8, width), f32), (shape, bf16)],
         [
-            (query_grad, None),
-            (kept, tile),
-            (arrived, tile),
-            (far, tile),
-            (stream, None),
-            (middle_grad, None),
-            (vec, None),
-        ]
-        + pack_inputs(pack, lambda i: i),
-        [
-            (stream.shape, f32, None),
-            ((tokens, 2 * TILE), bf16, None),
-            ((8, width), f32, None),
-            (far.shape, bf16, tile),
+            ((tokens, 2 * TILE), bf16),
+            (shape, bf16),
+            (shape, bf16),
+            (shape, bf16),
+            (stream.shape, stream.dtype),
+            (stream.shape, f32),
+            (vec.shape, f32),
+            ((rows, 3 * TILE), bf16),
+            (shape, bf16),
+            (stream.shape, f32),
+            ((8, width), f32),
+            (stream.shape, f32),
+            (stream.shape, f32),
         ],
-        [pltpu.VMEM((tokens, width), f32), pltpu.VMEM((tokens, width), f32)],
-        deps=deps,
-        cost=10,
+        7 + 2 * len(pack) + 4,
+        deps,
+        6,
     )
 
 
@@ -785,167 +858,181 @@
 
 class Group:
     def __init__(self, arrays, left_of, right_of):
-        self.left_of, self.right_of = left_of, right_of
-        self.inputs = [(side, spec) for pair, spec in arrays for side in pair]
+        self.arrays, self.left_of, self.right_of = arrays, left_of, right_of
+
+    def left(self, place, refs, tile):
+        array, stride, offset = self.left_of[tile]
+        return jnp.concatenate(
+            [refs[array][:, block_at(place, mask, stride, offset)] for mask in ORDERS[tile // 2]], axis=1
+        )
 
     def product(self, place, refs, tile):
-        array, stride, offset = self.left_of[tile]
-        left = [
-            jnp.concatenate(
-                [refs[2 * array + side][:, block_at(place, mask, stride, offset)] for mask in ORDERS[tile // 2]],
-                axis=1,
-            )
-            for side in range(2)
-        ]
-        array = self.right_of[tile]
+        array, start = self.right_of[tile]
         return lax.dot_general(
-            jnp.concatenate(left, axis=0), join(refs[2 * array : 2 * array + 2]), TN, preferred_element_type=f32
+            self.left(place, refs, tile), refs[array][:, start : start + TILE], TN, preferred_element_type=f32
         )
 
 
-def part_of(rows, first):
-    at = first if callable(first) else (lambda i: first)
-    return pl.BlockSpec((rows, TILE), lambda i, s: (0, at(i)))
-
-
 def reduce_group(kept, lower, block):
-    rows = kept[0].shape[0]
     return Group(
-        [(kept, pl.BlockSpec((rows, 4 * TILE), lambda i, s: (0, 0))), (lower, part_of(rows, block))],
-        [(0, 4 * BLOCK, u * BLOCK) for u in range(4)],
-        [1] * 4,
+        [(lower, block * TILE, TILE), (kept, ACTIVE, 4 * TILE)],
+        [(1, 4 * BLOCK, u * BLOCK) for u in range(4)],
+        [(0, 0)] * 4,
     )
 
 
 def expand_group(kept, back):
-    rows = kept[0].shape[0]
+    return Group(
+        [(kept, SECOND, TILE), (back[0], 0, 2 * TILE), (back[1], 0, 2 * TILE)],
+        [(0, BLOCK, 0)] * 4,
+        [(1, 0), (1, TILE), (2, 0), (2, TILE)],
+    )
+
+
+def attention_group(kept, back, lower, key_grad):
     return Group(
         [
-            (kept, part_of(rows, SECOND // TILE)),
-            (back[0], part_of(rows, lambda i: jnp.minimum(i, 1))),
-            (back[1], part_of(rows, lambda i: jnp.maximum(i - 2, 0))),
+            (kept, NORMED, TILE),
+            (lower, 0, TILE),
+            (key_grad, 0, 2 * TILE),
+            (kept, MIXTURE, TILE),
+            (back[2], 0, TILE),
         ],
-        [(0, BLOCK, 0)] * 4,
-        [1, 1, 2, 2],
-    )
-
-
-def attention_group(kept, back, lower, key_grad):
-    rows = kept[0].shape[0]
-    return Group(
-        [
-            (kept, part_of(rows, NORMED // TILE)),
-            (kept, part_of(rows, MIXTURE // TILE)),
-            (lower, part_of(rows, 0)),
-            (key_grad, part_of(rows, lambda i: jnp.clip(i - 1, 0, 1))),
-            (back[2], part_of(rows, 0)),
-        ],
-        [(0, BLOCK, 0)] * 3 + [(1, BLOCK, 0)],
-        [2, 3, 3, 4],
+        [(0, BLOCK, 0)] * 3 + [(3, BLOCK, 0)],
+        [(1, 0), (2, 0), (2, TILE), (4, 0)],
     )
 
 
 def wide(value):
     return value.astype(f32)
-
-
-def half_spec(rows, half):
-    return pl.BlockSpec((rows, TILE), lambda i, s: (0, jnp.maximum(i - 2, 0) if half else jnp.minimum(i, 1)))
-
-
-def both_spec(rows):
-    return pl.BlockSpec((1, rows, TILE), lambda i, s: (i // 2, 0, i % 2))
 
 
 class Reduction:
     def __init__(self, group, stacked=False):
         self.group, self.stacked = group, stacked
 
-
-def advance(seconds=(), thirds=(), fourths=(), joint=(), deps=()):
-    inputs, outputs, works = [], [], []
-    quarter, eighth = (2 * BLOCK, 2 * TILE), (BLOCK, 2 * TILE)
+    def scatter(self, *tokens):
+        piece = after(self.piece, *tokens) if tokens else self.piece
+        self.share = lax.psum_scatter(piece, "seq", scatter_dimension=0, tiled=True)
+
+
+def advance(seconds=(), thirds=(), fourths=(), joint=(), deps=(), later=False):
+    arrays, outputs, scratch, loads, works = [], [], [], [], []
+    half = 2 * TILE
+    quarter, eighth = (2 * BLOCK, half), (BLOCK, half)
+
+    def bring(array, shape, source, target=lambda ref: ref, key=None):
+        number = len(loads)
+        slot = len(scratch) if shape is not None else len(scratch) - 1
+        if shape is not None:
+            scratch.append((shape, array.dtype))
+        loads.append((len(arrays), slot, source, target, number if key is None else key))
+        arrays.append(array)
+        return slot, number
+
+    def make(shape):
+        outputs.append((shape, bf16))
+        scratch.append((shape, bf16))
+        return len(outputs) - 1, len(scratch) - 1
+
     for one in seconds:
-        group, base, out = one.group, len(inputs), len(outputs)
-        inputs += group.inputs
-        outputs += [
-            (quarter, bf16, half_spec(2 * BLOCK, 0)),
-            (quarter, bf16, half_spec(2 * BLOCK, 1)),
-            ((2,) + quarter, bf16, both_spec(2 * BLOCK)),
-        ]
-
-        def product(place, ins, outs, tile, group=group, base=base, out=out):
-            total = group.product(place, ins[base : base + len(group.inputs)], tile)
-            outs[out + tile // 2][...] = total[: 2 * BLOCK].astype(bf16)
-            outs[out + 2][0] = total[2 * BLOCK :].astype(bf16)
+        group, slots, keys = one.group, [], []
+        for pair, first, width in group.arrays:
+            tokens = pair[0].shape[0]
+            for side, array in enumerate(pair):
+                slot, key = bring(
+                    array,
+                    (2 * tokens, width) if side == 0 else None,
+                    lambda ref, first=first, width=width: ref.at[:, pl.ds(first, width)],
+                    lambda ref, side=side, tokens=tokens: ref.at[pl.ds(side * tokens, tokens), :],
+                )
+                keys.append(key)
+            slots.append(slot)
+        made = [make(quarter), make(quarter), make((2,) + quarter)]
+
+        def product(place, flow, held, outs, group=group, slots=slots, keys=keys, made=made):
+            refs = [held[slot] for slot in slots]
+            waited = 0
+            stay = made[2]
+            for tile in range(4):
+                needed = 2 * (max(group.left_of[tile][0], group.right_of[tile][0]) + 1)
+                while waited < needed:
+                    flow.wait(keys[waited])
+                    waited += 1
+                total = group.product(place, refs, tile)
+                leave = made[tile // 2]
+                held[leave[1]][:, columns(tile % 2)] = total[: 2 * BLOCK].astype(bf16)
+                held[stay[1]][tile // 2, :, columns(tile % 2)] = total[2 * BLOCK :].astype(bf16)
+                if tile % 2:
+                    flow.start("out", held[leave[1]], outs[leave[0]])
+                    flow.start("out", held[stay[1]].at[tile // 2], outs[stay[0]].at[tile // 2])
 
         works.append(product)
     for one in thirds:
-        base, out = len(inputs), len(outputs)
-        inputs += [
-            (one.staying, both_spec(2 * BLOCK)),
-            (one.from_x, half_spec(2 * BLOCK, 0)),
-            (one.from_y, half_spec(2 * BLOCK, 1)),
+        loaded = [
+            bring(one.staying, (2,) + quarter, lambda ref: ref),
+            bring(one.from_x, quarter, lambda ref: ref),
+            bring(one.from_y, quarter, lambda ref: ref),
         ]
-        outputs += [
-            (eighth, bf16, half_spec(BLOCK, 0)),
-            (eighth, bf16, half_spec(BLOCK, 1)),
-            ((2,) + eighth, bf16, both_spec(BLOCK)),
+        made = [make(eighth), make(eighth), make((2,) + eighth)]
+
+        def add(place, flow, held, outs, loaded=loaded, made=made):
+            flow.wait(loaded[0][1])
+            for number in range(2):
+                flow.wait(loaded[1 + number][1])
+                total = (wide(held[loaded[0][0]][number]) + wide(held[loaded[1 + number][0]][...])).astype(bf16)
+                held[made[number][1]][...] = total[:BLOCK]
+                held[made[2][1]][number] = total[BLOCK:]
+                flow.start("out", held[made[number][1]], outs[made[number][0]])
+                flow.start("out", held[made[2][1]].at[number], outs[made[2][0]].at[number])
+
+        works.append(add)
+    sums = [[one] for one in fourths] + ([list(joint)] if joint else [])
+    for members in sums:
+        alone = len(members) == 1
+        stacked = alone and members[0].stacked
+        loaded = [
+            [
+                bring(one.kept, (2,) + eighth, lambda ref: ref),
+                bring(one.second_y, eighth, lambda ref: ref),
+                bring(one.second_x, eighth, lambda ref: ref),
+            ]
+            for one in members
         ]
-
-        def add(place, ins, outs, tile, base=base, out=out):
-            total = (wide(ins[base][0]) + wide(ins[base + 1 + tile // 2][...])).astype(bf16)
-            outs[out + tile // 2][...] = total[:BLOCK]
-            outs[out + 2][0] = total[BLOCK:]
-
-        works.append(add)
-    for one in fourths:
-        base, out = len(inputs), len(outputs)
-        inputs += [
-            (one.kept, both_spec(BLOCK)),
-            (one.second_y, half_spec(BLOCK, 0)),
-            (one.second_x, half_spec(BLOCK, 1)),
-        ]
-        shape = (4 * BLOCK, TILE) if one.stacked else (BLOCK, 4 * TILE)
-        spec = pl.BlockSpec((BLOCK, TILE), lambda i, s, stacked=one.stacked: (i, 0) if stacked else (0, i))
-        outputs.append((shape, bf16, spec))
-
-        def finish(place, ins, outs, tile, base=base, out=out):
-            outs[out][...] = (wide(ins[base][0]) + wide(ins[base + 1 + tile // 2][...])).astype(bf16)
+        made = make((4 * BLOCK, TILE) if stacked else (len(members) * BLOCK, 4 * TILE))
+
+        def finish(place, flow, held, outs, loaded=loaded, made=made, stacked=stacked, alone=alone):
+            result, share = held[made[1]], BLOCK // 4
+            for number, (kept, *arrived) in enumerate(loaded):
+                flow.wait(kept[1])
+                for side in range(2):
+                    flow.wait(arrived[side][1])
+                    total = (wide(held[kept[0]][side]) + wide(held[arrived[side][0]][...])).astype(bf16)
+                    if stacked:
+                        for tile in range(2):
+                            at = (2 * side + tile) * BLOCK
+                            result[at : at + BLOCK, :] = total[:, tile * TILE : (tile + 1) * TILE]
+                    elif alone:
+                        result[:, columns(2 * side, 2)] = total
+                    else:
+                        for plane in range(4):
+                            start = (plane * len(loaded) + number) * share
+                            result[start : start + share, columns(2 * side, 2)] = total[
+                                plane * share : (plane + 1) * share
+                            ]
+            flow.start("out", result, outs[made[0]])
 
         works.append(finish)
 
-    if joint:
-        base, out, share = len(inputs), len(outputs), BLOCK // 4
-        for one in joint:
-            inputs += [
-                (one.kept, both_spec(BLOCK)),
-                (one.second_y, half_spec(BLOCK, 0)),
-                (one.second_x, half_spec(BLOCK, 1)),
-            ]
-        rows = len(joint) * BLOCK
-        outputs.append(((rows, 4 * TILE), bf16, pl.BlockSpec((rows, TILE), lambda i, s: (0, i))))
-
-        def interleave(place, ins, outs, tile):
-            for number in range(len(joint)):
-                at = base + 3 * number
-                total = (wide(ins[at][0]) + wide(ins[at + 1 + tile // 2][...])).astype(bf16)
-                for plane in range(4):
-                    start = (plane * len(joint) + number) * share
-                    outs[out][start : start + share, :] = total[plane * share : (plane + 1) * share]
-
-        works.append(interleave)
-
-    def body(place, ins, outs, _):
-        for tile in range(4):
-
-            @pl.when(pl.program_id(0) == tile)
-            def _(tile=tile):
-                for work in works:
-                    work(place, ins, outs, tile)
-
-    results = list(run(body, 4, inputs, outputs, deps=deps, cost=7 if seconds else 5))
-    token = results[0]
+    def body(place, flow, ins, _, outs, held):
+        for number, slot, source, target, key in loads:
+            flow.start(key, source(ins[number]), target(held[slot]))
+        for work in works:
+            work(place, flow, held, outs)
+        flow.drain()
+
+    results = list(run_flow(body, arrays, [], outputs, scratch, len(loads) + 2 * len(outputs) + 2, deps, 7 if seconds else 4))
+    token = results[-1] if joint and len(works) == 1 else results[0]
     for one in seconds:
         along_x, along_y, one.staying = results[:3]
         results = results[3:]
@@ -955,10 +1042,13 @@
         results = results[3:]
         one.second_y, one.second_x = swap(along_y, 4), swap(along_x, 2)
     for one in fourths:
-        one.share = lax.psum_scatter(results[0], "seq", scatter_dimension=0, tiled=True)
+        one.piece = results[0]
         results = results[1:]
+        if not later:
+            one.scatter()
     if joint:
         both = lax.psum_scatter(results[0], "seq", scatter_dimension=0, tiled=True)
+        share = BLOCK // 4
         for number, one in enumerate(joint):
             one.share = both[number * share : (number + 1) * share]
     return token
@@ -1237,6 +1327,13 @@
     return small, changes + arrived if add else jnp.concatenate([changes, arrived], axis=0)
 
 
+def relay(array, back):
+    moves = layout_moves(back)
+    moved = lax.ppermute(array, ("dp", "seq"), [(a, b) for a, b in moves if a != b])
+    core, plane = lax.axis_index("dp") % 2, lax.axis_index("seq")
+    return moved, lambda moved: jnp.where(plane == 3 * core, array, moved)
+
+
 def fast_device(
     inputs,
     noise_buckets,
@@ -1263,12 +1360,13 @@
     raw_of = {"attention": (attention_in, attention_out), "expand": (expand_weight,), "reduce": (reduce_weight,)}
     members = (first_gain, first_shift, attention_bias, second_gain, second_shift, reduce_bias, expand_bias)
     gather = Gather(kinds, [raw_of[kind] for kind, _ in kinds], time_table, members, noise_buckets)
-    moved = lax.ppermute(inputs[0], ("dp", "seq"), layout_moves(False))
-    grad_low = lax.ppermute(cotangent[0], ("dp", "seq"), layout_moves(False))
-    lower = (grad_low, swap(grad_low, 1))
-    token = gather.others((moved, gather.first))
-    gather.step((moved, lower[1], token))
-    gather.step()
+    moved, finish = relay(inputs[0], False)
+    moved = finish(moved)
+    token = gather.others((gather.first,))
+    token = gather.step((moved, token))
+    grad_low, finish = relay(after(cotangent[0], token), False)
+    grad_low = finish(grad_low)
+    gather.step((grad_low,))
     vectors, buckets = vectors_of(gather.extras(), members, layers, time_table.shape[1], width)
 
     saved = []
@@ -1299,10 +1397,9 @@
             token = gather.step((following,), following)
         saved.append([stream, own_kept, queries, chunks, tops, middle, slope, packs])
         stream, normed = result, following
-    outputs = lax.ppermute(following, ("dp", "seq"), layout_moves(True))
 
     grad = grad_low
-    block = 0
+    lower, block = (grad_low, swap(after(grad_low, following), 1)), 0
     sums = [None] * layers
     shares = {}
     for entry in reversed(saved):
@@ -1312,70 +1409,73 @@
         vec, bias = vectors[layer]
         stream, kept, queries, chunks, tops, middle, slope, packs = saved[layer]
         of_reduce = Reduction(reduce_group(kept, lower, block), True)
-        deps = (token,) if above is not None else ()
+        deps = ()
+        if above is not None:
+            upper_reduce, upper_expand, of_attention = above
+            deps = (advance([of_attention], deps=(token,)),)
         *own_back, expand_bias_grad, middle_grad, late_sums, mixture_grad = feed_forward_back(
             grad, (lower[0], block), slope, middle, packs, vec, deps
         )
-        back = [(own, swap(own, 1)) for own in own_back]
-        deps = tuple(other for _, other in back)
         if above is None:
+            back = [(own, swap(own, 1)) for own in own_back]
             token = advance([of_reduce], deps=(own_back[0], saved[0][1][1]))
+            deps = (token,) + tuple(other for _, other in back)
+            moved_result, finish = relay(after(result, token), True)
+            outputs = finish(lax.optimization_barrier(moved_result)).astype(bf16)
         else:
-            upper_reduce, upper_expand, of_attention = above
-            token = advance([of_attention], deps=(own_back[0], outputs, upper_reduce.share))
-            token = advance(fourths=[upper_expand], deps=(token,))
-            token = advance([of_reduce], deps=(token,) + deps)
-            deps = ()
+            deps = (upper_expand.second_x, upper_expand.second_y)
         query_grad, near, near_leave, far, far_leave = attend_fast_back(
-            queries, chunks, kept[0], mixture_grad, tops, (token,) + deps
+            queries, chunks, kept[0], mixture_grad, tops, deps
         )
         far_leave, near_leave = swap(far_leave, 1), swap(near_leave, 1)
-        of_expand = Reduction(expand_group(kept, back))
         token = query_grad
         if above is None:
+            of_expand = Reduction(expand_group(kept, back))
             token = advance([of_expand], deps=(token,))
-            token = advance(thirds=[of_reduce], deps=(token,))
+            token = advance(thirds=[of_reduce], deps=(token, moved_result))
         else:
-            token = advance(thirds=[of_attention], deps=(token, upper_expand.share))
+            token = advance(thirds=[of_attention], deps=(token, upper_reduce.share))
         far, near_leave = after(far, token, near_leave), after(near_leave, token)
         far = (wide(far) + wide(far_leave)).astype(bf16)
         far = (far, swap_seq(far, 1))
         token = far[0]
         if above is not None:
-            token = advance(thirds=[of_reduce], deps=(token,))
-            token = advance([of_expand], deps=(token, of_attention.second_x, of_attention.second_y))
-        deps = (token,)
-        if above is not None:
-            deps = (token, of_reduce.second_x, of_reduce.second_y)
+            back = [(own, swap(after(own, token), 1)) for own in own_back[:2]]
+            of_expand = Reduction(expand_group(kept, back))
+            token = advance([of_reduce], deps=(token, back[0][1], back[1][1], of_attention.second_x, of_attention.second_y))
+            token = advance([of_expand], deps=(token,))
         grad, own_lower, early_sums, key_grad = first_back(
-            query_grad, (near, near_leave, far[1]), packs[0], stream, middle_grad, vec, deps
+            query_grad, (near, near_leave, far[1]), packs[0], stream, middle_grad, vec, (token,)
         )
         lower, block = (own_lower, swap(own_lower, 1)), 1
         key_grad = (key_grad, swap(key_grad, 1))
-        deps = (own_lower,)
         if above is None:
-            deps = (own_lower,)
-        if above is None:
-            token = advance(thirds=[of_expand], fourths=[of_reduce], deps=deps)
-        if above is not None:
+            token = advance(thirds=[of_expand], fourths=[of_reduce], deps=(own_lower,))
+        else:
+            back.append((own_back[2], swap(after(own_back[2], own_lower), 1)))
+            token = own_lower
             shares[("attention", layer + 1)] = of_attention
             shares[("expand", layer + 1)] = upper_expand
-        upper_attention = of_attention if above is not None else None
+            upper_attention = of_attention
         of_attention = Reduction(attention_group(kept, back, lower, key_grad))
         shares[("reduce", layer)] = of_reduce
         above = (of_reduce, of_expand, of_attention)
         sums[layer] = (early_sums, late_sums, expand_bias_grad)
 
     of_reduce, of_expand, of_last = above
+    token = advance(thirds=[of_reduce], fourths=[upper_expand], deps=(token,))
+    token = advance([of_last], fourths=[upper_attention], deps=(token,), later=True)
+    token = advance(fourths=[of_reduce], deps=(token,))
+    upper_attention.scatter(token)
+    token = advance(thirds=[of_expand], deps=(token,))
+    token = advance(thirds=[of_last], deps=(token, upper_expand.share, upper_attention.share))
     small, changes = small_and_changes(sums)
+    small, changes = after(small, token), after(changes, token)
     small, changes = cross(small, changes, 4, plane % 2, lambda a: swap_seq(a, 1), True)
     small, changes = cross(small, changes, 3, plane // 2, lambda a: swap_seq(a, 2), False)
-    token = advance(thirds=[of_expand], deps=(own_lower, small, changes))
-    token = advance([of_last], deps=(token,))
-    token = advance(fourths=[upper_attention, of_reduce], deps=(token,))
-    token = advance(thirds=[of_last], deps=(token, upper_attention.share))
-    input_grad = lax.ppermute(after(own_lower[:, TILE:], token), ("dp", "seq"), layout_moves(True)).astype(f32)
-    token = advance(joint=(of_expand, of_last), deps=(token,))
+    token = advance(joint=(of_expand, of_last), deps=(token, small, changes))
+    input_grad, finish = relay(after(own_lower[:, TILE:], token), True)
+    input_grad = finish(input_grad).astype(f32)
     shares[("attention", 0)] = of_last
     shares[("expand", 0)] = of_expand
     shares = {name: reduction.share.astype(f32) for name, reduction in shares.items()}

time: 733 us -> 672 us (0.917)
  Pallas kernels: 330 us -> 279 us
  starting transfers between devices: 101 us -> 85 us
    pallas_call x43 -> x18, Pallas kernels: 330 us -> 119 us  [run(): pl.pallas_call(kernel, out_shape=shapes, grid_spec=pltpu.PrefetchScalarGr...]
    pallas_call x0 -> x24, Pallas kernels: none -> 160 us  [run_flow(): pl.pallas_call(kernel, out_shape=[jax.ShapeDtypeStruct(shape, kind) for s...]
    ppermute x78, waiting for transfers between devices: 144 us -> 162 us  [swap(): return lax.ppermute(array, 'dp', [(i, i ^ bit) for i in range(count)])]
    ppermute x6, starting transfers between devices: 25.9 us -> 11.5 us  [swap_seq(): return lax.ppermute(array, 'seq', [(i, i ^ bit) for i in range(count)])]
    ppermute x4, starting transfers between devices: 17.8 us -> 3.53 us  [relay(): lax.ppermute(array, ('dp', 'seq'), [(a, b) for a, b in moves if a != b])]
    ppermute x78, starting transfers between devices: 56.6 us -> 69.4 us  [swap(): return lax.ppermute(array, 'dp', [(i, i ^ bit) for i in range(count)])]
    unnamed x73 -> x82, local copies, waits for them, and re-layouts: 14.7 us -> 11.4 us
  transfers between devices with their start and end apart: 93 -> 93, of which waited for: 36 -> 40; matrix products, arithmetic and copies ran while one was open for 2% -> 3% of each run, Pallas kernels for 37% -> 38%
where the time goes in v3:
time: 672 us; the launch traced here: 661 us
  Pallas kernels  279 us (42%)
  waiting for transfers between devices  242 us (36%)
  starting transfers between devices  85 us (13%)
  other arithmetic  24 us (4%)
  between operations  15.7 us (2%)
  local copies, waits for them, and re-layouts  15.2 us (2%)
    ppermute x78, waiting for transfers between devices, swap(): return lax.ppermute(array, 'dp', [(i, i ^ bit) for i in range(count)])  162 us
    pallas_call x24, Pallas kernels, run_flow(): pl.pallas_call(kernel, out_shape=[jax.ShapeDtypeStruct(shape, kind) for s...  160 us
    pallas_call x18, Pallas kernels, run(): pl.pallas_call(kernel, out_shape=shapes, grid_spec=pltpu.PrefetchScalarGr...  119 us
    ppermute x78, starting transfers between devices, swap(): return lax.ppermute(array, 'dp', [(i, i ^ bit) for i in range(count)])  69.4 us
    ppermute x6, waiting for transfers between devices, swap_seq(): return lax.ppermute(array, 'seq', [(i, i ^ bit) for i in range(count)])  46.4 us
    reduce_scatter x1, waiting for transfers between devices, advance(): both = lax.psum_scatter(results[0], 'seq', scatter_dimension=0, tiled=True)  33.7 us
  transfers between devices with their start and end apart: 93, of which 40 were waited for; matrix products, arithmetic and copies ran while one was open for 3% of the time, Pallas kernels for 38%

profile of v3, /device:TPU:0, one launch (start us, length us, event | category | flops | bytes accessed | tf_op | source)
XLA Modules:
  0.0 661.1 jit_solution(4934546538830682201)
XLA Ops:
  9.0 3.8 shard_map.254.refs_6_.refs_0_.refs_1_.refs_5_.refs_7_
  12.7 3.0 collective-permute-start.3
  18.6 6.1 shard_map.255.refs_0_.refs_2_.refs_16_.refs_26_.refs_1_.refs_6_.refs_5_.refs_15_.refs_25_.refs_7_
  24.8 4.3 shard_map.256
  31.0 13.7 %collective-permute-done.3.refs_1_.refs_4_.refs_5_.refs_10_.refs_9_.refs_11_ = bf16[160,4096]{1,0:T(8,128)(2,1)S(1)} collective-permute-done((bf16[160,4096]{1,0:T(8,128)(2,1)}, bf16[160,4096]{1,0:T(8,128)(2,1)S(1)}, u32[]{:S(2)}, u32[]{:S(2)}) %collective-permute-start.3) | collective-permute-done | bytes 1310752 | tf_op jit(solution)/shard_map/ppermute | solution.py:29
  46.3 5.0 shard_map.257
  54.8 3.4 collective-permute-start.4
  58.2 4.7 collective-permute-start.5
  65.8 23.6 %collective-permute-done.7.refs_1_.refs_7_.refs_8_.refs_13_.refs_20_.refs_12_.refs_19_.refs_14_ = bf16[208,4096]{1,0:T(8,128)(2,1)} collective-permute-done((bf16[208,4096]{1,0:T(8,128)(2,1)}, bf16[208,4096]{1,0:T(8,128)(2,1)}, u32[]{:S(2)}, u32[]{:S(2)}) %collective-permute-start.7) | collective-permute-done | bytes 1703968 | tf_op jit(solution)/shard_map/ppermute | solution.py:29
  91.0 3.0 shard_map.258
  99.3 4.2 collective-permute-done.1.refs_1_.refs_2_.refs_7_.refs_6_.refs_8_
  104.6 3.3 shard_map.259
  107.9 2.9 shard_map.260.refs_0_.refs_5_
  110.8 4.8 shard_map.261.refs_11_.refs_1_
  115.5 4.0 collective-permute-start.13
  119.5 3.9 shard_map.262.refs_1_.refs_7_.refs_0_
  123.4 4.3 shard_map.263
  130.5 3.2 collective-permute-done.16.refs_1_.refs_23_.refs_30_.refs_22_.refs_29_
  139.8 3.4 collective-permute-done.13.refs_3_
  143.7 4.3 shard_map.265
  148.2 15.0 %shard_map.266 = (bf16[256,1024]{1,0:T(8,128)(2,1)}, f32[8,8,256]{2,1,0:T(8,128)}) custom-call(s32[2]{0:T(128)} %pad_add_fusion.place, bf16[256,1024]{1,0:T(8,128)(2,1)} %shard_map.262.refs_1_.refs_7_.refs_0_, bf16[256,2048]{1,0:T(8,128)(2,1)} %shard_map.261.refs_11_.refs_1_, bf16[256,2048]{1,0:T(8,128)(2,1)} %collective-permute-done.12.refs_2_, ...), custom_call_target="tpu_custom_call" | custom-call | bytes 45000000 | tf_op jit(solution)/shard_map/pallas_call | solution.py:332
  163.2 9.3 %collective-permute-done.20.refs_1_.refs_33_.refs_5_.refs_10_.refs_9_.refs_11_.refs_32_ = bf16[192,4096]{1,0:T(8,128)(2,1)} collective-permute-done((bf16[192,4096]{1,0:T(8,128)(2,1)}, bf16[192,4096]{1,0:T(8,128)(2,1)}, u32[]{:S(2)}, u32[]{:S(2)}) %collective-permute-start.20) | collective-permute-done | bytes 1572896 | tf_op jit(solution)/shard_map/ppermute | solution.py:29
  174.0 2.9 shard_map.267
  179.1 4.5 shard_map.268
  183.6 12.9 %shard_map.269 = (f32[256,1024]{1,0:T(8,128)}, bf16[256,7168]{1,0:T(8,128)(2,1)}, bf16[256,4096]{1,0:T(8,128)(2,1)}, f32[256,1024]{1,0:T(8,128)}, bf16[256,1024]{1,0:T(8,128)(2,1)}) custom-call(s32[2]{0:T(128)} %pad_add_fusion.place, bf16[256,1024]{1,0:T(8,128)(2,1)} %get-tuple-element.173.refs_6_.refs_0_, ...), custom_call_target="tpu_custom_call" | custom-call | bytes 36000000 | tf_op jit(solution)/shard_map/pallas_call | solution.py:392
  196.5 17.0 %collective-permute-done.24.refs_1_.refs_8_.refs_13_.refs_20_.refs_12_.refs_19_.refs_14_ = bf16[192,4096]{1,0:T(8,128)(2,1)} collective-permute-done((bf16[192,4096]{1,0:T(8,128)(2,1)}, bf16[192,4096]{1,0:T(8,128)(2,1)}, u32[]{:S(2)}, u32[]{:S(2)}) %collective-permute-start.24) | collective-permute-done | bytes 1572896 | tf_op jit(solution)/shard_map/ppermute | solution.py:29
  214.5 2.9 shard_map.270
  220.1 4.8 shard_map.271.refs_11_.refs_1_
  224.9 4.6 collective-permute-start.28
  229.5 3.9 shard_map.272.refs_4_.refs_5_.refs_0_
  233.5 19.6 %collective-permute-done.28.refs_3_ = bf16[256,2048]{1,0:T(8,128)(2,1)S(1)} collective-permute-done((bf16[256,2048]{1,0:T(8,128)(2,1)}, bf16[256,2048]{1,0:T(8,128)(2,1)S(1)}, u32[]{:S(2)}, u32[]{:S(2)}) %collective-permute-start.28) | collective-permute-done | bytes 1048608 | tf_op jit(solution)/shard_map/ppermute | solution.py:34
  255.0 2.9 shard_map.273
  260.2 15.4 %shard_map.274 = (bf16[256,1024]{1,0:T(8,128)(2,1)}, f32[8,8,256]{2,1,0:T(8,128)}) custom-call(s32[2]{0:T(128)} %pad_add_fusion.place, bf16[256,1024]{1,0:T(8,128)(2,1)} %shard_map.272.refs_4_.refs_5_.refs_0_, bf16[256,2048]{1,0:T(8,128)(2,1)} %shard_map.271.refs_11_.refs_1_, bf16[256,2048]{1,0:T(8,128)(2,1)} %collective-permute-done.27.refs_2_, ...), custom_call_target="tpu_custom_call" | custom-call | bytes 45000000 | tf_op jit(solution)/shard_map/pallas_call | solution.py:332
  279.3 13.1 %shard_map.275 = (f32[256,1024]{1,0:T(8,128)}, bf16[256,7168]{1,0:T(8,128)(2,1)}, bf16[256,4096]{1,0:T(8,128)(2,1)}, f32[256,1024]{1,0:T(8,128)}, bf16[256,1024]{1,0:T(8,128)(2,1)}) custom-call(s32[2]{0:T(128)} %pad_add_fusion.place, bf16[256,1024]{1,0:T(8,128)(2,1)} %get-tuple-element.192.refs_0_.refs_36_, f32[256,1024]{1,0:T(8,128)} %get-tuple-element.193.refs_1_.refs_4_, ...), custom_call_target="tpu_custom_call" | custom-call | bytes 36000000 | tf_op jit(solution)/shard_map/pallas_call | solution.py:392
  293.1 12.6 %shard_map.276 = (bf16[256,2048]{1,0:T(8,128)(2,1)}, bf16[256,2048]{1,0:T(8,128)(2,1)}, bf16[256,1024]{1,0:T(8,128)(2,1)}, f32[1,4096]{1,0:T(1,128)}, f32[256,10...) custom-call(s32[2]{0:T(128)} %pad_add_fusion.place, ...), custom_call_target="tpu_custom_call" | custom-call | bytes 36000000 | tf_op jit(solution)/shard_map/pallas_call | solution.py:392
  307.1 7.1 %shard_map.277 = (bf16[256,2048]{1,0:T(8,128)(2,1)}, bf16[256,2048]{1,0:T(8,128)(2,1)}, bf16[2,256,2048]{2,1,0:T(8,128)(2,1)}) custom-call(s32[2]{0:T(128)} %pad_add_fusion.place, bf16[256,1024]{1,0:T(8,128)(2,1)} %broadcast_select_fusion.refs_7_.refs_0_.refs_1_, bf16[256,1024]{1,0:T(8,128)(2,1)} %copy-done.28, ...), custom_call_target="tpu_custom_call" | custom-call | bytes 21000000 | tf_op jit(solution)/shard_map/pallas_call | solution.py:392
  316.8 17.8 %shard_map.278 = (bf16[256,1024]{1,0:T(8,128)(2,1)}, bf16[256,2048]{1,0:T(8,128)(2,1)}, bf16[256,2048]{1,0:T(8,128)(2,1)}, bf16[256,2048]{1,0:T(8,128)(2,1)}, bf16[256,2048]{1,0:T(8,128)(2,1)}) custom-call(s32[2]{0:T(128)} %pad_add_fusion.place, bf16[256,1024]{1,0:T(8,128)(2,1)} %shard_map.272.refs_4_.refs_5_.refs_0_, ...), custom_call_target="tpu_custom_call" | custom-call | bytes 54000000 | tf_op jit(solution)/shard_map/pallas_call | solution.py:332
  334.6 5.6 collective-permute-start.45
  340.3 6.5 shard_map.279
  347.8 4.0 shard_map.280
  360.0 19.4 %collective-permute-done.49.refs_3_ = bf16[256,2048]{1,0:T(8,128)(2,1)S(1)} collective-permute-done((bf16[256,2048]{1,0:T(8,128)(2,1)S(1)}, bf16[256,2048]{1,0:T(8,128)(2,1)S(1)}, u32[]{:S(2)}, u32[]{:S(2)}) %collective-permute-start.49) | collective-permute-done | bytes 1048608 | tf_op jit(solution)/shard_map/ppermute | solution.py:34
  380.4 8.4 %shard_map.281 = (f32[256,1024]{1,0:T(8,128)}, bf16[256,2048]{1,0:T(8,128)(2,1)}, f32[8,1024]{1,0:T(8,128)}, bf16[256,2048]{1,0:T(8,128)(2,1)}) custom-call(s32[2]{0:T(128)} %pad_add_fusion.place, bf16[256,1024]{1,0:T(8,128)(2,1)} %get-tuple-element.216.refs_6_.refs_0_, bf16[256,2048]{1,0:T(8,128)(2,1)} %get-tuple-element.217.refs_1_, ...), custom_call_target="tpu_custom_call" | custom-call | bytes 18000000 | tf_op jit(solution)/shard_map/pallas_call | solution.py:392
  389.4 3.5 collective-permute-done.55.refs_5_
  392.9 4.7 shard_map.282
  401.6 6.4 shard_map.283
  409.5 12.4 %shard_map.284 = (bf16[256,2048]{1,0:T(8,128)(2,1)}, bf16[256,2048]{1,0:T(8,128)(2,1)}, bf16[256,1024]{1,0:T(8,128)(2,1)}, f32[1,4096]{1,0:T(1,128)}, f32[256,10...) custom-call(s32[2]{0:T(128)} %pad_add_fusion.place, f32[256,1024]{1,0:T(8,128)} %get-tuple-element.228.refs_0_, ...), custom_call_target="tpu_custom_call" | custom-call | bytes 36000000 | tf_op jit(solution)/shard_map/pallas_call | solution.py:392
  422.0 18.2 %shard_map.285 = (bf16[256,1024]{1,0:T(8,128)(2,1)}, bf16[256,2048]{1,0:T(8,128)(2,1)}, bf16[256,2048]{1,0:T(8,128)(2,1)}, bf16[256,2048]{1,0:T(8,128)(2,1)}, bf16[256,2048]{1,0:T(8,128)(2,1)}) custom-call(s32[2]{0:T(128)} %pad_add_fusion.place, bf16[256,1024]{1,0:T(8,128)(2,1)} %shard_map.262.refs_1_.refs_7_.refs_0_, ...), custom_call_target="tpu_custom_call" | custom-call | bytes 54000000 | tf_op jit(solution)/shard_map/pallas_call | solution.py:332
  440.7 4.0 shard_map.286
  451.6 10.9 %collective-permute-done.65.refs_7_.refs_12_ = bf16[128,2048]{1,0:T(8,128)(2,1)} collective-permute-done((bf16[128,2048]{1,0:T(8,128)(2,1)S(1)}, bf16[128,2048]{1,0:T(8,128)(2,1)}, u32[]{:S(2)}, u32[]{:S(2)}) %collective-permute-start.65) | collective-permute-done | bytes 524320 | tf_op jit(solution)/shard_map/ppermute | solution.py:29
  463.8 7.0 %shard_map.287 = (bf16[256,2048]{1,0:T(8,128)(2,1)}, bf16[256,2048]{1,0:T(8,128)(2,1)}, bf16[2,256,2048]{2,1,0:T(8,128)(2,1)}) custom-call(s32[2]{0:T(128)} %pad_add_fusion.place, bf16[256,2048]{1,0:T(8,128)(2,1)} %get-tuple-element.229.refs_6_.refs_2_.refs_1_.refs_0_, bf16[256,2048]{1,0:T(8,128)(2,1)} %copy-done.13, ...), custom_call_target="tpu_custom_call" | custom-call | bytes 21000000 | tf_op jit(solution)/shard_map/pallas_call | solution.py:392
  472.7 6.5 shard_map.288
  479.3 8.7 %shard_map.289 = (f32[256,1024]{1,0:T(8,128)}, bf16[256,2048]{1,0:T(8,128)(2,1)}, f32[8,1024]{1,0:T(8,128)}, bf16[256,2048]{1,0:T(8,128)(2,1)}) custom-call(s32[2]{0:T(128)} %pad_add_fusion.place, bf16[256,1024]{1,0:T(8,128)(2,1)} %get-tuple-element.242.refs_3_.refs_0_, bf16[256,2048]{1,0:T(8,128)(2,1)} %get-tuple-element.243.refs_1_, ...), custom_call_target="tpu_custom_call" | custom-call | bytes 18000000 | tf_op jit(solution)/shard_map/pallas_call | solution.py:392
  487.9 7.3 %collective-permute-done.70.refs_2_ = bf16[256,2048]{1,0:T(8,128)(2,1)} collective-permute-done((bf16[256,2048]{1,0:T(8,128)(2,1)}, bf16[256,2048]{1,0:T(8,128)(2,1)}, u32[]{:S(2)}, u32[]{:S(2)}) %collective-permute-start.70) | collective-permute-done | bytes 1048608 | tf_op jit(solution)/shard_map/ppermute | solution.py:29
  496.0 4.8 shard_map.290
  508.3 6.8 %shard_map.291 = (bf16[256,2048]{1,0:T(8,128)(2,1)}, bf16[256,2048]{1,0:T(8,128)(2,1)}, bf16[2,256,2048]{2,1,0:T(8,128)(2,1)}, bf16[128,4096]{1,0:T(8,128)(2,1)}) custom-call(s32[2]{0:T(128)} %pad_add_fusion.place, bf16[256,7168]{1,0:T(8,128)(2,1)} %get-tuple-element.209.refs_5_.refs_2_.refs_0_.refs_6_, ...), custom_call_target="tpu_custom_call" | custom-call | bytes 21000000 | tf_op jit(solution)/shard_map/pallas_call | solution.py:392
  516.8 3.5 shard_map.292.refs_3_
  528.0 18.8 %collective-permute-done.68.refs_2_ = bf16[256,2048]{1,0:T(8,128)(2,1)S(1)} collective-permute-done((bf16[256,2048]{1,0:T(8,128)(2,1)}, bf16[256,2048]{1,0:T(8,128)(2,1)S(1)}, u32[]{:S(2)}, u32[]{:S(2)}) %collective-permute-start.68) | collective-permute-done | bytes 1048608 | tf_op jit(solution)/shard_map/ppermute | solution.py:29
  547.7 4.1 shard_map.293
  551.8 15.8 %collective-permute-done.79.refs_2_ = bf16[256,2048]{1,0:T(8,128)(2,1)} collective-permute-done((bf16[256,2048]{1,0:T(8,128)(2,1)}, bf16[256,2048]{1,0:T(8,128)(2,1)}, u32[]{:S(2)}, u32[]{:S(2)}) %collective-permute-start.79) | collective-permute-done | bytes 1048608 | tf_op jit(solution)/shard_map/ppermute | solution.py:29
  568.0 4.2 shard_map.294
  585.0 4.3 collective-permute-done.77.refs_2_
  589.3 7.8 %collective-permute-done.81.refs_5_ = bf16[128,2048]{1,0:T(8,128)(2,1)} collective-permute-done((bf16[128,2048]{1,0:T(8,128)(2,1)}, bf16[128,2048]{1,0:T(8,128)(2,1)}, u32[]{:S(2)}, u32[]{:S(2)}) %collective-permute-start.81) | collective-permute-done | bytes 524320 | tf_op jit(solution)/shard_map/ppermute | solution.py:29
  597.1 4.3 shard_map.295
  616.2 33.7 %reduce-scatter.12.cloned.1.call-done = bf16[64,4096]{1,0:T(8,128)(2,1)} async-done(((bf16[256,4096]{1,0:T(8,128)(2,1)}), bf16[64,4096]{1,0:T(8,128)(2,1)}) %reduce-scatter.12.cloned.1.call-update) | async-done | bytes 524304 | tf_op jit(solution)/shard_map/reduce_scatter | solution.py:1050
  (345 shorter events, 128.5 us)
Async XLA Ops:
  7.2 433.5 %reduce-scatter.6.cloned.1.call-start = ((), (), s32[]{:S(2)}) async-start(), calls=%async_computation.5 | async-start | bytes 1310720 | tf_op jit(solution)/shard_map/reduce_scatter | solution.py:916
  12.7 32.0 %collective-permute-start.3 = (bf16[160,4096]{1,0:T(8,128)(2,1)}, bf16[160,4096]{1,0:T(8,128)(2,1)S(1)}, u32[]{:S(2)}, u32[]{:S(2)}) collective-permute-start(bf16[160,4096]{1,0:T(8,128)(2,1)} %shard_map.254.refs_6_.refs_0_.refs_1_.refs_5_.refs_7_), channel_id=1, source_target_pairs={{0,16},{4,20},{8,24},{12,28},{16,0},{20,4},{24,8},{28,12},{1,17},{... | collective-permute-start | bytes 3932168 | tf_op jit(solution)/shard_map/ppermute | solution.py:29
  15.7 30.6 %collective-permute-start.2 = (bf16[160,4096]{1,0:T(8,128)(2,1)}, bf16[160,4096]{1,0:T(8,128)(2,1)}, u32[]{:S(2)}, u32[]{:S(2)}) collective-permute-start(bf16[160,4096]{1,0:T(8,128)(2,1)} %shard_map.254.refs_6_.refs_0_.refs_1_.refs_5_.refs_7_), channel_id=1, source_target_pairs={{0,8},{4,12},{8,0},{12,4},{16,24},{20,28},{24,16},{28,20},{1,9},{5... | collective-permute-start | bytes 3932168 | tf_op jit(solution)/shard_map/ppermute | solution.py:29
  17.2 11.9 %collective-permute-start = (bf16[256,1024]{1,0:T(8,128)(2,1)}, bf16[256,1024]{1,0:T(8,128)(2,1)}, u32[]{:S(2)}, u32[]{:S(2)}) collective-permute-start(bf16[256,1024]{1,0:T(8,128)(2,1)} %bitcast.102), channel_id=1, source_target_pairs={{1,4},{2,1},{3,5},{4,2},{5,6},{6,3},{9,12},{10,9},{11,13},{12,10},... | collective-permute-start | bytes 1572872 | tf_op jit(solution)/shard_map/ppermute | solution.py:1332
  51.3 39.7 %collective-permute-start.8 = (bf16[640,4096]{1,0:T(8,128)(2,1)}, bf16[640,4096]{1,0:T(8,128)(2,1)}, u32[]{:S(2)}, u32[]{:S(2)}) collective-permute-start(bf16[640,4096]{1,0:T(8,128)(2,1)} %shard_map.255.refs_0_.refs_2_.refs_16_.refs_26_.refs_1_.refs_6_.refs_5_.refs_15_.refs_25_.refs_7_), channel_id=1, source_target_pairs={{0,4},{4,0},{8,12},{12,8},{16,20},{20,16},{24,28},{28,24},{1,5},{5... | collective-permute-start | bytes 15728648 | tf_op jit(solution)/shard_map/ppermute | solution.py:29
  52.0 37.4 %collective-permute-start.7 = (bf16[208,4096]{1,0:T(8,128)(2,1)}, bf16[208,4096]{1,0:T(8,128)(2,1)}, u32[]{:S(2)}, u32[]{:S(2)}) collective-permute-start(bf16[208,4096]{1,0:T(8,128)(2,1)} %get-tuple-element.160), channel_id=1, source_target_pairs={{0,16},{4,20},{8,24},{12,28},{16,0},{20,4},{24,8},{28,12},{1,17},{... | collective-permute-start | bytes 5111816 | tf_op jit(solution)/shard_map/ppermute | solution.py:29
  53.3 37.7 %collective-permute-start.6 = (bf16[208,4096]{1,0:T(8,128)(2,1)}, bf16[208,4096]{1,0:T(8,128)(2,1)}, u32[]{:S(2)}, u32[]{:S(2)}) collective-permute-start(bf16[208,4096]{1,0:T(8,128)(2,1)} %get-tuple-element.157), channel_id=1, source_target_pairs={{0,8},{4,12},{8,0},{12,4},{16,24},{20,28},{24,16},{28,20},{1,9},{5... | collective-permute-start | bytes 5111816 | tf_op jit(solution)/shard_map/ppermute | solution.py:29
  97.1 36.6 %collective-permute-start.16 = (bf16[192,4096]{1,0:T(8,128)(2,1)}, bf16[192,4096]{1,0:T(8,128)(2,1)}, u32[]{:S(2)}, u32[]{:S(2)}) collective-permute-start(bf16[192,4096]{1,0:T(8,128)(2,1)} %get-tuple-element.168), channel_id=1, source_target_pairs={{0,16},{4,20},{8,24},{12,28},{16,0},{20,4},{24,8},{28,12},{1,17},{... | collective-permute-start | bytes 4718600 | tf_op jit(solution)/shard_map/ppermute | solution.py:29
  97.9 36.3 %collective-permute-start.15 = (bf16[192,4096]{1,0:T(8,128)(2,1)}, bf16[192,4096]{1,0:T(8,128)(2,1)}, u32[]{:S(2)}, u32[]{:S(2)}) collective-permute-start(bf16[192,4096]{1,0:T(8,128)(2,1)} %get-tuple-element.164), channel_id=1, source_target_pairs={{0,8},{4,12},{8,0},{12,4},{16,24},{20,28},{24,16},{28,20},{1,9},{5... | collective-permute-start | bytes 4718600 | tf_op jit(solution)/shard_map/ppermute | solution.py:29
  115.5 27.6 %collective-permute-start.13 = (bf16[256,2048]{1,0:T(8,128)(2,1)}, bf16[256,2048]{1,0:T(8,128)(2,1)S(1)}, u32[]{:S(2)}, u32[]{:S(2)}) collective-permute-start(bf16[256,2048]{1,0:T(8,128)(2,1)} %shard_map.261.refs_11_.refs_1_), channel_id=1, source_target_pairs={{0,1},{1,0},{2,3},{3,2},{4,5},{5,4},{6,7},{7,6},{8,9},{9,8},{10,11... | collective-permute-start | bytes 3145736 | tf_op jit(solution)/shard_map/ppermute | solution.py:34
  119.5 23.7 %collective-permute-start.12 = (bf16[256,2048]{1,0:T(8,128)(2,1)}, bf16[256,2048]{1,0:T(8,128)(2,1)}, u32[]{:S(2)}, u32[]{:S(2)}) collective-permute-start(bf16[256,2048]{1,0:T(8,128)(2,1)} %shard_map.261.refs_11_.refs_1_), channel_id=1, source_target_pairs={{0,4},{4,0},{8,12},{12,8},{16,20},{20,16},{24,28},{28,24},{1,5},{5... | collective-permute-start | bytes 3145736 | tf_op jit(solution)/shard_map/ppermute | solution.py:29
  137.1 35.4 %collective-permute-start.20 = (bf16[192,4096]{1,0:T(8,128)(2,1)}, bf16[192,4096]{1,0:T(8,128)(2,1)}, u32[]{:S(2)}, u32[]{:S(2)}) collective-permute-start(bf16[192,4096]{1,0:T(8,128)(2,1)} %get-tuple-element.178), channel_id=1, source_target_pairs={{0,16},{4,20},{8,24},{12,28},{16,0},{20,4},{24,8},{28,12},{1,17},{... | collective-permute-start | bytes 4718600 | tf_op jit(solution)/shard_map/ppermute | solution.py:29
  138.3 35.2 %collective-permute-start.19 = (bf16[192,4096]{1,0:T(8,128)(2,1)}, bf16[192,4096]{1,0:T(8,128)(2,1)}, u32[]{:S(2)}, u32[]{:S(2)}) collective-permute-start(bf16[192,4096]{1,0:T(8,128)(2,1)} %get-tuple-element.171.refs_1_), channel_id=1, source_target_pairs={{0,8},{4,12},{8,0},{12,4},{16,24},{20,28},{24,16},{28,20},{1,9},{5... | collective-permute-start | bytes 4718600 | tf_op jit(solution)/shard_map/ppermute | solution.py:29
  139.8 34.2 %collective-permute-start.17 = (bf16[192,4096]{1,0:T(8,128)(2,1)}, bf16[192,4096]{1,0:T(8,128)(2,1)}, u32[]{:S(2)}, u32[]{:S(2)}) collective-permute-start(bf16[192,4096]{1,0:T(8,128)(2,1)} %collective-permute-done.15.refs_0_.refs_22_.refs_28_.refs_21_.refs_27_), channel_id=1, source_target_pairs={{0,4},{4,0},{8,12},{12,8},{16,20},{20,16},{24,28},{28,24},{1,5},{5... | collective-permute-start | bytes 4718600 | tf_op jit(solution)/shard_map/ppermute | solution.py:29
  143.2 30.8 %collective-permute-start.18 = (bf16[192,4096]{1,0:T(8,128)(2,1)}, bf16[192,4096]{1,0:T(8,128)(2,1)}, u32[]{:S(2)}, u32[]{:S(2)}) collective-permute-start(bf16[192,4096]{1,0:T(8,128)(2,1)} %collective-permute-done.16.refs_1_.refs_23_.refs_30_.refs_22_.refs_29_), channel_id=1, source_target_pairs={{0,4},{4,0},{8,12},{12,8},{16,20},{20,16},{24,28},{28,24},{1,5},{5... | collective-permute-start | bytes 4718600 | tf_op jit(solution)/shard_map/ppermute | solution.py:29
  176.9 36.6 %collective-permute-start.24 = (bf16[192,4096]{1,0:T(8,128)(2,1)}, bf16[192,4096]{1,0:T(8,128)(2,1)}, u32[]{:S(2)}, u32[]{:S(2)}) collective-permute-start(bf16[192,4096]{1,0:T(8,128)(2,1)} %get-tuple-element.185), channel_id=1, source_target_pairs={{0,16},{4,20},{8,24},{12,28},{16,0},{20,4},{24,8},{28,12},{1,17},{... | collective-permute-start | bytes 4718600 | tf_op jit(solution)/shard_map/ppermute | solution.py:29
  177.6 36.3 %collective-permute-start.23 = (bf16[192,4096]{1,0:T(8,128)(2,1)}, bf16[192,4096]{1,0:T(8,128)(2,1)}, u32[]{:S(2)}, u32[]{:S(2)}) collective-permute-start(bf16[192,4096]{1,0:T(8,128)(2,1)} %get-tuple-element.182.refs_1_), channel_id=1, source_target_pairs={{0,8},{4,12},{8,0},{12,4},{16,24},{20,28},{24,16},{28,20},{1,9},{5... | collective-permute-start | bytes 4718600 | tf_op jit(solution)/shard_map/ppermute | solution.py:29
  217.4 36.6 %collective-permute-start.31 = (bf16[192,4096]{1,0:T(8,128)(2,1)}, bf16[192,4096]{1,0:T(8,128)(2,1)}, u32[]{:S(2)}, u32[]{:S(2)}) collective-permute-start(bf16[192,4096]{1,0:T(8,128)(2,1)} %get-tuple-element.190), channel_id=1, source_target_pairs={{0,16},{4,20},{8,24},{12,28},{16,0},{20,4},{24,8},{28,12},{1,17},{... | collective-permute-start | bytes 4718600 | tf_op jit(solution)/shard_map/ppermute | solution.py:29
  218.6 36.3 %collective-permute-start.30 = (bf16[192,4096]{1,0:T(8,128)(2,1)}, bf16[192,4096]{1,0:T(8,128)(2,1)}, u32[]{:S(2)}, u32[]{:S(2)}) collective-permute-start(bf16[192,4096]{1,0:T(8,128)(2,1)} %get-tuple-element.189.refs_11_), channel_id=1, source_target_pairs={{0,8},{4,12},{8,0},{12,4},{16,24},{20,28},{24,16},{28,20},{1,9},{5... | collective-permute-start | bytes 4718600 | tf_op jit(solution)/shard_map/ppermute | solution.py:29
  224.9 28.1 %collective-permute-start.28 = (bf16[256,2048]{1,0:T(8,128)(2,1)}, bf16[256,2048]{1,0:T(8,128)(2,1)S(1)}, u32[]{:S(2)}, u32[]{:S(2)}) collective-permute-start(bf16[256,2048]{1,0:T(8,128)(2,1)} %shard_map.271.refs_11_.refs_1_), channel_id=1, source_target_pairs={{0,1},{1,0},{2,3},{3,2},{4,5},{5,4},{6,7},{7,6},{8,9},{9,8},{10,11... | collective-permute-start | bytes 3145736 | tf_op jit(solution)/shard_map/ppermute | solution.py:34
  229.5 29.1 %collective-permute-start.27 = (bf16[256,2048]{1,0:T(8,128)(2,1)}, bf16[256,2048]{1,0:T(8,128)(2,1)}, u32[]{:S(2)}, u32[]{:S(2)}) collective-permute-start(bf16[256,2048]{1,0:T(8,128)(2,1)} %shard_map.271.refs_11_.refs_1_), channel_id=1, source_target_pairs={{0,4},{4,0},{8,12},{12,8},{16,20},{20,16},{24,28},{28,24},{1,5},{5... | collective-permute-start | bytes 3145736 | tf_op jit(solution)/shard_map/ppermute | solution.py:29
  254.0 22.2 %collective-permute-start.33 = (bf16[192,4096]{1,0:T(8,128)(2,1)}, bf16[192,4096]{1,0:T(8,128)(2,1)}, u32[]{:S(2)}, u32[]{:S(2)}) collective-permute-start(bf16[192,4096]{1,0:T(8,128)(2,1)} %collective-permute-done.31.refs_1_.refs_23_.refs_30_.refs_22_.refs_29_), channel_id=1, source_target_pairs={{0,4},{4,0},{8,12},{12,8},{16,20},{20,16},{24,28},{28,24},{1,5},{5... | collective-permute-start | bytes 4718600 | tf_op jit(solution)/shard_map/ppermute | solution.py:29
  255.0 21.2 %collective-permute-start.32 = (bf16[192,4096]{1,0:T(8,128)(2,1)}, bf16[192,4096]{1,0:T(8,128)(2,1)}, u32[]{:S(2)}, u32[]{:S(2)}) collective-permute-start(bf16[192,4096]{1,0:T(8,128)(2,1)} %collective-permute-done.30.refs_0_.refs_22_.refs_28_.refs_21_.refs_27_), channel_id=1, source_target_pairs={{0,4},{4,0},{8,12},{12,8},{16,20},{20,16},{24,28},{28,24},{1,5},{5... | collective-permute-start | bytes 4718600 | tf_op jit(solution)/shard_map/ppermute | solution.py:29
  257.9 17.7 %collective-permute-start.35 = (bf16[64,4096]{1,0:T(8,128)(2,1)}, bf16[64,4096]{1,0:T(8,128)(2,1)}, u32[]{:S(2)}, u32[]{:S(2)}) collective-permute-start(bf16[64,4096]{1,0:T(8,128)(2,1)} %get-tuple-element.197), channel_id=1, source_target_pairs={{0,16},{4,20},{8,24},{12,28},{16,0},{20,4},{24,8},{28,12},{1,17},{... | collective-permute-start | bytes 1572872 | tf_op jit(solution)/shard_map/ppermute | solution.py:29
  258.7 16.9 %collective-permute-start.34 = (bf16[64,4096]{1,0:T(8,128)(2,1)}, bf16[64,4096]{1,0:T(8,128)(2,1)}, u32[]{:S(2)}, u32[]{:S(2)}) collective-permute-start(bf16[64,4096]{1,0:T(8,128)(2,1)} %get-tuple-element.191.refs_5_), channel_id=1, source_target_pairs={{0,8},{4,12},{8,0},{12,4},{16,24},{20,28},{24,16},{28,20},{1,9},{5... | collective-permute-start | bytes 1572872 | tf_op jit(solution)/shard_map/ppermute | solution.py:29
  292.4 14.2 %collective-permute-start.39 = (bf16[256,7168]{1,0:T(8,128)(2,1)}, bf16[256,7168]{1,0:T(8,128)(2,1)}, u32[]{:S(2)}, u32[]{:S(2)}) collective-permute-start(bf16[256,7168]{1,0:T(8,128)(2,1)} %get-tuple-element.204.refs_2_.refs_5_.refs_0_.refs_6_), channel_id=1, source_target_pairs={{0,4},{4,0},{8,12},{12,8},{16,20},{20,16},{24,28},{28,24},{1,5},{5... | collective-permute-start | bytes 11010056 | tf_op jit(solution)/shard_map/ppermute | solution.py:29
  292.6 14.0 %collective-permute-start.40 = (bf16[256,7168]{1,0:T(8,128)(2,1)}, bf16[256,7168]{1,0:T(8,128)(2,1)}, u32[]{:S(2)}, u32[]{:S(2)}) collective-permute-start(bf16[256,7168]{1,0:T(8,128)(2,1)} %get-tuple-element.209.refs_5_.refs_2_.refs_0_.refs_6_), channel_id=1, source_target_pairs={{0,4},{4,0},{8,12},{12,8},{16,20},{20,16},{24,28},{28,24},{1,5},{5... | collective-permute-start | bytes 11010056 | tf_op jit(solution)/shard_map/ppermute | solution.py:29
  293.0 13.3 %collective-permute-start.38 = (bf16[256,1024]{1,0:T(8,128)(2,1)S(1)}, bf16[256,1024]{1,0:T(8,128)(2,1)S(1)}, u32[]{:S(2)}, u32[]{:S(2)}) collective-permute-start(bf16[256,1024]{1,0:T(8,128)(2,1)S(1)} %copy-done.5), channel_id=1, source_target_pairs={{0,4},{4,0},{8,12},{12,8},{16,20},{20,16},{24,28},{28,24},{1,5},{5... | collective-permute-start | bytes 1572872 | tf_op jit(solution)/shard_map/ppermute | solution.py:29
  314.2 32.6 %collective-permute-start.46 = (bf16[256,2048]{1,0:T(8,128)(2,1)}, bf16[256,2048]{1,0:T(8,128)(2,1)}, u32[]{:S(2)}, u32[]{:S(2)}) collective-permute-start(bf16[256,2048]{1,0:T(8,128)(2,1)} %get-tuple-element.210.refs_8_), channel_id=1, source_target_pairs={{0,8},{4,12},{8,0},{12,4},{16,24},{20,28},{24,16},{28,20},{1,9},{5... | collective-permute-start | bytes 3145736 | tf_op jit(solution)/shard_map/ppermute | solution.py:29
  314.7 32.1 %collective-permute-start.41 = (f32[256,1024]{1,0:T(8,128)}, f32[256,1024]{1,0:T(8,128)S(1)}, u32[]{:S(2)}, u32[]{:S(2)}) collective-permute-start(f32[256,1024]{1,0:T(8,128)} %get-tuple-element.211), channel_id=1, source_target_pairs={{4,1},{1,2},{5,3},{2,4},{6,5},{3,6},{12,9},{9,10},{13,11},{10,12},... | collective-permute-start | bytes 3145736 | tf_op jit(solution)/shard_map/ppermute | solution.py:1332
  315.5 31.3 %collective-permute-start.47 = (bf16[256,2048]{1,0:T(8,128)(2,1)}, bf16[256,2048]{1,0:T(8,128)(2,1)}, u32[]{:S(2)}, u32[]{:S(2)}) collective-permute-start(bf16[256,2048]{1,0:T(8,128)(2,1)} %get-tuple-element.220), channel_id=1, source_target_pairs={{0,16},{4,20},{8,24},{12,28},{16,0},{20,4},{24,8},{28,12},{1,17},{... | collective-permute-start | bytes 3145736 | tf_op jit(solution)/shard_map/ppermute | solution.py:29
  334.6 17.3 %collective-permute-start.45 = (bf16[256,2048]{1,0:T(8,128)(2,1)}, bf16[256,2048]{1,0:T(8,128)(2,1)}, u32[]{:S(2)}, u32[]{:S(2)}) collective-permute-start(bf16[256,2048]{1,0:T(8,128)(2,1)} %get-tuple-element.218), channel_id=1, source_target_pairs={{0,4},{4,0},{8,12},{12,8},{16,20},{20,16},{24,28},{28,24},{1,5},{5... | collective-permute-start | bytes 3145736 | tf_op jit(solution)/shard_map/ppermute | solution.py:29
  353.8 25.6 %collective-permute-start.49 = (bf16[256,2048]{1,0:T(8,128)(2,1)S(1)}, bf16[256,2048]{1,0:T(8,128)(2,1)S(1)}, u32[]{:S(2)}, u32[]{:S(2)}) collective-permute-start(bf16[256,2048]{1,0:T(8,128)(2,1)S(1)} %add_convert_fusion.1.refs_17_), channel_id=1, source_target_pairs={{0,1},{1,0},{2,3},{3,2},{4,5},{5,4},{6,7},{7,6},{8,9},{9,8},{10,11... | collective-permute-start | bytes 3145736 | tf_op jit(solution)/shard_map/ppermute | solution.py:34
  355.9 32.9 %collective-permute-start.53 = (bf16[256,2048]{1,0:T(8,128)(2,1)}, bf16[256,2048]{1,0:T(8,128)(2,1)}, u32[]{:S(2)}, u32[]{:S(2)}) collective-permute-start(bf16[256,2048]{1,0:T(8,128)(2,1)} %get-tuple-element.234), channel_id=1, source_target_pairs={{0,16},{4,20},{8,24},{12,28},{16,0},{20,4},{24,8},{28,12},{1,17},{... | collective-permute-start | bytes 3145736 | tf_op jit(solution)/shard_map/ppermute | solution.py:29
  356.7 32.7 %collective-permute-start.52 = (bf16[256,2048]{1,0:T(8,128)(2,1)}, bf16[256,2048]{1,0:T(8,128)(2,1)}, u32[]{:S(2)}, u32[]{:S(2)}) collective-permute-start(bf16[256,2048]{1,0:T(8,128)(2,1)} %get-tuple-element.221.refs_3_), channel_id=1, source_target_pairs={{0,8},{4,12},{8,0},{12,4},{16,24},{20,28},{24,16},{28,20},{1,9},{5... | collective-permute-start | bytes 3145736 | tf_op jit(solution)/shard_map/ppermute | solution.py:29
  358.2 34.6 %collective-permute-start.55 = (bf16[128,2048]{1,0:T(8,128)(2,1)}, bf16[128,2048]{1,0:T(8,128)(2,1)}, u32[]{:S(2)}, u32[]{:S(2)}) collective-permute-start(bf16[128,2048]{1,0:T(8,128)(2,1)} %get-tuple-element.236), channel_id=1, source_target_pairs={{0,8},{4,12},{8,0},{12,4},{16,24},{20,28},{24,16},{28,20},{1,9},{5... | collective-permute-start | bytes 1572872 | tf_op jit(solution)/shard_map/ppermute | solution.py:29
  358.7 34.1 %collective-permute-start.54 = (bf16[128,2048]{1,0:T(8,128)(2,1)}, bf16[128,2048]{1,0:T(8,128)(2,1)}, u32[]{:S(2)}, u32[]{:S(2)}) collective-permute-start(bf16[128,2048]{1,0:T(8,128)(2,1)} %get-tuple-element.222), channel_id=1, source_target_pairs={{0,16},{4,20},{8,24},{12,28},{16,0},{20,4},{24,8},{28,12},{1,17},{... | collective-permute-start | bytes 1572872 | tf_op jit(solution)/shard_map/ppermute | solution.py:29
  388.8 11.9 %collective-permute-start.51 = (bf16[256,2048]{1,0:T(8,128)(2,1)}, bf16[256,2048]{1,0:T(8,128)(2,1)}, u32[]{:S(2)}, u32[]{:S(2)}) collective-permute-start(bf16[256,2048]{1,0:T(8,128)(2,1)} %get-tuple-element.232.refs_4_), channel_id=1, source_target_pairs={{0,4},{4,0},{8,12},{12,8},{16,20},{20,16},{24,28},{28,24},{1,5},{5... | collective-permute-start | bytes 3145736 | tf_op jit(solution)/shard_map/ppermute | solution.py:29
  388.9 11.8 %collective-permute-start.50 = (bf16[256,2048]{1,0:T(8,128)(2,1)}, bf16[256,2048]{1,0:T(8,128)(2,1)S(1)}, u32[]{:S(2)}, u32[]{:S(2)}) collective-permute-start(bf16[256,2048]{1,0:T(8,128)(2,1)} %get-tuple-element.229.refs_6_.refs_2_.refs_1_.refs_0_), channel_id=1, source_target_pairs={{0,4},{4,0},{8,12},{12,8},{16,20},{20,16},{24,28},{28,24},{1,5},{5... | collective-permute-start | bytes 3145736 | tf_op jit(solution)/shard_map/ppermute | solution.py:29
  397.6 170.4 %reduce-scatter.8.cloned.1.call-start = ((), (), s32[]{:S(2)}) async-start(), calls=%async_computation.6 | async-start | bytes 1310720 | tf_op jit(solution)/shard_map/reduce_scatter | solution.py:916
  397.8 24.1 %collective-permute-start.56 = (bf16[128,2048]{1,0:T(8,128)(2,1)}, bf16[128,2048]{1,0:T(8,128)(2,1)}, u32[]{:S(2)}, u32[]{:S(2)}) collective-permute-start(bf16[128,2048]{1,0:T(8,128)(2,1)} %get-tuple-element.241), channel_id=1, source_target_pairs={{0,8},{4,12},{8,0},{12,4},{16,24},{20,28},{24,16},{28,20},{1,9},{5... | collective-permute-start | bytes 1572872 | tf_op jit(solution)/shard_map/ppermute | solution.py:29
  399.4 22.5 %collective-permute-start.57 = (bf16[128,2048]{1,0:T(8,128)(2,1)}, bf16[128,2048]{1,0:T(8,128)(2,1)}, u32[]{:S(2)}, u32[]{:S(2)}) collective-permute-start(bf16[128,2048]{1,0:T(8,128)(2,1)} %get-tuple-element.237.refs_10_), channel_id=1, source_target_pairs={{0,16},{4,20},{8,24},{12,28},{16,0},{20,4},{24,8},{28,12},{1,17},{... | collective-permute-start | bytes 1572872 | tf_op jit(solution)/shard_map/ppermute | solution.py:29
  408.1 32.6 %collective-permute-start.60 = (bf16[256,2048]{1,0:T(8,128)(2,1)}, bf16[256,2048]{1,0:T(8,128)(2,1)}, u32[]{:S(2)}, u32[]{:S(2)}) collective-permute-start(bf16[256,2048]{1,0:T(8,128)(2,1)} %get-tuple-element.246), channel_id=1, source_target_pairs={{0,16},{4,20},{8,24},{12,28},{16,0},{20,4},{24,8},{28,12},{1,17},{... | collective-permute-start | bytes 3145736 | tf_op jit(solution)/shard_map/ppermute | solution.py:29
  409.1 31.6 %collective-permute-start.59 = (bf16[256,2048]{1,0:T(8,128)(2,1)}, bf16[256,2048]{1,0:T(8,128)(2,1)}, u32[]{:S(2)}, u32[]{:S(2)}) collective-permute-start(bf16[256,2048]{1,0:T(8,128)(2,1)} %get-tuple-element.238.refs_35_), channel_id=1, source_target_pairs={{0,8},{4,12},{8,0},{12,4},{16,24},{20,28},{24,16},{28,20},{1,9},{5... | collective-permute-start | bytes 3145736 | tf_op jit(solution)/shard_map/ppermute | solution.py:29
  447.9 15.9 %collective-permute-start.63 = (bf16[256,2048]{1,0:T(8,128)(2,1)S(1)}, bf16[256,2048]{1,0:T(8,128)(2,1)}, u32[]{:S(2)}, u32[]{:S(2)}) collective-permute-start(bf16[256,2048]{1,0:T(8,128)(2,1)S(1)} %copy-done.19), channel_id=1, source_target_pairs={{0,4},{4,0},{8,12},{12,8},{16,20},{20,16},{24,28},{28,24},{1,5},{5... | collective-permute-start | bytes 3145736 | tf_op jit(solution)/shard_map/ppermute | solution.py:29
  448.0 15.8 %collective-permute-start.64 = (bf16[256,2048]{1,0:T(8,128)(2,1)S(1)}, bf16[256,2048]{1,0:T(8,128)(2,1)}, u32[]{:S(2)}, u32[]{:S(2)}) collective-permute-start(bf16[256,2048]{1,0:T(8,128)(2,1)S(1)} %copy-done.20), channel_id=1, source_target_pairs={{0,4},{4,0},{8,12},{12,8},{16,20},{20,16},{24,28},{28,24},{1,5},{5... | collective-permute-start | bytes 3145736 | tf_op jit(solution)/shard_map/ppermute | solution.py:29
  448.5 14.0 %collective-permute-start.65 = (bf16[128,2048]{1,0:T(8,128)(2,1)S(1)}, bf16[128,2048]{1,0:T(8,128)(2,1)}, u32[]{:S(2)}, u32[]{:S(2)}) collective-permute-start(bf16[128,2048]{1,0:T(8,128)(2,1)S(1)} %copy-done.38), channel_id=1, source_target_pairs={{0,8},{4,12},{8,0},{12,4},{16,24},{20,28},{24,16},{28,20},{1,9},{5... | collective-permute-start | bytes 1572872 | tf_op jit(solution)/shard_map/ppermute | solution.py:29
  450.1 13.7 %collective-permute-start.66 = (bf16[128,2048]{1,0:T(8,128)(2,1)S(1)}, bf16[128,2048]{1,0:T(8,128)(2,1)}, u32[]{:S(2)}, u32[]{:S(2)}) collective-permute-start(bf16[128,2048]{1,0:T(8,128)(2,1)S(1)} %copy-done.37), channel_id=1, source_target_pairs={{0,16},{4,20},{8,24},{12,28},{16,0},{20,4},{24,8},{28,12},{1,17},{... | collective-permute-start | bytes 1572872 | tf_op jit(solution)/shard_map/ppermute | solution.py:29
  451.1 28.1 %collective-permute-start.62 = (bf16[256,2048]{1,0:T(8,128)(2,1)S(1)}, bf16[256,2048]{1,0:T(8,128)(2,1)}, u32[]{:S(2)}, u32[]{:S(2)}) collective-permute-start(bf16[256,2048]{1,0:T(8,128)(2,1)S(1)} %add_convert_fusion.refs_4_), channel_id=1, source_target_pairs={{0,1},{1,0},{2,3},{3,2},{4,5},{5,4},{6,7},{7,6},{8,9},{9,8},{10,11... | collective-permute-start | bytes 3145736 | tf_op jit(solution)/shard_map/ppermute | solution.py:34
  470.9 24.4 %collective-permute-start.70 = (bf16[256,2048]{1,0:T(8,128)(2,1)}, bf16[256,2048]{1,0:T(8,128)(2,1)}, u32[]{:S(2)}, u32[]{:S(2)}) collective-permute-start(bf16[256,2048]{1,0:T(8,128)(2,1)} %get-tuple-element.265), channel_id=1, source_target_pairs={{0,16},{4,20},{8,24},{12,28},{16,0},{20,4},{24,8},{28,12},{1,17},{... | collective-permute-start | bytes 3145736 | tf_op jit(solution)/shard_map/ppermute | solution.py:29
  472.0 24.0 %collective-permute-start.69 = (bf16[256,2048]{1,0:T(8,128)(2,1)}, bf16[256,2048]{1,0:T(8,128)(2,1)}, u32[]{:S(2)}, u32[]{:S(2)}) collective-permute-start(bf16[256,2048]{1,0:T(8,128)(2,1)} %get-tuple-element.259.refs_6_), channel_id=1, source_target_pairs={{0,8},{4,12},{8,0},{12,4},{16,24},{20,28},{24,16},{28,20},{1,9},{5... | collective-permute-start | bytes 3145736 | tf_op jit(solution)/shard_map/ppermute | solution.py:29
  500.9 67.1 %reduce-scatter.10.cloned.1.call-start = ((), (), s32[]{:S(2)}) async-start(), calls=%async_computation.7 | async-start | bytes 1310720 | tf_op jit(solution)/shard_map/reduce_scatter | solution.py:916
  501.8 14.6 %collective-permute-start.72 = (bf16[128,2048]{1,0:T(8,128)(2,1)}, bf16[128,2048]{1,0:T(8,128)(2,1)}, u32[]{:S(2)}, u32[]{:S(2)}) collective-permute-start(bf16[128,2048]{1,0:T(8,128)(2,1)} %get-tuple-element.269), channel_id=1, source_target_pairs={{0,8},{4,12},{8,0},{12,4},{16,24},{20,28},{24,16},{28,20},{1,9},{5... | collective-permute-start | bytes 1572872 | tf_op jit(solution)/shard_map/ppermute | solution.py:29
  502.5 14.3 %collective-permute-start.71 = (bf16[128,2048]{1,0:T(8,128)(2,1)}, bf16[128,2048]{1,0:T(8,128)(2,1)}, u32[]{:S(2)}, u32[]{:S(2)}) collective-permute-start(bf16[128,2048]{1,0:T(8,128)(2,1)} %get-tuple-element.268.refs_13_), channel_id=1, source_target_pairs={{0,16},{4,20},{8,24},{12,28},{16,0},{20,4},{24,8},{28,12},{1,17},{... | collective-permute-start | bytes 1572872 | tf_op jit(solution)/shard_map/ppermute | solution.py:29
  520.3 88.4 %reduce-scatter.14.cloned.1.call-start = ((), (), s32[]{:S(2)}) async-start(), calls=%async_computation.9 | async-start | bytes 1310720 | tf_op jit(solution)/shard_map/reduce_scatter | solution.py:916
  520.4 26.4 %collective-permute-start.68 = (bf16[256,2048]{1,0:T(8,128)(2,1)}, bf16[256,2048]{1,0:T(8,128)(2,1)S(1)}, u32[]{:S(2)}, u32[]{:S(2)}) collective-permute-start(bf16[256,2048]{1,0:T(8,128)(2,1)} %get-tuple-element.263), channel_id=1, source_target_pairs={{0,16},{4,20},{8,24},{12,28},{16,0},{20,4},{24,8},{28,12},{1,17},{... | collective-permute-start | bytes 3145736 | tf_op jit(solution)/shard_map/ppermute | solution.py:29
  521.3 26.2 %collective-permute-start.67 = (bf16[256,2048]{1,0:T(8,128)(2,1)S(1)}, bf16[256,2048]{1,0:T(8,128)(2,1)}, u32[]{:S(2)}, u32[]{:S(2)}) collective-permute-start(bf16[256,2048]{1,0:T(8,128)(2,1)S(1)} %copy-done.18), channel_id=1, source_target_pairs={{0,8},{4,12},{8,0},{12,4},{16,24},{20,28},{24,16},{28,20},{1,9},{5... | collective-permute-start | bytes 3145736 | tf_op jit(solution)/shard_map/ppermute | solution.py:29
  522.7 44.9 %collective-permute-start.79 = (bf16[256,2048]{1,0:T(8,128)(2,1)}, bf16[256,2048]{1,0:T(8,128)(2,1)}, u32[]{:S(2)}, u32[]{:S(2)}) collective-permute-start(bf16[256,2048]{1,0:T(8,128)(2,1)} %get-tuple-element.279), channel_id=1, source_target_pairs={{0,16},{4,20},{8,24},{12,28},{16,0},{20,4},{24,8},{28,12},{1,17},{... | collective-permute-start | bytes 3145736 | tf_op jit(solution)/shard_map/ppermute | solution.py:29
  523.8 44.2 %collective-permute-start.78 = (bf16[256,2048]{1,0:T(8,128)(2,1)}, bf16[256,2048]{1,0:T(8,128)(2,1)}, u32[]{:S(2)}, u32[]{:S(2)}) collective-permute-start(bf16[256,2048]{1,0:T(8,128)(2,1)} %get-tuple-element.274.refs_3_), channel_id=1, source_target_pairs={{0,8},{4,12},{8,0},{12,4},{16,24},{20,28},{24,16},{28,20},{1,9},{5... | collective-permute-start | bytes 3145736 | tf_op jit(solution)/shard_map/ppermute | solution.py:29
  524.6 125.3 %reduce-scatter.12.cloned.1.call-start = ((), (), s32[]{:S(2)}) async-start(), calls=%async_computation.8 | async-start | bytes 2621440 | tf_op jit(solution)/shard_map/reduce_scatter | solution.py:1050
  572.7 16.6 %collective-permute-start.76 = (bf16[128,2048]{1,0:T(8,128)(2,1)}, bf16[128,2048]{1,0:T(8,128)(2,1)}, u32[]{:S(2)}, u32[]{:S(2)}) collective-permute-start(bf16[128,2048]{1,0:T(8,128)(2,1)} %get-tuple-element.276.refs_3_), channel_id=1, source_target_pairs={{0,16},{4,20},{8,24},{12,28},{16,0},{20,4},{24,8},{28,12},{1,17},{... | collective-permute-start | bytes 1572872 | tf_op jit(solution)/shard_map/ppermute | solution.py:29
  574.1 15.2 %collective-permute-start.77 = (bf16[128,2048]{1,0:T(8,128)(2,1)}, bf16[128,2048]{1,0:T(8,128)(2,1)}, u32[]{:S(2)}, u32[]{:S(2)}) collective-permute-start(bf16[128,2048]{1,0:T(8,128)(2,1)} %get-tuple-element.277), channel_id=1, source_target_pairs={{0,8},{4,12},{8,0},{12,4},{16,24},{20,28},{24,16},{28,20},{1,9},{5... | collective-permute-start | bytes 1572872 | tf_op jit(solution)/shard_map/ppermute | solution.py:29
  575.6 21.5 %collective-permute-start.80 = (bf16[128,2048]{1,0:T(8,128)(2,1)}, bf16[128,2048]{1,0:T(8,128)(2,1)}, u32[]{:S(2)}, u32[]{:S(2)}) collective-permute-start(bf16[128,2048]{1,0:T(8,128)(2,1)} %get-tuple-element.284.refs_6_), channel_id=1, source_target_pairs={{0,16},{4,20},{8,24},{12,28},{16,0},{20,4},{24,8},{28,12},{1,17},{... | collective-permute-start | bytes 1572872 | tf_op jit(solution)/shard_map/ppermute | solution.py:29
  576.2 20.8 %collective-permute-start.81 = (bf16[128,2048]{1,0:T(8,128)(2,1)}, bf16[128,2048]{1,0:T(8,128)(2,1)}, u32[]{:S(2)}, u32[]{:S(2)}) collective-permute-start(bf16[128,2048]{1,0:T(8,128)(2,1)} %get-tuple-element.285), channel_id=1, source_target_pairs={{0,8},{4,12},{8,0},{12,4},{16,24},{20,28},{24,16},{28,20},{1,9},{5... | collective-permute-start | bytes 1572872 | tf_op jit(solution)/shard_map/ppermute | solution.py:29
  (68 other events, 413.5 us)
Sparse Core Ops, SparseCore 0:
  397.7 25.5 reduce-scatter.5
  501.0 24.2 reduce-scatter.7
  527.6 25.7 reduce-scatter.9
  556.3 27.1 reduce-scatter.13
  601.6 48.3 reduce-scatter.11

commit v4 on v3

--- a/solution.py
+++ b/solution.py
@@ -303,7 +303,7 @@
     )
 
 
-VMEM_LIMIT = 64_000 * 1024
+VMEM_LIMIT = 65_400 * 1024
 TILE = 1024
 BLOCK = 128
 NT = (((1,), (1,)), ((), ()))
@@ -492,6 +492,11 @@
     return lane < HEAD, lane >= HEAD
 
 
+def both_heads(rows):
+    zeros = jnp.zeros_like(rows)
+    return jnp.concatenate([jnp.where(mask, rows, zeros) for mask in head_masks(rows.shape[0])], axis=0)
+
+
 def attend_fast(queries, chunks, deps=()):
     tokens, width = queries.shape
     pairs = width // (2 * HEAD)
@@ -499,20 +504,21 @@
     def body(place, ins, outs, _):
         both = join(ins[1:5])
         keys, values = both[:, : 2 * HEAD], both[:, 2 * HEAD :]
-        scaled = ins[0][...] * jnp.asarray(1.0 / math.sqrt(HEAD), bf16)
-        halves, tops = [], []
-        for head, mask in enumerate(head_masks(tokens)):
-            query = jnp.where(mask, scaled, jnp.zeros_like(scaled))
-            scores = lax.dot_general(keys, query, NT, preferred_element_type=f32)
-            most = jnp.max(scores, axis=0, keepdims=True)
-            exponent = jnp.exp(scores - most)
-            total = jnp.sum(exponent, axis=0, keepdims=True)
-            mixed = lax.dot_general(values, exponent.astype(bf16), TN, preferred_element_type=f32)
-            halves.append(mixed[head * HEAD : (head + 1) * HEAD] / total)
-            tops.append(most + jnp.log(total))
+        query = both_heads(ins[0][...] * jnp.asarray(1.0 / math.sqrt(HEAD), bf16))
+        scores = lax.dot_general(keys, query, NT, preferred_element_type=f32)
+        most = jnp.max(scores, axis=0, keepdims=True)
+        exponent = jnp.exp(scores - most)
+        total = jnp.sum(exponent, axis=0, keepdims=True)
+        mixed = lax.dot_general(values, exponent.astype(bf16), TN, preferred_element_type=f32)
+        halves = [
+            mixed[head * HEAD : (head + 1) * HEAD, head * tokens : (head + 1) * tokens]
+            / total[:, head * tokens : (head + 1) * tokens]
+            for head in range(2)
+        ]
         outs[0][...] = jnp.concatenate(halves, axis=0).T.astype(bf16)
-        outs[1][0, 0:1, :] = tops[0]
-        outs[1][0, 1:2, :] = tops[1]
+        top = most + jnp.log(total)
+        outs[1][0, 0:1, :] = top[:, :tokens]
+        outs[1][0, 1:2, :] = top[:, tokens:]
 
     return run(
         body,
@@ -545,21 +551,19 @@
             precision=lax.Precision.HIGHEST,
             preferred_element_type=f32,
         )
-        key_grad = value_grad = None
-        halves = []
-        for head, mask in enumerate(masks):
-            query = jnp.where(mask, scaled, jnp.zeros_like(scaled))
-            grad = jnp.where(mask, grads, jnp.zeros_like(grads))
-            scores = lax.dot_general(keys, query, NT, preferred_element_type=f32)
-            probs = jnp.exp(scores - ins[7][0, head : head + 1, :])
-            prob_grad = lax.dot_general(values, grad, NT, preferred_element_type=f32)
-            score_grad = (probs * (prob_grad - along[head : head + 1, :])).astype(bf16)
-            key_part = jnp.dot(score_grad, query, preferred_element_type=f32)
-            value_part = jnp.dot(probs.astype(bf16), grad, preferred_element_type=f32)
-            key_grad = key_part if head == 0 else key_grad + key_part
-            value_grad = value_part if head == 0 else value_grad + value_part
-            query_part = lax.dot_general(keys, score_grad, TN, preferred_element_type=f32)
-            halves.append(query_part[head * HEAD : (head + 1) * HEAD])
+        query, grad = both_heads(scaled), both_heads(grads)
+        scores = lax.dot_general(keys, query, NT, preferred_element_type=f32)
+        top = jnp.concatenate([ins[7][0, head : head + 1, :] for head in range(2)], axis=1)
+        probs = jnp.exp(scores - top)
+        prob_grad = lax.dot_general(values, grad, NT, preferred_element_type=f32)
+        pulled = jnp.concatenate([along[head : head + 1, :] for head in range(2)], axis=1)
+        score_grad = (probs * (prob_grad - pulled)).astype(bf16)
+        key_grad = jnp.dot(score_grad, query, preferred_element_type=f32)
+        value_grad = jnp.dot(probs.astype(bf16), grad, preferred_element_type=f32)
+        query_part = lax.dot_general(keys, score_grad, TN, preferred_element_type=f32)
+        halves = [
+            query_part[head * HEAD : (head + 1) * HEAD, head * tokens : (head + 1) * tokens] for head in range(2)
+        ]
         query_grad = jnp.concatenate(halves, axis=0) * (1.0 / math.sqrt(HEAD))
         outs[0][...] = query_grad.T.astype(bf16)
         for chunk in range(4):
@@ -1420,8 +1424,6 @@
             back = [(own, swap(own, 1)) for own in own_back]
             token = advance([of_reduce], deps=(own_back[0], saved[0][1][1]))
             deps = (token,) + tuple(other for _, other in back)
-            moved_result, finish = relay(after(result, token), True)
-            outputs = finish(lax.optimization_barrier(moved_result)).astype(bf16)
         else:
             deps = (upper_expand.second_x, upper_expand.second_y)
         query_grad, near, near_leave, far, far_leave = attend_fast_back(
@@ -1432,9 +1434,9 @@
         if above is None:
             of_expand = Reduction(expand_group(kept, back))
             token = advance([of_expand], deps=(token,))
-            token = advance(thirds=[of_reduce], deps=(token, moved_result))
+            token = advance(thirds=[of_reduce], deps=(token,))
         else:
-            token = advance(thirds=[of_attention], deps=(token, upper_reduce.share))
+            token = advance(thirds=[of_attention], deps=(token, upper_reduce.share, moved_result))
         far, near_leave = after(far, token, near_leave), after(near_leave, token)
         far = (wide(far) + wide(far_leave)).astype(bf16)
         far = (far, swap_seq(far, 1))
@@ -1444,13 +1446,16 @@
             of_expand = Reduction(expand_group(kept, back))
             token = advance([of_reduce], deps=(token, back[0][1], back[1][1], of_attention.second_x, of_attention.second_y))
             token = advance([of_expand], deps=(token,))
+        deps = (token, of_expand.from_x, of_expand.from_y) if above is None else (token,)
         grad, own_lower, early_sums, key_grad = first_back(
-            query_grad, (near, near_leave, far[1]), packs[0], stream, middle_grad, vec, (token,)
+            query_grad, (near, near_leave, far[1]), packs[0], stream, middle_grad, vec, deps
         )
         lower, block = (own_lower, swap(own_lower, 1)), 1
         key_grad = (key_grad, swap(key_grad, 1))
         if above is None:
             token = advance(thirds=[of_expand], fourths=[of_reduce], deps=(own_lower,))
+            moved_result, finish = relay(after(result, token), True)
+            outputs = finish(lax.optimization_barrier(moved_result)).astype(bf16)
         else:
             back.append((own_back[2], swap(after(own_back[2], own_lower), 1)))
             token = own_lower
@@ -1463,17 +1468,17 @@
         sums[layer] = (early_sums, late_sums, expand_bias_grad)
 
     of_reduce, of_expand, of_last = above
-    token = advance(thirds=[of_reduce], fourths=[upper_expand], deps=(token,))
-    token = advance([of_last], fourths=[upper_attention], deps=(token,), later=True)
+    token = advance(thirds=[of_reduce], joint=(upper_expand, upper_attention), deps=(token,))
+    token = advance([of_last], deps=(token,))
     token = advance(fourths=[of_reduce], deps=(token,))
-    upper_attention.scatter(token)
     token = advance(thirds=[of_expand], deps=(token,))
-    token = advance(thirds=[of_last], deps=(token, upper_expand.share, upper_attention.share))
+    token = advance(thirds=[of_last], deps=(token, upper_expand.share))
+    token = advance(fourths=[of_expand], deps=(token,))
     small, changes = small_and_changes(sums)
     small, changes = after(small, token), after(changes, token)
     small, changes = cross(small, changes, 4, plane % 2, lambda a: swap_seq(a, 1), True)
     small, changes = cross(small, changes, 3, plane // 2, lambda a: swap_seq(a, 2), False)
-    token = advance(joint=(of_expand, of_last), deps=(token, small, changes))
+    token = advance(fourths=[of_last], deps=(token, small, changes))
     input_grad, finish = relay(after(own_lower[:, TILE:], token), True)
     input_grad = finish(input_grad).astype(f32)
     shares[("attention", 0)] = of_last

time: 672 us -> 651 us (0.969)
  waiting for transfers between devices: 242 us -> 222 us
    reduce_scatter x1, waiting for transfers between devices: 33.7 us -> 0.01 us  [advance(): both = lax.psum_scatter(results[0], 'seq', scatter_dimension=0, tiled=True)]
    reduce_scatter x4, waiting for transfers between devices: 0.01 us -> 25.1 us  [scatter(): self.share = lax.psum_scatter(piece, 'seq', scatter_dimension=0, tiled=True)]
    ppermute x6, waiting for transfers between devices: 46.4 us -> 32.3 us  [swap_seq(): return lax.ppermute(array, 'seq', [(i, i ^ bit) for i in range(count)])]
    pallas_call x18, Pallas kernels: 119 us -> 110 us  [run(): pl.pallas_call(kernel, out_shape=shapes, grid_spec=pltpu.PrefetchScalarGr...]
    pallas_call x24 -> x25, Pallas kernels: 160 us -> 163 us  [run_flow(): pl.pallas_call(kernel, out_shape=[jax.ShapeDtypeStruct(shape, kind) for s...]
  transfers between devices with their start and end apart: 93 -> 93, of which waited for: 40 -> 42; matrix products, arithmetic and copies ran while one was open for 3% -> 5% of each run, Pallas kernels for 38% -> 38%
where the time goes in v4:
time: 651 us; the launch traced here: 643 us
  Pallas kernels  273 us (42%)
  waiting for transfers between devices  222 us (34%)
  starting transfers between devices  90.1 us (14%)
  other arithmetic  25.8 us (4%)
  local copies, waits for them, and re-layouts  16.9 us (3%)
  between operations  15.7 us (2%)
    ppermute x78, waiting for transfers between devices, swap(): return lax.ppermute(array, 'dp', [(i, i ^ bit) for i in range(count)])  164 us
    pallas_call x25, Pallas kernels, run_flow(): pl.pallas_call(kernel, out_shape=[jax.ShapeDtypeStruct(shape, kind) for s...  163 us
    pallas_call x18, Pallas kernels, run(): pl.pallas_call(kernel, out_shape=shapes, grid_spec=pltpu.PrefetchScalarGr...  110 us
    ppermute x78, starting transfers between devices, swap(): return lax.ppermute(array, 'dp', [(i, i ^ bit) for i in range(count)])  68.4 us
    ppermute x6, waiting for transfers between devices, swap_seq(): return lax.ppermute(array, 'seq', [(i, i ^ bit) for i in range(count)])  32.3 us
    reduce_scatter x4, waiting for transfers between devices, scatter(): self.share = lax.psum_scatter(piece, 'seq', scatter_dimension=0, tiled=True)  25.1 us
    ppermute x6, starting transfers between devices, swap_seq(): return lax.ppermute(array, 'seq', [(i, i ^ bit) for i in range(count)])  16.5 us
  transfers between devices with their start and end apart: 93, of which 42 were waited for; matrix products, arithmetic and copies ran while one was open for 5% of the time, Pallas kernels for 38%

profile of v4, /device:TPU:0, one launch (start us, length us, event | category | flops | bytes accessed | tf_op | source)
XLA Modules:
  0.0 643.3 jit_solution(16642258427617934152)
XLA Ops:
  9.0 3.8 shard_map.254.refs_6_.refs_0_.refs_1_.refs_5_.refs_7_
  12.8 3.0 collective-permute-start.3
  18.7 6.2 shard_map.255.refs_0_.refs_2_.refs_16_.refs_26_.refs_1_.refs_6_.refs_5_.refs_15_.refs_25_.refs_7_
  24.8 4.3 shard_map.256
  31.1 13.7 %collective-permute-done.3.refs_1_.refs_4_.refs_5_.refs_10_.refs_9_.refs_11_ = bf16[160,4096]{1,0:T(8,128)(2,1)} collective-permute-done((bf16[160,4096]{1,0:T(8,128)(2,1)}, bf16[160,4096]{1,0:T(8,128)(2,1)}, u32[]{:S(2)}, u32[]{:S(2)}) %collective-permute-start.3) | collective-permute-done | bytes 1310752 | tf_op jit(solution)/shard_map/ppermute | solution.py:29
  46.3 5.0 shard_map.257
  54.1 3.4 collective-permute-start.4
  57.4 5.5 collective-permute-start.5
  65.9 23.5 %collective-permute-done.7.refs_1_.refs_7_.refs_8_.refs_13_.refs_20_.refs_12_.refs_19_.refs_14_ = bf16[208,4096]{1,0:T(8,128)(2,1)} collective-permute-done((bf16[208,4096]{1,0:T(8,128)(2,1)}, bf16[208,4096]{1,0:T(8,128)(2,1)}, u32[]{:S(2)}, u32[]{:S(2)}) %collective-permute-start.7) | collective-permute-done | bytes 1703968 | tf_op jit(solution)/shard_map/ppermute | solution.py:29
  99.2 4.1 collective-permute-done.1.refs_1_.refs_2_.refs_7_.refs_6_.refs_8_
  103.3 3.3 shard_map.259
  106.6 2.9 shard_map.260.refs_0_.refs_5_
  109.5 4.8 shard_map.261.refs_11_.refs_1_
  114.3 3.8 collective-permute-start.13
  118.0 4.0 shard_map.262.refs_1_.refs_7_.refs_0_
  122.0 4.3 shard_map.263
  129.1 3.5 collective-permute-done.16.refs_1_.refs_23_.refs_30_.refs_22_.refs_29_
  138.9 2.9 collective-permute-done.13.refs_3_
  142.3 4.4 shard_map.265
  147.1 12.4 %shard_map.266 = (bf16[256,1024]{1,0:T(8,128)(2,1)}, f32[8,8,256]{2,1,0:T(8,128)}) custom-call(s32[2]{0:T(128)} %pad_add_fusion.place, bf16[256,1024]{1,0:T(8,128)(2,1)} %shard_map.262.refs_1_.refs_7_.refs_0_, bf16[256,2048]{1,0:T(8,128)(2,1)} %shard_map.261.refs_11_.refs_1_, bf16[256,2048]{1,0:T(8,128)(2,1)} %collective-permute-done.12.refs_2_, ...), custom_call_target="tpu_custom_call" | custom-call | bytes 45000000 | tf_op jit(solution)/shard_map/pallas_call | solution.py:332
  159.4 12.9 %collective-permute-done.20.refs_1_.refs_33_.refs_5_.refs_10_.refs_9_.refs_11_.refs_32_ = bf16[192,4096]{1,0:T(8,128)(2,1)} collective-permute-done((bf16[192,4096]{1,0:T(8,128)(2,1)}, bf16[192,4096]{1,0:T(8,128)(2,1)}, u32[]{:S(2)}, u32[]{:S(2)}) %collective-permute-start.20) | collective-permute-done | bytes 1572896 | tf_op jit(solution)/shard_map/ppermute | solution.py:29
  173.2 2.9 shard_map.267
  179.0 4.5 shard_map.268
  183.5 12.8 %shard_map.269 = (f32[256,1024]{1,0:T(8,128)}, bf16[256,7168]{1,0:T(8,128)(2,1)}, bf16[256,4096]{1,0:T(8,128)(2,1)}, f32[256,1024]{1,0:T(8,128)}, bf16[256,1024]{1,0:T(8,128)(2,1)}) custom-call(s32[2]{0:T(128)} %pad_add_fusion.place, bf16[256,1024]{1,0:T(8,128)(2,1)} %get-tuple-element.171.refs_6_.refs_0_, ...), custom_call_target="tpu_custom_call" | custom-call | bytes 36000000 | tf_op jit(solution)/shard_map/pallas_call | solution.py:392
  196.4 16.4 %collective-permute-done.24.refs_1_.refs_8_.refs_13_.refs_20_.refs_12_.refs_19_.refs_14_ = bf16[192,4096]{1,0:T(8,128)(2,1)} collective-permute-done((bf16[192,4096]{1,0:T(8,128)(2,1)}, bf16[192,4096]{1,0:T(8,128)(2,1)}, u32[]{:S(2)}, u32[]{:S(2)}) %collective-permute-start.24) | collective-permute-done | bytes 1572896 | tf_op jit(solution)/shard_map/ppermute | solution.py:29
  219.9 4.8 shard_map.271.refs_11_.refs_1_
  224.7 4.6 collective-permute-start.28
  229.3 3.9 shard_map.272.refs_4_.refs_5_.refs_0_
  233.3 19.8 %collective-permute-done.28.refs_3_ = bf16[256,2048]{1,0:T(8,128)(2,1)} collective-permute-done((bf16[256,2048]{1,0:T(8,128)(2,1)}, bf16[256,2048]{1,0:T(8,128)(2,1)}, u32[]{:S(2)}, u32[]{:S(2)}) %collective-permute-start.28) | collective-permute-done | bytes 1048608 | tf_op jit(solution)/shard_map/ppermute | solution.py:34
  260.1 12.6 %shard_map.274 = (bf16[256,1024]{1,0:T(8,128)(2,1)}, f32[8,8,256]{2,1,0:T(8,128)}) custom-call(s32[2]{0:T(128)} %pad_add_fusion.place, bf16[256,1024]{1,0:T(8,128)(2,1)} %shard_map.272.refs_4_.refs_5_.refs_0_, bf16[256,2048]{1,0:T(8,128)(2,1)} %shard_map.271.refs_11_.refs_1_, bf16[256,2048]{1,0:T(8,128)(2,1)} %collective-permute-done.27.refs_2_, ...), custom_call_target="tpu_custom_call" | custom-call | bytes 45000000 | tf_op jit(solution)/shard_map/pallas_call | solution.py:332
  275.9 12.9 %shard_map.275 = (f32[256,1024]{1,0:T(8,128)}, bf16[256,7168]{1,0:T(8,128)(2,1)}, bf16[256,4096]{1,0:T(8,128)(2,1)}, f32[256,1024]{1,0:T(8,128)}, bf16[256,1024]{1,0:T(8,128)(2,1)}) custom-call(s32[2]{0:T(128)} %pad_add_fusion.place, bf16[256,1024]{1,0:T(8,128)(2,1)} %get-tuple-element.190.refs_0_.refs_36_, f32[256,1024]{1,0:T(8,128)} %get-tuple-element.191.refs_1_.refs_4_, ...), custom_call_target="tpu_custom_call" | custom-call | bytes 36000000 | tf_op jit(solution)/shard_map/pallas_call | solution.py:392
  289.6 12.8 %shard_map.276 = (bf16[256,2048]{1,0:T(8,128)(2,1)}, bf16[256,2048]{1,0:T(8,128)(2,1)}, bf16[256,1024]{1,0:T(8,128)(2,1)}, f32[1,4096]{1,0:T(1,128)}, f32[256,10...) custom-call(s32[2]{0:T(128)} %pad_add_fusion.place, ...), custom_call_target="tpu_custom_call" | custom-call | bytes 36000000 | tf_op jit(solution)/shard_map/pallas_call | solution.py:392
  303.3 7.0 %shard_map.277 = (bf16[256,2048]{1,0:T(8,128)(2,1)}, bf16[256,2048]{1,0:T(8,128)(2,1)}, bf16[2,256,2048]{2,1,0:T(8,128)(2,1)}) custom-call(s32[2]{0:T(128)} %pad_add_fusion.place, bf16[256,1024]{1,0:T(8,128)(2,1)} %broadcast_select_fusion.refs_7_.refs_0_.refs_1_, bf16[256,1024]{1,0:T(8,128)(2,1)} %collective-permute-done.41.refs_1_, ...), custom_call_target="tpu_custom_call" | custom-call | bytes 21000000 | tf_op jit(solution)/shard_map/pallas_call | solution.py:392
  312.4 15.6 %shard_map.278 = (bf16[256,1024]{1,0:T(8,128)(2,1)}, bf16[256,2048]{1,0:T(8,128)(2,1)}, bf16[256,2048]{1,0:T(8,128)(2,1)}, bf16[256,2048]{1,0:T(8,128)(2,1)}, bf16[256,2048]{1,0:T(8,128)(2,1)}) custom-call(s32[2]{0:T(128)} %pad_add_fusion.place, bf16[256,1024]{1,0:T(8,128)(2,1)} %shard_map.272.refs_4_.refs_5_.refs_0_, ...), custom_call_target="tpu_custom_call" | custom-call | bytes 54000000 | tf_op jit(solution)/shard_map/pallas_call | solution.py:332
  328.6 6.5 %shard_map.279 = (bf16[256,2048]{1,0:T(8,128)(2,1)}, bf16[256,2048]{1,0:T(8,128)(2,1)}, bf16[2,256,2048]{2,1,0:T(8,128)(2,1)}) custom-call(s32[2]{0:T(128)} %pad_add_fusion.place, bf16[256,7168]{1,0:T(8,128)(2,1)} %get-tuple-element.201.refs_2_.refs_5_.refs_0_.refs_6_, bf16[256,7168]{1,0:T(8,128)(2,1)} %collective-permute-done.38.refs_3_.refs_1_.refs_7_, ...), custom_call_target="tpu_custom_call" | custom-call | bytes 21000000 | tf_op jit(solution)/shard_map/pallas_call | solution.py:392
  337.3 4.1 shard_map.280
  344.3 4.6 collective-permute-start.52
  350.8 10.7 %collective-permute-done.45.refs_19_.refs_2_ = bf16[256,2048]{1,0:T(8,128)(2,1)} collective-permute-done((bf16[256,2048]{1,0:T(8,128)(2,1)}, bf16[256,2048]{1,0:T(8,128)(2,1)}, u32[]{:S(2)}, u32[]{:S(2)}) %collective-permute-start.45) | collective-permute-done | bytes 1048608 | tf_op jit(solution)/shard_map/ppermute | solution.py:29
  363.0 8.5 %collective-permute-done.52.refs_3_ = bf16[256,2048]{1,0:T(8,128)(2,1)S(1)} collective-permute-done((bf16[256,2048]{1,0:T(8,128)(2,1)S(1)}, bf16[256,2048]{1,0:T(8,128)(2,1)S(1)}, u32[]{:S(2)}, u32[]{:S(2)}) %collective-permute-start.52) | collective-permute-done | bytes 1048608 | tf_op jit(solution)/shard_map/ppermute | solution.py:34
  372.6 8.5 %shard_map.281 = (f32[256,1024]{1,0:T(8,128)}, bf16[256,2048]{1,0:T(8,128)(2,1)}, f32[8,1024]{1,0:T(8,128)}, bf16[256,2048]{1,0:T(8,128)(2,1)}) custom-call(s32[2]{0:T(128)} %pad_add_fusion.place, bf16[256,1024]{1,0:T(8,128)(2,1)} %get-tuple-element.213.refs_6_.refs_0_, bf16[256,2048]{1,0:T(8,128)(2,1)} %get-tuple-element.222.refs_1_, ...), custom_call_target="tpu_custom_call" | custom-call | bytes 18000000 | tf_op jit(solution)/shard_map/pallas_call | solution.py:392
  381.7 4.7 shard_map.282
  390.4 6.6 %shard_map.283 = (bf16[256,2048]{1,0:T(8,128)(2,1)}, bf16[256,2048]{1,0:T(8,128)(2,1)}, bf16[2,256,2048]{2,1,0:T(8,128)(2,1)}) custom-call(s32[2]{0:T(128)} %pad_add_fusion.place, bf16[256,7168]{1,0:T(8,128)(2,1)} %get-tuple-element.201.refs_2_.refs_5_.refs_0_.refs_6_, bf16[256,7168]{1,0:T(8,128)(2,1)} %collective-permute-done.38.refs_3_.refs_1_.refs_7_, ...), custom_call_target="tpu_custom_call" | custom-call | bytes 21000000 | tf_op jit(solution)/shard_map/pallas_call | solution.py:392
  399.0 12.4 %shard_map.284 = (bf16[256,2048]{1,0:T(8,128)(2,1)}, bf16[256,2048]{1,0:T(8,128)(2,1)}, bf16[256,1024]{1,0:T(8,128)(2,1)}, f32[1,4096]{1,0:T(1,128)}, f32[256,10...) custom-call(s32[2]{0:T(128)} %pad_add_fusion.place, f32[256,1024]{1,0:T(8,128)} %get-tuple-element.232.refs_0_, ...), custom_call_target="tpu_custom_call" | custom-call | bytes 36000000 | tf_op jit(solution)/shard_map/pallas_call | solution.py:392
  411.4 15.8 %shard_map.285 = (bf16[256,1024]{1,0:T(8,128)(2,1)}, bf16[256,2048]{1,0:T(8,128)(2,1)}, bf16[256,2048]{1,0:T(8,128)(2,1)}, bf16[256,2048]{1,0:T(8,128)(2,1)}, bf16[256,2048]{1,0:T(8,128)(2,1)}) custom-call(s32[2]{0:T(128)} %pad_add_fusion.place, bf16[256,1024]{1,0:T(8,128)(2,1)} %shard_map.262.refs_1_.refs_7_.refs_0_, ...), custom_call_target="tpu_custom_call" | custom-call | bytes 54000000 | tf_op jit(solution)/shard_map/pallas_call | solution.py:332
  429.0 4.0 shard_map.286
  433.1 3.1 add_convert_fusion.refs_4_
  436.1 4.2 collective-permute-start.63
  443.2 11.7 %collective-permute-done.65.refs_7_.refs_8_ = bf16[128,2048]{1,0:T(8,128)(2,1)} collective-permute-done((bf16[128,2048]{1,0:T(8,128)(2,1)S(1)}, bf16[128,2048]{1,0:T(8,128)(2,1)}, u32[]{:S(2)}, u32[]{:S(2)}) %collective-permute-start.65) | collective-permute-done | bytes 524320 | tf_op jit(solution)/shard_map/ppermute | solution.py:29
  455.0 7.0 %shard_map.287 = (bf16[256,2048]{1,0:T(8,128)(2,1)}, bf16[256,2048]{1,0:T(8,128)(2,1)}, bf16[2,256,2048]{2,1,0:T(8,128)(2,1)}) custom-call(s32[2]{0:T(128)} %pad_add_fusion.place, bf16[256,2048]{1,0:T(8,128)(2,1)} %get-tuple-element.229.refs_6_.refs_2_.refs_1_.refs_0_, bf16[256,2048]{1,0:T(8,128)(2,1)} %collective-permute-done.54.refs_3_.refs_1_, ...), custom_call_target="tpu_custom_call" | custom-call | bytes 21000000 | tf_op jit(solution)/shard_map/pallas_call | solution.py:392
  465.1 6.6 %shard_map.288 = (bf16[256,2048]{1,0:T(8,128)(2,1)}, bf16[256,2048]{1,0:T(8,128)(2,1)}, bf16[2,256,2048]{2,1,0:T(8,128)(2,1)}) custom-call(s32[2]{0:T(128)} %pad_add_fusion.place, bf16[256,7168]{1,0:T(8,128)(2,1)} %get-tuple-element.210.refs_5_.refs_2_.refs_0_.refs_6_, bf16[256,7168]{1,0:T(8,128)(2,1)} %collective-permute-done.42.refs_5_.refs_3_.refs_1_.refs_7_, ...), custom_call_target="tpu_custom_call" | custom-call | bytes 21000000 | tf_op jit(solution)/shard_map/pallas_call | solution.py:392
  471.7 8.6 %shard_map.289 = (f32[256,1024]{1,0:T(8,128)}, bf16[256,2048]{1,0:T(8,128)(2,1)}, f32[8,1024]{1,0:T(8,128)}, bf16[256,2048]{1,0:T(8,128)(2,1)}) custom-call(s32[2]{0:T(128)} %pad_add_fusion.place, bf16[256,1024]{1,0:T(8,128)(2,1)} %get-tuple-element.240.refs_3_.refs_0_, bf16[256,2048]{1,0:T(8,128)(2,1)} %get-tuple-element.241.refs_1_, ...), custom_call_target="tpu_custom_call" | custom-call | bytes 18000000 | tf_op jit(solution)/shard_map/pallas_call | solution.py:392
  480.3 6.7 %collective-permute-done.71.refs_2_ = bf16[256,2048]{1,0:T(8,128)(2,1)} collective-permute-done((bf16[256,2048]{1,0:T(8,128)(2,1)}, bf16[256,2048]{1,0:T(8,128)(2,1)}, u32[]{:S(2)}, u32[]{:S(2)}) %collective-permute-start.71) | collective-permute-done | bytes 1048608 | tf_op jit(solution)/shard_map/ppermute | solution.py:29
  488.1 6.4 shard_map.290
  503.5 6.4 %shard_map.291 = (bf16[256,2048]{1,0:T(8,128)(2,1)}, bf16[256,2048]{1,0:T(8,128)(2,1)}, bf16[2,256,2048]{2,1,0:T(8,128)(2,1)}) custom-call(s32[2]{0:T(128)} %pad_add_fusion.place, bf16[256,7168]{1,0:T(8,128)(2,1)} %get-tuple-element.210.refs_5_.refs_2_.refs_0_.refs_6_, bf16[256,7168]{1,0:T(8,128)(2,1)} %collective-permute-done.42.refs_5_.refs_3_.refs_1_.refs_7_, ...), custom_call_target="tpu_custom_call" | custom-call | bytes 21000000 | tf_op jit(solution)/shard_map/pallas_call | solution.py:392
  513.1 3.5 shard_map.292.refs_3_
  523.6 12.0 %collective-permute-done.75.refs_2_ = bf16[256,2048]{1,0:T(8,128)(2,1)} collective-permute-done((bf16[256,2048]{1,0:T(8,128)(2,1)}, bf16[256,2048]{1,0:T(8,128)(2,1)}, u32[]{:S(2)}, u32[]{:S(2)}) %collective-permute-start.75) | collective-permute-done | bytes 1048608 | tf_op jit(solution)/shard_map/ppermute | solution.py:29
  535.6 4.1 shard_map.293
  542.9 15.1 %collective-permute-done.73.refs_2_ = bf16[256,2048]{1,0:T(8,128)(2,1)} collective-permute-done((bf16[256,2048]{1,0:T(8,128)(2,1)}, bf16[256,2048]{1,0:T(8,128)(2,1)}, u32[]{:S(2)}, u32[]{:S(2)}) %collective-permute-start.73) | collective-permute-done | bytes 1048608 | tf_op jit(solution)/shard_map/ppermute | solution.py:29
  558.1 4.1 shard_map.294
  562.1 5.0 collective-permute-done.81.refs_2_
  568.2 3.3 shard_map.295.refs_3_
  583.1 5.6 collective-permute-done.79.refs_2_
  588.7 3.5 shard_map.296
  608.2 25.1 %reduce-scatter.10.cloned.1.call-done = bf16[32,4096]{1,0:T(8,128)(2,1)} async-done(((bf16[128,4096]{1,0:T(8,128)(2,1)}), bf16[32,4096]{1,0:T(8,128)(2,1)}) %reduce-scatter.10.cloned.1.call-update) | async-done | bytes 262160 | tf_op jit(solution)/shard_map/reduce_scatter | solution.py:920
  (316 shorter events, 137.2 us)
Async XLA Ops:
  7.2 421.8 %reduce-scatter.6.cloned.1.call-start = ((), (), s32[]{:S(2)}) async-start(), calls=%async_computation.5 | async-start | bytes 1310720 | tf_op jit(solution)/shard_map/reduce_scatter | solution.py:920
  12.8 32.1 %collective-permute-start.3 = (bf16[160,4096]{1,0:T(8,128)(2,1)}, bf16[160,4096]{1,0:T(8,128)(2,1)}, u32[]{:S(2)}, u32[]{:S(2)}) collective-permute-start(bf16[160,4096]{1,0:T(8,128)(2,1)} %shard_map.254.refs_6_.refs_0_.refs_1_.refs_5_.refs_7_), channel_id=1, source_target_pairs={{0,16},{4,20},{8,24},{12,28},{16,0},{20,4},{24,8},{28,12},{1,17},{... | collective-permute-start | bytes 3932168 | tf_op jit(solution)/shard_map/ppermute | solution.py:29
  15.7 30.6 %collective-permute-start.2 = (bf16[160,4096]{1,0:T(8,128)(2,1)}, bf16[160,4096]{1,0:T(8,128)(2,1)}, u32[]{:S(2)}, u32[]{:S(2)}) collective-permute-start(bf16[160,4096]{1,0:T(8,128)(2,1)} %shard_map.254.refs_6_.refs_0_.refs_1_.refs_5_.refs_7_), channel_id=1, source_target_pairs={{0,8},{4,12},{8,0},{12,4},{16,24},{20,28},{24,16},{28,20},{1,9},{5... | collective-permute-start | bytes 3932168 | tf_op jit(solution)/shard_map/ppermute | solution.py:29
  17.2 12.0 %collective-permute-start = (bf16[256,1024]{1,0:T(8,128)(2,1)}, bf16[256,1024]{1,0:T(8,128)(2,1)}, u32[]{:S(2)}, u32[]{:S(2)}) collective-permute-start(bf16[256,1024]{1,0:T(8,128)(2,1)} %bitcast.101), channel_id=1, source_target_pairs={{1,4},{2,1},{3,5},{4,2},{5,6},{6,3},{9,12},{10,9},{11,13},{12,10},... | collective-permute-start | bytes 1572872 | tf_op jit(solution)/shard_map/ppermute | solution.py:1336
  51.3 38.5 %collective-permute-start.8 = (bf16[640,4096]{1,0:T(8,128)(2,1)}, bf16[640,4096]{1,0:T(8,128)(2,1)}, u32[]{:S(2)}, u32[]{:S(2)}) collective-permute-start(bf16[640,4096]{1,0:T(8,128)(2,1)} %shard_map.255.refs_0_.refs_2_.refs_16_.refs_26_.refs_1_.refs_6_.refs_5_.refs_15_.refs_25_.refs_7_), channel_id=1, source_target_pairs={{0,4},{4,0},{8,12},{12,8},{16,20},{20,16},{24,28},{28,24},{1,5},{5... | collective-permute-start | bytes 15728648 | tf_op jit(solution)/shard_map/ppermute | solution.py:29
  52.0 37.4 %collective-permute-start.7 = (bf16[208,4096]{1,0:T(8,128)(2,1)}, bf16[208,4096]{1,0:T(8,128)(2,1)}, u32[]{:S(2)}, u32[]{:S(2)}) collective-permute-start(bf16[208,4096]{1,0:T(8,128)(2,1)} %get-tuple-element.158), channel_id=1, source_target_pairs={{0,16},{4,20},{8,24},{12,28},{16,0},{20,4},{24,8},{28,12},{1,17},{... | collective-permute-start | bytes 5111816 | tf_op jit(solution)/shard_map/ppermute | solution.py:29
  52.4 37.4 %collective-permute-start.6 = (bf16[208,4096]{1,0:T(8,128)(2,1)}, bf16[208,4096]{1,0:T(8,128)(2,1)}, u32[]{:S(2)}, u32[]{:S(2)}) collective-permute-start(bf16[208,4096]{1,0:T(8,128)(2,1)} %get-tuple-element.155), channel_id=1, source_target_pairs={{0,8},{4,12},{8,0},{12,4},{16,24},{20,28},{24,16},{28,20},{1,9},{5... | collective-permute-start | bytes 5111816 | tf_op jit(solution)/shard_map/ppermute | solution.py:29
  95.9 36.6 %collective-permute-start.16 = (bf16[192,4096]{1,0:T(8,128)(2,1)}, bf16[192,4096]{1,0:T(8,128)(2,1)}, u32[]{:S(2)}, u32[]{:S(2)}) collective-permute-start(bf16[192,4096]{1,0:T(8,128)(2,1)} %get-tuple-element.166), channel_id=1, source_target_pairs={{0,16},{4,20},{8,24},{12,28},{16,0},{20,4},{24,8},{28,12},{1,17},{... | collective-permute-start | bytes 4718600 | tf_op jit(solution)/shard_map/ppermute | solution.py:29
  97.7 36.3 %collective-permute-start.15 = (bf16[192,4096]{1,0:T(8,128)(2,1)}, bf16[192,4096]{1,0:T(8,128)(2,1)}, u32[]{:S(2)}, u32[]{:S(2)}) collective-permute-start(bf16[192,4096]{1,0:T(8,128)(2,1)} %get-tuple-element.162), channel_id=1, source_target_pairs={{0,8},{4,12},{8,0},{12,4},{16,24},{20,28},{24,16},{28,20},{1,9},{5... | collective-permute-start | bytes 4718600 | tf_op jit(solution)/shard_map/ppermute | solution.py:29
  114.3 27.5 %collective-permute-start.13 = (bf16[256,2048]{1,0:T(8,128)(2,1)}, bf16[256,2048]{1,0:T(8,128)(2,1)}, u32[]{:S(2)}, u32[]{:S(2)}) collective-permute-start(bf16[256,2048]{1,0:T(8,128)(2,1)} %shard_map.261.refs_11_.refs_1_), channel_id=1, source_target_pairs={{0,1},{1,0},{2,3},{3,2},{4,5},{5,4},{6,7},{7,6},{8,9},{9,8},{10,11... | collective-permute-start | bytes 3145736 | tf_op jit(solution)/shard_map/ppermute | solution.py:34
  118.0 23.8 %collective-permute-start.12 = (bf16[256,2048]{1,0:T(8,128)(2,1)}, bf16[256,2048]{1,0:T(8,128)(2,1)}, u32[]{:S(2)}, u32[]{:S(2)}) collective-permute-start(bf16[256,2048]{1,0:T(8,128)(2,1)} %shard_map.261.refs_11_.refs_1_), channel_id=1, source_target_pairs={{0,4},{4,0},{8,12},{12,8},{16,20},{20,16},{24,28},{28,24},{1,5},{5... | collective-permute-start | bytes 3145736 | tf_op jit(solution)/shard_map/ppermute | solution.py:29
  136.9 35.4 %collective-permute-start.20 = (bf16[192,4096]{1,0:T(8,128)(2,1)}, bf16[192,4096]{1,0:T(8,128)(2,1)}, u32[]{:S(2)}, u32[]{:S(2)}) collective-permute-start(bf16[192,4096]{1,0:T(8,128)(2,1)} %get-tuple-element.176), channel_id=1, source_target_pairs={{0,16},{4,20},{8,24},{12,28},{16,0},{20,4},{24,8},{28,12},{1,17},{... | collective-permute-start | bytes 4718600 | tf_op jit(solution)/shard_map/ppermute | solution.py:29
  137.2 35.5 %collective-permute-start.19 = (bf16[192,4096]{1,0:T(8,128)(2,1)}, bf16[192,4096]{1,0:T(8,128)(2,1)}, u32[]{:S(2)}, u32[]{:S(2)}) collective-permute-start(bf16[192,4096]{1,0:T(8,128)(2,1)} %get-tuple-element.169.refs_1_), channel_id=1, source_target_pairs={{0,8},{4,12},{8,0},{12,4},{16,24},{20,28},{24,16},{28,20},{1,9},{5... | collective-permute-start | bytes 4718600 | tf_op jit(solution)/shard_map/ppermute | solution.py:29
  138.9 34.3 %collective-permute-start.17 = (bf16[192,4096]{1,0:T(8,128)(2,1)}, bf16[192,4096]{1,0:T(8,128)(2,1)}, u32[]{:S(2)}, u32[]{:S(2)}) collective-permute-start(bf16[192,4096]{1,0:T(8,128)(2,1)} %collective-permute-done.15.refs_0_.refs_22_.refs_28_.refs_21_.refs_27_), channel_id=1, source_target_pairs={{0,4},{4,0},{8,12},{12,8},{16,20},{20,16},{24,28},{28,24},{1,5},{5... | collective-permute-start | bytes 4718600 | tf_op jit(solution)/shard_map/ppermute | solution.py:29
  141.8 31.4 %collective-permute-start.18 = (bf16[192,4096]{1,0:T(8,128)(2,1)}, bf16[192,4096]{1,0:T(8,128)(2,1)}, u32[]{:S(2)}, u32[]{:S(2)}) collective-permute-start(bf16[192,4096]{1,0:T(8,128)(2,1)} %collective-permute-done.16.refs_1_.refs_23_.refs_30_.refs_22_.refs_29_), channel_id=1, source_target_pairs={{0,4},{4,0},{8,12},{12,8},{16,20},{20,16},{24,28},{28,24},{1,5},{5... | collective-permute-start | bytes 4718600 | tf_op jit(solution)/shard_map/ppermute | solution.py:29
  172.7 10.9 %collective-permute-start.22 = (bf16[192,4096]{1,0:T(8,128)(2,1)}, bf16[192,4096]{1,0:T(8,128)(2,1)}, u32[]{:S(2)}, u32[]{:S(2)}) collective-permute-start(bf16[192,4096]{1,0:T(8,128)(2,1)} %collective-permute-done.20.refs_1_.refs_33_.refs_5_.refs_10_.refs_9_.refs_11_.refs_32_), channel_id=1, source_target_pairs={{0,4},{4,0},{8,12},{12,8},{16,20},{20,16},{24,28},{28,24},{1,5},{5... | collective-permute-start | bytes 4718600 | tf_op jit(solution)/shard_map/ppermute | solution.py:29
  176.1 36.6 %collective-permute-start.24 = (bf16[192,4096]{1,0:T(8,128)(2,1)}, bf16[192,4096]{1,0:T(8,128)(2,1)}, u32[]{:S(2)}, u32[]{:S(2)}) collective-permute-start(bf16[192,4096]{1,0:T(8,128)(2,1)} %get-tuple-element.183), channel_id=1, source_target_pairs={{0,16},{4,20},{8,24},{12,28},{16,0},{20,4},{24,8},{28,12},{1,17},{... | collective-permute-start | bytes 4718600 | tf_op jit(solution)/shard_map/ppermute | solution.py:29
  177.5 36.3 %collective-permute-start.23 = (bf16[192,4096]{1,0:T(8,128)(2,1)}, bf16[192,4096]{1,0:T(8,128)(2,1)}, u32[]{:S(2)}, u32[]{:S(2)}) collective-permute-start(bf16[192,4096]{1,0:T(8,128)(2,1)} %get-tuple-element.180.refs_1_), channel_id=1, source_target_pairs={{0,8},{4,12},{8,0},{12,4},{16,24},{20,28},{24,16},{28,20},{1,9},{5... | collective-permute-start | bytes 4718600 | tf_op jit(solution)/shard_map/ppermute | solution.py:29
  217.3 36.6 %collective-permute-start.31 = (bf16[192,4096]{1,0:T(8,128)(2,1)}, bf16[192,4096]{1,0:T(8,128)(2,1)}, u32[]{:S(2)}, u32[]{:S(2)}) collective-permute-start(bf16[192,4096]{1,0:T(8,128)(2,1)} %get-tuple-element.188), channel_id=1, source_target_pairs={{0,16},{4,20},{8,24},{12,28},{16,0},{20,4},{24,8},{28,12},{1,17},{... | collective-permute-start | bytes 4718600 | tf_op jit(solution)/shard_map/ppermute | solution.py:29
  217.9 36.3 %collective-permute-start.30 = (bf16[192,4096]{1,0:T(8,128)(2,1)}, bf16[192,4096]{1,0:T(8,128)(2,1)}, u32[]{:S(2)}, u32[]{:S(2)}) collective-permute-start(bf16[192,4096]{1,0:T(8,128)(2,1)} %get-tuple-element.187.refs_11_), channel_id=1, source_target_pairs={{0,8},{4,12},{8,0},{12,4},{16,24},{20,28},{24,16},{28,20},{1,9},{5... | collective-permute-start | bytes 4718600 | tf_op jit(solution)/shard_map/ppermute | solution.py:29
  224.7 28.4 %collective-permute-start.28 = (bf16[256,2048]{1,0:T(8,128)(2,1)}, bf16[256,2048]{1,0:T(8,128)(2,1)}, u32[]{:S(2)}, u32[]{:S(2)}) collective-permute-start(bf16[256,2048]{1,0:T(8,128)(2,1)} %shard_map.271.refs_11_.refs_1_), channel_id=1, source_target_pairs={{0,1},{1,0},{2,3},{3,2},{4,5},{5,4},{6,7},{7,6},{8,9},{9,8},{10,11... | collective-permute-start | bytes 3145736 | tf_op jit(solution)/shard_map/ppermute | solution.py:34
  229.3 29.3 %collective-permute-start.27 = (bf16[256,2048]{1,0:T(8,128)(2,1)}, bf16[256,2048]{1,0:T(8,128)(2,1)}, u32[]{:S(2)}, u32[]{:S(2)}) collective-permute-start(bf16[256,2048]{1,0:T(8,128)(2,1)} %shard_map.271.refs_11_.refs_1_), channel_id=1, source_target_pairs={{0,4},{4,0},{8,12},{12,8},{16,20},{20,16},{24,28},{28,24},{1,5},{5... | collective-permute-start | bytes 3145736 | tf_op jit(solution)/shard_map/ppermute | solution.py:29
  253.9 19.5 %collective-permute-start.33 = (bf16[192,4096]{1,0:T(8,128)(2,1)}, bf16[192,4096]{1,0:T(8,128)(2,1)}, u32[]{:S(2)}, u32[]{:S(2)}) collective-permute-start(bf16[192,4096]{1,0:T(8,128)(2,1)} %collective-permute-done.31.refs_1_.refs_23_.refs_30_.refs_22_.refs_29_), channel_id=1, source_target_pairs={{0,4},{4,0},{8,12},{12,8},{16,20},{20,16},{24,28},{28,24},{1,5},{5... | collective-permute-start | bytes 4718600 | tf_op jit(solution)/shard_map/ppermute | solution.py:29
  254.2 19.2 %collective-permute-start.32 = (bf16[192,4096]{1,0:T(8,128)(2,1)}, bf16[192,4096]{1,0:T(8,128)(2,1)}, u32[]{:S(2)}, u32[]{:S(2)}) collective-permute-start(bf16[192,4096]{1,0:T(8,128)(2,1)} %collective-permute-done.30.refs_0_.refs_22_.refs_28_.refs_21_.refs_27_), channel_id=1, source_target_pairs={{0,4},{4,0},{8,12},{12,8},{16,20},{20,16},{24,28},{28,24},{1,5},{5... | collective-permute-start | bytes 4718600 | tf_op jit(solution)/shard_map/ppermute | solution.py:29
  257.3 15.3 %collective-permute-start.35 = (bf16[64,4096]{1,0:T(8,128)(2,1)}, bf16[64,4096]{1,0:T(8,128)(2,1)}, u32[]{:S(2)}, u32[]{:S(2)}) collective-permute-start(bf16[64,4096]{1,0:T(8,128)(2,1)} %get-tuple-element.195), channel_id=1, source_target_pairs={{0,16},{4,20},{8,24},{12,28},{16,0},{20,4},{24,8},{28,12},{1,17},{... | collective-permute-start | bytes 1572872 | tf_op jit(solution)/shard_map/ppermute | solution.py:29
  258.6 14.4 %collective-permute-start.34 = (bf16[64,4096]{1,0:T(8,128)(2,1)}, bf16[64,4096]{1,0:T(8,128)(2,1)}, u32[]{:S(2)}, u32[]{:S(2)}) collective-permute-start(bf16[64,4096]{1,0:T(8,128)(2,1)} %get-tuple-element.189.refs_5_), channel_id=1, source_target_pairs={{0,8},{4,12},{8,0},{12,4},{16,24},{20,28},{24,16},{28,20},{1,9},{5... | collective-permute-start | bytes 1572872 | tf_op jit(solution)/shard_map/ppermute | solution.py:29
  288.8 14.5 %collective-permute-start.38 = (bf16[256,7168]{1,0:T(8,128)(2,1)}, bf16[256,7168]{1,0:T(8,128)(2,1)}, u32[]{:S(2)}, u32[]{:S(2)}) collective-permute-start(bf16[256,7168]{1,0:T(8,128)(2,1)} %get-tuple-element.201.refs_2_.refs_5_.refs_0_.refs_6_), channel_id=1, source_target_pairs={{0,4},{4,0},{8,12},{12,8},{16,20},{20,16},{24,28},{28,24},{1,5},{5... | collective-permute-start | bytes 11010056 | tf_op jit(solution)/shard_map/ppermute | solution.py:29
  289.0 14.2 %collective-permute-start.42 = (bf16[256,7168]{1,0:T(8,128)(2,1)}, bf16[256,7168]{1,0:T(8,128)(2,1)}, u32[]{:S(2)}, u32[]{:S(2)}) collective-permute-start(bf16[256,7168]{1,0:T(8,128)(2,1)} %get-tuple-element.210.refs_5_.refs_2_.refs_0_.refs_6_), channel_id=1, source_target_pairs={{0,4},{4,0},{8,12},{12,8},{16,20},{20,16},{24,28},{28,24},{1,5},{5... | collective-permute-start | bytes 11010056 | tf_op jit(solution)/shard_map/ppermute | solution.py:29
  289.4 13.6 %collective-permute-start.41 = (bf16[256,1024]{1,0:T(8,128)(2,1)}, bf16[256,1024]{1,0:T(8,128)(2,1)}, u32[]{:S(2)}, u32[]{:S(2)}) collective-permute-start(bf16[256,1024]{1,0:T(8,128)(2,1)} %broadcast_select_fusion.refs_7_.refs_0_.refs_1_), channel_id=1, source_target_pairs={{0,4},{4,0},{8,12},{12,8},{16,20},{20,16},{24,28},{28,24},{1,5},{5... | collective-permute-start | bytes 1572872 | tf_op jit(solution)/shard_map/ppermute | solution.py:29
  310.2 26.4 %collective-permute-start.47 = (bf16[256,2048]{1,0:T(8,128)(2,1)}, bf16[256,2048]{1,0:T(8,128)(2,1)}, u32[]{:S(2)}, u32[]{:S(2)}) collective-permute-start(bf16[256,2048]{1,0:T(8,128)(2,1)} %get-tuple-element.218), channel_id=1, source_target_pairs={{0,16},{4,20},{8,24},{12,28},{16,0},{20,4},{24,8},{28,12},{1,17},{... | collective-permute-start | bytes 3145736 | tf_op jit(solution)/shard_map/ppermute | solution.py:29
  310.9 26.4 %collective-permute-start.46 = (bf16[256,2048]{1,0:T(8,128)(2,1)}, bf16[256,2048]{1,0:T(8,128)(2,1)}, u32[]{:S(2)}, u32[]{:S(2)}) collective-permute-start(bf16[256,2048]{1,0:T(8,128)(2,1)} %get-tuple-element.211.refs_8_), channel_id=1, source_target_pairs={{0,8},{4,12},{8,0},{12,4},{16,24},{20,28},{24,16},{28,20},{1,9},{5... | collective-permute-start | bytes 3145736 | tf_op jit(solution)/shard_map/ppermute | solution.py:29
  328.0 13.4 %collective-permute-start.50 = (bf16[256,2048]{1,0:T(8,128)(2,1)}, bf16[256,2048]{1,0:T(8,128)(2,1)}, u32[]{:S(2)}, u32[]{:S(2)}) collective-permute-start(bf16[256,2048]{1,0:T(8,128)(2,1)} %get-tuple-element.223), channel_id=1, source_target_pairs={{0,4},{4,0},{8,12},{12,8},{16,20},{20,16},{24,28},{28,24},{1,5},{5... | collective-permute-start | bytes 3145736 | tf_op jit(solution)/shard_map/ppermute | solution.py:29
  328.1 13.3 %collective-permute-start.51 = (bf16[256,2048]{1,0:T(8,128)(2,1)}, bf16[256,2048]{1,0:T(8,128)(2,1)}, u32[]{:S(2)}, u32[]{:S(2)}) collective-permute-start(bf16[256,2048]{1,0:T(8,128)(2,1)} %get-tuple-element.227), channel_id=1, source_target_pairs={{0,4},{4,0},{8,12},{12,8},{16,20},{20,16},{24,28},{28,24},{1,5},{5... | collective-permute-start | bytes 3145736 | tf_op jit(solution)/shard_map/ppermute | solution.py:29
  335.2 26.4 %collective-permute-start.45 = (bf16[256,2048]{1,0:T(8,128)(2,1)}, bf16[256,2048]{1,0:T(8,128)(2,1)}, u32[]{:S(2)}, u32[]{:S(2)}) collective-permute-start(bf16[256,2048]{1,0:T(8,128)(2,1)} %get-tuple-element.216), channel_id=1, source_target_pairs={{0,16},{4,20},{8,24},{12,28},{16,0},{20,4},{24,8},{28,12},{1,17},{... | collective-permute-start | bytes 3145736 | tf_op jit(solution)/shard_map/ppermute | solution.py:29
  336.7 26.4 %collective-permute-start.44 = (bf16[256,2048]{1,0:T(8,128)(2,1)}, bf16[256,2048]{1,0:T(8,128)(2,1)}, u32[]{:S(2)}, u32[]{:S(2)}) collective-permute-start(bf16[256,2048]{1,0:T(8,128)(2,1)} %get-tuple-element.215.refs_3_), channel_id=1, source_target_pairs={{0,8},{4,12},{8,0},{12,4},{16,24},{20,28},{24,16},{28,20},{1,9},{5... | collective-permute-start | bytes 3145736 | tf_op jit(solution)/shard_map/ppermute | solution.py:29
  344.3 27.2 %collective-permute-start.52 = (bf16[256,2048]{1,0:T(8,128)(2,1)S(1)}, bf16[256,2048]{1,0:T(8,128)(2,1)S(1)}, u32[]{:S(2)}, u32[]{:S(2)}) collective-permute-start(bf16[256,2048]{1,0:T(8,128)(2,1)S(1)} %add_convert_fusion.1.refs_17_), channel_id=1, source_target_pairs={{0,1},{1,0},{2,3},{3,2},{4,5},{5,4},{6,7},{7,6},{8,9},{9,8},{10,11... | collective-permute-start | bytes 3145736 | tf_op jit(solution)/shard_map/ppermute | solution.py:34
  348.9 32.8 %collective-permute-start.49 = (bf16[128,2048]{1,0:T(8,128)(2,1)}, bf16[128,2048]{1,0:T(8,128)(2,1)}, u32[]{:S(2)}, u32[]{:S(2)}) collective-permute-start(bf16[128,2048]{1,0:T(8,128)(2,1)} %get-tuple-element.221), channel_id=1, source_target_pairs={{0,8},{4,12},{8,0},{12,4},{16,24},{20,28},{24,16},{28,20},{1,9},{5... | collective-permute-start | bytes 1572872 | tf_op jit(solution)/shard_map/ppermute | solution.py:29
  350.2 31.4 %collective-permute-start.48 = (bf16[128,2048]{1,0:T(8,128)(2,1)}, bf16[128,2048]{1,0:T(8,128)(2,1)}, u32[]{:S(2)}, u32[]{:S(2)}) collective-permute-start(bf16[128,2048]{1,0:T(8,128)(2,1)} %get-tuple-element.220), channel_id=1, source_target_pairs={{0,16},{4,20},{8,24},{12,28},{16,0},{20,4},{24,8},{28,12},{1,17},{... | collective-permute-start | bytes 1572872 | tf_op jit(solution)/shard_map/ppermute | solution.py:29
  386.4 154.5 %reduce-scatter.8.cloned.1.call-start = ((), (), s32[]{:S(2)}) async-start(), calls=%async_computation.6 | async-start | bytes 2621440 | tf_op jit(solution)/shard_map/reduce_scatter | solution.py:1054
  386.4 25.0 %collective-permute-start.56 = (bf16[128,2048]{1,0:T(8,128)(2,1)}, bf16[128,2048]{1,0:T(8,128)(2,1)}, u32[]{:S(2)}, u32[]{:S(2)}) collective-permute-start(bf16[128,2048]{1,0:T(8,128)(2,1)} %get-tuple-element.239), channel_id=1, source_target_pairs={{0,8},{4,12},{8,0},{12,4},{16,24},{20,28},{24,16},{28,20},{1,9},{5... | collective-permute-start | bytes 1572872 | tf_op jit(solution)/shard_map/ppermute | solution.py:29
  388.0 23.4 %collective-permute-start.57 = (bf16[128,2048]{1,0:T(8,128)(2,1)}, bf16[128,2048]{1,0:T(8,128)(2,1)}, u32[]{:S(2)}, u32[]{:S(2)}) collective-permute-start(bf16[128,2048]{1,0:T(8,128)(2,1)} %get-tuple-element.230.refs_10_), channel_id=1, source_target_pairs={{0,16},{4,20},{8,24},{12,28},{16,0},{20,4},{24,8},{28,12},{1,17},{... | collective-permute-start | bytes 1572872 | tf_op jit(solution)/shard_map/ppermute | solution.py:29
  388.6 40.4 %collective-permute-start.53 = (f32[256,1024]{1,0:T(8,128)}, f32[256,1024]{1,0:T(8,128)}, u32[]{:S(2)}, u32[]{:S(2)}) collective-permute-start(f32[256,1024]{1,0:T(8,128)} %get-tuple-element.231), channel_id=1, source_target_pairs={{4,1},{1,2},{5,3},{2,4},{6,5},{3,6},{12,9},{9,10},{13,11},{10,12},... | collective-permute-start | bytes 3145736 | tf_op jit(solution)/shard_map/ppermute | solution.py:1336
  397.0 31.9 %collective-permute-start.60 = (bf16[256,2048]{1,0:T(8,128)(2,1)}, bf16[256,2048]{1,0:T(8,128)(2,1)}, u32[]{:S(2)}, u32[]{:S(2)}) collective-permute-start(bf16[256,2048]{1,0:T(8,128)(2,1)} %get-tuple-element.244), channel_id=1, source_target_pairs={{0,16},{4,20},{8,24},{12,28},{16,0},{20,4},{24,8},{28,12},{1,17},{... | collective-permute-start | bytes 3145736 | tf_op jit(solution)/shard_map/ppermute | solution.py:29
  398.6 30.4 %collective-permute-start.59 = (bf16[256,2048]{1,0:T(8,128)(2,1)}, bf16[256,2048]{1,0:T(8,128)(2,1)}, u32[]{:S(2)}, u32[]{:S(2)}) collective-permute-start(bf16[256,2048]{1,0:T(8,128)(2,1)} %get-tuple-element.236.refs_35_), channel_id=1, source_target_pairs={{0,8},{4,12},{8,0},{12,4},{16,24},{20,28},{24,16},{28,20},{1,9},{5... | collective-permute-start | bytes 3145736 | tf_op jit(solution)/shard_map/ppermute | solution.py:29
  436.1 18.9 %collective-permute-start.63 = (bf16[256,2048]{1,0:T(8,128)(2,1)S(1)}, bf16[256,2048]{1,0:T(8,128)(2,1)}, u32[]{:S(2)}, u32[]{:S(2)}) collective-permute-start(bf16[256,2048]{1,0:T(8,128)(2,1)S(1)} %copy-done.8), channel_id=1, source_target_pairs={{0,4},{4,0},{8,12},{12,8},{16,20},{20,16},{24,28},{28,24},{1,5},{5... | collective-permute-start | bytes 3145736 | tf_op jit(solution)/shard_map/ppermute | solution.py:29
  440.4 14.7 %collective-permute-start.64 = (bf16[256,2048]{1,0:T(8,128)(2,1)S(1)}, bf16[256,2048]{1,0:T(8,128)(2,1)}, u32[]{:S(2)}, u32[]{:S(2)}) collective-permute-start(bf16[256,2048]{1,0:T(8,128)(2,1)S(1)} %copy-done.9), channel_id=1, source_target_pairs={{0,4},{4,0},{8,12},{12,8},{16,20},{20,16},{24,28},{28,24},{1,5},{5... | collective-permute-start | bytes 3145736 | tf_op jit(solution)/shard_map/ppermute | solution.py:29
  440.4 14.4 %collective-permute-start.65 = (bf16[128,2048]{1,0:T(8,128)(2,1)S(1)}, bf16[128,2048]{1,0:T(8,128)(2,1)}, u32[]{:S(2)}, u32[]{:S(2)}) collective-permute-start(bf16[128,2048]{1,0:T(8,128)(2,1)S(1)} %copy-done.23), channel_id=1, source_target_pairs={{0,8},{4,12},{8,0},{12,4},{16,24},{20,28},{24,16},{28,20},{1,9},{5... | collective-permute-start | bytes 1572872 | tf_op jit(solution)/shard_map/ppermute | solution.py:29
  440.9 14.1 %collective-permute-start.66 = (bf16[128,2048]{1,0:T(8,128)(2,1)S(1)}, bf16[128,2048]{1,0:T(8,128)(2,1)}, u32[]{:S(2)}, u32[]{:S(2)}) collective-permute-start(bf16[128,2048]{1,0:T(8,128)(2,1)S(1)} %copy-done.22), channel_id=1, source_target_pairs={{0,16},{4,20},{8,24},{12,28},{16,0},{20,4},{24,8},{28,12},{1,17},{... | collective-permute-start | bytes 1572872 | tf_op jit(solution)/shard_map/ppermute | solution.py:29
  442.4 29.3 %collective-permute-start.62 = (bf16[256,2048]{1,0:T(8,128)(2,1)}, bf16[256,2048]{1,0:T(8,128)(2,1)}, u32[]{:S(2)}, u32[]{:S(2)}) collective-permute-start(bf16[256,2048]{1,0:T(8,128)(2,1)} %add_convert_fusion.refs_4_), channel_id=1, source_target_pairs={{0,1},{1,0},{2,3},{3,2},{4,5},{5,4},{6,7},{7,6},{8,9},{9,8},{10,11... | collective-permute-start | bytes 3145736 | tf_op jit(solution)/shard_map/ppermute | solution.py:34
  462.1 24.9 %collective-permute-start.71 = (bf16[256,2048]{1,0:T(8,128)(2,1)}, bf16[256,2048]{1,0:T(8,128)(2,1)}, u32[]{:S(2)}, u32[]{:S(2)}) collective-permute-start(bf16[256,2048]{1,0:T(8,128)(2,1)} %get-tuple-element.264), channel_id=1, source_target_pairs={{0,16},{4,20},{8,24},{12,28},{16,0},{20,4},{24,8},{28,12},{1,17},{... | collective-permute-start | bytes 3145736 | tf_op jit(solution)/shard_map/ppermute | solution.py:29
  463.6 24.5 %collective-permute-start.70 = (bf16[256,2048]{1,0:T(8,128)(2,1)}, bf16[256,2048]{1,0:T(8,128)(2,1)}, u32[]{:S(2)}, u32[]{:S(2)}) collective-permute-start(bf16[256,2048]{1,0:T(8,128)(2,1)} %get-tuple-element.257.refs_6_), channel_id=1, source_target_pairs={{0,8},{4,12},{8,0},{12,4},{16,24},{20,28},{24,16},{28,20},{1,9},{5... | collective-permute-start | bytes 3145736 | tf_op jit(solution)/shard_map/ppermute | solution.py:29
  494.6 78.2 %reduce-scatter.14.cloned.1.call-start = ((), (), s32[]{:S(2)}) async-start(), calls=%async_computation.9 | async-start | bytes 1310720 | tf_op jit(solution)/shard_map/reduce_scatter | solution.py:920
  496.6 15.1 %collective-permute-start.77 = (bf16[128,2048]{1,0:T(8,128)(2,1)}, bf16[128,2048]{1,0:T(8,128)(2,1)}, u32[]{:S(2)}, u32[]{:S(2)}) collective-permute-start(bf16[128,2048]{1,0:T(8,128)(2,1)} %get-tuple-element.274), channel_id=1, source_target_pairs={{0,8},{4,12},{8,0},{12,4},{16,24},{20,28},{24,16},{28,20},{1,9},{5... | collective-permute-start | bytes 1572872 | tf_op jit(solution)/shard_map/ppermute | solution.py:29
  498.0 15.1 %collective-permute-start.76 = (bf16[128,2048]{1,0:T(8,128)(2,1)}, bf16[128,2048]{1,0:T(8,128)(2,1)}, u32[]{:S(2)}, u32[]{:S(2)}) collective-permute-start(bf16[128,2048]{1,0:T(8,128)(2,1)} %get-tuple-element.267.refs_10_), channel_id=1, source_target_pairs={{0,16},{4,20},{8,24},{12,28},{16,0},{20,4},{24,8},{28,12},{1,17},{... | collective-permute-start | bytes 1572872 | tf_op jit(solution)/shard_map/ppermute | solution.py:29
  500.2 35.3 %collective-permute-start.74 = (bf16[256,2048]{1,0:T(8,128)(2,1)}, bf16[256,2048]{1,0:T(8,128)(2,1)}, u32[]{:S(2)}, u32[]{:S(2)}) collective-permute-start(bf16[256,2048]{1,0:T(8,128)(2,1)} %get-tuple-element.258.refs_17_), channel_id=1, source_target_pairs={{0,8},{4,12},{8,0},{12,4},{16,24},{20,28},{24,16},{28,20},{1,9},{5... | collective-permute-start | bytes 3145736 | tf_op jit(solution)/shard_map/ppermute | solution.py:29
  502.6 32.9 %collective-permute-start.75 = (bf16[256,2048]{1,0:T(8,128)(2,1)}, bf16[256,2048]{1,0:T(8,128)(2,1)}, u32[]{:S(2)}, u32[]{:S(2)}) collective-permute-start(bf16[256,2048]{1,0:T(8,128)(2,1)} %get-tuple-element.272), channel_id=1, source_target_pairs={{0,16},{4,20},{8,24},{12,28},{16,0},{20,4},{24,8},{28,12},{1,17},{... | collective-permute-start | bytes 3145736 | tf_op jit(solution)/shard_map/ppermute | solution.py:29
  516.7 89.5 %reduce-scatter.12.cloned.1.call-start = ((), (), s32[]{:S(2)}) async-start(), calls=%async_computation.8 | async-start | bytes 1310720 | tf_op jit(solution)/shard_map/reduce_scatter | solution.py:920
  519.2 38.9 %collective-permute-start.72 = (bf16[256,2048]{1,0:T(8,128)(2,1)}, bf16[256,2048]{1,0:T(8,128)(2,1)}, u32[]{:S(2)}, u32[]{:S(2)}) collective-permute-start(bf16[256,2048]{1,0:T(8,128)(2,1)} %get-tuple-element.269.refs_3_), channel_id=1, source_target_pairs={{0,8},{4,12},{8,0},{12,4},{16,24},{20,28},{24,16},{28,20},{1,9},{5... | collective-permute-start | bytes 3145736 | tf_op jit(solution)/shard_map/ppermute | solution.py:29
  519.8 38.3 %collective-permute-start.73 = (bf16[256,2048]{1,0:T(8,128)(2,1)}, bf16[256,2048]{1,0:T(8,128)(2,1)}, u32[]{:S(2)}, u32[]{:S(2)}) collective-permute-start(bf16[256,2048]{1,0:T(8,128)(2,1)} %get-tuple-element.270), channel_id=1, source_target_pairs={{0,16},{4,20},{8,24},{12,28},{16,0},{20,4},{24,8},{28,12},{1,17},{... | collective-permute-start | bytes 3145736 | tf_op jit(solution)/shard_map/ppermute | solution.py:29
  539.7 27.4 %collective-permute-start.81 = (bf16[128,2048]{1,0:T(8,128)(2,1)}, bf16[128,2048]{1,0:T(8,128)(2,1)}, u32[]{:S(2)}, u32[]{:S(2)}) collective-permute-start(bf16[128,2048]{1,0:T(8,128)(2,1)} %get-tuple-element.281), channel_id=1, source_target_pairs={{0,8},{4,12},{8,0},{12,4},{16,24},{20,28},{24,16},{28,20},{1,9},{5... | collective-permute-start | bytes 1572872 | tf_op jit(solution)/shard_map/ppermute | solution.py:29
  540.3 27.9 %collective-permute-start.80 = (bf16[128,2048]{1,0:T(8,128)(2,1)}, bf16[128,2048]{1,0:T(8,128)(2,1)}, u32[]{:S(2)}, u32[]{:S(2)}) collective-permute-start(bf16[128,2048]{1,0:T(8,128)(2,1)} %get-tuple-element.275.refs_3_), channel_id=1, source_target_pairs={{0,16},{4,20},{8,24},{12,28},{16,0},{20,4},{24,8},{28,12},{1,17},{... | collective-permute-start | bytes 1572872 | tf_op jit(solution)/shard_map/ppermute | solution.py:29
  575.0 58.3 %reduce-scatter.10.cloned.1.call-start = ((), (), s32[]{:S(2)}) async-start(), calls=%async_computation.7 | async-start | bytes 1310720 | tf_op jit(solution)/shard_map/reduce_scatter | solution.py:920
  575.0 13.7 %collective-permute-start.78 = (bf16[128,2048]{1,0:T(8,128)(2,1)S(1)}, bf16[128,2048]{1,0:T(8,128)(2,1)}, u32[]{:S(2)}, u32[]{:S(2)}) collective-permute-start(bf16[128,2048]{1,0:T(8,128)(2,1)S(1)} %copy-done.13), channel_id=1, source_target_pairs={{0,16},{4,20},{8,24},{12,28},{16,0},{20,4},{24,8},{28,12},{1,17},{... | collective-permute-start | bytes 1572872 | tf_op jit(solution)/shard_map/ppermute | solution.py:29
  575.9 12.8 %collective-permute-start.79 = (bf16[128,2048]{1,0:T(8,128)(2,1)S(1)}, bf16[128,2048]{1,0:T(8,128)(2,1)}, u32[]{:S(2)}, u32[]{:S(2)}) collective-permute-start(bf16[128,2048]{1,0:T(8,128)(2,1)S(1)} %copy-done.21), channel_id=1, source_target_pairs={{0,8},{4,12},{8,0},{12,4},{16,24},{20,28},{24,16},{28,20},{1,9},{5... | collective-permute-start | bytes 1572872 | tf_op jit(solution)/shard_map/ppermute | solution.py:29
  (53 other events, 285.1 us)
Sparse Core Ops, SparseCore 0:
  386.5 34.3 reduce-scatter.5
  494.7 42.4 reduce-scatter.7
  540.1 26.4 reduce-scatter.13
  575.1 26.1 reduce-scatter.11
  603.5 29.7 reduce-scatter.9

commit v5 on v4

--- a/solution.py
+++ b/solution.py
@@ -1437,6 +1437,7 @@
             token = advance(thirds=[of_reduce], deps=(token,))
         else:
             token = advance(thirds=[of_attention], deps=(token, upper_reduce.share, moved_result))
+            token = advance([of_reduce], deps=(token,))
         far, near_leave = after(far, token, near_leave), after(near_leave, token)
         far = (wide(far) + wide(far_leave)).astype(bf16)
         far = (far, swap_seq(far, 1))
@@ -1444,8 +1445,8 @@
         if above is not None:
             back = [(own, swap(after(own, token), 1)) for own in own_back[:2]]
             of_expand = Reduction(expand_group(kept, back))
-            token = advance([of_reduce], deps=(token, back[0][1], back[1][1], of_attention.second_x, of_attention.second_y))
-            token = advance([of_expand], deps=(token,))
+            deps = (back[0][1], back[1][1], of_attention.second_x, of_attention.second_y)
+            token = advance([of_expand], deps=(token,) + deps)
         deps = (token, of_expand.from_x, of_expand.from_y) if above is None else (token,)
         grad, own_lower, early_sums, key_grad = first_back(
             query_grad, (near, near_leave, far[1]), packs[0], stream, middle_grad, vec, deps

time: 651 us -> 647 us (level)
    ppermute x78, waiting for transfers between devices: 164 us -> 144 us  [swap(): return lax.ppermute(array, 'dp', [(i, i ^ bit) for i in range(count)])]
    ppermute x6, waiting for transfers between devices: 32.3 us -> 47.2 us  [swap_seq(): return lax.ppermute(array, 'seq', [(i, i ^ bit) for i in range(count)])]
  transfers between devices with their start and end apart: 93 -> 93, of which waited for: 42 -> 39; matrix products, arithmetic and copies ran while one was open for 5% -> 5% of each run, Pallas kernels for 38% -> 38%
where the time goes in v5:
time: 647 us; the launch traced here: 639 us
  Pallas kernels  273 us (42%)
  waiting for transfers between devices  217 us (34%)
  starting transfers between devices  90.5 us (14%)
  other arithmetic  25.9 us (4%)
  local copies, waits for them, and re-layouts  16.9 us (3%)
  between operations  15.6 us (2%)
    pallas_call x25, Pallas kernels, run_flow(): pl.pallas_call(kernel, out_shape=[jax.ShapeDtypeStruct(shape, kind) for s...  163 us
    ppermute x78, waiting for transfers between devices, swap(): return lax.ppermute(array, 'dp', [(i, i ^ bit) for i in range(count)])  144 us
    pallas_call x18, Pallas kernels, run(): pl.pallas_call(kernel, out_shape=shapes, grid_spec=pltpu.PrefetchScalarGr...  110 us
    ppermute x78, starting transfers between devices, swap(): return lax.ppermute(array, 'dp', [(i, i ^ bit) for i in range(count)])  67.5 us
    ppermute x6, waiting for transfers between devices, swap_seq(): return lax.ppermute(array, 'seq', [(i, i ^ bit) for i in range(count)])  47.2 us
    reduce_scatter x4, waiting for transfers between devices, scatter(): self.share = lax.psum_scatter(piece, 'seq', scatter_dimension=0, tiled=True)  25.5 us
    ppermute x6, starting transfers between devices, swap_seq(): return lax.ppermute(array, 'seq', [(i, i ^ bit) for i in range(count)])  17.8 us
  transfers between devices with their start and end apart: 93, of which 39 were waited for; matrix products, arithmetic and copies ran while one was open for 5% of the time, Pallas kernels for 38%

profile of v5, /device:TPU:0, one launch (start us, length us, event | category | flops | bytes accessed | tf_op | source)
XLA Modules:
  0.0 639.2 jit_solution(3861156838156263724)
XLA Ops:
  9.0 3.7 shard_map.254.refs_6_.refs_0_.refs_1_.refs_5_.refs_7_
  12.7 3.0 collective-permute-start.3
  18.6 6.2 shard_map.255.refs_0_.refs_2_.refs_16_.refs_26_.refs_1_.refs_6_.refs_5_.refs_15_.refs_25_.refs_7_
  24.8 4.3 shard_map.256
  31.0 13.7 %collective-permute-done.3.refs_1_.refs_4_.refs_5_.refs_10_.refs_9_.refs_11_ = bf16[160,4096]{1,0:T(8,128)(2,1)} collective-permute-done((bf16[160,4096]{1,0:T(8,128)(2,1)}, bf16[160,4096]{1,0:T(8,128)(2,1)}, u32[]{:S(2)}, u32[]{:S(2)}) %collective-permute-start.3) | collective-permute-done | bytes 1310752 | tf_op jit(solution)/shard_map/ppermute | solution.py:29
  46.2 5.1 shard_map.257
  54.1 3.4 collective-permute-start.4
  57.5 5.5 collective-permute-start.5
  66.0 23.5 %collective-permute-done.7.refs_1_.refs_7_.refs_8_.refs_13_.refs_20_.refs_12_.refs_19_.refs_14_ = bf16[208,4096]{1,0:T(8,128)(2,1)} collective-permute-done((bf16[208,4096]{1,0:T(8,128)(2,1)}, bf16[208,4096]{1,0:T(8,128)(2,1)}, u32[]{:S(2)}, u32[]{:S(2)}) %collective-permute-start.7) | collective-permute-done | bytes 1703968 | tf_op jit(solution)/shard_map/ppermute | solution.py:29
  99.2 4.2 collective-permute-done.1.refs_1_.refs_2_.refs_7_.refs_6_.refs_8_
  103.4 3.3 shard_map.259
  109.6 4.8 shard_map.261.refs_11_.refs_1_
  114.3 3.8 collective-permute-start.13
  118.1 3.9 shard_map.262.refs_1_.refs_7_.refs_0_
  122.1 4.4 shard_map.263
  129.2 3.5 collective-permute-done.16.refs_1_.refs_23_.refs_30_.refs_22_.refs_29_
  138.9 3.0 collective-permute-done.13.refs_3_
  142.4 4.3 shard_map.265
  147.2 12.4 %shard_map.266 = (bf16[256,1024]{1,0:T(8,128)(2,1)}, f32[8,8,256]{2,1,0:T(8,128)}) custom-call(s32[2]{0:T(128)} %pad_add_fusion.place, bf16[256,1024]{1,0:T(8,128)(2,1)} %shard_map.262.refs_1_.refs_7_.refs_0_, bf16[256,2048]{1,0:T(8,128)(2,1)} %shard_map.261.refs_11_.refs_1_, bf16[256,2048]{1,0:T(8,128)(2,1)} %collective-permute-done.12.refs_2_, ...), custom_call_target="tpu_custom_call" | custom-call | bytes 45000000 | tf_op jit(solution)/shard_map/pallas_call | solution.py:332
  159.5 12.8 %collective-permute-done.20.refs_1_.refs_33_.refs_5_.refs_10_.refs_9_.refs_11_.refs_32_ = bf16[192,4096]{1,0:T(8,128)(2,1)} collective-permute-done((bf16[192,4096]{1,0:T(8,128)(2,1)}, bf16[192,4096]{1,0:T(8,128)(2,1)}, u32[]{:S(2)}, u32[]{:S(2)}) %collective-permute-start.20) | collective-permute-done | bytes 1572896 | tf_op jit(solution)/shard_map/ppermute | solution.py:29
  173.2 2.9 shard_map.267
  179.0 4.5 shard_map.268
  183.5 12.9 %shard_map.269 = (f32[256,1024]{1,0:T(8,128)}, bf16[256,7168]{1,0:T(8,128)(2,1)}, bf16[256,4096]{1,0:T(8,128)(2,1)}, f32[256,1024]{1,0:T(8,128)}, bf16[256,1024]{1,0:T(8,128)(2,1)}) custom-call(s32[2]{0:T(128)} %pad_add_fusion.place, bf16[256,1024]{1,0:T(8,128)(2,1)} %get-tuple-element.171.refs_6_.refs_0_, ...), custom_call_target="tpu_custom_call" | custom-call | bytes 36000000 | tf_op jit(solution)/shard_map/pallas_call | solution.py:392
  196.4 16.3 %collective-permute-done.24.refs_1_.refs_8_.refs_13_.refs_20_.refs_12_.refs_19_.refs_14_ = bf16[192,4096]{1,0:T(8,128)(2,1)} collective-permute-done((bf16[192,4096]{1,0:T(8,128)(2,1)}, bf16[192,4096]{1,0:T(8,128)(2,1)}, u32[]{:S(2)}, u32[]{:S(2)}) %collective-permute-start.24) | collective-permute-done | bytes 1572896 | tf_op jit(solution)/shard_map/ppermute | solution.py:29
  214.4 2.9 shard_map.270
  219.9 4.8 shard_map.271.refs_11_.refs_1_
  224.7 4.6 collective-permute-start.28
  229.3 4.0 shard_map.272.refs_4_.refs_5_.refs_0_
  233.3 19.8 %collective-permute-done.28.refs_3_ = bf16[256,2048]{1,0:T(8,128)(2,1)} collective-permute-done((bf16[256,2048]{1,0:T(8,128)(2,1)}, bf16[256,2048]{1,0:T(8,128)(2,1)}, u32[]{:S(2)}, u32[]{:S(2)}) %collective-permute-start.28) | collective-permute-done | bytes 1048608 | tf_op jit(solution)/shard_map/ppermute | solution.py:34
  260.1 12.6 %shard_map.274 = (bf16[256,1024]{1,0:T(8,128)(2,1)}, f32[8,8,256]{2,1,0:T(8,128)}) custom-call(s32[2]{0:T(128)} %pad_add_fusion.place, bf16[256,1024]{1,0:T(8,128)(2,1)} %shard_map.272.refs_4_.refs_5_.refs_0_, bf16[256,2048]{1,0:T(8,128)(2,1)} %shard_map.271.refs_11_.refs_1_, bf16[256,2048]{1,0:T(8,128)(2,1)} %collective-permute-done.27.refs_2_, ...), custom_call_target="tpu_custom_call" | custom-call | bytes 45000000 | tf_op jit(solution)/shard_map/pallas_call | solution.py:332
  276.0 12.9 %shard_map.275 = (f32[256,1024]{1,0:T(8,128)}, bf16[256,7168]{1,0:T(8,128)(2,1)}, bf16[256,4096]{1,0:T(8,128)(2,1)}, f32[256,1024]{1,0:T(8,128)}, bf16[256,1024]{1,0:T(8,128)(2,1)}) custom-call(s32[2]{0:T(128)} %pad_add_fusion.place, bf16[256,1024]{1,0:T(8,128)(2,1)} %get-tuple-element.190.refs_0_.refs_36_, f32[256,1024]{1,0:T(8,128)} %get-tuple-element.191.refs_1_.refs_4_, ...), custom_call_target="tpu_custom_call" | custom-call | bytes 36000000 | tf_op jit(solution)/shard_map/pallas_call | solution.py:392
  289.6 12.8 %shard_map.276 = (bf16[256,2048]{1,0:T(8,128)(2,1)}, bf16[256,2048]{1,0:T(8,128)(2,1)}, bf16[256,1024]{1,0:T(8,128)(2,1)}, f32[1,4096]{1,0:T(1,128)}, f32[256,10...) custom-call(s32[2]{0:T(128)} %pad_add_fusion.place, ...), custom_call_target="tpu_custom_call" | custom-call | bytes 36000000 | tf_op jit(solution)/shard_map/pallas_call | solution.py:392
  303.3 7.0 %shard_map.277 = (bf16[256,2048]{1,0:T(8,128)(2,1)}, bf16[256,2048]{1,0:T(8,128)(2,1)}, bf16[2,256,2048]{2,1,0:T(8,128)(2,1)}) custom-call(s32[2]{0:T(128)} %pad_add_fusion.place, bf16[256,1024]{1,0:T(8,128)(2,1)} %broadcast_select_fusion.refs_7_.refs_0_.refs_1_, bf16[256,1024]{1,0:T(8,128)(2,1)} %collective-permute-done.41.refs_1_, ...), custom_call_target="tpu_custom_call" | custom-call | bytes 21000000 | tf_op jit(solution)/shard_map/pallas_call | solution.py:392
  312.4 15.6 %shard_map.278 = (bf16[256,1024]{1,0:T(8,128)(2,1)}, bf16[256,2048]{1,0:T(8,128)(2,1)}, bf16[256,2048]{1,0:T(8,128)(2,1)}, bf16[256,2048]{1,0:T(8,128)(2,1)}, bf16[256,2048]{1,0:T(8,128)(2,1)}) custom-call(s32[2]{0:T(128)} %pad_add_fusion.place, bf16[256,1024]{1,0:T(8,128)(2,1)} %shard_map.272.refs_4_.refs_5_.refs_0_, ...), custom_call_target="tpu_custom_call" | custom-call | bytes 54000000 | tf_op jit(solution)/shard_map/pallas_call | solution.py:332
  328.6 6.5 %shard_map.279 = (bf16[256,2048]{1,0:T(8,128)(2,1)}, bf16[256,2048]{1,0:T(8,128)(2,1)}, bf16[2,256,2048]{2,1,0:T(8,128)(2,1)}) custom-call(s32[2]{0:T(128)} %pad_add_fusion.place, bf16[256,7168]{1,0:T(8,128)(2,1)} %get-tuple-element.201.refs_2_.refs_5_.refs_0_.refs_6_, bf16[256,7168]{1,0:T(8,128)(2,1)} %collective-permute-done.38.refs_3_.refs_1_.refs_7_, ...), custom_call_target="tpu_custom_call" | custom-call | bytes 21000000 | tf_op jit(solution)/shard_map/pallas_call | solution.py:392
  337.3 4.0 shard_map.280
  344.3 4.5 collective-permute-start.52
  350.8 10.7 %collective-permute-done.45.refs_19_.refs_2_ = bf16[256,2048]{1,0:T(8,128)(2,1)} collective-permute-done((bf16[256,2048]{1,0:T(8,128)(2,1)}, bf16[256,2048]{1,0:T(8,128)(2,1)}, u32[]{:S(2)}, u32[]{:S(2)}) %collective-permute-start.45) | collective-permute-done | bytes 1048608 | tf_op jit(solution)/shard_map/ppermute | solution.py:29
  363.0 8.6 %collective-permute-done.52.refs_3_ = bf16[256,2048]{1,0:T(8,128)(2,1)S(1)} collective-permute-done((bf16[256,2048]{1,0:T(8,128)(2,1)S(1)}, bf16[256,2048]{1,0:T(8,128)(2,1)S(1)}, u32[]{:S(2)}, u32[]{:S(2)}) %collective-permute-start.52) | collective-permute-done | bytes 1048608 | tf_op jit(solution)/shard_map/ppermute | solution.py:34
  372.5 8.6 %shard_map.281 = (f32[256,1024]{1,0:T(8,128)}, bf16[256,2048]{1,0:T(8,128)(2,1)}, f32[8,1024]{1,0:T(8,128)}, bf16[256,2048]{1,0:T(8,128)(2,1)}) custom-call(s32[2]{0:T(128)} %pad_add_fusion.place, bf16[256,1024]{1,0:T(8,128)(2,1)} %get-tuple-element.213.refs_6_.refs_0_, bf16[256,2048]{1,0:T(8,128)(2,1)} %get-tuple-element.222.refs_1_, ...), custom_call_target="tpu_custom_call" | custom-call | bytes 18000000 | tf_op jit(solution)/shard_map/pallas_call | solution.py:392
  381.7 4.7 shard_map.282
  390.5 6.6 %shard_map.283 = (bf16[256,2048]{1,0:T(8,128)(2,1)}, bf16[256,2048]{1,0:T(8,128)(2,1)}, bf16[2,256,2048]{2,1,0:T(8,128)(2,1)}) custom-call(s32[2]{0:T(128)} %pad_add_fusion.place, bf16[256,7168]{1,0:T(8,128)(2,1)} %get-tuple-element.201.refs_2_.refs_5_.refs_0_.refs_6_, bf16[256,7168]{1,0:T(8,128)(2,1)} %collective-permute-done.38.refs_3_.refs_1_.refs_7_, ...), custom_call_target="tpu_custom_call" | custom-call | bytes 21000000 | tf_op jit(solution)/shard_map/pallas_call | solution.py:392
  399.1 12.4 %shard_map.284 = (bf16[256,2048]{1,0:T(8,128)(2,1)}, bf16[256,2048]{1,0:T(8,128)(2,1)}, bf16[256,1024]{1,0:T(8,128)(2,1)}, f32[1,4096]{1,0:T(1,128)}, f32[256,10...) custom-call(s32[2]{0:T(128)} %pad_add_fusion.place, f32[256,1024]{1,0:T(8,128)} %get-tuple-element.232.refs_0_, ...), custom_call_target="tpu_custom_call" | custom-call | bytes 36000000 | tf_op jit(solution)/shard_map/pallas_call | solution.py:392
  411.5 15.8 %shard_map.285 = (bf16[256,1024]{1,0:T(8,128)(2,1)}, bf16[256,2048]{1,0:T(8,128)(2,1)}, bf16[256,2048]{1,0:T(8,128)(2,1)}, bf16[256,2048]{1,0:T(8,128)(2,1)}, bf16[256,2048]{1,0:T(8,128)(2,1)}) custom-call(s32[2]{0:T(128)} %pad_add_fusion.place, bf16[256,1024]{1,0:T(8,128)(2,1)} %shard_map.262.refs_1_.refs_7_.refs_0_, ...), custom_call_target="tpu_custom_call" | custom-call | bytes 54000000 | tf_op jit(solution)/shard_map/pallas_call | solution.py:332
  429.0 4.0 shard_map.286
  435.2 7.0 %shard_map.287 = (bf16[256,2048]{1,0:T(8,128)(2,1)}, bf16[256,2048]{1,0:T(8,128)(2,1)}, bf16[2,256,2048]{2,1,0:T(8,128)(2,1)}) custom-call(s32[2]{0:T(128)} %pad_add_fusion.place, bf16[256,2048]{1,0:T(8,128)(2,1)} %get-tuple-element.229.refs_6_.refs_2_.refs_1_.refs_0_, bf16[256,2048]{1,0:T(8,128)(2,1)} %collective-permute-done.54.refs_3_.refs_1_, ...), custom_call_target="tpu_custom_call" | custom-call | bytes 21000000 | tf_op jit(solution)/shard_map/pallas_call | solution.py:392
  442.3 3.1 add_convert_fusion.refs_6_
  445.3 3.6 collective-permute-start.63
  452.8 6.6 %shard_map.288 = (bf16[256,2048]{1,0:T(8,128)(2,1)}, bf16[256,2048]{1,0:T(8,128)(2,1)}, bf16[2,256,2048]{2,1,0:T(8,128)(2,1)}) custom-call(s32[2]{0:T(128)} %pad_add_fusion.place, bf16[256,7168]{1,0:T(8,128)(2,1)} %get-tuple-element.210.refs_5_.refs_2_.refs_0_.refs_6_, bf16[256,7168]{1,0:T(8,128)(2,1)} %collective-permute-done.42.refs_5_.refs_3_.refs_1_.refs_7_, ...), custom_call_target="tpu_custom_call" | custom-call | bytes 21000000 | tf_op jit(solution)/shard_map/pallas_call | solution.py:392
  459.4 15.4 %collective-permute-done.62.refs_3_ = bf16[256,2048]{1,0:T(8,128)(2,1)} collective-permute-done((bf16[256,2048]{1,0:T(8,128)(2,1)}, bf16[256,2048]{1,0:T(8,128)(2,1)}, u32[]{:S(2)}, u32[]{:S(2)}) %collective-permute-start.62) | collective-permute-done | bytes 1048608 | tf_op jit(solution)/shard_map/ppermute | solution.py:34
  474.8 8.4 %shard_map.289 = (f32[256,1024]{1,0:T(8,128)}, bf16[256,2048]{1,0:T(8,128)(2,1)}, f32[8,1024]{1,0:T(8,128)}, bf16[256,2048]{1,0:T(8,128)(2,1)}) custom-call(s32[2]{0:T(128)} %pad_add_fusion.place, bf16[256,1024]{1,0:T(8,128)(2,1)} %get-tuple-element.240.refs_3_.refs_0_, bf16[256,2048]{1,0:T(8,128)(2,1)} %get-tuple-element.241.refs_1_, ...), custom_call_target="tpu_custom_call" | custom-call | bytes 18000000 | tf_op jit(solution)/shard_map/pallas_call | solution.py:392
  483.3 6.5 %shard_map.290 = (bf16[128,2048]{1,0:T(8,128)(2,1)}, bf16[128,2048]{1,0:T(8,128)(2,1)}, bf16[2,128,2048]{2,1,0:T(8,128)(2,1)}, bf16[256,4096]{1,0:T(8,128)(2,1)}) custom-call(s32[2]{0:T(128)} %pad_add_fusion.place, bf16[2,256,2048]{2,1,0:T(8,128)(2,1)} %get-tuple-element.263.refs_0_, bf16[256,2048]{1,0:T(8,128)(2,1)} %collective-permute-done.70.refs_1_, ...), custom_call_target="tpu_custom_call" | custom-call | bytes 12000000 | tf_op jit(solution)/shard_map/pallas_call | solution.py:392
  498.9 6.5 %shard_map.291 = (bf16[256,2048]{1,0:T(8,128)(2,1)}, bf16[256,2048]{1,0:T(8,128)(2,1)}, bf16[2,256,2048]{2,1,0:T(8,128)(2,1)}) custom-call(s32[2]{0:T(128)} %pad_add_fusion.place, bf16[256,7168]{1,0:T(8,128)(2,1)} %get-tuple-element.210.refs_5_.refs_2_.refs_0_.refs_6_, bf16[256,7168]{1,0:T(8,128)(2,1)} %collective-permute-done.42.refs_5_.refs_3_.refs_1_.refs_7_, ...), custom_call_target="tpu_custom_call" | custom-call | bytes 21000000 | tf_op jit(solution)/shard_map/pallas_call | solution.py:392
  508.4 3.5 shard_map.292.refs_3_
  518.9 12.0 %collective-permute-done.75.refs_2_ = bf16[256,2048]{1,0:T(8,128)(2,1)} collective-permute-done((bf16[256,2048]{1,0:T(8,128)(2,1)}, bf16[256,2048]{1,0:T(8,128)(2,1)}, u32[]{:S(2)}, u32[]{:S(2)}) %collective-permute-start.75) | collective-permute-done | bytes 1048608 | tf_op jit(solution)/shard_map/ppermute | solution.py:29
  530.9 4.0 shard_map.293
  538.3 15.1 %collective-permute-done.73.refs_2_ = bf16[256,2048]{1,0:T(8,128)(2,1)} collective-permute-done((bf16[256,2048]{1,0:T(8,128)(2,1)}, bf16[256,2048]{1,0:T(8,128)(2,1)}, u32[]{:S(2)}, u32[]{:S(2)}) %collective-permute-start.73) | collective-permute-done | bytes 1048608 | tf_op jit(solution)/shard_map/ppermute | solution.py:29
  553.4 4.1 shard_map.294
  557.5 4.9 collective-permute-done.81.refs_2_
  563.6 3.4 shard_map.295.refs_3_
  573.1 3.2 collective-permute-start.83
  579.4 4.8 collective-permute-done.79.refs_2_
  584.2 3.5 shard_map.296
  603.7 25.5 %reduce-scatter.10.cloned.1.call-done = bf16[32,4096]{1,0:T(8,128)(2,1)} async-done(((bf16[128,4096]{1,0:T(8,128)(2,1)}), bf16[32,4096]{1,0:T(8,128)(2,1)}) %reduce-scatter.10.cloned.1.call-update) | async-done | bytes 262160 | tf_op jit(solution)/shard_map/reduce_scatter | solution.py:920
  (312 shorter events, 133.8 us)
Async XLA Ops:
  7.2 421.8 %reduce-scatter.6.cloned.1.call-start = ((), (), s32[]{:S(2)}) async-start(), calls=%async_computation.5 | async-start | bytes 1310720 | tf_op jit(solution)/shard_map/reduce_scatter | solution.py:920
  12.7 32.1 %collective-permute-start.3 = (bf16[160,4096]{1,0:T(8,128)(2,1)}, bf16[160,4096]{1,0:T(8,128)(2,1)}, u32[]{:S(2)}, u32[]{:S(2)}) collective-permute-start(bf16[160,4096]{1,0:T(8,128)(2,1)} %shard_map.254.refs_6_.refs_0_.refs_1_.refs_5_.refs_7_), channel_id=1, source_target_pairs={{0,16},{4,20},{8,24},{12,28},{16,0},{20,4},{24,8},{28,12},{1,17},{... | collective-permute-start | bytes 3932168 | tf_op jit(solution)/shard_map/ppermute | solution.py:29
  15.7 30.6 %collective-permute-start.2 = (bf16[160,4096]{1,0:T(8,128)(2,1)}, bf16[160,4096]{1,0:T(8,128)(2,1)}, u32[]{:S(2)}, u32[]{:S(2)}) collective-permute-start(bf16[160,4096]{1,0:T(8,128)(2,1)} %shard_map.254.refs_6_.refs_0_.refs_1_.refs_5_.refs_7_), channel_id=1, source_target_pairs={{0,8},{4,12},{8,0},{12,4},{16,24},{20,28},{24,16},{28,20},{1,9},{5... | collective-permute-start | bytes 3932168 | tf_op jit(solution)/shard_map/ppermute | solution.py:29
  17.2 12.0 %collective-permute-start = (bf16[256,1024]{1,0:T(8,128)(2,1)}, bf16[256,1024]{1,0:T(8,128)(2,1)}, u32[]{:S(2)}, u32[]{:S(2)}) collective-permute-start(bf16[256,1024]{1,0:T(8,128)(2,1)} %bitcast.101), channel_id=1, source_target_pairs={{1,4},{2,1},{3,5},{4,2},{5,6},{6,3},{9,12},{10,9},{11,13},{12,10},... | collective-permute-start | bytes 1572872 | tf_op jit(solution)/shard_map/ppermute | solution.py:1336
  51.3 38.6 %collective-permute-start.8 = (bf16[640,4096]{1,0:T(8,128)(2,1)}, bf16[640,4096]{1,0:T(8,128)(2,1)}, u32[]{:S(2)}, u32[]{:S(2)}) collective-permute-start(bf16[640,4096]{1,0:T(8,128)(2,1)} %shard_map.255.refs_0_.refs_2_.refs_16_.refs_26_.refs_1_.refs_6_.refs_5_.refs_15_.refs_25_.refs_7_), channel_id=1, source_target_pairs={{0,4},{4,0},{8,12},{12,8},{16,20},{20,16},{24,28},{28,24},{1,5},{5... | collective-permute-start | bytes 15728648 | tf_op jit(solution)/shard_map/ppermute | solution.py:29
  52.0 37.4 %collective-permute-start.7 = (bf16[208,4096]{1,0:T(8,128)(2,1)}, bf16[208,4096]{1,0:T(8,128)(2,1)}, u32[]{:S(2)}, u32[]{:S(2)}) collective-permute-start(bf16[208,4096]{1,0:T(8,128)(2,1)} %get-tuple-element.158), channel_id=1, source_target_pairs={{0,16},{4,20},{8,24},{12,28},{16,0},{20,4},{24,8},{28,12},{1,17},{... | collective-permute-start | bytes 5111816 | tf_op jit(solution)/shard_map/ppermute | solution.py:29
  52.4 37.5 %collective-permute-start.6 = (bf16[208,4096]{1,0:T(8,128)(2,1)}, bf16[208,4096]{1,0:T(8,128)(2,1)}, u32[]{:S(2)}, u32[]{:S(2)}) collective-permute-start(bf16[208,4096]{1,0:T(8,128)(2,1)} %get-tuple-element.155), channel_id=1, source_target_pairs={{0,8},{4,12},{8,0},{12,4},{16,24},{20,28},{24,16},{28,20},{1,9},{5... | collective-permute-start | bytes 5111816 | tf_op jit(solution)/shard_map/ppermute | solution.py:29
  96.0 36.6 %collective-permute-start.16 = (bf16[192,4096]{1,0:T(8,128)(2,1)}, bf16[192,4096]{1,0:T(8,128)(2,1)}, u32[]{:S(2)}, u32[]{:S(2)}) collective-permute-start(bf16[192,4096]{1,0:T(8,128)(2,1)} %get-tuple-element.166), channel_id=1, source_target_pairs={{0,16},{4,20},{8,24},{12,28},{16,0},{20,4},{24,8},{28,12},{1,17},{... | collective-permute-start | bytes 4718600 | tf_op jit(solution)/shard_map/ppermute | solution.py:29
  97.7 36.3 %collective-permute-start.15 = (bf16[192,4096]{1,0:T(8,128)(2,1)}, bf16[192,4096]{1,0:T(8,128)(2,1)}, u32[]{:S(2)}, u32[]{:S(2)}) collective-permute-start(bf16[192,4096]{1,0:T(8,128)(2,1)} %get-tuple-element.162), channel_id=1, source_target_pairs={{0,8},{4,12},{8,0},{12,4},{16,24},{20,28},{24,16},{28,20},{1,9},{5... | collective-permute-start | bytes 4718600 | tf_op jit(solution)/shard_map/ppermute | solution.py:29
  114.3 27.6 %collective-permute-start.13 = (bf16[256,2048]{1,0:T(8,128)(2,1)}, bf16[256,2048]{1,0:T(8,128)(2,1)}, u32[]{:S(2)}, u32[]{:S(2)}) collective-permute-start(bf16[256,2048]{1,0:T(8,128)(2,1)} %shard_map.261.refs_11_.refs_1_), channel_id=1, source_target_pairs={{0,1},{1,0},{2,3},{3,2},{4,5},{5,4},{6,7},{7,6},{8,9},{9,8},{10,11... | collective-permute-start | bytes 3145736 | tf_op jit(solution)/shard_map/ppermute | solution.py:34
  118.1 23.8 %collective-permute-start.12 = (bf16[256,2048]{1,0:T(8,128)(2,1)}, bf16[256,2048]{1,0:T(8,128)(2,1)}, u32[]{:S(2)}, u32[]{:S(2)}) collective-permute-start(bf16[256,2048]{1,0:T(8,128)(2,1)} %shard_map.261.refs_11_.refs_1_), channel_id=1, source_target_pairs={{0,4},{4,0},{8,12},{12,8},{16,20},{20,16},{24,28},{28,24},{1,5},{5... | collective-permute-start | bytes 3145736 | tf_op jit(solution)/shard_map/ppermute | solution.py:29
  136.9 35.4 %collective-permute-start.20 = (bf16[192,4096]{1,0:T(8,128)(2,1)}, bf16[192,4096]{1,0:T(8,128)(2,1)}, u32[]{:S(2)}, u32[]{:S(2)}) collective-permute-start(bf16[192,4096]{1,0:T(8,128)(2,1)} %get-tuple-element.176), channel_id=1, source_target_pairs={{0,16},{4,20},{8,24},{12,28},{16,0},{20,4},{24,8},{28,12},{1,17},{... | collective-permute-start | bytes 4718600 | tf_op jit(solution)/shard_map/ppermute | solution.py:29
  137.2 35.4 %collective-permute-start.19 = (bf16[192,4096]{1,0:T(8,128)(2,1)}, bf16[192,4096]{1,0:T(8,128)(2,1)}, u32[]{:S(2)}, u32[]{:S(2)}) collective-permute-start(bf16[192,4096]{1,0:T(8,128)(2,1)} %get-tuple-element.169.refs_1_), channel_id=1, source_target_pairs={{0,8},{4,12},{8,0},{12,4},{16,24},{20,28},{24,16},{28,20},{1,9},{5... | collective-permute-start | bytes 4718600 | tf_op jit(solution)/shard_map/ppermute | solution.py:29
  138.9 34.3 %collective-permute-start.17 = (bf16[192,4096]{1,0:T(8,128)(2,1)}, bf16[192,4096]{1,0:T(8,128)(2,1)}, u32[]{:S(2)}, u32[]{:S(2)}) collective-permute-start(bf16[192,4096]{1,0:T(8,128)(2,1)} %collective-permute-done.15.refs_0_.refs_22_.refs_28_.refs_21_.refs_27_), channel_id=1, source_target_pairs={{0,4},{4,0},{8,12},{12,8},{16,20},{20,16},{24,28},{28,24},{1,5},{5... | collective-permute-start | bytes 4718600 | tf_op jit(solution)/shard_map/ppermute | solution.py:29
  141.9 31.3 %collective-permute-start.18 = (bf16[192,4096]{1,0:T(8,128)(2,1)}, bf16[192,4096]{1,0:T(8,128)(2,1)}, u32[]{:S(2)}, u32[]{:S(2)}) collective-permute-start(bf16[192,4096]{1,0:T(8,128)(2,1)} %collective-permute-done.16.refs_1_.refs_23_.refs_30_.refs_22_.refs_29_), channel_id=1, source_target_pairs={{0,4},{4,0},{8,12},{12,8},{16,20},{20,16},{24,28},{28,24},{1,5},{5... | collective-permute-start | bytes 4718600 | tf_op jit(solution)/shard_map/ppermute | solution.py:29
  172.7 10.8 %collective-permute-start.22 = (bf16[192,4096]{1,0:T(8,128)(2,1)}, bf16[192,4096]{1,0:T(8,128)(2,1)}, u32[]{:S(2)}, u32[]{:S(2)}) collective-permute-start(bf16[192,4096]{1,0:T(8,128)(2,1)} %collective-permute-done.20.refs_1_.refs_33_.refs_5_.refs_10_.refs_9_.refs_11_.refs_32_), channel_id=1, source_target_pairs={{0,4},{4,0},{8,12},{12,8},{16,20},{20,16},{24,28},{28,24},{1,5},{5... | collective-permute-start | bytes 4718600 | tf_op jit(solution)/shard_map/ppermute | solution.py:29
  176.1 36.6 %collective-permute-start.24 = (bf16[192,4096]{1,0:T(8,128)(2,1)}, bf16[192,4096]{1,0:T(8,128)(2,1)}, u32[]{:S(2)}, u32[]{:S(2)}) collective-permute-start(bf16[192,4096]{1,0:T(8,128)(2,1)} %get-tuple-element.183), channel_id=1, source_target_pairs={{0,16},{4,20},{8,24},{12,28},{16,0},{20,4},{24,8},{28,12},{1,17},{... | collective-permute-start | bytes 4718600 | tf_op jit(solution)/shard_map/ppermute | solution.py:29
  177.5 36.3 %collective-permute-start.23 = (bf16[192,4096]{1,0:T(8,128)(2,1)}, bf16[192,4096]{1,0:T(8,128)(2,1)}, u32[]{:S(2)}, u32[]{:S(2)}) collective-permute-start(bf16[192,4096]{1,0:T(8,128)(2,1)} %get-tuple-element.180.refs_1_), channel_id=1, source_target_pairs={{0,8},{4,12},{8,0},{12,4},{16,24},{20,28},{24,16},{28,20},{1,9},{5... | collective-permute-start | bytes 4718600 | tf_op jit(solution)/shard_map/ppermute | solution.py:29
  217.3 36.6 %collective-permute-start.31 = (bf16[192,4096]{1,0:T(8,128)(2,1)}, bf16[192,4096]{1,0:T(8,128)(2,1)}, u32[]{:S(2)}, u32[]{:S(2)}) collective-permute-start(bf16[192,4096]{1,0:T(8,128)(2,1)} %get-tuple-element.188), channel_id=1, source_target_pairs={{0,16},{4,20},{8,24},{12,28},{16,0},{20,4},{24,8},{28,12},{1,17},{... | collective-permute-start | bytes 4718600 | tf_op jit(solution)/shard_map/ppermute | solution.py:29
  217.9 36.3 %collective-permute-start.30 = (bf16[192,4096]{1,0:T(8,128)(2,1)}, bf16[192,4096]{1,0:T(8,128)(2,1)}, u32[]{:S(2)}, u32[]{:S(2)}) collective-permute-start(bf16[192,4096]{1,0:T(8,128)(2,1)} %get-tuple-element.187.refs_11_), channel_id=1, source_target_pairs={{0,8},{4,12},{8,0},{12,4},{16,24},{20,28},{24,16},{28,20},{1,9},{5... | collective-permute-start | bytes 4718600 | tf_op jit(solution)/shard_map/ppermute | solution.py:29
  224.7 28.4 %collective-permute-start.28 = (bf16[256,2048]{1,0:T(8,128)(2,1)}, bf16[256,2048]{1,0:T(8,128)(2,1)}, u32[]{:S(2)}, u32[]{:S(2)}) collective-permute-start(bf16[256,2048]{1,0:T(8,128)(2,1)} %shard_map.271.refs_11_.refs_1_), channel_id=1, source_target_pairs={{0,1},{1,0},{2,3},{3,2},{4,5},{5,4},{6,7},{7,6},{8,9},{9,8},{10,11... | collective-permute-start | bytes 3145736 | tf_op jit(solution)/shard_map/ppermute | solution.py:34
  229.3 29.3 %collective-permute-start.27 = (bf16[256,2048]{1,0:T(8,128)(2,1)}, bf16[256,2048]{1,0:T(8,128)(2,1)}, u32[]{:S(2)}, u32[]{:S(2)}) collective-permute-start(bf16[256,2048]{1,0:T(8,128)(2,1)} %shard_map.271.refs_11_.refs_1_), channel_id=1, source_target_pairs={{0,4},{4,0},{8,12},{12,8},{16,20},{20,16},{24,28},{28,24},{1,5},{5... | collective-permute-start | bytes 3145736 | tf_op jit(solution)/shard_map/ppermute | solution.py:29
  253.9 19.5 %collective-permute-start.33 = (bf16[192,4096]{1,0:T(8,128)(2,1)}, bf16[192,4096]{1,0:T(8,128)(2,1)}, u32[]{:S(2)}, u32[]{:S(2)}) collective-permute-start(bf16[192,4096]{1,0:T(8,128)(2,1)} %collective-permute-done.31.refs_1_.refs_23_.refs_30_.refs_22_.refs_29_), channel_id=1, source_target_pairs={{0,4},{4,0},{8,12},{12,8},{16,20},{20,16},{24,28},{28,24},{1,5},{5... | collective-permute-start | bytes 4718600 | tf_op jit(solution)/shard_map/ppermute | solution.py:29
  254.3 19.2 %collective-permute-start.32 = (bf16[192,4096]{1,0:T(8,128)(2,1)}, bf16[192,4096]{1,0:T(8,128)(2,1)}, u32[]{:S(2)}, u32[]{:S(2)}) collective-permute-start(bf16[192,4096]{1,0:T(8,128)(2,1)} %collective-permute-done.30.refs_0_.refs_22_.refs_28_.refs_21_.refs_27_), channel_id=1, source_target_pairs={{0,4},{4,0},{8,12},{12,8},{16,20},{20,16},{24,28},{28,24},{1,5},{5... | collective-permute-start | bytes 4718600 | tf_op jit(solution)/shard_map/ppermute | solution.py:29
  257.3 15.3 %collective-permute-start.35 = (bf16[64,4096]{1,0:T(8,128)(2,1)}, bf16[64,4096]{1,0:T(8,128)(2,1)}, u32[]{:S(2)}, u32[]{:S(2)}) collective-permute-start(bf16[64,4096]{1,0:T(8,128)(2,1)} %get-tuple-element.195), channel_id=1, source_target_pairs={{0,16},{4,20},{8,24},{12,28},{16,0},{20,4},{24,8},{28,12},{1,17},{... | collective-permute-start | bytes 1572872 | tf_op jit(solution)/shard_map/ppermute | solution.py:29
  258.6 14.4 %collective-permute-start.34 = (bf16[64,4096]{1,0:T(8,128)(2,1)}, bf16[64,4096]{1,0:T(8,128)(2,1)}, u32[]{:S(2)}, u32[]{:S(2)}) collective-permute-start(bf16[64,4096]{1,0:T(8,128)(2,1)} %get-tuple-element.189.refs_5_), channel_id=1, source_target_pairs={{0,8},{4,12},{8,0},{12,4},{16,24},{20,28},{24,16},{28,20},{1,9},{5... | collective-permute-start | bytes 1572872 | tf_op jit(solution)/shard_map/ppermute | solution.py:29
  288.8 14.4 %collective-permute-start.38 = (bf16[256,7168]{1,0:T(8,128)(2,1)}, bf16[256,7168]{1,0:T(8,128)(2,1)}, u32[]{:S(2)}, u32[]{:S(2)}) collective-permute-start(bf16[256,7168]{1,0:T(8,128)(2,1)} %get-tuple-element.201.refs_2_.refs_5_.refs_0_.refs_6_), channel_id=1, source_target_pairs={{0,4},{4,0},{8,12},{12,8},{16,20},{20,16},{24,28},{28,24},{1,5},{5... | collective-permute-start | bytes 11010056 | tf_op jit(solution)/shard_map/ppermute | solution.py:29
  289.0 14.2 %collective-permute-start.42 = (bf16[256,7168]{1,0:T(8,128)(2,1)}, bf16[256,7168]{1,0:T(8,128)(2,1)}, u32[]{:S(2)}, u32[]{:S(2)}) collective-permute-start(bf16[256,7168]{1,0:T(8,128)(2,1)} %get-tuple-element.210.refs_5_.refs_2_.refs_0_.refs_6_), channel_id=1, source_target_pairs={{0,4},{4,0},{8,12},{12,8},{16,20},{20,16},{24,28},{28,24},{1,5},{5... | collective-permute-start | bytes 11010056 | tf_op jit(solution)/shard_map/ppermute | solution.py:29
  289.4 13.6 %collective-permute-start.41 = (bf16[256,1024]{1,0:T(8,128)(2,1)}, bf16[256,1024]{1,0:T(8,128)(2,1)}, u32[]{:S(2)}, u32[]{:S(2)}) collective-permute-start(bf16[256,1024]{1,0:T(8,128)(2,1)} %broadcast_select_fusion.refs_7_.refs_0_.refs_1_), channel_id=1, source_target_pairs={{0,4},{4,0},{8,12},{12,8},{16,20},{20,16},{24,28},{28,24},{1,5},{5... | collective-permute-start | bytes 1572872 | tf_op jit(solution)/shard_map/ppermute | solution.py:29
  310.2 26.4 %collective-permute-start.47 = (bf16[256,2048]{1,0:T(8,128)(2,1)}, bf16[256,2048]{1,0:T(8,128)(2,1)}, u32[]{:S(2)}, u32[]{:S(2)}) collective-permute-start(bf16[256,2048]{1,0:T(8,128)(2,1)} %get-tuple-element.218), channel_id=1, source_target_pairs={{0,16},{4,20},{8,24},{12,28},{16,0},{20,4},{24,8},{28,12},{1,17},{... | collective-permute-start | bytes 3145736 | tf_op jit(solution)/shard_map/ppermute | solution.py:29
  310.9 26.4 %collective-permute-start.46 = (bf16[256,2048]{1,0:T(8,128)(2,1)}, bf16[256,2048]{1,0:T(8,128)(2,1)}, u32[]{:S(2)}, u32[]{:S(2)}) collective-permute-start(bf16[256,2048]{1,0:T(8,128)(2,1)} %get-tuple-element.211.refs_8_), channel_id=1, source_target_pairs={{0,8},{4,12},{8,0},{12,4},{16,24},{20,28},{24,16},{28,20},{1,9},{5... | collective-permute-start | bytes 3145736 | tf_op jit(solution)/shard_map/ppermute | solution.py:29
  328.0 13.3 %collective-permute-start.50 = (bf16[256,2048]{1,0:T(8,128)(2,1)}, bf16[256,2048]{1,0:T(8,128)(2,1)}, u32[]{:S(2)}, u32[]{:S(2)}) collective-permute-start(bf16[256,2048]{1,0:T(8,128)(2,1)} %get-tuple-element.223), channel_id=1, source_target_pairs={{0,4},{4,0},{8,12},{12,8},{16,20},{20,16},{24,28},{28,24},{1,5},{5... | collective-permute-start | bytes 3145736 | tf_op jit(solution)/shard_map/ppermute | solution.py:29
  328.1 13.3 %collective-permute-start.51 = (bf16[256,2048]{1,0:T(8,128)(2,1)}, bf16[256,2048]{1,0:T(8,128)(2,1)}, u32[]{:S(2)}, u32[]{:S(2)}) collective-permute-start(bf16[256,2048]{1,0:T(8,128)(2,1)} %get-tuple-element.227), channel_id=1, source_target_pairs={{0,4},{4,0},{8,12},{12,8},{16,20},{20,16},{24,28},{28,24},{1,5},{5... | collective-permute-start | bytes 3145736 | tf_op jit(solution)/shard_map/ppermute | solution.py:29
  335.1 26.4 %collective-permute-start.45 = (bf16[256,2048]{1,0:T(8,128)(2,1)}, bf16[256,2048]{1,0:T(8,128)(2,1)}, u32[]{:S(2)}, u32[]{:S(2)}) collective-permute-start(bf16[256,2048]{1,0:T(8,128)(2,1)} %get-tuple-element.216), channel_id=1, source_target_pairs={{0,16},{4,20},{8,24},{12,28},{16,0},{20,4},{24,8},{28,12},{1,17},{... | collective-permute-start | bytes 3145736 | tf_op jit(solution)/shard_map/ppermute | solution.py:29
  336.6 26.4 %collective-permute-start.44 = (bf16[256,2048]{1,0:T(8,128)(2,1)}, bf16[256,2048]{1,0:T(8,128)(2,1)}, u32[]{:S(2)}, u32[]{:S(2)}) collective-permute-start(bf16[256,2048]{1,0:T(8,128)(2,1)} %get-tuple-element.215.refs_3_), channel_id=1, source_target_pairs={{0,8},{4,12},{8,0},{12,4},{16,24},{20,28},{24,16},{28,20},{1,9},{5... | collective-permute-start | bytes 3145736 | tf_op jit(solution)/shard_map/ppermute | solution.py:29
  344.3 27.2 %collective-permute-start.52 = (bf16[256,2048]{1,0:T(8,128)(2,1)S(1)}, bf16[256,2048]{1,0:T(8,128)(2,1)S(1)}, u32[]{:S(2)}, u32[]{:S(2)}) collective-permute-start(bf16[256,2048]{1,0:T(8,128)(2,1)S(1)} %add_convert_fusion.1.refs_17_), channel_id=1, source_target_pairs={{0,1},{1,0},{2,3},{3,2},{4,5},{5,4},{6,7},{7,6},{8,9},{9,8},{10,11... | collective-permute-start | bytes 3145736 | tf_op jit(solution)/shard_map/ppermute | solution.py:34
  348.9 32.9 %collective-permute-start.49 = (bf16[128,2048]{1,0:T(8,128)(2,1)}, bf16[128,2048]{1,0:T(8,128)(2,1)}, u32[]{:S(2)}, u32[]{:S(2)}) collective-permute-start(bf16[128,2048]{1,0:T(8,128)(2,1)} %get-tuple-element.221), channel_id=1, source_target_pairs={{0,8},{4,12},{8,0},{12,4},{16,24},{20,28},{24,16},{28,20},{1,9},{5... | collective-permute-start | bytes 1572872 | tf_op jit(solution)/shard_map/ppermute | solution.py:29
  350.2 31.5 %collective-permute-start.48 = (bf16[128,2048]{1,0:T(8,128)(2,1)}, bf16[128,2048]{1,0:T(8,128)(2,1)}, u32[]{:S(2)}, u32[]{:S(2)}) collective-permute-start(bf16[128,2048]{1,0:T(8,128)(2,1)} %get-tuple-element.220), channel_id=1, source_target_pairs={{0,16},{4,20},{8,24},{12,28},{16,0},{20,4},{24,8},{28,12},{1,17},{... | collective-permute-start | bytes 1572872 | tf_op jit(solution)/shard_map/ppermute | solution.py:29
  386.4 149.8 %reduce-scatter.8.cloned.1.call-start = ((), (), s32[]{:S(2)}) async-start(), calls=%async_computation.6 | async-start | bytes 2621440 | tf_op jit(solution)/shard_map/reduce_scatter | solution.py:1054
  386.5 25.0 %collective-permute-start.56 = (bf16[128,2048]{1,0:T(8,128)(2,1)}, bf16[128,2048]{1,0:T(8,128)(2,1)}, u32[]{:S(2)}, u32[]{:S(2)}) collective-permute-start(bf16[128,2048]{1,0:T(8,128)(2,1)} %get-tuple-element.239), channel_id=1, source_target_pairs={{0,8},{4,12},{8,0},{12,4},{16,24},{20,28},{24,16},{28,20},{1,9},{5... | collective-permute-start | bytes 1572872 | tf_op jit(solution)/shard_map/ppermute | solution.py:29
  388.0 23.5 %collective-permute-start.57 = (bf16[128,2048]{1,0:T(8,128)(2,1)}, bf16[128,2048]{1,0:T(8,128)(2,1)}, u32[]{:S(2)}, u32[]{:S(2)}) collective-permute-start(bf16[128,2048]{1,0:T(8,128)(2,1)} %get-tuple-element.230.refs_10_), channel_id=1, source_target_pairs={{0,16},{4,20},{8,24},{12,28},{16,0},{20,4},{24,8},{28,12},{1,17},{... | collective-permute-start | bytes 1572872 | tf_op jit(solution)/shard_map/ppermute | solution.py:29
  388.6 40.4 %collective-permute-start.53 = (f32[256,1024]{1,0:T(8,128)}, f32[256,1024]{1,0:T(8,128)}, u32[]{:S(2)}, u32[]{:S(2)}) collective-permute-start(f32[256,1024]{1,0:T(8,128)} %get-tuple-element.231), channel_id=1, source_target_pairs={{4,1},{1,2},{5,3},{2,4},{6,5},{3,6},{12,9},{9,10},{13,11},{10,12},... | collective-permute-start | bytes 3145736 | tf_op jit(solution)/shard_map/ppermute | solution.py:1336
  397.1 31.9 %collective-permute-start.60 = (bf16[256,2048]{1,0:T(8,128)(2,1)}, bf16[256,2048]{1,0:T(8,128)(2,1)}, u32[]{:S(2)}, u32[]{:S(2)}) collective-permute-start(bf16[256,2048]{1,0:T(8,128)(2,1)} %get-tuple-element.244), channel_id=1, source_target_pairs={{0,16},{4,20},{8,24},{12,28},{16,0},{20,4},{24,8},{28,12},{1,17},{... | collective-permute-start | bytes 3145736 | tf_op jit(solution)/shard_map/ppermute | solution.py:29
  398.7 30.4 %collective-permute-start.59 = (bf16[256,2048]{1,0:T(8,128)(2,1)}, bf16[256,2048]{1,0:T(8,128)(2,1)}, u32[]{:S(2)}, u32[]{:S(2)}) collective-permute-start(bf16[256,2048]{1,0:T(8,128)(2,1)} %get-tuple-element.236.refs_35_), channel_id=1, source_target_pairs={{0,8},{4,12},{8,0},{12,4},{16,24},{20,28},{24,16},{28,20},{1,9},{5... | collective-permute-start | bytes 3145736 | tf_op jit(solution)/shard_map/ppermute | solution.py:29
  427.4 14.9 %collective-permute-start.58 = (bf16[256,2048]{1,0:T(8,128)(2,1)}, bf16[256,2048]{1,0:T(8,128)(2,1)}, u32[]{:S(2)}, u32[]{:S(2)}) collective-permute-start(bf16[256,2048]{1,0:T(8,128)(2,1)} %get-tuple-element.242), channel_id=1, source_target_pairs={{0,4},{4,0},{8,12},{12,8},{16,20},{20,16},{24,28},{28,24},{1,5},{5... | collective-permute-start | bytes 3145736 | tf_op jit(solution)/shard_map/ppermute | solution.py:29
  428.9 13.3 %collective-permute-start.61 = (bf16[256,2048]{1,0:T(8,128)(2,1)}, bf16[256,2048]{1,0:T(8,128)(2,1)}, u32[]{:S(2)}, u32[]{:S(2)}) collective-permute-start(bf16[256,2048]{1,0:T(8,128)(2,1)} %get-tuple-element.251), channel_id=1, source_target_pairs={{0,4},{4,0},{8,12},{12,8},{16,20},{20,16},{24,28},{28,24},{1,5},{5... | collective-permute-start | bytes 3145736 | tf_op jit(solution)/shard_map/ppermute | solution.py:29
  433.1 17.2 %collective-permute-start.65 = (bf16[128,2048]{1,0:T(8,128)(2,1)}, bf16[128,2048]{1,0:T(8,128)(2,1)}, u32[]{:S(2)}, u32[]{:S(2)}) collective-permute-start(bf16[128,2048]{1,0:T(8,128)(2,1)} %get-tuple-element.257), channel_id=1, source_target_pairs={{0,8},{4,12},{8,0},{12,4},{16,24},{20,28},{24,16},{28,20},{1,9},{5... | collective-permute-start | bytes 1572872 | tf_op jit(solution)/shard_map/ppermute | solution.py:29
  434.6 16.3 %collective-permute-start.66 = (bf16[128,2048]{1,0:T(8,128)(2,1)}, bf16[128,2048]{1,0:T(8,128)(2,1)}, u32[]{:S(2)}, u32[]{:S(2)}) collective-permute-start(bf16[128,2048]{1,0:T(8,128)(2,1)} %get-tuple-element.246.refs_4_), channel_id=1, source_target_pairs={{0,16},{4,20},{8,24},{12,28},{16,0},{20,4},{24,8},{28,12},{1,17},{... | collective-permute-start | bytes 1572872 | tf_op jit(solution)/shard_map/ppermute | solution.py:29
  449.0 25.8 %collective-permute-start.62 = (bf16[256,2048]{1,0:T(8,128)(2,1)}, bf16[256,2048]{1,0:T(8,128)(2,1)}, u32[]{:S(2)}, u32[]{:S(2)}) collective-permute-start(bf16[256,2048]{1,0:T(8,128)(2,1)} %add_convert_fusion.refs_6_), channel_id=1, source_target_pairs={{0,1},{1,0},{2,3},{3,2},{4,5},{5,4},{6,7},{7,6},{8,9},{9,8},{10,11... | collective-permute-start | bytes 3145736 | tf_op jit(solution)/shard_map/ppermute | solution.py:34
  450.3 32.9 %collective-permute-start.71 = (bf16[256,2048]{1,0:T(8,128)(2,1)}, bf16[256,2048]{1,0:T(8,128)(2,1)}, u32[]{:S(2)}, u32[]{:S(2)}) collective-permute-start(bf16[256,2048]{1,0:T(8,128)(2,1)} %get-tuple-element.264), channel_id=1, source_target_pairs={{0,16},{4,20},{8,24},{12,28},{16,0},{20,4},{24,8},{28,12},{1,17},{... | collective-permute-start | bytes 3145736 | tf_op jit(solution)/shard_map/ppermute | solution.py:29
  450.9 32.4 %collective-permute-start.70 = (bf16[256,2048]{1,0:T(8,128)(2,1)}, bf16[256,2048]{1,0:T(8,128)(2,1)}, u32[]{:S(2)}, u32[]{:S(2)}) collective-permute-start(bf16[256,2048]{1,0:T(8,128)(2,1)} %get-tuple-element.247), channel_id=1, source_target_pairs={{0,8},{4,12},{8,0},{12,4},{16,24},{20,28},{24,16},{28,20},{1,9},{5... | collective-permute-start | bytes 3145736 | tf_op jit(solution)/shard_map/ppermute | solution.py:29
  489.8 78.7 %reduce-scatter.14.cloned.1.call-start = ((), (), s32[]{:S(2)}) async-start(), calls=%async_computation.9 | async-start | bytes 1310720 | tf_op jit(solution)/shard_map/reduce_scatter | solution.py:920
  491.8 15.1 %collective-permute-start.77 = (bf16[128,2048]{1,0:T(8,128)(2,1)}, bf16[128,2048]{1,0:T(8,128)(2,1)}, u32[]{:S(2)}, u32[]{:S(2)}) collective-permute-start(bf16[128,2048]{1,0:T(8,128)(2,1)} %get-tuple-element.274), channel_id=1, source_target_pairs={{0,8},{4,12},{8,0},{12,4},{16,24},{20,28},{24,16},{28,20},{1,9},{5... | collective-permute-start | bytes 1572872 | tf_op jit(solution)/shard_map/ppermute | solution.py:29
  493.3 15.1 %collective-permute-start.76 = (bf16[128,2048]{1,0:T(8,128)(2,1)}, bf16[128,2048]{1,0:T(8,128)(2,1)}, u32[]{:S(2)}, u32[]{:S(2)}) collective-permute-start(bf16[128,2048]{1,0:T(8,128)(2,1)} %get-tuple-element.267.refs_10_), channel_id=1, source_target_pairs={{0,16},{4,20},{8,24},{12,28},{16,0},{20,4},{24,8},{28,12},{1,17},{... | collective-permute-start | bytes 1572872 | tf_op jit(solution)/shard_map/ppermute | solution.py:29
  495.5 35.4 %collective-permute-start.74 = (bf16[256,2048]{1,0:T(8,128)(2,1)}, bf16[256,2048]{1,0:T(8,128)(2,1)}, u32[]{:S(2)}, u32[]{:S(2)}) collective-permute-start(bf16[256,2048]{1,0:T(8,128)(2,1)} %get-tuple-element.258.refs_17_), channel_id=1, source_target_pairs={{0,8},{4,12},{8,0},{12,4},{16,24},{20,28},{24,16},{28,20},{1,9},{5... | collective-permute-start | bytes 3145736 | tf_op jit(solution)/shard_map/ppermute | solution.py:29
  498.0 32.9 %collective-permute-start.75 = (bf16[256,2048]{1,0:T(8,128)(2,1)}, bf16[256,2048]{1,0:T(8,128)(2,1)}, u32[]{:S(2)}, u32[]{:S(2)}) collective-permute-start(bf16[256,2048]{1,0:T(8,128)(2,1)} %get-tuple-element.272), channel_id=1, source_target_pairs={{0,16},{4,20},{8,24},{12,28},{16,0},{20,4},{24,8},{28,12},{1,17},{... | collective-permute-start | bytes 3145736 | tf_op jit(solution)/shard_map/ppermute | solution.py:29
  512.0 89.7 %reduce-scatter.12.cloned.1.call-start = ((), (), s32[]{:S(2)}) async-start(), calls=%async_computation.8 | async-start | bytes 1310720 | tf_op jit(solution)/shard_map/reduce_scatter | solution.py:920
  514.5 38.9 %collective-permute-start.72 = (bf16[256,2048]{1,0:T(8,128)(2,1)}, bf16[256,2048]{1,0:T(8,128)(2,1)}, u32[]{:S(2)}, u32[]{:S(2)}) collective-permute-start(bf16[256,2048]{1,0:T(8,128)(2,1)} %get-tuple-element.269.refs_3_), channel_id=1, source_target_pairs={{0,8},{4,12},{8,0},{12,4},{16,24},{20,28},{24,16},{28,20},{1,9},{5... | collective-permute-start | bytes 3145736 | tf_op jit(solution)/shard_map/ppermute | solution.py:29
  515.0 38.4 %collective-permute-start.73 = (bf16[256,2048]{1,0:T(8,128)(2,1)}, bf16[256,2048]{1,0:T(8,128)(2,1)}, u32[]{:S(2)}, u32[]{:S(2)}) collective-permute-start(bf16[256,2048]{1,0:T(8,128)(2,1)} %get-tuple-element.270), channel_id=1, source_target_pairs={{0,16},{4,20},{8,24},{12,28},{16,0},{20,4},{24,8},{28,12},{1,17},{... | collective-permute-start | bytes 3145736 | tf_op jit(solution)/shard_map/ppermute | solution.py:29
  535.0 27.4 %collective-permute-start.81 = (bf16[128,2048]{1,0:T(8,128)(2,1)}, bf16[128,2048]{1,0:T(8,128)(2,1)}, u32[]{:S(2)}, u32[]{:S(2)}) collective-permute-start(bf16[128,2048]{1,0:T(8,128)(2,1)} %get-tuple-element.281), channel_id=1, source_target_pairs={{0,8},{4,12},{8,0},{12,4},{16,24},{20,28},{24,16},{28,20},{1,9},{5... | collective-permute-start | bytes 1572872 | tf_op jit(solution)/shard_map/ppermute | solution.py:29
  535.6 28.0 %collective-permute-start.80 = (bf16[128,2048]{1,0:T(8,128)(2,1)}, bf16[128,2048]{1,0:T(8,128)(2,1)}, u32[]{:S(2)}, u32[]{:S(2)}) collective-permute-start(bf16[128,2048]{1,0:T(8,128)(2,1)} %get-tuple-element.275.refs_3_), channel_id=1, source_target_pairs={{0,16},{4,20},{8,24},{12,28},{16,0},{20,4},{24,8},{28,12},{1,17},{... | collective-permute-start | bytes 1572872 | tf_op jit(solution)/shard_map/ppermute | solution.py:29
  570.7 58.5 %reduce-scatter.10.cloned.1.call-start = ((), (), s32[]{:S(2)}) async-start(), calls=%async_computation.7 | async-start | bytes 1310720 | tf_op jit(solution)/shard_map/reduce_scatter | solution.py:920
  570.7 13.4 %collective-permute-start.78 = (bf16[128,2048]{1,0:T(8,128)(2,1)S(1)}, bf16[128,2048]{1,0:T(8,128)(2,1)}, u32[]{:S(2)}, u32[]{:S(2)}) collective-permute-start(bf16[128,2048]{1,0:T(8,128)(2,1)S(1)} %copy-done.13), channel_id=1, source_target_pairs={{0,16},{4,20},{8,24},{12,28},{16,0},{20,4},{24,8},{28,12},{1,17},{... | collective-permute-start | bytes 1572872 | tf_op jit(solution)/shard_map/ppermute | solution.py:29
  571.6 12.5 %collective-permute-start.79 = (bf16[128,2048]{1,0:T(8,128)(2,1)S(1)}, bf16[128,2048]{1,0:T(8,128)(2,1)}, u32[]{:S(2)}, u32[]{:S(2)}) collective-permute-start(bf16[128,2048]{1,0:T(8,128)(2,1)S(1)} %copy-done.21), channel_id=1, source_target_pairs={{0,8},{4,12},{8,0},{12,4},{16,24},{20,28},{24,16},{28,20},{1,9},{5... | collective-permute-start | bytes 1572872 | tf_op jit(solution)/shard_map/ppermute | solution.py:29
  (51 other events, 271.0 us)
Sparse Core Ops, SparseCore 0:
  386.6 34.3 reduce-scatter.5
  490.0 43.5 reduce-scatter.7
  536.4 26.4 reduce-scatter.13
  570.8 26.9 reduce-scatter.11
  599.9 29.2 reduce-scatter.9
